TPU v7x, 32 devices: a whole 2x2x4 slice. The times are simulated.
32 devices in a mesh: groups: 2 (over y), sector: 4 (over z), env: 2 (over x), rep: 2 (over core).
Axes of the slice: x: 2, y: 2, z: 4, core: 2. Of those that a mesh axis runs over, the one named last changes fastest.
Arguments:
- vectors: bfloat16 [2, 192, 256, 256], P(None, ('groups', 'sector'), ('env', 'rep')), parts along dimension 1, may hold values from -6 to 6
- left_env: bfloat16 [2, 192, 256, 256], P('env', ('groups', 'sector'), 'rep'), parts along dimension 1, may hold values from -0.375 to 0.375
- right_env: bfloat16 [2, 192, 256, 256], P('env', ('groups', 'sector'), 'rep'), parts along dimension 1, may hold values from -0.375 to 0.375
- energy: float32 [192], P(('groups', 'sector')), parts along dimension 0, may hold values from 0.5 to 4
- partner: int32 [2, 192], P('env', 'groups'), parts along dimension 1, may hold values from 0 to 95, as said below
Outputs:
- image: float32 [2, 192, 256, 256], P(None, ('groups', 'sector'), ('env', 'rep')), parts along dimension 1
- expectation: float32 [4], P('groups'), parts along dimension 0
There are 2 independent parts, one for each index of `groups`. A program takes and returns all parts, laid end to end along the dimension named above; each array names one. Nothing has to cross between parts.
Inputs may be any that keep to these rules, and one draw needn't show every extreme that they name: For each term, partner is a permutation of the sectors. Reading sectors in groups of 24 (one group an index of sector), the sectors at one position of every group take their partners from the group the same number of groups below (modulo the number of groups), at one common position; for one term no group takes partners for more than 6 of its sectors from one group, and some group takes exactly 6.
All inputs are finite; a program needn't handle non-finite values.
Results may differ from a plain program's by a relative error of at most 0.0035.
Values may be sent and summed in bfloat16 or wider, within the bound.
No kernel may reach another device: no remote copies, remote signals or barrier semaphores. Data moves between devices by JAX's collectives and lax.ppermute only.
A program may use at most 64 MiB of HBM per device.

v0:
```python
import jax
import jax.numpy as jnp
from jax import lax
from jax.sharding import PartitionSpec as P


def on_device(vectors, left_env, right_env, energy, partner):
    sector_count = lax.axis_size("sector")
    per_device = left_env.shape[1]
    order_m = left_env.shape[3]
    half_cols = right_env.shape[2]
    capacity = 2 * ((per_device + 2 * sector_count - 1) // (2 * sector_count))
    sources = partner[0]
    source_dev = sources // per_device
    source_slot = sources % per_device
    my_index = lax.axis_index("sector")
    grid_dev = source_dev.reshape(sector_count, per_device)
    grid_slot = source_slot.reshape(sector_count, per_device)
    from_mine = (grid_dev == my_index).astype(jnp.int32)
    ranking = jnp.cumsum(from_mine, axis=1) - 1
    slot_ids = jnp.arange(capacity, dtype=jnp.int32)
    matches = from_mine[:, :, None] * (ranking[:, :, None] == slot_ids[None, None, :]).astype(
        jnp.int32
    )
    send_rows = jnp.sum(matches * grid_slot[:, :, None], axis=1).reshape(-1)
    own_sources = lax.dynamic_slice_in_dim(source_dev, my_index * per_device, per_device)
    position = jnp.arange(per_device, dtype=jnp.int32)
    earlier = (own_sources[:, None] == own_sources[None, :]) & (
        position[None, :] < position[:, None]
    )
    take_rows = own_sources * capacity + jnp.sum(earlier.astype(jnp.int32), axis=1)
    left_half = left_env[0]
    right_half = right_env[0]
    gathered = lax.all_gather(vectors, ("env", "rep"), axis=2, tiled=True)
    products = jnp.einsum(
        "vsac,sbc->vsab", gathered, right_half, preferred_element_type=jnp.float32
    ).astype(jnp.bfloat16)
    batch = products.shape[0]
    chosen = jnp.take(products, send_rows, axis=1)
    arrived = lax.all_to_all(
        chosen.reshape(batch, sector_count, capacity, order_m, half_cols),
        "sector",
        split_axis=1,
        concat_axis=1,
        tiled=True,
    )
    batch = arrived.shape[0]
    merged = arrived.reshape(batch, sector_count * capacity, order_m, half_cols)
    picked = jnp.take(merged, take_rows, axis=1)
    contributions = jnp.einsum(
        "sia,vsab->vsib",
        lax.all_gather(left_half, "rep", axis=1, tiled=True),
        picked,
        preferred_element_type=jnp.float32,
    )
    shares = lax.psum_scatter(
        contributions.astype(jnp.bfloat16), "env", scatter_dimension=2, tiled=True
    ).astype(jnp.float32)
    traded = lax.all_to_all(
        shares.astype(jnp.bfloat16), "rep", split_axis=2, concat_axis=3, tiled=True
    ).astype(shares.dtype)
    own_block = vectors.astype(jnp.float32)
    applied = traded + energy[None, :, None, None] * own_block
    partial_sum = jnp.sum(own_block * applied, axis=(1, 2, 3))
    summed = lax.psum(partial_sum, ("sector", "env", "rep"))
    entries = per_device * sector_count * order_m * order_m
    return (applied, summed / entries)


def solution(mesh):
    return jax.shard_map(
        on_device,
        mesh=mesh,
        in_specs=(
            P(None, ("groups", "sector"), ("env", "rep"), None),
            P("env", ("groups", "sector"), "rep", None),
            P("env", ("groups", "sector"), "rep", None),
            P(("groups", "sector")),
            P("env", "groups"),
        ),
        out_specs=(P(None, ("groups", "sector"), ("env", "rep"), None), P("groups")),
        check_vma=False,
    )
```

profile of v0, /device:TPU:0, one launch (start us, length us, event | category | flops | bytes accessed | tf_op | source)
XLA Modules:
  0.0 271.8 jit_solution(16902288954003352951)
XLA Ops:
  8.0 0.0 copy-start
  8.0 0.0 copy-start.3
  8.0 0.0 all-gather.4.cloned.1.call-start
  8.1 2.8 %copy.19 = bf16[2,24,64,256]{3,2,0,1:T(8,128)(2,1)} copy(bf16[2,24,64,256]{3,2,1,0:T(8,128)(2,1)} %param.7) | data formatting | bytes 3145728 | tf_op args[0]
  10.9 0.0 all-gather.4.cloned.1.call-update
  10.9 0.0 copy-done.3
  11.0 0.5 broadcast.188
  11.5 0.7 reduce.11
  12.1 0.1 div.25
  12.2 0.1 rem.32
  12.4 0.1 ne.58
  12.5 0.2 reduce_window_sum.11
  12.7 0.2 multiply_reduce_fusion
  12.8 0.1 copy.18
  12.9 0.1 reshape.97
  13.1 47.1 %all-gather.4.cloned.1.call-done = bf16[2,24,256,256]{3,2,0,1:T(8,128)(2,1)} async-done(((bf16[2,24,64,256]{3,2,0,1:T(8,128)(2,1)}), bf16[2,24,256,256]{3,2,0,1:T(8,128)(2,1)}) %all-gather.4.cloned.1.call-update) | async-done | bytes 6291472 | tf_op jit(solution)/shard_map/all_gather | solution.py:34
  60.2 0.0 copy-done
  60.2 6.6 %convert_bitcast_fusion.2 = bf16[2,24,256,128]{2,3,0,1:T(8,128)(2,1)} fusion(bf16[2,24,256,256]{3,2,0,1:T(8,128)(2,1)} %all-gather.4.cloned.1.call-done, bf16[1,24,128,256]{3,2,1,0:T(8,128)(2,1)S(1)} %copy-done), kind=kOutput, calls=%fused_computation.12 | convolution fusion | flops 806879232 | bytes 11010048 | tf_op jit(solution)/shard_map/vsac,sbc->vsab/dot_general | solution.py:35
  66.8 4.4 %gather_fusion = bf16[24,2,256,128]{2,3,1,0:T(8,128)(2,1)} fusion(bf16[2,24,256,128]{2,3,0,1:T(8,128)(2,1)} %convert_bitcast_fusion.2, s32[1024]{0:T(1024)S(1)} %pad_clamp_fusion.1), kind=kCustom, calls=%fused_computation.clone | custom fusion | bytes 6291552 | tf_op jit(solution)/shard_map/jit(_take)/gather | solution.py:39
  71.2 3.9 %broadcast_select_fusion = bf16[24,2,256,128]{2,3,1,0:T(8,128)(2,1)} fusion(bf16[24,2,256,128]{2,3,1,0:T(8,128)(2,1)} %gather_fusion, pred[24]{0:T(512)(128)(4,1)S(1)} %compare_and_fusion.1), kind=kLoop, calls=%fused_computation.14 | loop fusion | flops 1572864 | bytes 6291480 | tf_op jit(solution)/shard_map/jit(_take)/select_n | solution.py:39
  75.1 4.6 %all-to-all-start = ((bf16[2,4,6,256,128]{3,4,0,2,1:T(8,128)(2,1)}), bf16[2,4,6,256,128]{3,4,0,2,1:T(8,128)(2,1)}, u32[]{:S(2)}, u32[]{:S(2)}) async-start(bf16[2,4,6,256,128]{3,4,0,2,1:T(8,128)(2,1)} %bitcast.44), calls=%async_computation | async-start | bytes 6291456 | tf_op jit(solution)/shard_map/all_to_all | solution.py:40
  79.7 0.0 all-gather.6.cloned.1.call-start
  79.8 0.5 all-gather.6.cloned.1.call-update
  80.3 0.0 reduce-scatter.4.cloned.1.call-start
  80.4 0.1 dynamic_slice.3
  80.5 0.2 convert_reduce_fusion
  80.6 0.1 compare_and_fusion
  80.7 70.4 %all-to-all-done = bf16[2,4,6,256,128]{3,4,0,2,1:T(8,128)(2,1)} async-done(((bf16[2,4,6,256,128]{3,4,0,2,1:T(8,128)(2,1)}), bf16[2,4,6,256,128]{3,4,0,2,1:T(8,128)(2,1)}, u32[]{:S(2)}, u32[]{:S(2)}) %all-to-all-start) | async-done | bytes 3145760 | tf_op jit(solution)/shard_map/all_to_all | solution.py:40
  151.2 4.4 %gather_fusion.1 = bf16[24,2,256,128]{2,3,1,0:T(8,128)(2,1)} fusion(bf16[2,24,256,128]{2,3,0,1:T(8,128)(2,1)} %bitcast.8, s32[1024]{0:T(1024)S(1)} %pad_clamp_fusion), kind=kCustom, calls=%fused_computation.1.clone | custom fusion | bytes 6291552 | tf_op jit(solution)/shard_map/jit(_take)/gather | solution.py:49
  155.6 0.0 all-gather.6.cloned.1.call-done
  155.6 5.6 %convert_bitcast_fusion.1 = bf16[2,24,256,128]{2,3,0,1:T(8,128)(2,1)} fusion(bf16[1,24,256,256]{3,2,1,0:T(8,128)(2,1)} %all-gather.6.cloned.1.call-done, bf16[24,2,256,128]{2,3,1,0:T(8,128)(2,1)} %gather_fusion.1, pred[24]{0:T(512)(128)(4,1)S(1)} %get-tuple-element.5), kind=kOutput, calls=%fused_computation.11 | convolution fusion | flops 808452096 | bytes 9437208 | tf_op jit(solution)/shard_map/sia,vsab->vsib/dot_general | solution.py:50
  161.2 8.6 %copy.25 = bf16[2,24,256,128]{3,0,1,2:T(2,128)(2,1)} copy(bf16[2,24,256,128]{2,3,0,1:T(8,128)(2,1)} %convert_bitcast_fusion.1) | data formatting | bytes 6291456
  169.8 7.8 %reshape.127 = bf16[256,6144]{1,0:T(8,128)(2,1)} reshape(bf16[256,24,2,128]{3,2,1,0:T(2,128)(2,1)} %bitcast.45) | data formatting | bytes 6291456
  177.6 0.0 reduce-scatter.4.cloned.1.call-update
  177.6 41.5 %reduce-scatter.4.cloned.1.call-done = bf16[128,6144]{1,0:T(8,128)(2,1)} async-done(((bf16[256,6144]{1,0:T(8,128)(2,1)}), bf16[128,6144]{1,0:T(8,128)(2,1)}) %reduce-scatter.4.cloned.1.call-update) | async-done | bytes 1572880
  219.1 4.1 %reshape.128 = bf16[128,24,2,128]{3,2,1,0:T(2,128)(2,1)S(1)} reshape(bf16[128,6144]{1,0:T(8,128)(2,1)} %reduce-scatter.4.cloned.1.call-done) | data formatting | bytes 3145728
  223.2 0.0 copy-start.1
  223.2 0.0 copy-start.2
  223.2 5.1 %all_to_all.14 = bf16[2,24,128,128]{3,0,1,2:T(2,128)(2,1)S(1)} all-to-all(bf16[2,24,128,128]{3,0,1,2:T(2,128)(2,1)S(1)} %bitcast.46), channel_id=1, replica_groups=mesh['groups'=2,'sector'=4,'env'=2,'rep'=2] {'rep'}, dimensions={2} | all-to-all | bytes 3145728 | tf_op jit(solution)/shard_map/all_to_all | solution.py:59
  228.3 0.4 copy.21
  228.7 0.0 copy-done.1
  228.7 0.0 copy-done.2
  228.7 2.5 fusion.1
  231.3 32.5 %psum.7 = f32[2]{0:T(128)S(1)} all-reduce(f32[2]{0:T(128)S(1)} %get-tuple-element.3), channel_id=1, replica_groups=mesh['groups'=2,'sector'=4,'env'=2,'rep'=2] {'sector','env','rep'}, use_global_device_ids=true, to_apply=%region_5.7 | all-reduce | flops 2 | bytes 16 | tf_op jit(solution)/shard_map/psum | solution.py:65
  263.8 0.5 broadcast_multiply_fusion
  (9 shorter events, 0.1 us)
Async XLA Ops:
  8.0 52.2 %copy-start = (bf16[1,24,128,256]{3,2,1,0:T(8,128)(2,1)S(1)}, bf16[1,24,128,256]{3,2,1,0:T(8,128)(2,1)}, u32[]{:S(2)}) copy-start(bf16[1,24,128,256]{3,2,1,0:T(8,128)(2,1)} %param.9) | copy-start | bytes 4718596
  8.0 2.9 %copy-start.3 = (s32[1,96]{1,0:T(1,128)S(1)}, s32[1,96]{1,0:T(1,128)}, u32[]{:S(2)}) copy-start(s32[1,96]{1,0:T(1,128)} %param.11) | copy-start | bytes 1156
  8.0 52.1 %all-gather.4.cloned.1.call-start = ((), (), s32[]{:S(2)}) async-start(), calls=%async_computation.3 | async-start | bytes 7864320 | tf_op jit(solution)/shard_map/all_gather | solution.py:34
  75.1 76.1 %all-to-all-start = ((bf16[2,4,6,256,128]{3,4,0,2,1:T(8,128)(2,1)}), bf16[2,4,6,256,128]{3,4,0,2,1:T(8,128)(2,1)}, u32[]{:S(2)}, u32[]{:S(2)}) async-start(bf16[2,4,6,256,128]{3,4,0,2,1:T(8,128)(2,1)} %bitcast.44), calls=%async_computation | async-start | bytes 6291456 | tf_op jit(solution)/shard_map/all_to_all | solution.py:40
  79.7 75.8 %all-gather.6.cloned.1.call-start = ((), (), s32[]{:S(2)}) async-start(), calls=%async_computation.4 | async-start | bytes 4718592 | tf_op jit(solution)/shard_map/all_gather | solution.py:52
  80.3 138.8 %reduce-scatter.4.cloned.1.call-start = ((), (), s32[]{:S(2)}) async-start(), calls=%async_computation.5 | async-start | bytes 4718592
  223.2 5.6 %copy-start.1 = (bf16[2,24,64,256]{3,2,1,0:T(8,128)(2,1)S(1)}, bf16[2,24,64,256]{3,2,1,0:T(8,128)(2,1)}, u32[]{:S(2)}) copy-start(bf16[2,24,64,256]{3,2,1,0:T(8,128)(2,1)} %param.7) | copy-start | bytes 4718596
  223.2 5.6 %copy-start.2 = (f32[24]{0:T(128)S(1)}, f32[24]{0:T(128)}, u32[]{:S(2)}) copy-start(f32[24]{0:T(128)} %param.10) | copy-start | bytes 292
Sparse Core Ops, SparseCore 0:
  11.0 49.0 all-gather.3
Sparse Core Ops, SparseCore 1:
  81.8 12.4 all-gather.5
  177.7 41.3 reduce-scatter.3
where the time goes:
time: 273 us; the launch traced here: 272 us
  waiting for transfers between devices  160 us (59%)
  blocking collectives  37.7 us (14%)
  local copies, waits for them, and re-layouts  33.6 us (12%)
  between operations  15.6 us (6%)
  matrix products  12.2 us (4%)
  other arithmetic  8.4 us (3%)
  starting transfers between devices  4.76 us (2%)
    all_to_all x1, waiting for transfers between devices, on_device(): lax.all_to_all(chosen.reshape(batch, sector_count, capacity, order_m, hal...  70.4 us
    all_gather x1, waiting for transfers between devices, on_device(): gathered = lax.all_gather(vectors, ('env', 'rep'), axis=2, tiled=True)  47.1 us
    unnamed x4, waiting for transfers between devices  42 us
    psum x1, blocking collectives, on_device(): summed = lax.psum(partial_sum, ('sector', 'env', 'rep'))  32.5 us
    unnamed x12, local copies, waits for them, and re-layouts  23.3 us
    dot_general x1, matrix products, on_device(): jnp.einsum('vsac,sbc->vsab', gathered, right_half, preferred_element_type...  6.61 us
    dot_general x1, matrix products, on_device(): jnp.einsum('sia,vsab->vsib', lax.all_gather(left_half, 'rep', axis=1, til...  5.59 us
  transfers between devices with their start and end apart: 4, of which 3 were waited for; matrix products, arithmetic and copies ran while one was open for 3% of the time, Pallas kernels for 0%

commit v1 on v0

v1 whole, which is shorter than its diff:
```python
import functools

import jax
import jax.numpy as jnp
from jax import lax
from jax.experimental import pallas as pl
from jax.experimental.pallas import tpu as pltpu
from jax.sharding import PartitionSpec as P

HBM = pl.BlockSpec(memory_space=pl.ANY)
SMEM = pl.BlockSpec(memory_space=pltpu.SMEM)
VMEM = pl.BlockSpec(memory_space=pltpu.VMEM)


def aligned(index, size):
    return pl.multiple_of(index * size, size)


class Sizes:
    def __init__(self, vectors, left_env):
        self.env = lax.axis_size("env")
        self.rep = lax.axis_size("rep")
        self.sector = lax.axis_size("sector")
        self.batch, self.slots, self.own_rows, self.order = vectors.shape
        assert self.batch == self.rep
        self.half = left_env.shape[2]
        self.chip_rows = self.own_rows * self.rep
        self.capacity = 2 * ((self.slots + 2 * self.sector - 1) // (2 * self.sector))
        self.flat = self.sector * self.capacity
        self.source, self.target, self.valid = 0, self.flat, 2 * self.flat
        self.core, self.chip = 3 * self.flat, 3 * self.flat + 1


def plan_body(z, partner, ids, plan, count):
    def clear(i, carry):
        plan[i] = 0
        return carry

    lax.fori_loop(0, 3 * z.flat, clear, 0)
    for d in range(z.sector):
        count[d] = 0

    def place(j, carry):
        sector = partner[0, j]
        group = lax.div(sector, z.slots)
        slot = sector - group * z.slots
        distance = lax.rem(z.sector - group, z.sector)
        rank = count[distance]
        count[distance] = rank + 1
        index = distance * z.capacity + rank
        plan[z.source + index] = slot
        plan[z.target + index] = j
        plan[z.valid + index] = 1
        return carry

    lax.fori_loop(0, z.slots, place, 0)
    plan[z.core] = ids[0]
    plan[z.chip] = ids[1]


def make_plan(z, partner, ids):
    return pl.pallas_call(
        functools.partial(plan_body, z),
        out_shape=jax.ShapeDtypeStruct((3 * z.flat + 2,), jnp.int32),
        in_specs=[SMEM, SMEM],
        out_specs=SMEM,
        scratch_shapes=[pltpu.SMEM((z.sector,), jnp.int32)],
    )(partner, ids)


def products_body(z, first, count, pieces, *refs):
    per_piece = z.rep
    plan = refs[0]
    right = refs[1 : 1 + z.rep]
    rows = refs[1 + z.rep : 1 + z.rep + pieces * per_piece]
    outs = refs[1 + z.rep + pieces * per_piece : -3]
    vbuf, rbuf, sem = refs[-3:]
    core = plan[z.core]

    def copies(n):
        slot = plan[z.source + first + n]
        made = []
        for s in range(z.rep):
            who = lax.rem(core + z.rep - s, z.rep)
            made.append(
                pltpu.make_async_copy(
                    right[s].at[0, slot],
                    rbuf.at[n, pl.ds(aligned(who, z.half), z.half)],
                    sem.at[n, s],
                )
            )
            for piece in range(pieces):
                ref = rows[piece * per_piece + s]
                source = ref.at[core, slot] if s == 0 else ref.at[slot]
                start = pl.multiple_of(piece * z.chip_rows + who * z.own_rows, z.own_rows)
                made.append(
                    pltpu.make_async_copy(
                        source,
                        vbuf.at[n, pl.ds(start, z.own_rows)],
                        sem.at[n, z.rep + piece * per_piece + s],
                    )
                )
        return made

    def begin(n, carry):
        for copy in copies(n):
            copy.start()
        return carry

    lax.fori_loop(0, count, begin, 0)
    each = z.capacity
    for d, out in enumerate(outs):

        def work(i, carry):
            n = d * each + i
            for copy in copies(n):
                copy.wait()
            out[i] = lax.dot_general(
                vbuf[n], rbuf[n], (((1,), (1,)), ((), ())), preferred_element_type=jnp.float32
            ).astype(jnp.bfloat16)
            return carry

        lax.fori_loop(0, each, work, 0)


def products(z, plan, right, rows, distances, pieces):
    count = len(distances) * z.capacity
    height = pieces * z.chip_rows
    block = jax.ShapeDtypeStruct((z.capacity, height, z.order), jnp.bfloat16)
    return pl.pallas_call(
        functools.partial(products_body, z, distances[0] * z.capacity, count, pieces),
        out_shape=[block] * len(distances),
        in_specs=[SMEM] + [HBM] * (len(right) + len(rows)),
        out_specs=[VMEM] * len(distances),
        scratch_shapes=[
            pltpu.VMEM((count, height, z.order), jnp.bfloat16),
            pltpu.VMEM((count, z.order, z.order), jnp.bfloat16),
            pltpu.SemaphoreType.DMA((count, z.rep * (1 + pieces))),
        ],
        cost_estimate=pl.CostEstimate(
            flops=2 * count * height * z.order * z.order,
            bytes_accessed=2 * count * z.order * (z.order + 2 * height),
            transcendentals=0,
        ),
    )(plan, *right, *rows)


def terms_body(z, first, groups, *refs):
    count = groups * z.capacity
    refs = list(refs)
    plan = refs.pop(0)
    left = [refs.pop(0) for _ in range(z.rep)]
    near = [refs.pop(0) for _ in range(groups)]
    far = [refs.pop(0) for _ in range(groups)]
    vec = [[refs.pop(0) for _ in range(z.rep)] for _ in range(z.env)]
    outs = [[refs.pop(0) for _ in range(z.rep)] for _ in range(z.env)]
    dots = refs.pop(0)
    lbuf, pbuf, vbuf, tbuf, sem = refs
    core, chip = plan[z.core], plan[z.chip]

    def copies(d, i):
        n = d * z.capacity + i
        slot = plan[z.target + first + n]
        pairs = []
        for s in range(z.rep):
            who = lax.rem(core + z.rep - s, z.rep)
            pairs.append((left[s].at[0, slot], lbuf.at[n, pl.ds(aligned(who, z.half), z.half)]))
            for e in range(z.env):
                place = lax.rem(chip + z.env - e, z.env) * z.rep + who
                ref = vec[e][s]
                source = ref.at[core, slot] if s == 0 else ref.at[slot]
                pairs.append((source, vbuf.at[n, pl.ds(aligned(place, z.own_rows), z.own_rows)]))
        for e in range(z.env):
            place = lax.rem(chip + z.env - e, z.env)
            if e == 0:
                source = near[d].at[i]
            else:
                source = far[d].at[i, pl.ds((e - 1) * z.chip_rows, z.chip_rows)]
            pairs.append((source, pbuf.at[n, pl.ds(aligned(place, z.chip_rows), z.chip_rows)]))
        return [pltpu.make_async_copy(a, b, sem.at[n, k]) for k, (a, b) in enumerate(pairs)]

    for d in range(groups):

        def begin(i, carry):
            for copy in copies(d, i):
                copy.start()
            return carry

        lax.fori_loop(0, z.capacity, begin, 0)
    dots[...] = jnp.zeros_like(dots)
    for d in range(groups):

        def work(i, carry):
            n = d * z.capacity + i
            for copy in copies(d, i):
                copy.wait()
            term = jnp.dot(lbuf[n], pbuf[n], preferred_element_type=jnp.float32).astype(
                jnp.bfloat16
            )
            tbuf[...] = term
            for e in range(z.env):
                for s in range(z.rep):
                    place = lax.rem(chip + e, z.env) * z.rep + lax.rem(core + s, z.rep)
                    outs[e][s][n] = tbuf[pl.ds(aligned(place, z.own_rows), z.own_rows)]
            both = vbuf[n].astype(jnp.float32) * term.astype(jnp.float32)
            both = jnp.where(plan[z.valid + first + n] == 1, both, 0.0)
            folded = jnp.sum(both.reshape(z.order // 8, 8, z.order), axis=0)
            dots[...] += folded
            return carry

        lax.fori_loop(0, z.capacity, work, 0)


def terms(z, plan, left, near, far, vec, distances):
    groups = len(distances)
    count = groups * z.capacity
    flat = [ref for piece in vec for ref in piece]
    block = jax.ShapeDtypeStruct((count, z.own_rows, z.order), jnp.bfloat16)
    kinds = z.rep * (1 + z.env) + z.env
    whole = (count, z.order, z.order)
    made = pl.pallas_call(
        functools.partial(terms_body, z, distances[0] * z.capacity, groups),
        out_shape=[block] * (z.env * z.rep) + [jax.ShapeDtypeStruct((8, z.order), jnp.float32)],
        in_specs=[SMEM] + [HBM] * (len(left) + len(near) + len(far) + len(flat)),
        out_specs=[VMEM] * (z.env * z.rep + 1),
        scratch_shapes=[
            pltpu.VMEM(whole, jnp.bfloat16),
            pltpu.VMEM(whole, jnp.bfloat16),
            pltpu.VMEM(whole, jnp.bfloat16),
            pltpu.VMEM((z.order, z.order), jnp.bfloat16),
            pltpu.SemaphoreType.DMA((count, kinds)),
        ],
        cost_estimate=pl.CostEstimate(
            flops=2 * count * z.order**3,
            bytes_accessed=8 * count * z.order * z.order,
            transcendentals=0,
        ),
    )(plan, *left, *near, *far, *flat)
    blocks = [made[e * z.rep : (e + 1) * z.rep] for e in range(z.env)]
    return blocks, made[-1]


def image_body(z, sizes, *refs):
    refs = list(refs)
    plans = [refs.pop(0) for _ in range(z.env)]
    energy, vectors = refs.pop(0), refs.pop(0)
    parts = [[[refs.pop(0) for _ in sizes] for _ in range(z.rep)] for _ in range(z.env)]
    image = refs.pop(0)
    core = plans[0][z.core]

    def start(j, carry):
        for v in range(z.batch):
            image[v, j] = energy[j] * vectors[v, j].astype(jnp.float32)
        return carry

    lax.fori_loop(0, z.slots, start, 0)
    for e, plan in enumerate(plans):
        first = 0
        for g, count in enumerate(sizes):

            def add(n, carry):
                slot = plan[z.target + first + n]

                @pl.when(plan[z.valid + first + n] == 1)
                def _():
                    for s in range(z.rep):
                        v = lax.rem(core + z.rep - s, z.rep)
                        image[v, slot] += parts[e][s][g][n].astype(jnp.float32)

                return carry

            lax.fori_loop(0, count, add, 0)
            first += count


def make_image(z, plans, energy, vectors, parts):
    sizes = tuple(block.shape[0] for block in parts[0][0])
    flat = [ref for piece in parts for kind in piece for ref in kind]
    return pl.pallas_call(
        functools.partial(image_body, z, sizes),
        out_shape=jax.ShapeDtypeStruct(vectors.shape, jnp.float32),
        in_specs=[SMEM] * (z.env + 1) + [VMEM] * (len(flat) + 1),
        out_specs=VMEM,
    )(*plans, energy, vectors, *flat)


def shift(array, axis, size, step):
    return lax.ppermute(array, axis, [(i, (i + step) % size) for i in range(size)])


def shift_both(z, array, e, s):
    perm = []
    for x in range(z.env):
        for c in range(z.rep):
            perm.append((x * z.rep + c, (x + e) % z.env * z.rep + (c + s) % z.rep))
    return lax.ppermute(array, ("env", "rep"), perm)


def total_over(array, axis):
    size = lax.axis_size(axis)
    if size & (size - 1):
        return lax.psum(array, axis)
    step = 1
    while step < size:
        array = array + lax.ppermute(array, axis, [(i, i ^ step) for i in range(size)])
        step *= 2
    return array


def on_device(vectors, left_env, right_env, energy, partner):
    z = Sizes(vectors, left_env)
    core, chip = lax.axis_index("rep"), lax.axis_index("env")
    ids = jnp.stack([core, chip]).astype(jnp.int32)

    def rows_for(array, s):
        wanted = lax.rem(core + s, z.rep)
        own = lax.dynamic_index_in_dim(array, wanted, axis=0, keepdims=False)
        return shift(own, "rep", z.rep, s)

    others = [shift(vectors, "env", z.env, e) for e in range(1, z.env)]
    plan = make_plan(z, partner, ids)
    plans = [plan]
    for e in range(1, z.env):
        plans.append(make_plan(z, shift(partner, "env", z.env, e), ids))
    right = [right_env] + [shift(right_env, "rep", z.rep, s) for s in range(1, z.rep)]
    near_rows = [vectors] + [rows_for(vectors, s) for s in range(1, z.rep)]
    left = [left_env] + [shift(left_env, "rep", z.rep, s) for s in range(1, z.rep)]

    many = min(z.sector, 4)
    each = z.sector // many
    groups = [list(range(g * each, (g + 1) * each)) for g in range(many)]
    order = groups[1:] + groups[:1]

    def across(array, distance):
        return shift(array, "sector", z.sector, distance) if distance else array

    near = {}
    for distances in order:
        made = products(z, plan, right, near_rows, distances, 1)
        for distance, block in zip(distances, made):
            near[distance] = across(block, distance)
    vec = [near_rows]
    for other in others:
        vec.append([other] + [rows_for(other, s) for s in range(1, z.rep)])
    far_rows = [ref for piece in vec[1:] for ref in piece]
    far = {}
    for distances in order:
        made = products(z, plan, right, far_rows, distances, z.env - 1)
        for distance, block in zip(distances, made):
            far[distance] = across(block, distance)

    own_block = vectors.astype(jnp.float32)
    partial_sum = jnp.sum(energy[None, :, None, None] * own_block * own_block, axis=(1, 2, 3))
    parts = [[[] for _ in range(z.rep)] for _ in range(z.env)]
    dots = 0.0
    for distances in groups:
        blocks, folded = terms(
            z, plan, left, [near[d] for d in distances], [far[d] for d in distances], vec, distances
        )
        dots = dots + folded
        for e in range(z.env):
            for s in range(z.rep):
                block = blocks[e][s]
                parts[e][s].append(block if e + s == 0 else shift_both(z, block, e, s))
    image = make_image(z, plans, energy, vectors, parts)
    own_vector = (jnp.arange(z.batch) == core).astype(jnp.float32)
    partial_sum = partial_sum + own_vector * jnp.sum(dots)
    for axis in ("rep", "env", "sector"):
        partial_sum = total_over(partial_sum, axis)
    entries = z.slots * z.sector * z.order * z.order
    return (image, partial_sum / entries)


def solution(mesh):
    return jax.shard_map(
        on_device,
        mesh=mesh,
        in_specs=(
            P(None, ("groups", "sector"), ("env", "rep"), None),
            P("env", ("groups", "sector"), "rep", None),
            P("env", ("groups", "sector"), "rep", None),
            P(("groups", "sector")),
            P("env", "groups"),
        ),
        out_specs=(P(None, ("groups", "sector"), ("env", "rep"), None), P("groups")),
        check_vma=False,
    )
```

time: 273 us -> 175 us (0.64)
  waiting for transfers between devices: 160 us -> 60.4 us
  Pallas kernels: 0 us -> 58.7 us
  starting transfers between devices: 4.76 us -> 42.5 us
  blocking collectives: 37.7 us -> 0 us
  local copies, waits for them, and re-layouts: 33.6 us -> 6.04 us
  between operations: 15.6 us -> 1.17 us
  matrix products: 12.2 us -> 0 us
  other arithmetic: 8.4 us -> 4.54 us
    all_to_all x1 -> x0, waiting for transfers between devices: 70.4 us -> none  [on_device(): lax.all_to_all(chosen.reshape(batch, sector_count, capacity, order_m, hal...]
    ppermute x0 -> x28, waiting for transfers between devices: none -> 60.4 us  [the longest x12 40.5 us: shift(): lax.ppermute(array, axis, [(i, (i + step) % size) for i in range(size)])]
    pallas_call x0 -> x15, Pallas kernels: none -> 58.7 us  [the longest x8 30.5 us: products(): pl.pallas_call(functools.partial(products_body, z, distances[0] * z.capac...]
    all_gather x2 -> x0, waiting for transfers between devices: 47.1 us -> none  [the longest x1 47.1 us: on_device(): gathered = lax.all_gather(vectors, ('env', 'rep'), axis=2, tiled=True)]
    ppermute x0 -> x28, starting transfers between devices: none -> 42.5 us  [the longest x4 20.7 us: total_over(): lax.ppermute(array, axis, [(i, i ^ step) for i in range(size)])]
    unnamed x4 -> x0, waiting for transfers between devices: 42 us -> none
    psum x1 -> x0, blocking collectives: 32.5 us -> none  [on_device(): summed = lax.psum(partial_sum, ('sector', 'env', 'rep'))]
    unnamed x12 -> x68, local copies, waits for them, and re-layouts: 23.3 us -> 2.93 us
  transfers between devices with their start and end apart: 4 -> 28, of which waited for: 3 -> 11; matrix products, arithmetic and copies ran while one was open for 3% -> 4% of each run, Pallas kernels for 0% -> 30%
where the time goes in v1:
time: 175 us; the launch traced here: 173 us
  waiting for transfers between devices  60.4 us (35%)
  Pallas kernels  58.7 us (34%)
  starting transfers between devices  42.5 us (24%)
  local copies, waits for them, and re-layouts  6.04 us (3%)
  other arithmetic  4.54 us (3%)
    ppermute x12, waiting for transfers between devices, shift(): lax.ppermute(array, axis, [(i, (i + step) % size) for i in range(size)])  40.5 us
    pallas_call x8, Pallas kernels, products(): pl.pallas_call(functools.partial(products_body, z, distances[0] * z.capac...  30.5 us
    ppermute x4, starting transfers between devices, total_over(): lax.ppermute(array, axis, [(i, i ^ step) for i in range(size)])  20.7 us
    pallas_call x4, Pallas kernels, terms(): pl.pallas_call(functools.partial(terms_body, z, distances[0] * z.capacity...  18.1 us
    ppermute x12, starting transfers between devices, shift(): lax.ppermute(array, axis, [(i, (i + step) % size) for i in range(size)])  14.4 us
    ppermute x12, waiting for transfers between devices, shift_both(): return lax.ppermute(array, ('env', 'rep'), perm)  13.8 us
    ppermute x12, starting transfers between devices, shift_both(): return lax.ppermute(array, ('env', 'rep'), perm)  7.42 us
    ppermute x4, waiting for transfers between devices, total_over(): lax.ppermute(array, axis, [(i, i ^ step) for i in range(size)])  6.13 us
  transfers between devices with their start and end apart: 28, of which 11 were waited for; matrix products, arithmetic and copies ran while one was open for 4% of the time, Pallas kernels for 30%

profile of v1, /device:TPU:0, one launch (start us, length us, event | category | flops | bytes accessed | tf_op | source)
XLA Modules:
  0.0 173.4 jit_solution(4711533507316021965)
XLA Ops:
  0.6 3.0 %collective-permute-start.4 = (bf16[2,24,64,256]{3,2,1,0:T(8,128)(2,1)}, bf16[2,24,64,256]{3,2,1,0:T(8,128)(2,1)S(1)}, u32[]{:S(2)}, u32[]{:S(2)}) collective-permute-start(bf16[2,24,64,256]{3,2,1,0:T(8,128)(2,1)} %refs_3_.9), channel_id=1, source_target_pairs={{0,2},{2,0},{1,3},{3,1},{4,6},{6,4},{5,7},{7,5},{8,10},{10,8},{9,1... | collective-permute-start | bytes 4718600 | tf_op jit(solution)/shard_map/ppermute | solution.py:288
  3.6 0.5 collective-permute-start.1
  4.1 2.1 %dynamic-slice_bitcast_fusion.1 = bf16[24,64,256]{2,1,0:T(8,128)(2,1)} fusion(bf16[2,24,64,256]{3,2,1,0:T(8,128)(2,1)} %refs_3_.9, s32[]{:T(128)S(6)} %select_n.5), kind=kLoop, calls=%fused_computation.3 | loop fusion | bytes 1572868 | tf_op jit(solution)/shard_map/jit(dynamic_index_in_dim)/squeeze | solution.py:317
  6.2 32.0 %collective-permute-done.4.refs_3_.refs_7_ = bf16[2,24,64,256]{3,2,1,0:T(8,128)(2,1)S(1)} collective-permute-done((bf16[2,24,64,256]{3,2,1,0:T(8,128)(2,1)}, bf16[2,24,64,256]{3,2,1,0:T(8,128)(2,1)S(1)}, u32[]{:S(2)}, u32[]{:S(2)}) %collective-permute-start.4) | collective-permute-done | bytes 1572896 | tf_op jit(solution)/shard_map/ppermute | solution.py:288
  38.2 1.0 dynamic-slice_bitcast_fusion
  39.3 0.6 pad_add_fusion.ids
  39.8 2.1 %shard_map.68.refs_0_ = s32[74]{0:T(128)} custom-call(s32[1,96]{1,0:T(1,128)} %partner.1, s32[2]{0:T(128)} %pad_add_fusion.ids), custom_call_target="tpu_custom_call" | custom-call | tf_op jit(solution)/shard_map/pallas_call | solution.py:62
  42.0 1.1 copy-done.2
  43.1 3.8 %shard_map.73 = bf16[6,128,256]{2,1,0:T(8,128)(2,1)} custom-call(s32[74]{0:T(128)} %shard_map.68.refs_0_, bf16[1,24,128,256]{3,2,1,0:T(8,128)(2,1)} %refs_1_.22, bf16[1,24,128,256]{3,2,1,0:T(8,128)(2,1)} %copy-done.2, bf16[2,24,64,256]{3,2,1,0:T(8,128)(2,1)} %refs_3_.9, bf16[24,64,256]{2,1,0:T(8,128)(2,1)} %collective-permute-done.3.refs_4_.refs_6_), custom_call_target="tpu_custom_call" | custom-call | flops 100663296 | bytes 1572864 | tf_op jit(solution)/shard_map/pallas_call | solution.py:130
  47.0 1.9 %collective-permute-start.6 = (bf16[6,128,256]{2,1,0:T(8,128)(2,1)}, bf16[6,128,256]{2,1,0:T(8,128)(2,1)S(1)}, u32[]{:S(2)}, u32[]{:S(2)}) collective-permute-start(bf16[6,128,256]{2,1,0:T(8,128)(2,1)} %shard_map.73), channel_id=1, source_target_pairs={{0,4},{4,8},{8,12},{12,0},{1,5},{5,9},{9,13},{13,1},{2,6},{6,10},{... | collective-permute-start | bytes 1179656 | tf_op jit(solution)/shard_map/ppermute | solution.py:288
  48.8 3.8 %shard_map.74 = bf16[6,128,256]{2,1,0:T(8,128)(2,1)} custom-call(s32[74]{0:T(128)} %shard_map.68.refs_0_, bf16[1,24,128,256]{3,2,1,0:T(8,128)(2,1)} %refs_1_.22, bf16[1,24,128,256]{3,2,1,0:T(8,128)(2,1)} %copy-done.2, bf16[2,24,64,256]{3,2,1,0:T(8,128)(2,1)} %copy-done.1, bf16[24,64,256]{2,1,0:T(8,128)(2,1)} %collective-permute-done.5.refs_4_.refs_8_), custom_call_target="tpu_custom_call" | custom-call | flops 100663296 | bytes 1572864 | tf_op jit(solution)/shard_map/pallas_call | solution.py:130
  52.7 1.6 collective-permute-start.7
  54.3 3.8 %shard_map.76 = bf16[6,128,256]{2,1,0:T(8,128)(2,1)} custom-call(s32[74]{0:T(128)} %shard_map.68.refs_0_, bf16[1,24,128,256]{3,2,1,0:T(8,128)(2,1)} %refs_1_.22, bf16[1,24,128,256]{3,2,1,0:T(8,128)(2,1)} %copy-done.2, bf16[2,24,64,256]{3,2,1,0:T(8,128)(2,1)} %refs_3_.9, bf16[24,64,256]{2,1,0:T(8,128)(2,1)} %collective-permute-done.3.refs_4_.refs_6_), custom_call_target="tpu_custom_call" | custom-call | flops 100663296 | bytes 1572864 | tf_op jit(solution)/shard_map/pallas_call | solution.py:130
  58.1 1.1 collective-permute-start.8
  59.2 3.8 %shard_map.77 = bf16[6,128,256]{2,1,0:T(8,128)(2,1)} custom-call(s32[74]{0:T(128)} %shard_map.68.refs_0_, bf16[1,24,128,256]{3,2,1,0:T(8,128)(2,1)} %refs_1_.22, bf16[1,24,128,256]{3,2,1,0:T(8,128)(2,1)} %copy-done.2, bf16[2,24,64,256]{3,2,1,0:T(8,128)(2,1)} %copy-done.1, bf16[24,64,256]{2,1,0:T(8,128)(2,1)} %collective-permute-done.5.refs_4_.refs_8_), custom_call_target="tpu_custom_call" | custom-call | flops 100663296 | bytes 1572864 | tf_op jit(solution)/shard_map/pallas_call | solution.py:130
  63.0 1.9 %collective-permute-start.9 = (bf16[6,128,256]{2,1,0:T(8,128)(2,1)}, bf16[6,128,256]{2,1,0:T(8,128)(2,1)S(1)}, u32[]{:S(2)}, u32[]{:S(2)}) collective-permute-start(bf16[6,128,256]{2,1,0:T(8,128)(2,1)} %shard_map.77), channel_id=1, source_target_pairs={{0,8},{4,12},{8,0},{12,4},{1,9},{5,13},{9,1},{13,5},{2,10},{6,14},... | collective-permute-start | bytes 1179656 | tf_op jit(solution)/shard_map/ppermute | solution.py:288
  65.0 3.8 %shard_map.79 = bf16[6,128,256]{2,1,0:T(8,128)(2,1)} custom-call(s32[74]{0:T(128)} %shard_map.68.refs_0_, bf16[1,24,128,256]{3,2,1,0:T(8,128)(2,1)} %refs_1_.22, bf16[1,24,128,256]{3,2,1,0:T(8,128)(2,1)} %copy-done.2, bf16[2,24,64,256]{3,2,1,0:T(8,128)(2,1)} %refs_3_.9, bf16[24,64,256]{2,1,0:T(8,128)(2,1)} %collective-permute-done.3.refs_4_.refs_6_), custom_call_target="tpu_custom_call" | custom-call | flops 100663296 | bytes 1572864 | tf_op jit(solution)/shard_map/pallas_call | solution.py:130
  68.7 0.0 copy-start.23
  68.8 2.3 %collective-permute-start.10 = (bf16[6,128,256]{2,1,0:T(8,128)(2,1)}, bf16[6,128,256]{2,1,0:T(8,128)(2,1)S(1)}, u32[]{:S(2)}, u32[]{:S(2)}) collective-permute-start(bf16[6,128,256]{2,1,0:T(8,128)(2,1)} %shard_map.79), channel_id=1, source_target_pairs={{0,12},{4,0},{8,4},{12,8},{1,13},{5,1},{9,5},{13,9},{2,14},{6,2},{... | collective-permute-start | bytes 1179656 | tf_op jit(solution)/shard_map/ppermute | solution.py:288
  71.1 3.8 %shard_map.80 = bf16[6,128,256]{2,1,0:T(8,128)(2,1)} custom-call(s32[74]{0:T(128)} %shard_map.68.refs_0_, bf16[1,24,128,256]{3,2,1,0:T(8,128)(2,1)} %refs_1_.22, bf16[1,24,128,256]{3,2,1,0:T(8,128)(2,1)} %copy-done.2, bf16[2,24,64,256]{3,2,1,0:T(8,128)(2,1)} %copy-done.1, bf16[24,64,256]{2,1,0:T(8,128)(2,1)} %collective-permute-done.5.refs_4_.refs_8_), custom_call_target="tpu_custom_call" | custom-call | flops 100663296 | bytes 1572864 | tf_op jit(solution)/shard_map/pallas_call | solution.py:130
  74.9 0.4 collective-permute-start.11
  75.3 0.9 fusion
  76.2 3.8 %shard_map.70.refs_3_ = bf16[6,128,256]{2,1,0:T(8,128)(2,1)} custom-call(s32[74]{0:T(128)} %shard_map.68.refs_0_, bf16[1,24,128,256]{3,2,1,0:T(8,128)(2,1)} %refs_1_.22, bf16[1,24,128,256]{3,2,1,0:T(8,128)(2,1)} %copy-done.2, bf16[2,24,64,256]{3,2,1,0:T(8,128)(2,1)} %refs_3_.9, bf16[24,64,256]{2,1,0:T(8,128)(2,1)} %collective-permute-done.3.refs_4_.refs_6_), custom_call_target="tpu_custom_call" | custom-call | flops 100663296 | bytes 1572864 | tf_op jit(solution)/shard_map/pallas_call | solution.py:130
  80.0 3.8 %shard_map.71.refs_4_ = bf16[6,128,256]{2,1,0:T(8,128)(2,1)} custom-call(s32[74]{0:T(128)} %shard_map.68.refs_0_, bf16[1,24,128,256]{3,2,1,0:T(8,128)(2,1)} %refs_1_.22, bf16[1,24,128,256]{3,2,1,0:T(8,128)(2,1)} %copy-done.2, bf16[2,24,64,256]{3,2,1,0:T(8,128)(2,1)} %copy-done.1, bf16[24,64,256]{2,1,0:T(8,128)(2,1)} %collective-permute-done.5.refs_4_.refs_8_), custom_call_target="tpu_custom_call" | custom-call | flops 100663296 | bytes 1572864 | tf_op jit(solution)/shard_map/pallas_call | solution.py:130
  83.9 0.0 copy-start.32
  83.9 4.5 %shard_map.72 = (bf16[6,64,256]{2,1,0:T(8,128)(2,1)}, bf16[6,64,256]{2,1,0:T(8,128)(2,1)}, bf16[6,64,256]{2,1,0:T(8,128)(2,1)}, bf16[6,64,256]{2,1,0:T(8,128)(2,1)}, f32[8,256]{1,0:T(8,128)}) custom-call(s32[74]{0:T(128)} %shard_map.68.refs_0_, bf16[1,24,128,256]{3,2,1,0:T(8,128)(2,1)} %refs_1_.23, bf16[1,24,128,256]{3,2,1,0:T(8,128)(2,1)} %collective-permute-done.1.refs_2_, ...), custom_call_target="tpu_custom_call" | custom-call | flops 201326592 | bytes 3145728 | tf_op jit(solution)/shard_map/pallas_call | solution.py:221
  88.5 1.6 collective-permute-start
  90.1 4.5 %shard_map.75 = (bf16[6,64,256]{2,1,0:T(8,128)(2,1)}, bf16[6,64,256]{2,1,0:T(8,128)(2,1)}, bf16[6,64,256]{2,1,0:T(8,128)(2,1)}, bf16[6,64,256]{2,1,0:T(8,128)(2,1)}, f32[8,256]{1,0:T(8,128)}) custom-call(s32[74]{0:T(128)} %shard_map.68.refs_0_, bf16[1,24,128,256]{3,2,1,0:T(8,128)(2,1)} %refs_1_.23, bf16[1,24,128,256]{3,2,1,0:T(8,128)(2,1)} %collective-permute-done.1.refs_2_, ...), custom_call_target="tpu_custom_call" | custom-call | flops 201326592 | bytes 3145728 | tf_op jit(solution)/shard_map/pallas_call | solution.py:221
  94.6 0.1 collective-permute-done.8.refs_3_
  94.8 8.4 %collective-permute-done.9.refs_4_ = bf16[6,128,256]{2,1,0:T(8,128)(2,1)S(1)} collective-permute-done((bf16[6,128,256]{2,1,0:T(8,128)(2,1)}, bf16[6,128,256]{2,1,0:T(8,128)(2,1)S(1)}, u32[]{:S(2)}, u32[]{:S(2)}) %collective-permute-start.9) | collective-permute-done | bytes 393248 | tf_op jit(solution)/shard_map/ppermute | solution.py:288
  103.1 1.5 collective-permute-start.16
  104.6 4.5 %shard_map.78 = (bf16[6,64,256]{2,1,0:T(8,128)(2,1)}, bf16[6,64,256]{2,1,0:T(8,128)(2,1)}, bf16[6,64,256]{2,1,0:T(8,128)(2,1)}, bf16[6,64,256]{2,1,0:T(8,128)(2,1)}, f32[8,256]{1,0:T(8,128)}) custom-call(s32[74]{0:T(128)} %shard_map.68.refs_0_, bf16[1,24,128,256]{3,2,1,0:T(8,128)(2,1)} %refs_1_.23, bf16[1,24,128,256]{3,2,1,0:T(8,128)(2,1)} %collective-permute-done.1.refs_2_, ...), custom_call_target="tpu_custom_call" | custom-call | flops 201326592 | bytes 3145728 | tf_op jit(solution)/shard_map/pallas_call | solution.py:221
  109.2 0.0 copy-start.3
  109.3 0.3 collective-permute-start.20
  109.6 0.3 copy-done.3
  109.9 0.8 copy-done.4
  110.7 4.5 %shard_map.81 = (bf16[6,64,256]{2,1,0:T(8,128)(2,1)}, bf16[6,64,256]{2,1,0:T(8,128)(2,1)}, bf16[6,64,256]{2,1,0:T(8,128)(2,1)}, bf16[6,64,256]{2,1,0:T(8,128)(2,1)}, f32[8,256]{1,0:T(8,128)}) custom-call(s32[74]{0:T(128)} %shard_map.68.refs_0_, bf16[1,24,128,256]{3,2,1,0:T(8,128)(2,1)} %refs_1_.23, bf16[1,24,128,256]{3,2,1,0:T(8,128)(2,1)} %collective-permute-done.1.refs_2_, ...), custom_call_target="tpu_custom_call" | custom-call | flops 201326592 | bytes 3145728 | tf_op jit(solution)/shard_map/pallas_call | solution.py:221
  115.2 1.3 add_reduce_fusion
  116.5 0.6 fusion.1
  117.2 0.4 collective-permute-start.24
  117.5 0.8 collective-permute-done.24
  118.4 0.6 fusion.2
  119.0 1.3 collective-permute-start.25
  120.4 2.3 %collective-permute-done.25 = f32[2]{0:T(128)S(1)} collective-permute-done((f32[2]{0:T(128)S(1)}, f32[2]{0:T(128)S(1)}, u32[]{:S(2)}, u32[]{:S(2)}) %collective-permute-start.25) | collective-permute-done | bytes 40 | tf_op jit(solution)/shard_map/ppermute | solution.py:305
  122.6 0.0 copy-start.33
  122.7 1.3 collective-permute-start.17
  124.0 0.6 collective-permute-start.21
  124.6 15.6 %collective-permute-start.26 = (f32[2]{0:T(128)S(1)}, f32[2]{0:T(128)S(1)}, u32[]{:S(2)}, u32[]{:S(2)}) collective-permute-start(f32[2]{0:T(128)S(1)} %add.40), channel_id=1, source_target_pairs={{0,4},{4,0},{8,12},{12,8},{1,5},{5,1},{9,13},{13,9},{2,6},{6,2},{1... | collective-permute-start | bytes 32 | tf_op jit(solution)/shard_map/ppermute | solution.py:305
  140.3 1.5 collective-permute-done.26
  141.8 2.1 %shard_map.69.refs_1_ = s32[74]{0:T(128)} custom-call(s32[1,96]{1,0:T(1,128)} %copy-done.33, s32[2]{0:T(128)} %pad_add_fusion.ids), custom_call_target="tpu_custom_call" | custom-call | tf_op jit(solution)/shard_map/pallas_call | solution.py:62
  144.0 3.3 %collective-permute-start.27 = (f32[2]{0:T(128)S(1)}, f32[2]{0:T(128)S(1)}, u32[]{:S(2)}, u32[]{:S(2)}) collective-permute-start(f32[2]{0:T(128)S(1)} %add.41), channel_id=1, source_target_pairs={{0,8},{4,12},{8,0},{12,4},{1,9},{5,13},{9,1},{13,5},{2,10},{6,14},... | collective-permute-start | bytes 32 | tf_op jit(solution)/shard_map/ppermute | solution.py:305
  147.3 1.5 collective-permute-done.27
  148.9 1.3 collective-permute-start.18
  150.1 0.1 collective-permute-start.22
  150.2 0.8 collective-permute-start.15
  151.1 1.3 collective-permute-start.19
  152.4 0.2 collective-permute-start.23
  152.5 0.5 add_multiply_fusion
  153.0 3.6 %collective-permute-done.18.refs_14_ = bf16[6,64,256]{2,1,0:T(8,128)(2,1)S(1)} collective-permute-done((bf16[6,64,256]{2,1,0:T(8,128)(2,1)S(1)}, bf16[6,64,256]{2,1,0:T(8,128)(2,1)S(1)}, u32[]{:S(2)}, u32[]{:S(2)}) %collective-permute-start.18) | collective-permute-done | bytes 196640 | tf_op jit(solution)/shard_map/ppermute | solution.py:296
  156.7 3.0 %collective-permute-done.22.refs_18_ = bf16[6,64,256]{2,1,0:T(8,128)(2,1)S(1)} collective-permute-done((bf16[6,64,256]{2,1,0:T(8,128)(2,1)S(1)}, bf16[6,64,256]{2,1,0:T(8,128)(2,1)S(1)}, u32[]{:S(2)}, u32[]{:S(2)}) %collective-permute-start.22) | collective-permute-done | bytes 196640 | tf_op jit(solution)/shard_map/ppermute | solution.py:296
  159.7 5.4 %collective-permute-done.19.refs_15_ = bf16[6,64,256]{2,1,0:T(8,128)(2,1)S(1)} collective-permute-done((bf16[6,64,256]{2,1,0:T(8,128)(2,1)}, bf16[6,64,256]{2,1,0:T(8,128)(2,1)S(1)}, u32[]{:S(2)}, u32[]{:S(2)}) %collective-permute-start.19) | collective-permute-done | bytes 196640 | tf_op jit(solution)/shard_map/ppermute | solution.py:296
  165.1 1.7 collective-permute-done.23.refs_19_
  166.9 0.6 copy-done.19
  167.5 5.9 %shard_map.82 = f32[2,24,64,256]{3,2,1,0:T(8,128)} custom-call(s32[74]{0:T(128)} %shard_map.68.refs_0_, s32[74]{0:T(128)} %shard_map.69.refs_1_, f32[24]{0:T(128)} %refs_2_.1, bf16[2,24,64,256]{3,2,1,0:T(8,128)(2,1)} %refs_3_.9, bf16[6,64,256]{2,1,0:T(8,128)(2,1)} %get-tuple-element.22.refs_4_, bf16[6,64,256]{2,1,0:T(8,128)(2,1)} %get-tuple-element.23.refs_5_, ...), custom_call_target="tpu_custom_call" | custom-call | tf_op jit(solution)/shard_map/pallas_call | solution.py:279
  (85 shorter events, 0.2 us)
Async XLA Ops:
  0.6 37.6 %collective-permute-start.4 = (bf16[2,24,64,256]{3,2,1,0:T(8,128)(2,1)}, bf16[2,24,64,256]{3,2,1,0:T(8,128)(2,1)S(1)}, u32[]{:S(2)}, u32[]{:S(2)}) collective-permute-start(bf16[2,24,64,256]{3,2,1,0:T(8,128)(2,1)} %refs_3_.9), channel_id=1, source_target_pairs={{0,2},{2,0},{1,3},{3,1},{4,6},{6,4},{5,7},{7,5},{8,10},{10,8},{9,1... | collective-permute-start | bytes 4718600 | tf_op jit(solution)/shard_map/ppermute | solution.py:288
  3.6 38.4 %collective-permute-start.2 = (bf16[1,24,128,256]{3,2,1,0:T(8,128)(2,1)}, bf16[1,24,128,256]{3,2,1,0:T(8,128)(2,1)S(1)}, u32[]{:S(2)}, u32[]{:S(2)}) collective-permute-start(bf16[1,24,128,256]{3,2,1,0:T(8,128)(2,1)} %refs_1_.22), channel_id=1, source_target_pairs={{0,1},{1,0},{2,3},{3,2},{4,5},{5,4},{6,7},{7,6},{8,9},{9,8},{10,11... | collective-permute-start | bytes 4718600 | tf_op jit(solution)/shard_map/ppermute | solution.py:288
  3.6 65.1 %collective-permute-start.1 = (bf16[1,24,128,256]{3,2,1,0:T(8,128)(2,1)}, bf16[1,24,128,256]{3,2,1,0:T(8,128)(2,1)}, u32[]{:S(2)}, u32[]{:S(2)}) collective-permute-start(bf16[1,24,128,256]{3,2,1,0:T(8,128)(2,1)} %refs_1_.23), channel_id=1, source_target_pairs={{0,1},{1,0},{2,3},{3,2},{4,5},{5,4},{6,7},{7,6},{8,9},{9,8},{10,11... | collective-permute-start | bytes 4718600 | tf_op jit(solution)/shard_map/ppermute | solution.py:288
  6.2 35.8 %collective-permute-start.3 = (bf16[24,64,256]{2,1,0:T(8,128)(2,1)}, bf16[24,64,256]{2,1,0:T(8,128)(2,1)}, u32[]{:S(2)}, u32[]{:S(2)}) collective-permute-start(bf16[24,64,256]{2,1,0:T(8,128)(2,1)} %dynamic-slice_bitcast_fusion.1), channel_id=1, source_target_pairs={{0,1},{1,0},{2,3},{3,2},{4,5},{5,4},{6,7},{7,6},{8,9},{9,8},{10,11... | collective-permute-start | bytes 2359304 | tf_op jit(solution)/shard_map/ppermute | solution.py:288
  38.2 8.7 %copy-start.1 = (bf16[2,24,64,256]{3,2,1,0:T(8,128)(2,1)}, bf16[2,24,64,256]{3,2,1,0:T(8,128)(2,1)S(1)}, u32[]{:S(2)}) copy-start(bf16[2,24,64,256]{3,2,1,0:T(8,128)(2,1)S(1)} %collective-permute-done.4.refs_3_.refs_7_) | copy-start | bytes 4718596
  39.3 9.6 %collective-permute-start.5 = (bf16[24,64,256]{2,1,0:T(8,128)(2,1)}, bf16[24,64,256]{2,1,0:T(8,128)(2,1)}, u32[]{:S(2)}, u32[]{:S(2)}) collective-permute-start(bf16[24,64,256]{2,1,0:T(8,128)(2,1)} %dynamic-slice_bitcast_fusion), channel_id=1, source_target_pairs={{0,1},{1,0},{2,3},{3,2},{4,5},{5,4},{6,7},{7,6},{8,9},{9,8},{10,11... | collective-permute-start | bytes 2359304 | tf_op jit(solution)/shard_map/ppermute | solution.py:288
  42.0 1.1 copy-start.2
  47.0 27.9 %collective-permute-start.6 = (bf16[6,128,256]{2,1,0:T(8,128)(2,1)}, bf16[6,128,256]{2,1,0:T(8,128)(2,1)S(1)}, u32[]{:S(2)}, u32[]{:S(2)}) collective-permute-start(bf16[6,128,256]{2,1,0:T(8,128)(2,1)} %shard_map.73), channel_id=1, source_target_pairs={{0,4},{4,8},{8,12},{12,0},{1,5},{5,9},{9,13},{13,1},{2,6},{6,10},{... | collective-permute-start | bytes 1179656 | tf_op jit(solution)/shard_map/ppermute | solution.py:288
  52.7 35.8 %collective-permute-start.7 = (bf16[6,128,256]{2,1,0:T(8,128)(2,1)}, bf16[6,128,256]{2,1,0:T(8,128)(2,1)}, u32[]{:S(2)}, u32[]{:S(2)}) collective-permute-start(bf16[6,128,256]{2,1,0:T(8,128)(2,1)} %shard_map.74), channel_id=1, source_target_pairs={{0,4},{4,8},{8,12},{12,0},{1,5},{5,9},{9,13},{13,1},{2,6},{6,10},{... | collective-permute-start | bytes 1179656 | tf_op jit(solution)/shard_map/ppermute | solution.py:288
  58.1 36.7 %collective-permute-start.8 = (bf16[6,128,256]{2,1,0:T(8,128)(2,1)}, bf16[6,128,256]{2,1,0:T(8,128)(2,1)S(1)}, u32[]{:S(2)}, u32[]{:S(2)}) collective-permute-start(bf16[6,128,256]{2,1,0:T(8,128)(2,1)} %shard_map.76), channel_id=1, source_target_pairs={{0,8},{4,12},{8,0},{12,4},{1,9},{5,13},{9,1},{13,5},{2,10},{6,14},... | collective-permute-start | bytes 1179656 | tf_op jit(solution)/shard_map/ppermute | solution.py:288
  63.0 40.1 %collective-permute-start.9 = (bf16[6,128,256]{2,1,0:T(8,128)(2,1)}, bf16[6,128,256]{2,1,0:T(8,128)(2,1)S(1)}, u32[]{:S(2)}, u32[]{:S(2)}) collective-permute-start(bf16[6,128,256]{2,1,0:T(8,128)(2,1)} %shard_map.77), channel_id=1, source_target_pairs={{0,8},{4,12},{8,0},{12,4},{1,9},{5,13},{9,1},{13,5},{2,10},{6,14},... | collective-permute-start | bytes 1179656 | tf_op jit(solution)/shard_map/ppermute | solution.py:288
  68.7 6.6 %copy-start = (bf16[2,24,64,256]{3,2,1,0:T(8,128)(2,1)S(1)}, bf16[2,24,64,256]{3,2,1,0:T(8,128)(2,1)}, u32[]{:S(2)}) copy-start(bf16[2,24,64,256]{3,2,1,0:T(8,128)(2,1)} %refs_3_.9) | copy-start | bytes 4718596
  68.7 6.6 %copy-start.23 = (f32[24]{0:T(128)S(1)}, f32[24]{0:T(128)}, u32[]{:S(2)}) copy-start(f32[24]{0:T(128)} %refs_2_.1) | copy-start | bytes 292
  68.8 40.4 %collective-permute-start.10 = (bf16[6,128,256]{2,1,0:T(8,128)(2,1)}, bf16[6,128,256]{2,1,0:T(8,128)(2,1)S(1)}, u32[]{:S(2)}, u32[]{:S(2)}) collective-permute-start(bf16[6,128,256]{2,1,0:T(8,128)(2,1)} %shard_map.79), channel_id=1, source_target_pairs={{0,12},{4,0},{8,4},{12,8},{1,13},{5,1},{9,5},{13,9},{2,14},{6,2},{... | collective-permute-start | bytes 1179656 | tf_op jit(solution)/shard_map/ppermute | solution.py:288
  74.9 5.2 %copy-start.7 = (bf16[6,128,256]{2,1,0:T(8,128)(2,1)}, bf16[6,128,256]{2,1,0:T(8,128)(2,1)S(1)}, u32[]{:S(2)}) copy-start(bf16[6,128,256]{2,1,0:T(8,128)(2,1)S(1)} %collective-permute-done.6.refs_3_) | copy-start | bytes 1179652
  74.9 34.7 %collective-permute-start.11 = (bf16[6,128,256]{2,1,0:T(8,128)(2,1)}, bf16[6,128,256]{2,1,0:T(8,128)(2,1)S(1)}, u32[]{:S(2)}, u32[]{:S(2)}) collective-permute-start(bf16[6,128,256]{2,1,0:T(8,128)(2,1)} %shard_map.80), channel_id=1, source_target_pairs={{0,12},{4,0},{8,4},{12,8},{1,13},{5,1},{9,5},{13,9},{2,14},{6,2},{... | collective-permute-start | bytes 1179656 | tf_op jit(solution)/shard_map/ppermute | solution.py:288
  83.9 4.5 %copy-start.32 = (s32[1,96]{1,0:T(1,128)S(1)}, s32[1,96]{1,0:T(1,128)}, u32[]{:S(2)}) copy-start(s32[1,96]{1,0:T(1,128)} %partner.1) | copy-start | bytes 1156
  88.4 14.7 %copy-start.31 = (bf16[6,64,256]{2,1,0:T(8,128)(2,1)S(1)}, bf16[6,64,256]{2,1,0:T(8,128)(2,1)}, u32[]{:S(2)}) copy-start(bf16[6,64,256]{2,1,0:T(8,128)(2,1)} %get-tuple-element.30) | copy-start | bytes 589828
  88.5 34.2 %collective-permute-start = (s32[1,96]{1,0:T(1,128)S(1)}, s32[1,96]{1,0:T(1,128)S(1)}, u32[]{:S(2)}, u32[]{:S(2)}) collective-permute-start(s32[1,96]{1,0:T(1,128)S(1)} %copy-done.32), channel_id=1, source_target_pairs={{0,2},{2,0},{1,3},{3,1},{4,6},{6,4},{5,7},{7,5},{8,10},{10,8},{9,1... | collective-permute-start | bytes 1160 | tf_op jit(solution)/shard_map/ppermute | solution.py:288
  94.8 9.9 %copy-start.5 = (bf16[6,128,256]{2,1,0:T(8,128)(2,1)}, bf16[6,128,256]{2,1,0:T(8,128)(2,1)S(1)}, u32[]{:S(2)}) copy-start(bf16[6,128,256]{2,1,0:T(8,128)(2,1)S(1)} %collective-permute-done.8.refs_3_) | copy-start | bytes 1179652
  94.8 29.2 %collective-permute-start.12 = (bf16[6,64,256]{2,1,0:T(8,128)(2,1)}, bf16[6,64,256]{2,1,0:T(8,128)(2,1)S(1)}, u32[]{:S(2)}, u32[]{:S(2)}) collective-permute-start(bf16[6,64,256]{2,1,0:T(8,128)(2,1)} %get-tuple-element.26), channel_id=1, source_target_pairs={{0,1},{1,0},{2,3},{3,2},{4,5},{5,4},{6,7},{7,6},{8,9},{9,8},{10,11... | collective-permute-start | bytes 589832 | tf_op jit(solution)/shard_map/ppermute | solution.py:296
  103.1 1.5 copy-start.6
  103.1 6.0 %copy-start.30 = (bf16[6,64,256]{2,1,0:T(8,128)(2,1)S(1)}, bf16[6,64,256]{2,1,0:T(8,128)(2,1)}, u32[]{:S(2)}) copy-start(bf16[6,64,256]{2,1,0:T(8,128)(2,1)} %get-tuple-element.34) | copy-start | bytes 589828
  103.1 21.5 %collective-permute-start.16 = (bf16[6,64,256]{2,1,0:T(8,128)(2,1)S(1)}, bf16[6,64,256]{2,1,0:T(8,128)(2,1)S(1)}, u32[]{:S(2)}, u32[]{:S(2)}) collective-permute-start(bf16[6,64,256]{2,1,0:T(8,128)(2,1)S(1)} %copy-done.31), channel_id=1, source_target_pairs={{0,2},{1,3},{2,0},{3,1},{4,6},{5,7},{6,4},{7,5},{8,10},{9,11},{10,... | collective-permute-start | bytes 589832 | tf_op jit(solution)/shard_map/ppermute | solution.py:296
  109.2 0.7 copy-start.3
  109.2 6.0 %copy-start.20 = (f32[8,256]{1,0:T(8,128)S(1)}, f32[8,256]{1,0:T(8,128)}, u32[]{:S(2)}) copy-start(f32[8,256]{1,0:T(8,128)} %get-tuple-element.38) | copy-start | bytes 24580
  109.2 6.0 %copy-start.21 = (f32[8,256]{1,0:T(8,128)S(1)}, f32[8,256]{1,0:T(8,128)}, u32[]{:S(2)}) copy-start(f32[8,256]{1,0:T(8,128)} %get-tuple-element.39) | copy-start | bytes 24580
  109.2 6.0 %copy-start.22 = (f32[8,256]{1,0:T(8,128)S(1)}, f32[8,256]{1,0:T(8,128)}, u32[]{:S(2)}) copy-start(f32[8,256]{1,0:T(8,128)} %get-tuple-element.40) | copy-start | bytes 24580
  109.2 13.4 %copy-start.28 = (bf16[6,64,256]{2,1,0:T(8,128)(2,1)S(1)}, bf16[6,64,256]{2,1,0:T(8,128)(2,1)}, u32[]{:S(2)}) copy-start(bf16[6,64,256]{2,1,0:T(8,128)(2,1)} %get-tuple-element.27) | copy-start | bytes 589828
  109.2 13.4 %copy-start.27 = (bf16[6,64,256]{2,1,0:T(8,128)(2,1)S(1)}, bf16[6,64,256]{2,1,0:T(8,128)(2,1)}, u32[]{:S(2)}) copy-start(bf16[6,64,256]{2,1,0:T(8,128)(2,1)} %get-tuple-element.31) | copy-start | bytes 589828
  109.2 14.8 %copy-start.24 = (bf16[6,64,256]{2,1,0:T(8,128)(2,1)S(1)}, bf16[6,64,256]{2,1,0:T(8,128)(2,1)}, u32[]{:S(2)}) copy-start(bf16[6,64,256]{2,1,0:T(8,128)(2,1)} %get-tuple-element.35) | copy-start | bytes 589828
  109.2 32.6 %copy-start.29 = (bf16[6,64,256]{2,1,0:T(8,128)(2,1)S(1)}, bf16[6,64,256]{2,1,0:T(8,128)(2,1)}, u32[]{:S(2)}) copy-start(bf16[6,64,256]{2,1,0:T(8,128)(2,1)} %get-tuple-element.28) | copy-start | bytes 589828
  109.2 39.6 %copy-start.26 = (bf16[6,64,256]{2,1,0:T(8,128)(2,1)S(1)}, bf16[6,64,256]{2,1,0:T(8,128)(2,1)}, u32[]{:S(2)}) copy-start(bf16[6,64,256]{2,1,0:T(8,128)(2,1)} %get-tuple-element.32) | copy-start | bytes 589828
  109.3 40.9 %copy-start.25 = (bf16[6,64,256]{2,1,0:T(8,128)(2,1)S(1)}, bf16[6,64,256]{2,1,0:T(8,128)(2,1)}, u32[]{:S(2)}) copy-start(bf16[6,64,256]{2,1,0:T(8,128)(2,1)} %get-tuple-element.36) | copy-start | bytes 589828
  109.3 34.7 %collective-permute-start.20 = (bf16[6,64,256]{2,1,0:T(8,128)(2,1)S(1)}, bf16[6,64,256]{2,1,0:T(8,128)(2,1)S(1)}, u32[]{:S(2)}, u32[]{:S(2)}) collective-permute-start(bf16[6,64,256]{2,1,0:T(8,128)(2,1)S(1)} %copy-done.30), channel_id=1, source_target_pairs={{0,3},{1,2},{2,1},{3,0},{4,7},{5,6},{6,5},{7,4},{8,11},{9,10},{10,... | collective-permute-start | bytes 589832 | tf_op jit(solution)/shard_map/ppermute | solution.py:296
  109.9 0.8 copy-start.4
  117.2 1.2 collective-permute-start.24
  119.0 3.6 %collective-permute-start.25 = (f32[2]{0:T(128)S(1)}, f32[2]{0:T(128)S(1)}, u32[]{:S(2)}, u32[]{:S(2)}) collective-permute-start(f32[2]{0:T(128)S(1)} %fusion.2), channel_id=1, source_target_pairs={{0,2},{2,0},{1,3},{3,1},{4,6},{6,4},{5,7},{7,5},{8,10},{10,8},{9,1... | collective-permute-start | bytes 32 | tf_op jit(solution)/shard_map/ppermute | solution.py:305
  122.6 27.5 %collective-permute-start.13 = (bf16[6,64,256]{2,1,0:T(8,128)(2,1)S(1)}, bf16[6,64,256]{2,1,0:T(8,128)(2,1)S(1)}, u32[]{:S(2)}, u32[]{:S(2)}) collective-permute-start(bf16[6,64,256]{2,1,0:T(8,128)(2,1)S(1)} %copy-done.28), channel_id=1, source_target_pairs={{0,1},{1,0},{2,3},{3,2},{4,5},{5,4},{6,7},{7,6},{8,9},{9,8},{10,11... | collective-permute-start | bytes 589832 | tf_op jit(solution)/shard_map/ppermute | solution.py:296
  122.6 19.2 %copy-start.33 = (s32[1,96]{1,0:T(1,128)}, s32[1,96]{1,0:T(1,128)S(1)}, u32[]{:S(2)}) copy-start(s32[1,96]{1,0:T(1,128)S(1)} %collective-permute-done.partner) | copy-start | bytes 1156
  122.7 27.6 %collective-permute-start.17 = (bf16[6,64,256]{2,1,0:T(8,128)(2,1)S(1)}, bf16[6,64,256]{2,1,0:T(8,128)(2,1)S(1)}, u32[]{:S(2)}, u32[]{:S(2)}) collective-permute-start(bf16[6,64,256]{2,1,0:T(8,128)(2,1)S(1)} %copy-done.27), channel_id=1, source_target_pairs={{0,2},{1,3},{2,0},{3,1},{4,6},{5,7},{6,4},{7,5},{8,10},{9,11},{10,... | collective-permute-start | bytes 589832 | tf_op jit(solution)/shard_map/ppermute | solution.py:296
  124.0 42.8 %copy-start.8 = (bf16[6,64,256]{2,1,0:T(8,128)(2,1)}, bf16[6,64,256]{2,1,0:T(8,128)(2,1)S(1)}, u32[]{:S(2)}) copy-start(bf16[6,64,256]{2,1,0:T(8,128)(2,1)S(1)} %collective-permute-done.12.refs_8_) | copy-start | bytes 589828
  124.0 27.1 %collective-permute-start.21 = (bf16[6,64,256]{2,1,0:T(8,128)(2,1)S(1)}, bf16[6,64,256]{2,1,0:T(8,128)(2,1)S(1)}, u32[]{:S(2)}, u32[]{:S(2)}) collective-permute-start(bf16[6,64,256]{2,1,0:T(8,128)(2,1)S(1)} %copy-done.24), channel_id=1, source_target_pairs={{0,3},{1,2},{2,1},{3,0},{4,7},{5,6},{6,5},{7,4},{8,11},{9,10},{10,... | collective-permute-start | bytes 589832 | tf_op jit(solution)/shard_map/ppermute | solution.py:296
  124.6 42.2 %copy-start.9 = (bf16[6,64,256]{2,1,0:T(8,128)(2,1)}, bf16[6,64,256]{2,1,0:T(8,128)(2,1)S(1)}, u32[]{:S(2)}) copy-start(bf16[6,64,256]{2,1,0:T(8,128)(2,1)S(1)} %collective-permute-done.16.refs_12_) | copy-start | bytes 589828
  124.6 17.1 %collective-permute-start.26 = (f32[2]{0:T(128)S(1)}, f32[2]{0:T(128)S(1)}, u32[]{:S(2)}, u32[]{:S(2)}) collective-permute-start(f32[2]{0:T(128)S(1)} %add.40), channel_id=1, source_target_pairs={{0,4},{4,0},{8,12},{12,8},{1,5},{5,1},{9,13},{13,9},{2,6},{6,2},{1... | collective-permute-start | bytes 32 | tf_op jit(solution)/shard_map/ppermute | solution.py:305
  141.8 10.6 %collective-permute-start.14 = (bf16[6,64,256]{2,1,0:T(8,128)(2,1)S(1)}, bf16[6,64,256]{2,1,0:T(8,128)(2,1)S(1)}, u32[]{:S(2)}, u32[]{:S(2)}) collective-permute-start(bf16[6,64,256]{2,1,0:T(8,128)(2,1)S(1)} %copy-done.29), channel_id=1, source_target_pairs={{0,1},{1,0},{2,3},{3,2},{4,5},{5,4},{6,7},{7,6},{8,9},{9,8},{10,11... | collective-permute-start | bytes 589832 | tf_op jit(solution)/shard_map/ppermute | solution.py:296
  144.0 22.9 %copy-start.10 = (bf16[6,64,256]{2,1,0:T(8,128)(2,1)}, bf16[6,64,256]{2,1,0:T(8,128)(2,1)S(1)}, u32[]{:S(2)}) copy-start(bf16[6,64,256]{2,1,0:T(8,128)(2,1)S(1)} %collective-permute-done.20.refs_16_) | copy-start | bytes 589828
  144.0 4.9 %collective-permute-start.27 = (f32[2]{0:T(128)S(1)}, f32[2]{0:T(128)S(1)}, u32[]{:S(2)}, u32[]{:S(2)}) collective-permute-start(f32[2]{0:T(128)S(1)} %add.41), channel_id=1, source_target_pairs={{0,8},{4,12},{8,0},{12,4},{1,9},{5,13},{9,1},{13,5},{2,10},{6,14},... | collective-permute-start | bytes 32 | tf_op jit(solution)/shard_map/ppermute | solution.py:305
  148.9 7.8 %collective-permute-start.18 = (bf16[6,64,256]{2,1,0:T(8,128)(2,1)S(1)}, bf16[6,64,256]{2,1,0:T(8,128)(2,1)S(1)}, u32[]{:S(2)}, u32[]{:S(2)}) collective-permute-start(bf16[6,64,256]{2,1,0:T(8,128)(2,1)S(1)} %copy-done.26), channel_id=1, source_target_pairs={{0,2},{1,3},{2,0},{3,1},{4,6},{5,7},{6,4},{7,5},{8,10},{9,11},{10,... | collective-permute-start | bytes 589832 | tf_op jit(solution)/shard_map/ppermute | solution.py:296
  150.1 16.7 %copy-start.11 = (bf16[6,64,256]{2,1,0:T(8,128)(2,1)}, bf16[6,64,256]{2,1,0:T(8,128)(2,1)S(1)}, u32[]{:S(2)}) copy-start(bf16[6,64,256]{2,1,0:T(8,128)(2,1)S(1)} %collective-permute-done.13.refs_9_) | copy-start | bytes 589828
  150.1 9.5 %collective-permute-start.22 = (bf16[6,64,256]{2,1,0:T(8,128)(2,1)S(1)}, bf16[6,64,256]{2,1,0:T(8,128)(2,1)S(1)}, u32[]{:S(2)}, u32[]{:S(2)}) collective-permute-start(bf16[6,64,256]{2,1,0:T(8,128)(2,1)S(1)} %copy-done.25), channel_id=1, source_target_pairs={{0,3},{1,2},{2,1},{3,0},{4,7},{5,6},{6,5},{7,4},{8,11},{9,10},{10,... | collective-permute-start | bytes 589832 | tf_op jit(solution)/shard_map/ppermute | solution.py:296
  150.2 16.6 %copy-start.12 = (bf16[6,64,256]{2,1,0:T(8,128)(2,1)}, bf16[6,64,256]{2,1,0:T(8,128)(2,1)S(1)}, u32[]{:S(2)}) copy-start(bf16[6,64,256]{2,1,0:T(8,128)(2,1)S(1)} %collective-permute-done.17.refs_13_) | copy-start | bytes 589828
  150.2 9.5 %collective-permute-start.15 = (bf16[6,64,256]{2,1,0:T(8,128)(2,1)}, bf16[6,64,256]{2,1,0:T(8,128)(2,1)S(1)}, u32[]{:S(2)}, u32[]{:S(2)}) collective-permute-start(bf16[6,64,256]{2,1,0:T(8,128)(2,1)} %get-tuple-element.29), channel_id=1, source_target_pairs={{0,1},{1,0},{2,3},{3,2},{4,5},{5,4},{6,7},{7,6},{8,9},{9,8},{10,11... | collective-permute-start | bytes 589832 | tf_op jit(solution)/shard_map/ppermute | solution.py:296
  151.1 15.8 %copy-start.13 = (bf16[6,64,256]{2,1,0:T(8,128)(2,1)}, bf16[6,64,256]{2,1,0:T(8,128)(2,1)S(1)}, u32[]{:S(2)}) copy-start(bf16[6,64,256]{2,1,0:T(8,128)(2,1)S(1)} %collective-permute-done.21.refs_17_) | copy-start | bytes 589828
  151.1 14.0 %collective-permute-start.19 = (bf16[6,64,256]{2,1,0:T(8,128)(2,1)}, bf16[6,64,256]{2,1,0:T(8,128)(2,1)S(1)}, u32[]{:S(2)}, u32[]{:S(2)}) collective-permute-start(bf16[6,64,256]{2,1,0:T(8,128)(2,1)} %get-tuple-element.33), channel_id=1, source_target_pairs={{0,2},{1,3},{2,0},{3,1},{4,6},{5,7},{6,4},{7,5},{8,10},{9,11},{10,... | collective-permute-start | bytes 589832 | tf_op jit(solution)/shard_map/ppermute | solution.py:296
  152.4 14.5 %copy-start.14 = (bf16[6,64,256]{2,1,0:T(8,128)(2,1)}, bf16[6,64,256]{2,1,0:T(8,128)(2,1)S(1)}, u32[]{:S(2)}) copy-start(bf16[6,64,256]{2,1,0:T(8,128)(2,1)S(1)} %collective-permute-done.14.refs_10_) | copy-start | bytes 589828
  152.4 14.5 %collective-permute-start.23 = (bf16[6,64,256]{2,1,0:T(8,128)(2,1)}, bf16[6,64,256]{2,1,0:T(8,128)(2,1)S(1)}, u32[]{:S(2)}, u32[]{:S(2)}) collective-permute-start(bf16[6,64,256]{2,1,0:T(8,128)(2,1)} %get-tuple-element.37), channel_id=1, source_target_pairs={{0,3},{1,2},{2,1},{3,0},{4,7},{5,6},{6,5},{7,4},{8,11},{9,10},{10,... | collective-permute-start | bytes 589832 | tf_op jit(solution)/shard_map/ppermute | solution.py:296
  156.7 10.2 %copy-start.15 = (bf16[6,64,256]{2,1,0:T(8,128)(2,1)}, bf16[6,64,256]{2,1,0:T(8,128)(2,1)S(1)}, u32[]{:S(2)}) copy-start(bf16[6,64,256]{2,1,0:T(8,128)(2,1)S(1)} %collective-permute-done.18.refs_14_) | copy-start | bytes 589828
  159.7 7.2 %copy-start.16 = (bf16[6,64,256]{2,1,0:T(8,128)(2,1)}, bf16[6,64,256]{2,1,0:T(8,128)(2,1)S(1)}, u32[]{:S(2)}) copy-start(bf16[6,64,256]{2,1,0:T(8,128)(2,1)S(1)} %collective-permute-done.22.refs_18_) | copy-start | bytes 589828
  159.7 7.2 %copy-start.17 = (bf16[6,64,256]{2,1,0:T(8,128)(2,1)}, bf16[6,64,256]{2,1,0:T(8,128)(2,1)S(1)}, u32[]{:S(2)}) copy-start(bf16[6,64,256]{2,1,0:T(8,128)(2,1)S(1)} %collective-permute-done.15.refs_11_) | copy-start | bytes 589828
  165.1 1.8 %copy-start.18 = (bf16[6,64,256]{2,1,0:T(8,128)(2,1)}, bf16[6,64,256]{2,1,0:T(8,128)(2,1)S(1)}, u32[]{:S(2)}) copy-start(bf16[6,64,256]{2,1,0:T(8,128)(2,1)S(1)} %collective-permute-done.19.refs_15_) | copy-start | bytes 589828
  166.8 0.7 copy-start.19

commit v2 on v1

v2 whole, which is shorter than its diff:
```python
import functools

import jax
import jax.numpy as jnp
from jax import lax
from jax.experimental import pallas as pl
from jax.experimental.pallas import tpu as pltpu
from jax.sharding import PartitionSpec as P

HBM = pl.BlockSpec(memory_space=pl.ANY)
SMEM = pl.BlockSpec(memory_space=pltpu.SMEM)
VMEM = pl.BlockSpec(memory_space=pltpu.VMEM)
LIMIT = 40 * 1024 * 1024
BRIEF = pl.CostEstimate(flops=0, bytes_accessed=0, transcendentals=0)


def aligned(index, size):
    return pl.multiple_of(index * size, size)


class Sizes:
    def __init__(self, vectors, left_env):
        self.env = lax.axis_size("env")
        self.rep = lax.axis_size("rep")
        self.sector = lax.axis_size("sector")
        self.batch, self.slots, self.own_rows, self.order = vectors.shape
        assert self.batch == self.rep
        self.half = left_env.shape[2]
        self.chip_rows = self.own_rows * self.rep
        self.capacity = 2 * ((self.slots + 2 * self.sector - 1) // (2 * self.sector))
        self.flat = self.sector * self.capacity
        self.source, self.target, self.valid = 0, self.flat, 2 * self.flat
        self.core, self.chip = 3 * self.flat, 3 * self.flat + 1


def plan_body(z, partner, ids, plan, count):
    def clear(i, carry):
        plan[i] = 0
        return carry

    lax.fori_loop(0, 3 * z.flat, clear, 0)
    for d in range(z.sector):
        count[d] = 0

    def place(j, carry):
        sector = partner[0, j]
        group = lax.div(sector, z.slots)
        slot = sector - group * z.slots
        distance = lax.rem(z.sector - group, z.sector)
        rank = count[distance]
        count[distance] = rank + 1
        index = distance * z.capacity + rank
        plan[z.source + index] = slot
        plan[z.target + index] = j
        plan[z.valid + index] = 1
        return carry

    lax.fori_loop(0, z.slots, place, 0)
    plan[z.core] = ids[0]
    plan[z.chip] = ids[1]


def make_plan(z, partner, ids):
    return pl.pallas_call(
        functools.partial(plan_body, z),
        out_shape=jax.ShapeDtypeStruct((3 * z.flat + 2,), jnp.int32),
        in_specs=[SMEM, SMEM],
        out_specs=SMEM,
        scratch_shapes=[pltpu.SMEM((z.sector,), jnp.int32)],
        cost_estimate=BRIEF,
    )(partner, ids)


def pick(z, core, place, candidates):
    chosen = candidates[0]
    for s in range(1, z.rep):
        chosen = jnp.where(lax.rem(core + z.rep - s, z.rep) == place, candidates[s], chosen)
    return chosen


def products_body(z, first, pieces, blocks, *refs):
    refs = list(refs)
    plan = refs.pop(0)
    right = [refs.pop(0) for _ in range(z.rep)]
    rows = [[refs.pop(0) for _ in range(z.rep)] for _ in range(pieces)]
    outs = refs[-blocks:]
    core = plan[z.core]
    for d, out in enumerate(outs):
        for i in range(out.shape[0]):
            slot = plan[z.source + first + d * z.capacity + i]
            halves = [ref[0, slot] for ref in right]
            parts = [[ref[core, slot] for ref in piece] for piece in rows]
            block = jnp.concatenate([pick(z, core, k, halves) for k in range(z.rep)], axis=0)
            lines = jnp.concatenate(
                [pick(z, core, k, part) for part in parts for k in range(z.rep)], axis=0
            )
            out[i] = lax.dot_general(
                lines, block, (((1,), (1,)), ((), ())), preferred_element_type=jnp.float32
            ).astype(jnp.bfloat16)


def products(z, plan, right, rows, first, sizes, after=()):
    pieces = len(rows)
    flat = [ref for piece in rows for ref in piece]
    height = pieces * z.chip_rows
    count = sum(sizes)
    return pl.pallas_call(
        functools.partial(products_body, z, first, pieces, len(sizes)),
        out_shape=[
            jax.ShapeDtypeStruct((size, height, z.order), jnp.bfloat16) for size in sizes
        ],
        in_specs=[SMEM] + [VMEM] * (len(right) + len(flat)) + [HBM] * len(after),
        out_specs=[VMEM] * len(sizes),
        compiler_params=pltpu.CompilerParams(vmem_limit_bytes=LIMIT),
        cost_estimate=BRIEF,
    )(plan, *right, *flat, *after)


def terms_body(z, first, groups, *refs):
    refs = list(refs)
    plan = refs.pop(0)
    left = [refs.pop(0) for _ in range(z.rep)]
    near = [refs.pop(0) for _ in range(groups)]
    far = [refs.pop(0) for _ in range(groups)]
    vec = [[refs.pop(0) for _ in range(z.rep)] for _ in range(z.env)]
    pbuf, tbuf = refs[-2:]
    dots = refs[-3]
    outs = refs[-3 - z.env * z.rep : -3]
    core, chip = plan[z.core], plan[z.chip]
    total = jnp.zeros(dots.shape, jnp.float32)
    n = 0
    for d in range(groups):
        for i in range(near[d].shape[0]):
            flat = first + d * z.capacity + i
            slot = plan[z.target + flat]
            for e in range(z.env):
                place = lax.rem(chip + z.env - e, z.env)
                if e == 0:
                    lines = near[d][i]
                else:
                    lines = far[d][i, (e - 1) * z.chip_rows : e * z.chip_rows]
                pbuf[n, pl.ds(aligned(place, z.chip_rows), z.chip_rows)] = lines
            halves = [ref[0, slot] for ref in left]
            block = jnp.concatenate([pick(z, core, k, halves) for k in range(z.rep)], axis=0)
            tbuf[n] = jnp.dot(block, pbuf[n], preferred_element_type=jnp.float32).astype(
                jnp.bfloat16
            )
            folded = jnp.zeros(dots.shape, jnp.float32)
            for e in range(z.env):
                for s in range(z.rep):
                    place = lax.rem(chip + e, z.env) * z.rep + lax.rem(core + s, z.rep)
                    term = tbuf[n, pl.ds(aligned(place, z.own_rows), z.own_rows)]
                    outs[e * z.rep + s][n] = term
                    lines = vec[(z.env - e) % z.env][(z.rep - s) % z.rep][core, slot]
                    both = lines.astype(jnp.float32) * term.astype(jnp.float32)
                    folded += jnp.sum(both.reshape(-1, *dots.shape), axis=0)
            total += jnp.where(plan[z.valid + flat] == 1, folded, 0.0)
            n += 1
    dots[...] = total


def terms(z, plan, left, near, far, vec, first, after=()):
    groups = len(near)
    count = sum(block.shape[0] for block in near)
    flat = [ref for piece in vec for ref in piece]
    block = jax.ShapeDtypeStruct((count, z.own_rows, z.order), jnp.bfloat16)
    whole = (count, z.order, z.order)
    made = pl.pallas_call(
        functools.partial(terms_body, z, first, groups),
        out_shape=[block] * (z.env * z.rep) + [jax.ShapeDtypeStruct((8, z.order), jnp.float32)],
        in_specs=[SMEM]
        + [VMEM] * (len(left) + len(near) + len(far) + len(flat))
        + [HBM] * len(after),
        out_specs=[VMEM] * (z.env * z.rep + 1),
        scratch_shapes=[pltpu.VMEM(whole, jnp.bfloat16), pltpu.VMEM(whole, jnp.bfloat16)],
        compiler_params=pltpu.CompilerParams(vmem_limit_bytes=LIMIT),
        cost_estimate=BRIEF,
    )(plan, *left, *near, *far, *flat, *after)
    blocks = [made[e * z.rep : (e + 1) * z.rep] for e in range(z.env)]
    return blocks, made[-1]


def image_body(z, sizes, *refs):
    refs = list(refs)
    plans = [refs.pop(0) for _ in range(z.env)]
    energy, vectors = refs.pop(0), refs.pop(0)
    parts = [[[refs.pop(0) for _ in sizes] for _ in range(z.rep)] for _ in range(z.env)]
    image = refs.pop(0)
    core = plans[0][z.core]

    def start(j, carry):
        for v in range(z.batch):
            image[v, j] = energy[j] * vectors[v, j].astype(jnp.float32)
        return carry

    lax.fori_loop(0, z.slots, start, 0)
    for e, plan in enumerate(plans):
        first = 0
        for g, count in enumerate(sizes):

            def add(n, carry):
                slot = plan[z.target + first + n]

                @pl.when(plan[z.valid + first + n] == 1)
                def _():
                    for s in range(z.rep):
                        v = lax.rem(core + z.rep - s, z.rep)
                        image[v, slot] += parts[e][s][g][n].astype(jnp.float32)

                return carry

            lax.fori_loop(0, count, add, 0)
            first += count


def make_image(z, plans, energy, vectors, parts):
    sizes = tuple(block.shape[0] for block in parts[0][0])
    flat = [ref for piece in parts for kind in piece for ref in kind]
    return pl.pallas_call(
        functools.partial(image_body, z, sizes),
        out_shape=jax.ShapeDtypeStruct(vectors.shape, jnp.float32),
        in_specs=[SMEM] * (z.env + 1) + [VMEM] * (len(flat) + 1),
        out_specs=VMEM,
        compiler_params=pltpu.CompilerParams(vmem_limit_bytes=LIMIT),
        cost_estimate=BRIEF,
    )(*plans, energy, vectors, *flat)


def shift(array, axis, size, step):
    return lax.ppermute(array, axis, [(i, (i + step) % size) for i in range(size)])


def shift_both(z, array, e, s):
    perm = []
    for x in range(z.env):
        for c in range(z.rep):
            perm.append((x * z.rep + c, (x + e) % z.env * z.rep + (c + s) % z.rep))
    return lax.ppermute(array, ("env", "rep"), perm)


def total_over(array, axis):
    size = lax.axis_size(axis)
    if size & (size - 1):
        return lax.psum(array, axis)
    step = 1
    while step < size:
        array = array + lax.ppermute(array, axis, [(i, i ^ step) for i in range(size)])
        step *= 2
    return array


def on_device(vectors, left_env, right_env, energy, partner):
    z = Sizes(vectors, left_env)
    core, chip = lax.axis_index("rep"), lax.axis_index("env")
    ids = jnp.stack([core, chip]).astype(jnp.int32)

    def around(array):
        return [array] + [shift(array, "rep", z.rep, s) for s in range(1, z.rep)]

    def across(array, distance):
        return shift(array, "sector", z.sector, distance) if distance else array

    others = [shift(vectors, "env", z.env, e) for e in range(1, z.env)]
    right = around(right_env)
    near_rows = around(vectors)
    plan = make_plan(z, partner, ids)
    plans = [plan]
    for e in range(1, z.env):
        plans.append(make_plan(z, shift(partner, "env", z.env, e), ids))

    many = min(z.sector, 4)
    each = z.sector // many
    sizes = [z.capacity] * each

    near, made_near, chain = {}, [], ()
    for g in [*range(1, many), 0]:
        made = products(z, plan, right, [near_rows], g * each * z.capacity, sizes, chain)
        chain = made[:1]
        made_near += made[:1]
        near[g] = [across(block, g * each + d) for d, block in enumerate(made)]
    left_env, *made_near = lax.optimization_barrier((left_env, *made_near))
    left = around(left_env)

    others, chain = lax.optimization_barrier((others, chain))
    vec = [near_rows] + [around(other) for other in others]
    far, parts, dots = {}, [[[None] * many for _ in range(z.rep)] for _ in range(z.env)], 0.0

    def send_products(g, after):
        made = products(z, plan, right, vec[1:], g * each * z.capacity, sizes, after)
        far[g] = [across(block, g * each + d) for d, block in enumerate(made)]
        return made[:1]

    def send_terms(g, after):
        blocks, folded = terms(z, plan, left, near[g], far[g], vec, g * each * z.capacity, after)
        for e in range(z.env):
            for s in range(z.rep):
                block = blocks[e][s]
                parts[e][s][g] = block if e + s == 0 else shift_both(z, block, e, s)
        return folded

    ways = [*range(1, many, 2), *range(2, many, 2)]
    chain = send_products(ways[0], chain)
    chain = send_products(0, chain)
    folded = send_terms(0, chain)
    dots += folded
    chain = (folded,)
    for i, g in enumerate(ways[1:]):
        held = near[ways[i]] if i == 0 else far[ways[i - 1]]
        chain = send_products(g, (*chain, held[-1]))
    for g in ways:
        folded = send_terms(g, chain)
        dots += folded
        chain = (folded,)
    image = make_image(z, plans, energy, vectors, parts)
    own_block = vectors.astype(jnp.float32)
    partial_sum = jnp.sum(energy[None, :, None, None] * own_block * own_block, axis=(1, 2, 3))
    own_vector = (jnp.arange(z.batch) == core).astype(jnp.float32)
    partial_sum = partial_sum + own_vector * jnp.sum(dots)
    for axis in ("rep", "env", "sector"):
        partial_sum = total_over(partial_sum, axis)
    entries = z.slots * z.sector * z.order * z.order
    return (image, partial_sum / entries)


def solution(mesh):
    return jax.shard_map(
        on_device,
        mesh=mesh,
        in_specs=(
            P(None, ("groups", "sector"), ("env", "rep"), None),
            P("env", ("groups", "sector"), "rep", None),
            P("env", ("groups", "sector"), "rep", None),
            P(("groups", "sector")),
            P("env", "groups"),
        ),
        out_specs=(P(None, ("groups", "sector"), ("env", "rep"), None), P("groups")),
        check_vma=False,
    )
```

time: 175 us -> 156 us (0.89)
  Pallas kernels: 58.7 us -> 29.8 us
  starting transfers between devices: 42.5 us -> 53 us
    ppermute x12, starting transfers between devices: 14.4 us -> 43.6 us  [shift(): lax.ppermute(array, axis, [(i, (i + step) % size) for i in range(size)])]
    pallas_call x12, Pallas kernels: 48.5 us -> 21 us  [the longest x8 11.1 us: products(): pl.pallas_call(functools.partial(products_body, z, first, pieces, len(siz...]
    ppermute x4, starting transfers between devices: 20.7 us -> 1.81 us  [total_over(): lax.ppermute(array, axis, [(i, i ^ step) for i in range(size)])]
    ppermute x4, waiting for transfers between devices: 6.13 us -> 10.9 us  [total_over(): lax.ppermute(array, axis, [(i, i ^ step) for i in range(size)])]
    squeeze x2 -> x0, local copies, waits for them, and re-layouts: 3.11 us -> none  [rows_for(): own = lax.dynamic_index_in_dim(array, wanted, axis=0, keepdims=False)]
    unnamed x68 -> x36, local copies, waits for them, and re-layouts: 2.93 us -> 5.36 us
    ppermute x12, waiting for transfers between devices: 13.8 us -> 11.7 us  [shift_both(): return lax.ppermute(array, ('env', 'rep'), perm)]
  transfers between devices with their start and end apart: 28 -> 28, of which waited for: 11 -> 12; matrix products, arithmetic and copies ran while one was open for 4% -> 3% of each run, Pallas kernels for 30% -> 16%
where the time goes in v2:
time: 156 us
  waiting for transfers between devices  62 us (40%)
  starting transfers between devices  53 us (34%)
  Pallas kernels  29.8 us (19%)
  local copies, waits for them, and re-layouts  5.36 us (3%)
  other arithmetic  4.56 us (3%)
    ppermute x12, starting transfers between devices, shift(): lax.ppermute(array, axis, [(i, (i + step) % size) for i in range(size)])  43.6 us
    ppermute x12, waiting for transfers between devices, shift(): lax.ppermute(array, axis, [(i, (i + step) % size) for i in range(size)])  39.4 us
    ppermute x12, waiting for transfers between devices, shift_both(): return lax.ppermute(array, ('env', 'rep'), perm)  11.7 us
    pallas_call x8, Pallas kernels, products(): pl.pallas_call(functools.partial(products_body, z, first, pieces, len(siz...  11.1 us
    ppermute x4, waiting for transfers between devices, total_over(): lax.ppermute(array, axis, [(i, i ^ step) for i in range(size)])  10.9 us
    pallas_call x4, Pallas kernels, terms(): pl.pallas_call(functools.partial(terms_body, z, first, groups), out_shape...  9.93 us
    ppermute x12, starting transfers between devices, shift_both(): return lax.ppermute(array, ('env', 'rep'), perm)  7.56 us
    unnamed x36, local copies, waits for them, and re-layouts  5.36 us
  transfers between devices with their start and end apart: 28, of which 12 were waited for; matrix products, arithmetic and copies ran while one was open for 3% of the time, Pallas kernels for 16%

profile of v2, /device:TPU:0, one launch (start us, length us, event | category | flops | bytes accessed | tf_op | source)
XLA Modules:
  0.0 155.7 jit_solution(14643750912556631683)
XLA Ops:
  0.6 0.5 collective-permute-start.1
  1.1 0.1 collective-permute-start.2
  1.2 2.9 %collective-permute-start.4 = (bf16[2,24,64,256]{3,2,1,0:T(8,128)(2,1)}, bf16[2,24,64,256]{3,2,1,0:T(8,128)(2,1)}, u32[]{:S(2)}, u32[]{:S(2)}) collective-permute-start(bf16[2,24,64,256]{3,2,1,0:T(8,128)(2,1)} %refs_3_.9), channel_id=1, source_target_pairs={{0,2},{2,0},{1,3},{3,1},{4,6},{6,4},{5,7},{7,5},{8,10},{10,8},{9,1... | collective-permute-start | bytes 4718600 | tf_op jit(solution)/shard_map/ppermute | solution.py:230
  4.1 0.7 pad_add_fusion.ids
  4.8 2.1 %shard_map.68.refs_0_ = s32[74]{0:T(128)} custom-call(s32[1,96]{1,0:T(1,128)} %partner.1, s32[2]{0:T(128)} %pad_add_fusion.ids), custom_call_target="tpu_custom_call" | custom-call | tf_op jit(solution)/shard_map/pallas_call | solution.py:64
  7.0 1.4 copy-done
  8.4 1.4 copy-done.2
  9.8 0.7 copy-done.6
  10.5 0.9 shard_map.70.refs_5_
  11.4 0.9 shard_map.71.refs_5_
  12.4 0.9 shard_map.72.refs_5_
  13.4 1.0 shard_map.73.refs_5_.refs_3_
  14.3 24.8 %collective-permute-done.4.refs_3_.refs_7_ = bf16[2,24,64,256]{3,2,1,0:T(8,128)(2,1)} collective-permute-done((bf16[2,24,64,256]{3,2,1,0:T(8,128)(2,1)}, bf16[2,24,64,256]{3,2,1,0:T(8,128)(2,1)}, u32[]{:S(2)}, u32[]{:S(2)}) %collective-permute-start.4) | collective-permute-done | bytes 1572896 | tf_op jit(solution)/shard_map/ppermute | solution.py:230
  39.1 0.5 collective-permute-start.3
  39.6 1.8 %collective-permute-start.6 = (bf16[6,128,256]{2,1,0:T(8,128)(2,1)S(1)}, bf16[6,128,256]{2,1,0:T(8,128)(2,1)S(1)}, u32[]{:S(2)}, u32[]{:S(2)}) collective-permute-start(bf16[6,128,256]{2,1,0:T(8,128)(2,1)S(1)} %shard_map.70.refs_5_), channel_id=1, source_target_pairs={{0,4},{4,8},{8,12},{12,0},{1,5},{5,9},{9,13},{13,1},{2,6},{6,10},{... | collective-permute-start | bytes 1179656 | tf_op jit(solution)/shard_map/ppermute | solution.py:230
  41.4 3.5 %collective-permute-done.5.refs_4_.refs_8_ = bf16[2,24,64,256]{3,2,1,0:T(8,128)(2,1)S(1)} collective-permute-done((bf16[2,24,64,256]{3,2,1,0:T(8,128)(2,1)}, bf16[2,24,64,256]{3,2,1,0:T(8,128)(2,1)S(1)}, u32[]{:S(2)}, u32[]{:S(2)}) %collective-permute-start.5) | collective-permute-done | bytes 1572896 | tf_op jit(solution)/shard_map/ppermute | solution.py:230
  44.9 1.8 %shard_map.74.refs_5_ = bf16[6,128,256]{2,1,0:T(8,128)(2,1)S(1)} custom-call(s32[74]{0:T(128)S(1)} %copy-done.6, bf16[1,24,128,256]{3,2,1,0:T(8,128)(2,1)S(1)} %copy-done.2, bf16[1,24,128,256]{3,2,1,0:T(8,128)(2,1)S(1)} %collective-permute-done.1.refs_2_, bf16[2,24,64,256]{3,2,1,0:T(8,128)(2,1)} %collective-permute-done.4.refs_3_.refs_7_, ...), custom_call_target="tpu_custom_call" | custom-call | tf_op jit(solution)/shard_map/pallas_call | solution.py:107
  46.7 0.0 copy-start.4
  46.7 1.9 %collective-permute-start.7 = (bf16[6,128,256]{2,1,0:T(8,128)(2,1)S(1)}, bf16[6,128,256]{2,1,0:T(8,128)(2,1)S(1)}, u32[]{:S(2)}, u32[]{:S(2)}) collective-permute-start(bf16[6,128,256]{2,1,0:T(8,128)(2,1)S(1)} %shard_map.74.refs_5_), channel_id=1, source_target_pairs={{0,4},{4,8},{8,12},{12,0},{1,5},{5,9},{9,13},{13,1},{2,6},{6,10},{... | collective-permute-start | bytes 1179656 | tf_op jit(solution)/shard_map/ppermute | solution.py:230
  48.6 2.1 %collective-permute-start.10 = (bf16[6,128,256]{2,1,0:T(8,128)(2,1)S(1)}, bf16[6,128,256]{2,1,0:T(8,128)(2,1)S(1)}, u32[]{:S(2)}, u32[]{:S(2)}) collective-permute-start(bf16[6,128,256]{2,1,0:T(8,128)(2,1)S(1)} %shard_map.72.refs_5_), channel_id=1, source_target_pairs={{0,12},{4,0},{8,4},{12,8},{1,13},{5,1},{9,5},{13,9},{2,14},{6,2},{... | collective-permute-start | bytes 1179656 | tf_op jit(solution)/shard_map/ppermute | solution.py:230
  50.7 1.8 %shard_map.75.refs_4_.refs_9_ = bf16[6,128,256]{2,1,0:T(8,128)(2,1)S(1)} custom-call(s32[74]{0:T(128)S(1)} %copy-done.6, bf16[1,24,128,256]{3,2,1,0:T(8,128)(2,1)S(1)} %copy-done.2, bf16[1,24,128,256]{3,2,1,0:T(8,128)(2,1)S(1)} %collective-permute-done.1.refs_2_, bf16[2,24,64,256]{3,2,1,0:T(8,128)(2,1)} %collective-permute-done.4.refs_3_.refs_7_, ...), custom_call_target="tpu_custom_call" | custom-call | tf_op jit(solution)/shard_map/pallas_call | solution.py:107
  52.6 2.6 %shard_map.76 = (bf16[6,64,256]{2,1,0:T(8,128)(2,1)S(1)}, bf16[6,64,256]{2,1,0:T(8,128)(2,1)S(1)}, bf16[6,64,256]{2,1,0:T(8,128)(2,1)S(1)}, bf16[6,64,256]{2,1,0:T(8,128)(2,1)}, f32[8,256]{1,0:T(8,128)S(1)}) custom-call(s32[74]{0:T(128)S(1)} %copy-done.6, bf16[1,24,128,256]{3,2,1,0:T(8,128)(2,1)S(1)} %copy-done.5, ...), custom_call_target="tpu_custom_call" | custom-call | tf_op jit(solution)/shard_map/pallas_call | solution.py:168
  55.2 1.8 %shard_map.77.refs_5_ = bf16[6,128,256]{2,1,0:T(8,128)(2,1)S(1)} custom-call(s32[74]{0:T(128)S(1)} %copy-done.6, bf16[1,24,128,256]{3,2,1,0:T(8,128)(2,1)S(1)} %copy-done.2, bf16[1,24,128,256]{3,2,1,0:T(8,128)(2,1)S(1)} %collective-permute-done.1.refs_2_, bf16[2,24,64,256]{3,2,1,0:T(8,128)(2,1)} %collective-permute-done.4.refs_3_.refs_7_, ...), custom_call_target="tpu_custom_call" | custom-call | tf_op jit(solution)/shard_map/pallas_call | solution.py:107
  57.0 0.0 copy-start.15
  57.0 0.0 copy-start.8
  57.1 2.0 %collective-permute-start.11 = (bf16[6,128,256]{2,1,0:T(8,128)(2,1)S(1)}, bf16[6,128,256]{2,1,0:T(8,128)(2,1)S(1)}, u32[]{:S(2)}, u32[]{:S(2)}) collective-permute-start(bf16[6,128,256]{2,1,0:T(8,128)(2,1)S(1)} %shard_map.77.refs_5_), channel_id=1, source_target_pairs={{0,12},{4,0},{8,4},{12,8},{1,13},{5,1},{9,5},{13,9},{2,14},{6,2},{... | collective-permute-start | bytes 1179656 | tf_op jit(solution)/shard_map/ppermute | solution.py:230
  59.1 2.8 %collective-permute-done.7.refs_6_.refs_4_ = bf16[6,128,256]{2,1,0:T(8,128)(2,1)S(1)} collective-permute-done((bf16[6,128,256]{2,1,0:T(8,128)(2,1)S(1)}, bf16[6,128,256]{2,1,0:T(8,128)(2,1)S(1)}, u32[]{:S(2)}, u32[]{:S(2)}) %collective-permute-start.7) | collective-permute-done | bytes 393248 | tf_op jit(solution)/shard_map/ppermute | solution.py:230
  61.9 1.8 %shard_map.78.refs_9_ = bf16[6,128,256]{2,1,0:T(8,128)(2,1)S(1)} custom-call(s32[74]{0:T(128)S(1)} %copy-done.6, bf16[1,24,128,256]{3,2,1,0:T(8,128)(2,1)S(1)} %copy-done.2, bf16[1,24,128,256]{3,2,1,0:T(8,128)(2,1)S(1)} %collective-permute-done.1.refs_2_, bf16[2,24,64,256]{3,2,1,0:T(8,128)(2,1)} %collective-permute-done.4.refs_3_.refs_7_, ...), custom_call_target="tpu_custom_call" | custom-call | tf_op jit(solution)/shard_map/pallas_call | solution.py:107
  63.7 30.3 %collective-permute-start.9 = (bf16[6,128,256]{2,1,0:T(8,128)(2,1)S(1)}, bf16[6,128,256]{2,1,0:T(8,128)(2,1)S(1)}, u32[]{:S(2)}, u32[]{:S(2)}) collective-permute-start(bf16[6,128,256]{2,1,0:T(8,128)(2,1)S(1)} %shard_map.78.refs_9_), channel_id=1, source_target_pairs={{0,8},{4,12},{8,0},{12,4},{1,9},{5,13},{9,1},{13,5},{2,10},{6,14},... | collective-permute-start | bytes 1179656 | tf_op jit(solution)/shard_map/ppermute | solution.py:230
  94.0 1.5 collective-permute-start
  95.5 0.9 fusion
  96.4 2.7 %shard_map.79 = (bf16[6,64,256]{2,1,0:T(8,128)(2,1)S(1)}, bf16[6,64,256]{2,1,0:T(8,128)(2,1)}, bf16[6,64,256]{2,1,0:T(8,128)(2,1)}, bf16[6,64,256]{2,1,0:T(8,128)(2,1)S(1)}, f32[8,256]{1,0:T(8,128)S(1)}) custom-call(s32[74]{0:T(128)S(1)} %copy-done.6, bf16[1,24,128,256]{3,2,1,0:T(8,128)(2,1)S(1)} %copy-done.5, ...), custom_call_target="tpu_custom_call" | custom-call | tf_op jit(solution)/shard_map/pallas_call | solution.py:168
  99.0 0.0 collective-permute-start.12
  99.1 0.6 collective-permute-start.16
  99.7 2.7 %shard_map.80 = (bf16[6,64,256]{2,1,0:T(8,128)(2,1)S(1)}, bf16[6,64,256]{2,1,0:T(8,128)(2,1)}, bf16[6,64,256]{2,1,0:T(8,128)(2,1)}, bf16[6,64,256]{2,1,0:T(8,128)(2,1)S(1)}, f32[8,256]{1,0:T(8,128)S(1)}) custom-call(s32[74]{0:T(128)S(1)} %copy-done.6, bf16[1,24,128,256]{3,2,1,0:T(8,128)(2,1)S(1)} %copy-done.5, ...), custom_call_target="tpu_custom_call" | custom-call | tf_op jit(solution)/shard_map/pallas_call | solution.py:168
  102.4 1.0 collective-permute-done.8.refs_3_
  103.4 1.0 collective-permute-start.20
  104.4 7.3 %collective-permute-done.9.refs_4_ = bf16[6,128,256]{2,1,0:T(8,128)(2,1)S(1)} collective-permute-done((bf16[6,128,256]{2,1,0:T(8,128)(2,1)S(1)}, bf16[6,128,256]{2,1,0:T(8,128)(2,1)S(1)}, u32[]{:S(2)}, u32[]{:S(2)}) %collective-permute-start.9) | collective-permute-done | bytes 393248 | tf_op jit(solution)/shard_map/ppermute | solution.py:230
  111.7 1.9 %shard_map.81 = (bf16[6,64,256]{2,1,0:T(8,128)(2,1)S(1)}, bf16[6,64,256]{2,1,0:T(8,128)(2,1)S(1)}, bf16[6,64,256]{2,1,0:T(8,128)(2,1)S(1)}, bf16[6,64,256]{2,1,0:T(8,128)(2,1)S(1)}, f32[8,256]{1,0:T(8,128)S(1)}) custom-call(s32[74]{0:T(128)S(1)} %copy-done.6, bf16[1,24,128,256]{3,2,1,0:T(8,128)(2,1)S(1)} %copy-done.5, ...), custom_call_target="tpu_custom_call" | custom-call | tf_op jit(solution)/shard_map/pallas_call | solution.py:168
  113.7 0.7 copy-done.14
  114.4 0.6 add_reduce_fusion
  115.0 0.6 fusion.1
  115.7 0.1 collective-permute-start.24
  115.7 1.1 collective-permute-done.24
  116.8 0.6 fusion.2
  117.5 1.6 %collective-permute-start.25 = (f32[2]{0:T(128)S(1)}, f32[2]{0:T(128)S(1)}, u32[]{:S(2)}, u32[]{:S(2)}) collective-permute-start(f32[2]{0:T(128)S(1)} %fusion.2), channel_id=1, source_target_pairs={{0,2},{2,0},{1,3},{3,1},{4,6},{6,4},{5,7},{7,5},{8,10},{10,8},{9,1... | collective-permute-start | bytes 32 | tf_op jit(solution)/shard_map/ppermute | solution.py:247
  119.1 2.0 %collective-permute-done.25 = f32[2]{0:T(128)S(1)} collective-permute-done((f32[2]{0:T(128)S(1)}, f32[2]{0:T(128)S(1)}, u32[]{:S(2)}, u32[]{:S(2)}) %collective-permute-start.25) | collective-permute-done | bytes 40 | tf_op jit(solution)/shard_map/ppermute | solution.py:247
  121.1 0.6 collective-permute-start.15
  121.7 1.5 collective-permute-start.17
  123.2 3.5 %collective-permute-done.26 = f32[2]{0:T(128)S(1)} collective-permute-done((f32[2]{0:T(128)S(1)}, f32[2]{0:T(128)S(1)}, u32[]{:S(2)}, u32[]{:S(2)}) %collective-permute-start.26) | collective-permute-done | bytes 40 | tf_op jit(solution)/shard_map/ppermute | solution.py:247
  126.7 0.5 copy-done.17
  127.3 0.5 collective-permute-start.19
  127.8 2.1 %shard_map.69.refs_1_ = s32[74]{0:T(128)} custom-call(s32[1,96]{1,0:T(1,128)} %copy-done.16, s32[2]{0:T(128)} %pad_add_fusion.ids), custom_call_target="tpu_custom_call" | custom-call | tf_op jit(solution)/shard_map/pallas_call | solution.py:64
  129.9 0.6 add.30
  130.6 1.7 %collective-permute-start.23 = (bf16[6,64,256]{2,1,0:T(8,128)(2,1)}, bf16[6,64,256]{2,1,0:T(8,128)(2,1)S(1)}, u32[]{:S(2)}, u32[]{:S(2)}) collective-permute-start(bf16[6,64,256]{2,1,0:T(8,128)(2,1)} %copy-done.11), channel_id=1, source_target_pairs={{0,3},{1,2},{2,1},{3,0},{4,7},{5,6},{6,5},{7,4},{8,11},{9,10},{10,... | collective-permute-start | bytes 589832 | tf_op jit(solution)/shard_map/ppermute | solution.py:238
  132.3 1.6 %collective-permute-start.18 = (bf16[6,64,256]{2,1,0:T(8,128)(2,1)}, bf16[6,64,256]{2,1,0:T(8,128)(2,1)S(1)}, u32[]{:S(2)}, u32[]{:S(2)}) collective-permute-start(bf16[6,64,256]{2,1,0:T(8,128)(2,1)} %copy-done.13), channel_id=1, source_target_pairs={{0,2},{1,3},{2,0},{3,1},{4,6},{5,7},{6,4},{7,5},{8,10},{9,11},{10,... | collective-permute-start | bytes 589832 | tf_op jit(solution)/shard_map/ppermute | solution.py:238
  133.9 0.2 collective-permute-start.27
  134.1 4.3 %collective-permute-done.27 = f32[2]{0:T(128)S(1)} collective-permute-done((f32[2]{0:T(128)S(1)}, f32[2]{0:T(128)S(1)}, u32[]{:S(2)}, u32[]{:S(2)}) %collective-permute-start.27) | collective-permute-done | bytes 40 | tf_op jit(solution)/shard_map/ppermute | solution.py:247
  138.3 0.5 add_multiply_fusion
  138.8 3.3 %collective-permute-done.23.refs_19_ = bf16[6,64,256]{2,1,0:T(8,128)(2,1)S(1)} collective-permute-done((bf16[6,64,256]{2,1,0:T(8,128)(2,1)}, bf16[6,64,256]{2,1,0:T(8,128)(2,1)S(1)}, u32[]{:S(2)}, u32[]{:S(2)}) %collective-permute-start.23) | collective-permute-done | bytes 196640 | tf_op jit(solution)/shard_map/ppermute | solution.py:238
  142.1 4.3 %collective-permute-done.18.refs_14_ = bf16[6,64,256]{2,1,0:T(8,128)(2,1)S(1)} collective-permute-done((bf16[6,64,256]{2,1,0:T(8,128)(2,1)}, bf16[6,64,256]{2,1,0:T(8,128)(2,1)S(1)}, u32[]{:S(2)}, u32[]{:S(2)}) %collective-permute-start.18) | collective-permute-done | bytes 196640 | tf_op jit(solution)/shard_map/ppermute | solution.py:238
  146.4 4.1 %collective-permute-done.22.refs_18_ = bf16[6,64,256]{2,1,0:T(8,128)(2,1)S(1)} collective-permute-done((bf16[6,64,256]{2,1,0:T(8,128)(2,1)}, bf16[6,64,256]{2,1,0:T(8,128)(2,1)S(1)}, u32[]{:S(2)}, u32[]{:S(2)}) %collective-permute-start.22) | collective-permute-done | bytes 196640 | tf_op jit(solution)/shard_map/ppermute | solution.py:238
  150.6 0.6 copy-done.9
  151.2 4.5 %shard_map.82 = f32[2,24,64,256]{3,2,1,0:T(8,128)} custom-call(s32[74]{0:T(128)S(1)} %copy-done.7, s32[74]{0:T(128)S(1)} %copy-done.9, f32[24]{0:T(128)S(1)} %copy-done.8, bf16[2,24,64,256]{3,2,1,0:T(8,128)(2,1)S(1)} %copy-done.1, bf16[6,64,256]{2,1,0:T(8,128)(2,1)S(1)} %get-tuple-element.28.refs_4_, bf16[6,64,256]{2,1,0:T(8,128)(2,1)S(1)} %get-tuple-element.30.refs_5_, ...), custom_call_target="tpu_custom_call" | custom-call | tf_op jit(solution)/shard_map/pallas_call | solution.py:219
  (51 shorter events, 0.1 us)
Async XLA Ops:
  0.6 6.3 %collective-permute-start.1 = (bf16[1,24,128,256]{3,2,1,0:T(8,128)(2,1)}, bf16[1,24,128,256]{3,2,1,0:T(8,128)(2,1)S(1)}, u32[]{:S(2)}, u32[]{:S(2)}) collective-permute-start(bf16[1,24,128,256]{3,2,1,0:T(8,128)(2,1)} %refs_1_.16), channel_id=1, source_target_pairs={{0,1},{1,0},{2,3},{3,2},{4,5},{5,4},{6,7},{7,6},{8,9},{9,8},{10,11... | collective-permute-start | bytes 4718600 | tf_op jit(solution)/shard_map/ppermute | solution.py:230
  1.1 5.8 %collective-permute-start.2 = (bf16[2,24,64,256]{3,2,1,0:T(8,128)(2,1)}, bf16[2,24,64,256]{3,2,1,0:T(8,128)(2,1)S(1)}, u32[]{:S(2)}, u32[]{:S(2)}) collective-permute-start(bf16[2,24,64,256]{3,2,1,0:T(8,128)(2,1)} %refs_3_.9), channel_id=1, source_target_pairs={{0,1},{1,0},{2,3},{3,2},{4,5},{5,4},{6,7},{7,6},{8,9},{9,8},{10,11... | collective-permute-start | bytes 4718600 | tf_op jit(solution)/shard_map/ppermute | solution.py:230
  1.2 37.9 %collective-permute-start.4 = (bf16[2,24,64,256]{3,2,1,0:T(8,128)(2,1)}, bf16[2,24,64,256]{3,2,1,0:T(8,128)(2,1)}, u32[]{:S(2)}, u32[]{:S(2)}) collective-permute-start(bf16[2,24,64,256]{3,2,1,0:T(8,128)(2,1)} %refs_3_.9), channel_id=1, source_target_pairs={{0,2},{2,0},{1,3},{3,1},{4,6},{6,4},{5,7},{7,5},{8,10},{10,8},{9,1... | collective-permute-start | bytes 4718600 | tf_op jit(solution)/shard_map/ppermute | solution.py:230
  7.0 1.4 copy-start
  8.4 1.4 copy-start.2
  9.8 0.7 copy-start.6
  10.5 2.9 %copy-start.3 = (bf16[2,24,64,256]{3,2,1,0:T(8,128)(2,1)}, bf16[2,24,64,256]{3,2,1,0:T(8,128)(2,1)S(1)}, u32[]{:S(2)}) copy-start(bf16[2,24,64,256]{3,2,1,0:T(8,128)(2,1)S(1)} %collective-permute-done.2.refs_4_.refs_6_) | copy-start | bytes 4718596
  13.3 25.8 %copy-start.5 = (bf16[1,24,128,256]{3,2,1,0:T(8,128)(2,1)S(1)}, bf16[1,24,128,256]{3,2,1,0:T(8,128)(2,1)}, u32[]{:S(2)}) copy-start(bf16[1,24,128,256]{3,2,1,0:T(8,128)(2,1)} %refs_1_.19) | copy-start | bytes 4718596
  39.1 5.8 %collective-permute-start.5 = (bf16[2,24,64,256]{3,2,1,0:T(8,128)(2,1)}, bf16[2,24,64,256]{3,2,1,0:T(8,128)(2,1)S(1)}, u32[]{:S(2)}, u32[]{:S(2)}) collective-permute-start(bf16[2,24,64,256]{3,2,1,0:T(8,128)(2,1)} %collective-permute-done.4.refs_3_.refs_7_), channel_id=1, source_target_pairs={{0,1},{1,0},{2,3},{3,2},{4,5},{5,4},{6,7},{7,6},{8,9},{9,8},{10,11... | collective-permute-start | bytes 4718600 | tf_op jit(solution)/shard_map/ppermute | solution.py:230
  39.1 13.4 %collective-permute-start.3 = (bf16[1,24,128,256]{3,2,1,0:T(8,128)(2,1)S(1)}, bf16[1,24,128,256]{3,2,1,0:T(8,128)(2,1)S(1)}, u32[]{:S(2)}, u32[]{:S(2)}) collective-permute-start(bf16[1,24,128,256]{3,2,1,0:T(8,128)(2,1)S(1)} %copy-done.5), channel_id=1, source_target_pairs={{0,1},{1,0},{2,3},{3,2},{4,5},{5,4},{6,7},{7,6},{8,9},{9,8},{10,11... | collective-permute-start | bytes 4718600 | tf_op jit(solution)/shard_map/ppermute | solution.py:230
  39.6 15.6 %collective-permute-start.6 = (bf16[6,128,256]{2,1,0:T(8,128)(2,1)S(1)}, bf16[6,128,256]{2,1,0:T(8,128)(2,1)S(1)}, u32[]{:S(2)}, u32[]{:S(2)}) collective-permute-start(bf16[6,128,256]{2,1,0:T(8,128)(2,1)S(1)} %shard_map.70.refs_5_), channel_id=1, source_target_pairs={{0,4},{4,8},{8,12},{12,0},{1,5},{5,9},{9,13},{13,1},{2,6},{6,10},{... | collective-permute-start | bytes 1179656 | tf_op jit(solution)/shard_map/ppermute | solution.py:230
  46.7 5.8 %copy-start.1 = (bf16[2,24,64,256]{3,2,1,0:T(8,128)(2,1)S(1)}, bf16[2,24,64,256]{3,2,1,0:T(8,128)(2,1)}, u32[]{:S(2)}) copy-start(bf16[2,24,64,256]{3,2,1,0:T(8,128)(2,1)} %refs_3_.9) | copy-start | bytes 4718596
  46.7 5.8 %copy-start.4 = (bf16[2,24,64,256]{3,2,1,0:T(8,128)(2,1)S(1)}, bf16[2,24,64,256]{3,2,1,0:T(8,128)(2,1)}, u32[]{:S(2)}) copy-start(bf16[2,24,64,256]{3,2,1,0:T(8,128)(2,1)} %copy-done.3) | copy-start | bytes 4718596
  46.7 15.1 %collective-permute-start.7 = (bf16[6,128,256]{2,1,0:T(8,128)(2,1)S(1)}, bf16[6,128,256]{2,1,0:T(8,128)(2,1)S(1)}, u32[]{:S(2)}, u32[]{:S(2)}) collective-permute-start(bf16[6,128,256]{2,1,0:T(8,128)(2,1)S(1)} %shard_map.74.refs_5_), channel_id=1, source_target_pairs={{0,4},{4,8},{8,12},{12,0},{1,5},{5,9},{9,13},{13,1},{2,6},{6,10},{... | collective-permute-start | bytes 1179656 | tf_op jit(solution)/shard_map/ppermute | solution.py:230
  48.6 50.4 %collective-permute-start.10 = (bf16[6,128,256]{2,1,0:T(8,128)(2,1)S(1)}, bf16[6,128,256]{2,1,0:T(8,128)(2,1)S(1)}, u32[]{:S(2)}, u32[]{:S(2)}) collective-permute-start(bf16[6,128,256]{2,1,0:T(8,128)(2,1)S(1)} %shard_map.72.refs_5_), channel_id=1, source_target_pairs={{0,12},{4,0},{8,4},{12,8},{1,13},{5,1},{9,5},{13,9},{2,14},{6,2},{... | collective-permute-start | bytes 1179656 | tf_op jit(solution)/shard_map/ppermute | solution.py:230
  57.0 37.0 %copy-start.15 = (s32[1,96]{1,0:T(1,128)S(1)}, s32[1,96]{1,0:T(1,128)}, u32[]{:S(2)}) copy-start(s32[1,96]{1,0:T(1,128)} %partner.1) | copy-start | bytes 1156
  57.0 38.5 %copy-start.8 = (f32[24]{0:T(128)S(1)}, f32[24]{0:T(128)}, u32[]{:S(2)}) copy-start(f32[24]{0:T(128)} %refs_2_.1) | copy-start | bytes 292
  57.1 42.0 %collective-permute-start.11 = (bf16[6,128,256]{2,1,0:T(8,128)(2,1)S(1)}, bf16[6,128,256]{2,1,0:T(8,128)(2,1)S(1)}, u32[]{:S(2)}, u32[]{:S(2)}) collective-permute-start(bf16[6,128,256]{2,1,0:T(8,128)(2,1)S(1)} %shard_map.77.refs_5_), channel_id=1, source_target_pairs={{0,12},{4,0},{8,4},{12,8},{1,13},{5,1},{9,5},{13,9},{2,14},{6,2},{... | collective-permute-start | bytes 1179656 | tf_op jit(solution)/shard_map/ppermute | solution.py:230
  59.1 44.3 %collective-permute-start.8 = (bf16[6,128,256]{2,1,0:T(8,128)(2,1)S(1)}, bf16[6,128,256]{2,1,0:T(8,128)(2,1)S(1)}, u32[]{:S(2)}, u32[]{:S(2)}) collective-permute-start(bf16[6,128,256]{2,1,0:T(8,128)(2,1)S(1)} %shard_map.71.refs_5_), channel_id=1, source_target_pairs={{0,8},{4,12},{8,0},{12,4},{1,9},{5,13},{9,1},{13,5},{2,10},{6,14},... | collective-permute-start | bytes 1179656 | tf_op jit(solution)/shard_map/ppermute | solution.py:230
  63.7 48.0 %collective-permute-start.9 = (bf16[6,128,256]{2,1,0:T(8,128)(2,1)S(1)}, bf16[6,128,256]{2,1,0:T(8,128)(2,1)S(1)}, u32[]{:S(2)}, u32[]{:S(2)}) collective-permute-start(bf16[6,128,256]{2,1,0:T(8,128)(2,1)S(1)} %shard_map.78.refs_9_), channel_id=1, source_target_pairs={{0,8},{4,12},{8,0},{12,4},{1,9},{5,13},{9,1},{13,5},{2,10},{6,14},... | collective-permute-start | bytes 1179656 | tf_op jit(solution)/shard_map/ppermute | solution.py:230
  94.0 27.1 %collective-permute-start = (s32[1,96]{1,0:T(1,128)S(1)}, s32[1,96]{1,0:T(1,128)S(1)}, u32[]{:S(2)}, u32[]{:S(2)}) collective-permute-start(s32[1,96]{1,0:T(1,128)S(1)} %copy-done.15), channel_id=1, source_target_pairs={{0,2},{2,0},{1,3},{3,1},{4,6},{6,4},{5,7},{7,5},{8,10},{10,8},{9,1... | collective-permute-start | bytes 1160 | tf_op jit(solution)/shard_map/ppermute | solution.py:230
  99.0 3.4 %copy-start.10 = (bf16[6,64,256]{2,1,0:T(8,128)(2,1)}, bf16[6,64,256]{2,1,0:T(8,128)(2,1)S(1)}, u32[]{:S(2)}) copy-start(bf16[6,64,256]{2,1,0:T(8,128)(2,1)S(1)} %get-tuple-element.44) | copy-start | bytes 589828
  99.0 22.7 %collective-permute-start.12 = (bf16[6,64,256]{2,1,0:T(8,128)(2,1)S(1)}, bf16[6,64,256]{2,1,0:T(8,128)(2,1)S(1)}, u32[]{:S(2)}, u32[]{:S(2)}) collective-permute-start(bf16[6,64,256]{2,1,0:T(8,128)(2,1)S(1)} %get-tuple-element.35), channel_id=1, source_target_pairs={{0,1},{1,0},{2,3},{3,2},{4,5},{5,4},{6,7},{7,6},{8,9},{9,8},{10,11... | collective-permute-start | bytes 589832 | tf_op jit(solution)/shard_map/ppermute | solution.py:238
  99.1 24.1 %collective-permute-start.16 = (bf16[6,64,256]{2,1,0:T(8,128)(2,1)S(1)}, bf16[6,64,256]{2,1,0:T(8,128)(2,1)S(1)}, u32[]{:S(2)}, u32[]{:S(2)}) collective-permute-start(bf16[6,64,256]{2,1,0:T(8,128)(2,1)S(1)} %get-tuple-element.39), channel_id=1, source_target_pairs={{0,2},{1,3},{2,0},{3,1},{4,6},{5,7},{6,4},{7,5},{8,10},{9,11},{10,... | collective-permute-start | bytes 589832 | tf_op jit(solution)/shard_map/ppermute | solution.py:238
  102.4 9.3 %copy-start.11 = (bf16[6,64,256]{2,1,0:T(8,128)(2,1)}, bf16[6,64,256]{2,1,0:T(8,128)(2,1)S(1)}, u32[]{:S(2)}) copy-start(bf16[6,64,256]{2,1,0:T(8,128)(2,1)S(1)} %get-tuple-element.46) | copy-start | bytes 589828
  103.4 27.2 %collective-permute-start.20 = (bf16[6,64,256]{2,1,0:T(8,128)(2,1)}, bf16[6,64,256]{2,1,0:T(8,128)(2,1)S(1)}, u32[]{:S(2)}, u32[]{:S(2)}) collective-permute-start(bf16[6,64,256]{2,1,0:T(8,128)(2,1)} %get-tuple-element.43), channel_id=1, source_target_pairs={{0,3},{1,2},{2,1},{3,0},{4,7},{5,6},{6,5},{7,4},{8,11},{9,10},{10,... | collective-permute-start | bytes 589832 | tf_op jit(solution)/shard_map/ppermute | solution.py:238
  111.7 38.8 %copy-start.7 = (s32[74]{0:T(128)S(1)}, s32[74]{0:T(128)}, u32[]{:S(2)}) copy-start(s32[74]{0:T(128)} %shard_map.68.refs_0_) | copy-start | bytes 892
  113.7 0.7 copy-start.14
  114.4 8.8 %copy-start.12 = (bf16[6,64,256]{2,1,0:T(8,128)(2,1)}, bf16[6,64,256]{2,1,0:T(8,128)(2,1)S(1)}, u32[]{:S(2)}) copy-start(bf16[6,64,256]{2,1,0:T(8,128)(2,1)S(1)} %get-tuple-element.45) | copy-start | bytes 589828
  114.4 8.8 %copy-start.13 = (bf16[6,64,256]{2,1,0:T(8,128)(2,1)}, bf16[6,64,256]{2,1,0:T(8,128)(2,1)S(1)}, u32[]{:S(2)}) copy-start(bf16[6,64,256]{2,1,0:T(8,128)(2,1)S(1)} %get-tuple-element.41) | copy-start | bytes 589828
  115.7 1.2 collective-permute-start.24
  117.5 3.6 %collective-permute-start.25 = (f32[2]{0:T(128)S(1)}, f32[2]{0:T(128)S(1)}, u32[]{:S(2)}, u32[]{:S(2)}) collective-permute-start(f32[2]{0:T(128)S(1)} %fusion.2), channel_id=1, source_target_pairs={{0,2},{2,0},{1,3},{3,1},{4,6},{6,4},{5,7},{7,5},{8,10},{10,8},{9,1... | collective-permute-start | bytes 32 | tf_op jit(solution)/shard_map/ppermute | solution.py:247
  121.1 9.5 %collective-permute-start.13 = (bf16[6,64,256]{2,1,0:T(8,128)(2,1)}, bf16[6,64,256]{2,1,0:T(8,128)(2,1)S(1)}, u32[]{:S(2)}, u32[]{:S(2)}) collective-permute-start(bf16[6,64,256]{2,1,0:T(8,128)(2,1)} %get-tuple-element.36), channel_id=1, source_target_pairs={{0,1},{1,0},{2,3},{3,2},{4,5},{5,4},{6,7},{7,6},{8,9},{9,8},{10,11... | collective-permute-start | bytes 589832 | tf_op jit(solution)/shard_map/ppermute | solution.py:238
  121.1 6.7 %copy-start.16 = (s32[1,96]{1,0:T(1,128)}, s32[1,96]{1,0:T(1,128)S(1)}, u32[]{:S(2)}) copy-start(s32[1,96]{1,0:T(1,128)S(1)} %collective-permute-done.partner) | copy-start | bytes 1156
  121.1 11.2 %collective-permute-start.15 = (bf16[6,64,256]{2,1,0:T(8,128)(2,1)}, bf16[6,64,256]{2,1,0:T(8,128)(2,1)S(1)}, u32[]{:S(2)}, u32[]{:S(2)}) collective-permute-start(bf16[6,64,256]{2,1,0:T(8,128)(2,1)} %get-tuple-element.38), channel_id=1, source_target_pairs={{0,1},{1,0},{2,3},{3,2},{4,5},{5,4},{6,7},{7,6},{8,9},{9,8},{10,11... | collective-permute-start | bytes 589832 | tf_op jit(solution)/shard_map/ppermute | solution.py:238
  121.7 10.6 %collective-permute-start.17 = (bf16[6,64,256]{2,1,0:T(8,128)(2,1)}, bf16[6,64,256]{2,1,0:T(8,128)(2,1)S(1)}, u32[]{:S(2)}, u32[]{:S(2)}) collective-permute-start(bf16[6,64,256]{2,1,0:T(8,128)(2,1)} %get-tuple-element.40), channel_id=1, source_target_pairs={{0,2},{1,3},{2,0},{3,1},{4,6},{5,7},{6,4},{7,5},{8,10},{9,11},{10,... | collective-permute-start | bytes 589832 | tf_op jit(solution)/shard_map/ppermute | solution.py:238
  123.2 3.5 %collective-permute-start.26 = (f32[2]{0:T(128)S(1)}, f32[2]{0:T(128)S(1)}, u32[]{:S(2)}, u32[]{:S(2)}) collective-permute-start(f32[2]{0:T(128)S(1)} %add.29), channel_id=1, source_target_pairs={{0,4},{4,0},{8,12},{12,8},{1,5},{5,1},{9,13},{13,9},{2,6},{6,2},{1... | collective-permute-start | bytes 32 | tf_op jit(solution)/shard_map/ppermute | solution.py:247
  126.7 0.5 copy-start.17
  127.3 6.6 %collective-permute-start.19 = (bf16[6,64,256]{2,1,0:T(8,128)(2,1)}, bf16[6,64,256]{2,1,0:T(8,128)(2,1)}, u32[]{:S(2)}, u32[]{:S(2)}) collective-permute-start(bf16[6,64,256]{2,1,0:T(8,128)(2,1)} %get-tuple-element.42), channel_id=1, source_target_pairs={{0,2},{1,3},{2,0},{3,1},{4,6},{5,7},{6,4},{7,5},{8,10},{9,11},{10,... | collective-permute-start | bytes 589832 | tf_op jit(solution)/shard_map/ppermute | solution.py:238
  130.6 8.3 %collective-permute-start.21 = (bf16[6,64,256]{2,1,0:T(8,128)(2,1)}, bf16[6,64,256]{2,1,0:T(8,128)(2,1)S(1)}, u32[]{:S(2)}, u32[]{:S(2)}) collective-permute-start(bf16[6,64,256]{2,1,0:T(8,128)(2,1)} %copy-done.10), channel_id=1, source_target_pairs={{0,3},{1,2},{2,1},{3,0},{4,7},{5,6},{6,5},{7,4},{8,11},{9,10},{10,... | collective-permute-start | bytes 589832 | tf_op jit(solution)/shard_map/ppermute | solution.py:238
  130.6 11.6 %collective-permute-start.23 = (bf16[6,64,256]{2,1,0:T(8,128)(2,1)}, bf16[6,64,256]{2,1,0:T(8,128)(2,1)S(1)}, u32[]{:S(2)}, u32[]{:S(2)}) collective-permute-start(bf16[6,64,256]{2,1,0:T(8,128)(2,1)} %copy-done.11), channel_id=1, source_target_pairs={{0,3},{1,2},{2,1},{3,0},{4,7},{5,6},{6,5},{7,4},{8,11},{9,10},{10,... | collective-permute-start | bytes 589832 | tf_op jit(solution)/shard_map/ppermute | solution.py:238
  132.3 9.8 %collective-permute-start.14 = (bf16[6,64,256]{2,1,0:T(8,128)(2,1)}, bf16[6,64,256]{2,1,0:T(8,128)(2,1)S(1)}, u32[]{:S(2)}, u32[]{:S(2)}) collective-permute-start(bf16[6,64,256]{2,1,0:T(8,128)(2,1)} %copy-done.14), channel_id=1, source_target_pairs={{0,1},{1,0},{2,3},{3,2},{4,5},{5,4},{6,7},{7,6},{8,9},{9,8},{10,11... | collective-permute-start | bytes 589832 | tf_op jit(solution)/shard_map/ppermute | solution.py:238
  132.3 14.1 %collective-permute-start.18 = (bf16[6,64,256]{2,1,0:T(8,128)(2,1)}, bf16[6,64,256]{2,1,0:T(8,128)(2,1)S(1)}, u32[]{:S(2)}, u32[]{:S(2)}) collective-permute-start(bf16[6,64,256]{2,1,0:T(8,128)(2,1)} %copy-done.13), channel_id=1, source_target_pairs={{0,2},{1,3},{2,0},{3,1},{4,6},{5,7},{6,4},{7,5},{8,10},{9,11},{10,... | collective-permute-start | bytes 589832 | tf_op jit(solution)/shard_map/ppermute | solution.py:238
  133.9 4.4 %collective-permute-start.27 = (f32[2]{0:T(128)S(1)}, f32[2]{0:T(128)S(1)}, u32[]{:S(2)}, u32[]{:S(2)}) collective-permute-start(f32[2]{0:T(128)S(1)} %add.30), channel_id=1, source_target_pairs={{0,8},{4,12},{8,0},{12,4},{1,9},{5,13},{9,1},{13,5},{2,10},{6,14},... | collective-permute-start | bytes 32 | tf_op jit(solution)/shard_map/ppermute | solution.py:247
  138.3 12.2 %collective-permute-start.22 = (bf16[6,64,256]{2,1,0:T(8,128)(2,1)}, bf16[6,64,256]{2,1,0:T(8,128)(2,1)S(1)}, u32[]{:S(2)}, u32[]{:S(2)}) collective-permute-start(bf16[6,64,256]{2,1,0:T(8,128)(2,1)} %copy-done.12), channel_id=1, source_target_pairs={{0,3},{1,2},{2,1},{3,0},{4,7},{5,6},{6,5},{7,4},{8,11},{9,10},{10,... | collective-permute-start | bytes 589832 | tf_op jit(solution)/shard_map/ppermute | solution.py:238
  150.6 0.6 copy-start.9

commit v3 on v2

v3 whole, which is shorter than its diff:
```python
import functools

import jax
import jax.numpy as jnp
from jax import lax
from jax.experimental import pallas as pl
from jax.experimental.pallas import tpu as pltpu
from jax.sharding import PartitionSpec as P

ANY = pl.BlockSpec(memory_space=pl.ANY)
HBM = pl.BlockSpec(memory_space=pltpu.HBM)
SMEM = pl.BlockSpec(memory_space=pltpu.SMEM)
VMEM = pl.BlockSpec(memory_space=pltpu.VMEM)
LIMIT = 40 * 1024 * 1024
BRIEF = pl.CostEstimate(flops=0, bytes_accessed=0, transcendentals=0)


def aligned(index, size):
    return pl.multiple_of(index * size, size)


class Sizes:
    def __init__(self, vectors, left_env):
        self.env = lax.axis_size("env")
        self.rep = lax.axis_size("rep")
        self.sector = lax.axis_size("sector")
        self.batch, self.slots, self.own_rows, self.order = vectors.shape
        assert self.batch == self.rep and self.sector % 4 == 0
        self.half = left_env.shape[2]
        self.chip_rows = self.own_rows * self.rep
        self.capacity = 2 * ((self.slots + 2 * self.sector - 1) // (2 * self.sector))
        self.flat = self.sector * self.capacity
        self.full = self.flat == self.slots
        self.source, self.target, self.valid = 0, self.flat, 2 * self.flat
        self.core, self.chip = 3 * self.flat, 3 * self.flat + 1

    def when_valid(self, plan, flat, action):
        if self.full:
            action()
        else:
            pl.when(plan[self.valid + flat] == 1)(action)


def write_plan(z, partner, plan, count):
    if not z.full:

        def clear(i, carry):
            plan[i] = 0
            return carry

        lax.fori_loop(0, 3 * z.flat, clear, 0)
    for d in range(z.sector):
        count[d] = 0
    for j in range(z.slots):
        sector = partner[0, j]
        group = lax.div(sector, z.slots)
        slot = sector - group * z.slots
        distance = lax.rem(z.sector - group, z.sector)
        rank = count[distance]
        count[distance] = rank + 1
        index = distance * z.capacity + rank
        plan[z.source + index] = slot
        plan[z.target + index] = j
        plan[z.valid + index] = 1
    plan[z.core] = lax.axis_index("rep")
    plan[z.chip] = lax.axis_index("env")


def load_body(z, partner, vectors, right, plan, *refs):
    rows, block, count, sem = refs[: z.rep], refs[z.rep], refs[-2], refs[-1]
    core = lax.axis_index("rep")
    copies = [pltpu.make_async_copy(right, block, sem.at[z.rep])]
    for s, ref in enumerate(rows):
        copies.append(
            pltpu.make_async_copy(vectors.at[lax.rem(core + s, z.rep)], ref, sem.at[s])
        )
    for copy in copies:
        copy.start()
    write_plan(z, partner, plan, count)
    for copy in copies:
        copy.wait()


def load(z, partner, vectors, right_env):
    row = jax.ShapeDtypeStruct(vectors.shape[1:], jnp.bfloat16)
    plan, *made = pl.pallas_call(
        functools.partial(load_body, z),
        out_shape=[jax.ShapeDtypeStruct((3 * z.flat + 2,), jnp.int32)]
        + [row] * z.rep
        + [jax.ShapeDtypeStruct(right_env.shape, jnp.bfloat16)],
        in_specs=[SMEM, HBM, HBM],
        out_specs=[SMEM] + [VMEM] * (z.rep + 1),
        scratch_shapes=[pltpu.SMEM((z.sector,), jnp.int32), pltpu.SemaphoreType.DMA((z.rep + 1,))],
        compiler_params=pltpu.CompilerParams(vmem_limit_bytes=LIMIT),
        cost_estimate=BRIEF,
    )(
        partner,
        pltpu.with_memory_space_constraint(vectors, pltpu.HBM),
        pltpu.with_memory_space_constraint(right_env, pltpu.HBM),
    )
    return plan, made[: z.rep], made[z.rep]


def plan_only(z, partner):
    return pl.pallas_call(
        functools.partial(write_plan, z),
        out_shape=jax.ShapeDtypeStruct((3 * z.flat + 2,), jnp.int32),
        in_specs=[SMEM],
        out_specs=SMEM,
        scratch_shapes=[pltpu.SMEM((z.sector,), jnp.int32)],
        cost_estimate=BRIEF,
    )(partner)


def gate(arrays, after):
    def body(*refs):
        pass

    return pl.pallas_call(
        body,
        out_shape=[jax.ShapeDtypeStruct(a.shape, a.dtype) for a in arrays],
        in_specs=[ANY] * (len(arrays) + len(after)),
        out_specs=[ANY] * len(arrays),
        input_output_aliases={i: i for i in range(len(arrays))},
        cost_estimate=BRIEF,
    )(*arrays, *after)


def pick(z, core, place, candidates):
    chosen = candidates[0]
    for s in range(1, z.rep):
        chosen = jnp.where(lax.rem(core + z.rep - s, z.rep) == place, candidates[s], chosen)
    return chosen


def products_body(z, pieces, spans, copied, *refs):
    refs = list(refs)
    if copied:
        sem = refs.pop()
        copy = pltpu.make_async_copy(refs[1 + z.rep * (1 + pieces)], refs.pop(), sem)
        copy.start()
    plan = refs.pop(0)
    right = [refs.pop(0) for _ in range(z.rep)]
    rows = [[refs.pop(0) for _ in range(z.rep)] for _ in range(pieces)]
    outs = refs[-len(spans) :]
    core = plan[z.core]
    for (first, count), out in zip(spans, outs):
        for i in range(count):
            slot = plan[z.source + first + i]
            halves = [ref[0, slot] for ref in right]
            parts = [[ref[slot] for ref in piece] for piece in rows]
            block = jnp.concatenate([pick(z, core, k, halves) for k in range(z.rep)], axis=0)
            lines = jnp.concatenate(
                [pick(z, core, k, part) for part in parts for k in range(z.rep)], axis=0
            )
            out[i] = lax.dot_general(
                lines, block, (((1,), (1,)), ((), ())), preferred_element_type=jnp.float32
            ).astype(jnp.bfloat16)
    if copied:
        copy.wait()


def products(z, plan, right, rows, spans, after=(), copied=None):
    pieces = len(rows)
    flat = [ref for piece in rows for ref in piece]
    height = pieces * z.chip_rows
    shapes = [(count, height, z.order) for _, count in spans]
    scratch = []
    if copied is not None:
        shapes.append(copied.shape)
        scratch = [pltpu.SemaphoreType.DMA]
        after = (pltpu.with_memory_space_constraint(copied, pltpu.HBM), *after)
    return pl.pallas_call(
        functools.partial(products_body, z, pieces, spans, copied is not None),
        out_shape=[jax.ShapeDtypeStruct(shape, jnp.bfloat16) for shape in shapes],
        in_specs=[SMEM]
        + [VMEM] * (len(right) + len(flat))
        + [HBM if copied is not None and i == 0 else ANY for i in range(len(after))],
        out_specs=[VMEM] * len(shapes),
        scratch_shapes=scratch,
        compiler_params=pltpu.CompilerParams(vmem_limit_bytes=LIMIT),
        cost_estimate=BRIEF,
    )(plan, *right, *flat, *after)


def terms_body(z, spans, *refs):
    refs = list(refs)
    plan = refs.pop(0)
    left = [refs.pop(0) for _ in range(z.rep)]
    near = [refs.pop(0) for _ in spans]
    far = [refs.pop(0) for _ in spans]
    vec = [[refs.pop(0) for _ in range(z.rep)] for _ in range(z.env)]
    pbuf, tbuf = refs[-2:]
    dots = refs[-3]
    outs = refs[-3 - z.env * z.rep : -3]
    core, chip = plan[z.core], plan[z.chip]
    total = jnp.zeros(dots.shape, jnp.float32)
    n = 0
    for d, (first, count, skip) in enumerate(spans):
        for i in range(count):
            slot = plan[z.target + first + i]
            for e in range(z.env):
                place = lax.rem(chip + z.env - e, z.env)
                if e == 0:
                    lines = near[d][skip + i]
                else:
                    lines = far[d][i, (e - 1) * z.chip_rows : e * z.chip_rows]
                pbuf[n, pl.ds(aligned(place, z.chip_rows), z.chip_rows)] = lines
            halves = [ref[0, slot] for ref in left]
            block = jnp.concatenate([pick(z, core, k, halves) for k in range(z.rep)], axis=0)
            tbuf[n] = jnp.dot(block, pbuf[n], preferred_element_type=jnp.float32).astype(
                jnp.bfloat16
            )
            folded = jnp.zeros(dots.shape, jnp.float32)
            for e in range(z.env):
                for s in range(z.rep):
                    place = lax.rem(chip + e, z.env) * z.rep + lax.rem(core + s, z.rep)
                    term = tbuf[n, pl.ds(aligned(place, z.own_rows), z.own_rows)]
                    outs[e * z.rep + s][n] = term
                    lines = vec[(z.env - e) % z.env][(z.rep - s) % z.rep][slot]
                    both = lines.astype(jnp.float32) * term.astype(jnp.float32)
                    folded += jnp.sum(both.reshape(-1, *dots.shape), axis=0)
            if not z.full:
                folded = jnp.where(plan[z.valid + first + i] == 1, folded, 0.0)
            total += folded
            n += 1
    dots[...] = total


def terms(z, plan, left, near, far, vec, spans, after=()):
    count = sum(span[1] for span in spans)
    flat = [ref for piece in vec for ref in piece]
    shapes = [(count, z.own_rows, z.order)] * (z.env * z.rep)
    whole = (count, z.order, z.order)
    *made, dots = pl.pallas_call(
        functools.partial(terms_body, z, spans),
        out_shape=[jax.ShapeDtypeStruct(shape, jnp.bfloat16) for shape in shapes]
        + [jax.ShapeDtypeStruct((8, z.order), jnp.float32)],
        in_specs=[SMEM]
        + [VMEM] * (len(left) + len(near) + len(far) + len(flat))
        + [ANY] * len(after),
        out_specs=[VMEM] * (len(shapes) + 1),
        scratch_shapes=[pltpu.VMEM(whole, jnp.bfloat16), pltpu.VMEM(whole, jnp.bfloat16)],
        compiler_params=pltpu.CompilerParams(vmem_limit_bytes=LIMIT),
        cost_estimate=BRIEF,
    )(plan, *left, *near, *far, *flat, *after)
    return made, dots


def add_terms(z, plans, image, parts, spans):
    core = plans[0][z.core]
    n = 0
    for first, count, _ in spans:
        for i in range(count):
            for e, plan in enumerate(plans):

                def add():
                    slot = plan[z.target + first + i]
                    for s in range(z.rep):
                        v = lax.rem(core + z.rep - s, z.rep)
                        image[v, slot] += parts[e][s][n].astype(jnp.float32)

                z.when_valid(plan, first + i, add)
            n += 1


def gather_body(z, chunks, *refs):
    refs = list(refs)
    plans = [refs.pop(0) for _ in range(z.env)]
    energy, vectors, image = refs.pop(0), refs.pop(0), refs[-1]

    def start(j, carry):
        for v in range(z.batch):
            image[v, j] = energy[j] * vectors[v, j].astype(jnp.float32)
        return carry

    lax.fori_loop(0, z.slots, start, 0, unroll=2)
    for spans in chunks:
        parts = [[refs.pop(0) for _ in range(z.rep)] for _ in range(z.env)]
        add_terms(z, plans, image, parts, spans)


def gather_terms(z, plans, energy, vectors, parts, chunks, after=()):
    flat = [ref for chunk in parts for piece in chunk for ref in piece]
    return pl.pallas_call(
        functools.partial(gather_body, z, chunks),
        out_shape=jax.ShapeDtypeStruct(vectors.shape, jnp.float32),
        in_specs=[SMEM] * (z.env + 1) + [VMEM] * (1 + len(flat)) + [ANY] * len(after),
        out_specs=VMEM,
        compiler_params=pltpu.CompilerParams(vmem_limit_bytes=LIMIT),
        cost_estimate=BRIEF,
    )(*plans, energy, vectors, *flat, *after)


def image_body(z, spans, *refs):
    refs = list(refs)
    plans = [refs.pop(0) for _ in range(z.env)]
    so_far = refs.pop(0)
    image = refs.pop()
    parts = [[refs.pop(0) for _ in range(z.rep)] for _ in range(z.env)]

    def start(j, carry):
        for v in range(z.batch):
            image[v, j] = so_far[v, j]
        return carry

    lax.fori_loop(0, z.slots, start, 0, unroll=2)
    add_terms(z, plans, image, parts, spans)


def make_image(z, plans, so_far, parts, spans):
    flat = [ref for piece in parts for ref in piece]
    return pl.pallas_call(
        functools.partial(image_body, z, spans),
        out_shape=jax.ShapeDtypeStruct(so_far.shape, jnp.float32),
        in_specs=[SMEM] * z.env + [VMEM] * (1 + len(flat)),
        out_specs=VMEM,
        compiler_params=pltpu.CompilerParams(vmem_limit_bytes=LIMIT),
        cost_estimate=BRIEF,
    )(*plans, so_far, *flat)


def shift(array, axis, size, step):
    return lax.ppermute(array, axis, [(i, (i + step) % size) for i in range(size)])


def shift_both(z, array, e, s):
    perm = []
    for x in range(z.env):
        for c in range(z.rep):
            perm.append((x * z.rep + c, (x + e) % z.env * z.rep + (c + s) % z.rep))
    return lax.ppermute(array, ("env", "rep"), perm)


def total_over(array, axis):
    size = lax.axis_size(axis)
    if size & (size - 1):
        return lax.psum(array, axis)
    step = 1
    while step < size:
        array = array + lax.ppermute(array, axis, [(i, i ^ step) for i in range(size)])
        step *= 2
    return array


def on_device(vectors, left_env, right_env, energy, partner):
    z = Sizes(vectors, left_env)
    each = z.sector // 4
    span = z.capacity

    def spans_of(g, low=0, count=span):
        return [((g * each + d) * span + low, count, low) for d in range(each)]

    def plain(spans):
        return tuple(piece[:2] for piece in spans)

    def around(array):
        return [array] + [shift(array, "rep", z.rep, s) for s in range(1, z.rep)]

    def across(arrays, g):
        steps = [g * each + d for d in range(each)]
        return [shift(a, "sector", z.sector, k) if k else a for a, k in zip(arrays, steps)]

    right_others = around(right_env)[1:]
    plan, own, right_own = load(z, partner, vectors, right_env)
    right = [right_own] + right_others
    near_rows = [own[0]] + [shift(own[s], "rep", z.rep, s) for s in range(1, z.rep)]
    vec = [near_rows]
    for e in range(1, z.env):
        vec.append([shift_both(z, own[s], e, s) for s in range(z.rep)])
    plans = [plan]
    for e in range(1, z.env):
        plans.append(plan_only(z, shift(partner, "env", z.env, e)))

    near = {}
    *made, left_own = products(z, plan, right, [near_rows], plain(spans_of(1)), (), left_env)
    near[1] = across(made, 1)
    left = around(left_own)
    made = products(z, plan, right, [near_rows], plain(spans_of(3)), made[:1])
    near[3] = across(made, 3)
    made = products(z, plan, right, [near_rows], plain(spans_of(2)), (made[0], *left[1:]))
    near[2] = across(made, 2)
    chain = (made[0], *plans[1:])

    chunks = {g: spans_of(g) for g in range(4)}
    far, parts = {}, {}

    def far_products(g, spans, after):
        return products(z, plan, right, vec[1:], plain(spans), after)

    def send_terms(g, after):
        made, folded = terms(z, plan, left, near[g], far[g], vec, chunks[g], after)
        parts[g] = [
            [
                shift_both(z, made[e * z.rep + s], e, s) if e + s else made[0]
                for s in range(z.rep)
            ]
            for e in range(z.env)
        ]
        return folded

    def arrived(g):
        return [part for piece in parts[g] for part in piece][1:]

    made = far_products(1, chunks[1], chain)
    sent = [array for g in (1, 3, 2) for array in near[g]]
    far[1] = across(gate(made, sent), 1)
    near[0] = products(z, plan, right, [near_rows], plain(chunks[0]), made[:1])
    far[0] = far_products(0, chunks[0], near[0][:1])
    dot0 = send_terms(0, ())
    made = far_products(3, chunks[3], (dot0,))
    far[3] = across(made, 3)
    made = far_products(2, chunks[2], (made[0], far[1][0]))
    far[2] = across(made, 2)
    dot1 = send_terms(1, made[:1])
    dot3 = send_terms(3, (dot1, *arrived(0)))
    dot2 = send_terms(2, (dot3, *arrived(1), *arrived(3)))
    early = (0, 1, 3)
    so_far = gather_terms(
        z,
        plans,
        energy,
        vectors,
        [parts[g] for g in early],
        [chunks[g] for g in early],
        (dot2,),
    )
    image = make_image(z, plans, so_far, parts[2], chunks[2])

    own_block = vectors.astype(jnp.float32)
    partial_sum = jnp.sum(energy[None, :, None, None] * own_block * own_block, axis=(1, 2, 3))
    own_vector = (jnp.arange(z.batch) == lax.axis_index("rep")).astype(jnp.float32)
    partial_sum = partial_sum + own_vector * jnp.sum(dot0 + dot1 + dot2 + dot3)
    for axis in ("sector", "env", "rep"):
        partial_sum = total_over(partial_sum, axis)
    entries = z.slots * z.sector * z.order * z.order
    return (image, partial_sum / entries)


def solution(mesh):
    return jax.shard_map(
        on_device,
        mesh=mesh,
        in_specs=(
            P(None, ("groups", "sector"), ("env", "rep"), None),
            P("env", ("groups", "sector"), "rep", None),
            P("env", ("groups", "sector"), "rep", None),
            P(("groups", "sector")),
            P("env", "groups"),
        ),
        out_specs=(P(None, ("groups", "sector"), ("env", "rep"), None), P("groups")),
        check_vma=False,
    )
```

time: 156 us -> 135 us (0.87)
  starting transfers between devices: 53 us -> 27.3 us
  Pallas kernels: 29.8 us -> 38.6 us
  waiting for transfers between devices: 62 us -> 56.1 us
  local copies, waits for them, and re-layouts: 5.36 us -> 7.98 us
    ppermute x12 -> x10, starting transfers between devices: 43.6 us -> 13 us  [shift(): lax.ppermute(array, axis, [(i, (i + step) % size) for i in range(size)])]
    pallas_call x15 -> x17, Pallas kernels: 29.8 us -> 38.6 us  [the longest x8 18.4 us: products(): pl.pallas_call(functools.partial(products_body, z, pieces, spans, copied...]
    ppermute x12 -> x14, starting transfers between devices: 7.56 us -> 11.6 us  [shift_both(): return lax.ppermute(array, ('env', 'rep'), perm)]
    ppermute x12 -> x14, waiting for transfers between devices: 11.7 us -> 8.09 us  [shift_both(): return lax.ppermute(array, ('env', 'rep'), perm)]
    ppermute x4, waiting for transfers between devices: 10.9 us -> 8.25 us  [total_over(): lax.ppermute(array, axis, [(i, i ^ step) for i in range(size)])]
    unnamed x36 -> x58, local copies, waits for them, and re-layouts: 5.36 us -> 7.98 us
    ppermute x12 -> x10, waiting for transfers between devices: 39.4 us -> 39.7 us  [shift(): lax.ppermute(array, axis, [(i, (i + step) % size) for i in range(size)])]
  transfers between devices with their start and end apart: 28 -> 28, of which waited for: 12 -> 10; matrix products, arithmetic and copies ran while one was open for 3% -> 2% of each run, Pallas kernels for 16% -> 22%
where the time goes in v3:
time: 135 us; the launch traced here: 134 us
  waiting for transfers between devices  56.1 us (42%)
  Pallas kernels  38.6 us (29%)
  starting transfers between devices  27.3 us (20%)
  local copies, waits for them, and re-layouts  7.98 us (6%)
  other arithmetic  3.31 us (2%)
    ppermute x10, waiting for transfers between devices, shift(): lax.ppermute(array, axis, [(i, (i + step) % size) for i in range(size)])  39.7 us
    pallas_call x8, Pallas kernels, products(): pl.pallas_call(functools.partial(products_body, z, pieces, spans, copied...  18.4 us
    ppermute x10, starting transfers between devices, shift(): lax.ppermute(array, axis, [(i, (i + step) % size) for i in range(size)])  13 us
    ppermute x14, starting transfers between devices, shift_both(): return lax.ppermute(array, ('env', 'rep'), perm)  11.6 us
    pallas_call x4, Pallas kernels, terms(): pl.pallas_call(functools.partial(terms_body, z, spans), out_shape=[jax.Sh...  10.9 us
    ppermute x4, waiting for transfers between devices, total_over(): lax.ppermute(array, axis, [(i, i ^ step) for i in range(size)])  8.25 us
    ppermute x14, waiting for transfers between devices, shift_both(): return lax.ppermute(array, ('env', 'rep'), perm)  8.09 us
    unnamed x58, local copies, waits for them, and re-layouts  7.98 us
  transfers between devices with their start and end apart: 28, of which 10 were waited for; matrix products, arithmetic and copies ran while one was open for 2% of the time, Pallas kernels for 22%

profile of v3, /device:TPU:0, one launch (start us, length us, event | category | flops | bytes accessed | tf_op | source)
XLA Modules:
  0.0 134.2 jit_solution(7992634083899651272)
XLA Ops:
  0.6 0.5 collective-permute-start.1
  1.1 0.7 copy-done.26
  1.8 3.6 %shard_map.68 = (s32[74]{0:T(128)S(1)}, bf16[24,64,256]{2,1,0:T(8,128)(2,1)}, bf16[24,64,256]{2,1,0:T(8,128)(2,1)}, bf16[1,24,128,256]{3,2,1,0:T(8,128)(2,1)S(1)}) custom-call(s32[1,96]{1,0:T(1,128)S(1)} %copy-done.26, bf16[2,24,64,256]{3,2,1,0:T(8,128)(2,1)} %refs_3_.1, bf16[1,24,128,256]{3,2,1,0:T(8,128)(2,1)} %right.1), custom_call_target="tpu_custom_call" | custom-call | tf_op jit(solution)/shard_map/pallas_call | solution.py:86
  5.5 2.4 %collective-permute-done.2.refs_4_.refs_6_ = bf16[24,64,256]{2,1,0:T(8,128)(2,1)S(1)} collective-permute-done((bf16[24,64,256]{2,1,0:T(8,128)(2,1)}, bf16[24,64,256]{2,1,0:T(8,128)(2,1)S(1)}, u32[]{:S(2)}, u32[]{:S(2)}) %collective-permute-start.2) | collective-permute-done | bytes 786464 | tf_op jit(solution)/shard_map/ppermute | solution.py:324
  8.0 3.8 %shard_map.70 = (bf16[6,128,256]{2,1,0:T(8,128)(2,1)}, bf16[1,24,128,256]{3,2,1,0:T(8,128)(2,1)S(1)}) custom-call(s32[74]{0:T(128)S(1)} %get-tuple-element.28.refs_0_, bf16[1,24,128,256]{3,2,1,0:T(8,128)(2,1)S(1)} %get-tuple-element.29.refs_1_, bf16[1,24,128,256]{3,2,1,0:T(8,128)(2,1)S(1)} %collective-permute-done.1.refs_2_, ...), custom_call_target="tpu_custom_call" | custom-call | tf_op jit(solution)/shard_map/pallas_call | solution.py:173
  11.8 0.2 collective-permute-start.3
  12.0 2.9 %collective-permute-start.4 = (bf16[24,64,256]{2,1,0:T(8,128)(2,1)}, bf16[24,64,256]{2,1,0:T(8,128)(2,1)}, u32[]{:S(2)}, u32[]{:S(2)}) collective-permute-start(bf16[24,64,256]{2,1,0:T(8,128)(2,1)} %get-tuple-element.30.refs_3_.refs_5_), channel_id=1, source_target_pairs={{0,2},{1,3},{2,0},{3,1},{4,6},{5,7},{6,4},{7,5},{8,10},{9,11},{10,... | collective-permute-start | bytes 2359304 | tf_op jit(solution)/shard_map/ppermute | solution.py:332
  14.8 1.5 %collective-permute-start = (s32[1,96]{1,0:T(1,128)S(1)}, s32[1,96]{1,0:T(1,128)S(1)}, u32[]{:S(2)}, u32[]{:S(2)}) collective-permute-start(s32[1,96]{1,0:T(1,128)S(1)} %copy-done.26), channel_id=1, source_target_pairs={{0,2},{2,0},{1,3},{3,1},{4,6},{6,4},{5,7},{7,5},{8,10},{10,8},{9,1... | collective-permute-start | bytes 1160 | tf_op jit(solution)/shard_map/ppermute | solution.py:324
  16.3 1.6 %collective-permute-start.9 = (bf16[6,128,256]{2,1,0:T(8,128)(2,1)}, bf16[6,128,256]{2,1,0:T(8,128)(2,1)}, u32[]{:S(2)}, u32[]{:S(2)}) collective-permute-start(bf16[6,128,256]{2,1,0:T(8,128)(2,1)} %get-tuple-element.33.refs_5_), channel_id=1, source_target_pairs={{0,4},{4,8},{8,12},{12,0},{1,5},{5,9},{9,13},{13,1},{2,6},{6,10},{... | collective-permute-start | bytes 1179656 | tf_op jit(solution)/shard_map/ppermute | solution.py:324
  17.9 2.3 %shard_map.71.refs_5_ = bf16[6,128,256]{2,1,0:T(8,128)(2,1)} custom-call(s32[74]{0:T(128)S(1)} %get-tuple-element.28.refs_0_, bf16[1,24,128,256]{3,2,1,0:T(8,128)(2,1)S(1)} %get-tuple-element.29.refs_1_, bf16[1,24,128,256]{3,2,1,0:T(8,128)(2,1)S(1)} %collective-permute-done.1.refs_2_, bf16[24,64,256]{2,1,0:T(8,128)(2,1)} %get-tuple-element.30.refs_3_.refs_5_, ...), custom_call_target="tpu_custom_call" | custom-call | tf_op jit(solution)/shard_map/pallas_call | solution.py:173
  20.2 2.3 %collective-permute-start.10 = (bf16[6,128,256]{2,1,0:T(8,128)(2,1)}, bf16[6,128,256]{2,1,0:T(8,128)(2,1)}, u32[]{:S(2)}, u32[]{:S(2)}) collective-permute-start(bf16[6,128,256]{2,1,0:T(8,128)(2,1)} %shard_map.71.refs_5_), channel_id=1, source_target_pairs={{0,12},{4,0},{8,4},{12,8},{1,13},{5,1},{9,5},{13,9},{2,14},{6,2},{... | collective-permute-start | bytes 1179656 | tf_op jit(solution)/shard_map/ppermute | solution.py:324
  22.5 2.3 %shard_map.72.refs_5_ = bf16[6,128,256]{2,1,0:T(8,128)(2,1)} custom-call(s32[74]{0:T(128)S(1)} %get-tuple-element.28.refs_0_, bf16[1,24,128,256]{3,2,1,0:T(8,128)(2,1)S(1)} %get-tuple-element.29.refs_1_, bf16[1,24,128,256]{3,2,1,0:T(8,128)(2,1)S(1)} %collective-permute-done.1.refs_2_, bf16[24,64,256]{2,1,0:T(8,128)(2,1)} %get-tuple-element.30.refs_3_.refs_5_, ...), custom_call_target="tpu_custom_call" | custom-call | tf_op jit(solution)/shard_map/pallas_call | solution.py:173
  24.9 24.8 %collective-permute-done.partner = s32[1,96]{1,0:T(1,128)S(1)} collective-permute-done((s32[1,96]{1,0:T(1,128)S(1)}, s32[1,96]{1,0:T(1,128)S(1)}, u32[]{:S(2)}, u32[]{:S(2)}) %collective-permute-start) | collective-permute-done | bytes 416 | tf_op jit(solution)/shard_map/ppermute | solution.py:324
  49.7 2.8 %collective-permute-start.11 = (bf16[6,128,256]{2,1,0:T(8,128)(2,1)}, bf16[6,128,256]{2,1,0:T(8,128)(2,1)}, u32[]{:S(2)}, u32[]{:S(2)}) collective-permute-start(bf16[6,128,256]{2,1,0:T(8,128)(2,1)} %shard_map.72.refs_5_), channel_id=1, source_target_pairs={{0,8},{4,12},{8,0},{12,4},{1,9},{5,13},{9,1},{13,5},{2,10},{6,14},... | collective-permute-start | bytes 1179656 | tf_op jit(solution)/shard_map/ppermute | solution.py:324
  52.6 1.4 %shard_map.69.refs_6_.refs_1_ = s32[74]{0:T(128)} custom-call(s32[1,96]{1,0:T(1,128)} %copy-done.28), custom_call_target="tpu_custom_call" | custom-call | tf_op jit(solution)/shard_map/pallas_call | solution.py:105
  54.0 0.7 copy-done.23
  54.6 1.8 %shard_map.73.refs_5_.refs_0_ = bf16[6,128,256]{2,1,0:T(8,128)(2,1)S(1)} custom-call(s32[74]{0:T(128)S(1)} %get-tuple-element.28.refs_0_, bf16[1,24,128,256]{3,2,1,0:T(8,128)(2,1)S(1)} %get-tuple-element.29.refs_1_, bf16[1,24,128,256]{3,2,1,0:T(8,128)(2,1)S(1)} %collective-permute-done.1.refs_2_, ...), custom_call_target="tpu_custom_call" | custom-call | tf_op jit(solution)/shard_map/pallas_call | solution.py:173
  56.5 1.7 %shard_map.74.refs_5_.refs_3_ = bf16[6,128,256]{2,1,0:T(8,128)(2,1)S(1)} custom-call(s32[74]{0:T(128)S(1)} %get-tuple-element.28.refs_0_, bf16[1,24,128,256]{3,2,1,0:T(8,128)(2,1)S(1)} %get-tuple-element.29.refs_1_, bf16[1,24,128,256]{3,2,1,0:T(8,128)(2,1)S(1)} %collective-permute-done.1.refs_2_, bf16[24,64,256]{2,1,0:T(8,128)(2,1)} %get-tuple-element.30.refs_3_.refs_5_, ...), custom_call_target="tpu_custom_call" | custom-call | tf_op jit(solution)/shard_map/pallas_call | solution.py:173
  58.2 11.9 %collective-permute-done.11.refs_3_ = bf16[6,128,256]{2,1,0:T(8,128)(2,1)} collective-permute-done((bf16[6,128,256]{2,1,0:T(8,128)(2,1)}, bf16[6,128,256]{2,1,0:T(8,128)(2,1)}, u32[]{:S(2)}, u32[]{:S(2)}) %collective-permute-start.11) | collective-permute-done | bytes 393248 | tf_op jit(solution)/shard_map/ppermute | solution.py:324
  70.1 0.6 collective-permute-start.12
  70.7 2.1 %shard_map.75.refs_4_ = bf16[6,128,256]{2,1,0:T(8,128)(2,1)S(1)} custom-call(s32[74]{0:T(128)S(1)} %get-tuple-element.28.refs_0_, bf16[1,24,128,256]{3,2,1,0:T(8,128)(2,1)S(1)} %get-tuple-element.29.refs_1_, bf16[1,24,128,256]{3,2,1,0:T(8,128)(2,1)S(1)} %collective-permute-done.1.refs_2_, bf16[24,64,256]{2,1,0:T(8,128)(2,1)} %collective-permute-done.4.refs_3_.refs_7_, ...), custom_call_target="tpu_custom_call" | custom-call | tf_op jit(solution)/shard_map/pallas_call | solution.py:173
  72.8 2.8 %shard_map.76 = (bf16[6,64,256]{2,1,0:T(8,128)(2,1)S(1)}, bf16[6,64,256]{2,1,0:T(8,128)(2,1)S(1)}, bf16[6,64,256]{2,1,0:T(8,128)(2,1)S(1)}, bf16[6,64,256]{2,1,0:T(8,128)(2,1)}, f32[8,256]{1,0:T(8,128)S(1)}) custom-call(s32[74]{0:T(128)S(1)} %get-tuple-element.28.refs_0_, bf16[1,24,128,256]{3,2,1,0:T(8,128)(2,1)S(1)} %copy-done.8, ...), custom_call_target="tpu_custom_call" | custom-call | tf_op jit(solution)/shard_map/pallas_call | solution.py:235
  75.6 2.6 %shard_map.78.refs_5_ = bf16[6,128,256]{2,1,0:T(8,128)(2,1)} custom-call(s32[74]{0:T(128)S(1)} %get-tuple-element.28.refs_0_, bf16[1,24,128,256]{3,2,1,0:T(8,128)(2,1)S(1)} %get-tuple-element.29.refs_1_, bf16[1,24,128,256]{3,2,1,0:T(8,128)(2,1)S(1)} %collective-permute-done.1.refs_2_, bf16[24,64,256]{2,1,0:T(8,128)(2,1)} %collective-permute-done.4.refs_3_.refs_7_, ...), custom_call_target="tpu_custom_call" | custom-call | tf_op jit(solution)/shard_map/pallas_call | solution.py:173
  78.3 3.3 %collective-permute-start.16 = (bf16[6,128,256]{2,1,0:T(8,128)(2,1)}, bf16[6,128,256]{2,1,0:T(8,128)(2,1)}, u32[]{:S(2)}, u32[]{:S(2)}) collective-permute-start(bf16[6,128,256]{2,1,0:T(8,128)(2,1)} %shard_map.78.refs_5_), channel_id=1, source_target_pairs={{0,12},{4,0},{8,4},{12,8},{1,13},{5,1},{9,5},{13,9},{2,14},{6,2},{... | collective-permute-start | bytes 1179656 | tf_op jit(solution)/shard_map/ppermute | solution.py:324
  81.5 1.5 %collective-permute-start.7 = (bf16[6,64,256]{2,1,0:T(8,128)(2,1)S(1)}, bf16[6,64,256]{2,1,0:T(8,128)(2,1)S(1)}, u32[]{:S(2)}, u32[]{:S(2)}) collective-permute-start(bf16[6,64,256]{2,1,0:T(8,128)(2,1)S(1)} %get-tuple-element.36), channel_id=1, source_target_pairs={{0,2},{1,3},{2,0},{3,1},{4,6},{5,7},{6,4},{7,5},{8,10},{9,11},{10,... | collective-permute-start | bytes 589832 | tf_op jit(solution)/shard_map/ppermute | solution.py:332
  83.0 0.4 collective-permute-start.8
  83.4 1.8 %shard_map.79.refs_9_ = bf16[6,128,256]{2,1,0:T(8,128)(2,1)S(1)} custom-call(s32[74]{0:T(128)S(1)} %get-tuple-element.28.refs_0_, bf16[1,24,128,256]{3,2,1,0:T(8,128)(2,1)S(1)} %get-tuple-element.29.refs_1_, bf16[1,24,128,256]{3,2,1,0:T(8,128)(2,1)S(1)} %collective-permute-done.1.refs_2_, bf16[24,64,256]{2,1,0:T(8,128)(2,1)} %collective-permute-done.4.refs_3_.refs_7_, ...), custom_call_target="tpu_custom_call" | custom-call | tf_op jit(solution)/shard_map/pallas_call | solution.py:173
  85.2 3.2 %shard_map.80 = (bf16[6,64,256]{2,1,0:T(8,128)(2,1)S(1)}, bf16[6,64,256]{2,1,0:T(8,128)(2,1)}, bf16[6,64,256]{2,1,0:T(8,128)(2,1)}, bf16[6,64,256]{2,1,0:T(8,128)(2,1)S(1)}, f32[8,256]{1,0:T(8,128)S(1)}) custom-call(s32[74]{0:T(128)S(1)} %get-tuple-element.28.refs_0_, bf16[1,24,128,256]{3,2,1,0:T(8,128)(2,1)S(1)} %copy-done.8, ...), custom_call_target="tpu_custom_call" | custom-call | tf_op jit(solution)/shard_map/pallas_call | solution.py:235
  88.4 0.6 copy-done.20
  89.0 0.7 copy-done.27
  89.7 0.3 collective-permute-start.13
  90.0 0.7 copy-done.12
  90.6 1.5 %collective-permute-start.14 = (bf16[6,64,256]{2,1,0:T(8,128)(2,1)}, bf16[6,64,256]{2,1,0:T(8,128)(2,1)S(1)}, u32[]{:S(2)}, u32[]{:S(2)}) collective-permute-start(bf16[6,64,256]{2,1,0:T(8,128)(2,1)} %get-tuple-element.41), channel_id=1, source_target_pairs={{0,2},{1,3},{2,0},{3,1},{4,6},{5,7},{6,4},{7,5},{8,10},{9,11},{10,... | collective-permute-start | bytes 589832 | tf_op jit(solution)/shard_map/ppermute | solution.py:332
  92.1 0.7 copy-done.15
  92.8 1.3 collective-permute-start.15
  94.1 1.4 %copy-done.9 = bf16[1,24,128,256]{3,2,1,0:T(8,128)(2,1)S(1)} copy-done((bf16[1,24,128,256]{3,2,1,0:T(8,128)(2,1)S(1)}, bf16[1,24,128,256]{3,2,1,0:T(8,128)(2,1)}, u32[]{:S(2)}) %copy-start.9) | copy-done | bytes 1572888
  95.5 0.9 copy-done.13
  96.4 0.9 copy-done.16
  97.3 0.7 copy-done.21
  98.0 2.5 %shard_map.81 = (bf16[6,64,256]{2,1,0:T(8,128)(2,1)S(1)}, bf16[6,64,256]{2,1,0:T(8,128)(2,1)S(1)}, bf16[6,64,256]{2,1,0:T(8,128)(2,1)S(1)}, bf16[6,64,256]{2,1,0:T(8,128)(2,1)S(1)}, f32[8,256]{1,0:T(8,128)S(1)}) custom-call(s32[74]{0:T(128)S(1)} %get-tuple-element.28.refs_0_, bf16[1,24,128,256]{3,2,1,0:T(8,128)(2,1)S(1)} %copy-done.9, ...), custom_call_target="tpu_custom_call" | custom-call | tf_op jit(solution)/shard_map/pallas_call | solution.py:235
  100.5 0.4 collective-permute-start.17
  100.9 0.6 collective-permute-start.18
  101.5 1.0 collective-permute-start.19
  102.5 0.9 fusion
  103.4 5.3 %collective-permute-done.18.refs_14_ = bf16[6,64,256]{2,1,0:T(8,128)(2,1)S(1)} collective-permute-done((bf16[6,64,256]{2,1,0:T(8,128)(2,1)S(1)}, bf16[6,64,256]{2,1,0:T(8,128)(2,1)S(1)}, u32[]{:S(2)}, u32[]{:S(2)}) %collective-permute-start.18) | collective-permute-done | bytes 196640 | tf_op jit(solution)/shard_map/ppermute | solution.py:332
  108.6 2.8 %collective-permute-done.19.refs_15_ = bf16[6,64,256]{2,1,0:T(8,128)(2,1)S(1)} collective-permute-done((bf16[6,64,256]{2,1,0:T(8,128)(2,1)S(1)}, bf16[6,64,256]{2,1,0:T(8,128)(2,1)S(1)}, u32[]{:S(2)}, u32[]{:S(2)}) %collective-permute-start.19) | collective-permute-done | bytes 196640 | tf_op jit(solution)/shard_map/ppermute | solution.py:332
  111.4 0.5 collective-permute-done.20.refs_4_
  112.0 2.5 %shard_map.82 = (bf16[6,64,256]{2,1,0:T(8,128)(2,1)S(1)}, bf16[6,64,256]{2,1,0:T(8,128)(2,1)S(1)}, bf16[6,64,256]{2,1,0:T(8,128)(2,1)S(1)}, bf16[6,64,256]{2,1,0:T(8,128)(2,1)S(1)}, f32[8,256]{1,0:T(8,128)S(1)}) custom-call(s32[74]{0:T(128)S(1)} %get-tuple-element.28.refs_0_, bf16[1,24,128,256]{3,2,1,0:T(8,128)(2,1)S(1)} %copy-done.9, ...), custom_call_target="tpu_custom_call" | custom-call | tf_op jit(solution)/shard_map/pallas_call | solution.py:235
  114.4 0.2 collective-permute-start.21
  114.6 0.6 collective-permute-start.22
  115.2 1.1 collective-permute-start.23
  116.3 0.6 add_reduce_fusion
  117.0 0.6 fusion.1
  117.6 0.6 collective-permute-start.24
  118.2 1.7 %shard_map.83.refs_2_ = f32[2,24,64,256]{3,2,1,0:T(8,128)S(1)} custom-call(s32[74]{0:T(128)S(1)} %get-tuple-element.28.refs_0_, s32[74]{0:T(128)S(1)} %copy-done.24, f32[24]{0:T(128)S(1)} %copy-done.25, bf16[2,24,64,256]{3,2,1,0:T(8,128)(2,1)S(1)} %copy-done.10, bf16[6,64,256]{2,1,0:T(8,128)(2,1)S(1)} %copy-done.19, bf16[6,64,256]{2,1,0:T(8,128)(2,1)S(1)} %copy-done.14, ...), custom_call_target="tpu_custom_call" | custom-call | tf_op jit(solution)/shard_map/pallas_call | solution.py:285
  119.9 1.3 collective-permute-done.24
  121.2 0.6 fusion.2
  121.9 1.6 %collective-permute-start.25 = (f32[2]{0:T(128)S(1)}, f32[2]{0:T(128)S(1)}, u32[]{:S(2)}, u32[]{:S(2)}) collective-permute-start(f32[2]{0:T(128)S(1)} %fusion.2), channel_id=1, source_target_pairs={{0,8},{4,12},{8,0},{12,4},{1,9},{5,13},{9,1},{13,5},{2,10},{6,14},... | collective-permute-start | bytes 32 | tf_op jit(solution)/shard_map/ppermute | solution.py:341
  123.5 2.9 %collective-permute-done.25 = f32[2]{0:T(128)S(1)} collective-permute-done((f32[2]{0:T(128)S(1)}, f32[2]{0:T(128)S(1)}, u32[]{:S(2)}, u32[]{:S(2)}) %collective-permute-start.25) | collective-permute-done | bytes 40 | tf_op jit(solution)/shard_map/ppermute | solution.py:341
  126.4 0.6 collective-permute-start.26
  127.0 3.0 %collective-permute-done.26 = f32[2]{0:T(128)S(1)} collective-permute-done((f32[2]{0:T(128)S(1)}, f32[2]{0:T(128)S(1)}, u32[]{:S(2)}, u32[]{:S(2)}) %collective-permute-start.26) | collective-permute-done | bytes 40 | tf_op jit(solution)/shard_map/ppermute | solution.py:341
  129.9 1.1 collective-permute-done.27
  131.0 0.5 add_multiply_fusion
  131.6 2.6 %shard_map.84 = f32[2,24,64,256]{3,2,1,0:T(8,128)} custom-call(s32[74]{0:T(128)S(1)} %get-tuple-element.28.refs_0_, s32[74]{0:T(128)S(1)} %copy-done.24, f32[2,24,64,256]{3,2,1,0:T(8,128)S(1)} %shard_map.83.refs_2_, bf16[6,64,256]{2,1,0:T(8,128)(2,1)S(1)} %get-tuple-element.50.refs_3_, bf16[6,64,256]{2,1,0:T(8,128)(2,1)S(1)} %collective-permute-done.21.refs_4_, ...), custom_call_target="tpu_custom_call" | custom-call | tf_op jit(solution)/shard_map/pallas_call | solution.py:313
  (74 shorter events, 0.3 us)
Async XLA Ops:
  0.6 7.3 %collective-permute-start.1 = (bf16[1,24,128,256]{3,2,1,0:T(8,128)(2,1)}, bf16[1,24,128,256]{3,2,1,0:T(8,128)(2,1)S(1)}, u32[]{:S(2)}, u32[]{:S(2)}) collective-permute-start(bf16[1,24,128,256]{3,2,1,0:T(8,128)(2,1)} %right.1), channel_id=1, source_target_pairs={{0,1},{1,0},{2,3},{3,2},{4,5},{5,4},{6,7},{7,6},{8,9},{9,8},{10,11... | collective-permute-start | bytes 4718600 | tf_op jit(solution)/shard_map/ppermute | solution.py:324
  1.1 0.7 copy-start.26
  5.4 2.6 %collective-permute-start.2 = (bf16[24,64,256]{2,1,0:T(8,128)(2,1)}, bf16[24,64,256]{2,1,0:T(8,128)(2,1)S(1)}, u32[]{:S(2)}, u32[]{:S(2)}) collective-permute-start(bf16[24,64,256]{2,1,0:T(8,128)(2,1)} %get-tuple-element.31), channel_id=1, source_target_pairs={{0,1},{1,0},{2,3},{3,2},{4,5},{5,4},{6,7},{7,6},{8,9},{9,8},{10,11... | collective-permute-start | bytes 2359304 | tf_op jit(solution)/shard_map/ppermute | solution.py:324
  8.0 14.6 %copy-start = (bf16[24,64,256]{2,1,0:T(8,128)(2,1)}, bf16[24,64,256]{2,1,0:T(8,128)(2,1)S(1)}, u32[]{:S(2)}) copy-start(bf16[24,64,256]{2,1,0:T(8,128)(2,1)S(1)} %collective-permute-done.2.refs_4_.refs_6_) | copy-start | bytes 2359300
  11.7 8.5 %copy-start.7 = (bf16[1,24,128,256]{3,2,1,0:T(8,128)(2,1)}, bf16[1,24,128,256]{3,2,1,0:T(8,128)(2,1)S(1)}, u32[]{:S(2)}) copy-start(bf16[1,24,128,256]{3,2,1,0:T(8,128)(2,1)S(1)} %get-tuple-element.32.refs_1_) | copy-start | bytes 4718596
  11.8 8.4 %collective-permute-start.3 = (bf16[1,24,128,256]{3,2,1,0:T(8,128)(2,1)S(1)}, bf16[1,24,128,256]{3,2,1,0:T(8,128)(2,1)S(1)}, u32[]{:S(2)}, u32[]{:S(2)}) collective-permute-start(bf16[1,24,128,256]{3,2,1,0:T(8,128)(2,1)S(1)} %get-tuple-element.32.refs_1_), channel_id=1, source_target_pairs={{0,1},{1,0},{2,3},{3,2},{4,5},{5,4},{6,7},{7,6},{8,9},{9,8},{10,11... | collective-permute-start | bytes 4718600 | tf_op jit(solution)/shard_map/ppermute | solution.py:324
  12.0 42.0 %collective-permute-start.4 = (bf16[24,64,256]{2,1,0:T(8,128)(2,1)}, bf16[24,64,256]{2,1,0:T(8,128)(2,1)}, u32[]{:S(2)}, u32[]{:S(2)}) collective-permute-start(bf16[24,64,256]{2,1,0:T(8,128)(2,1)} %get-tuple-element.30.refs_3_.refs_5_), channel_id=1, source_target_pairs={{0,2},{1,3},{2,0},{3,1},{4,6},{5,7},{6,4},{7,5},{8,10},{9,11},{10,... | collective-permute-start | bytes 2359304 | tf_op jit(solution)/shard_map/ppermute | solution.py:332
  14.8 39.1 %collective-permute-start.5 = (bf16[24,64,256]{2,1,0:T(8,128)(2,1)}, bf16[24,64,256]{2,1,0:T(8,128)(2,1)}, u32[]{:S(2)}, u32[]{:S(2)}) collective-permute-start(bf16[24,64,256]{2,1,0:T(8,128)(2,1)} %get-tuple-element.31), channel_id=1, source_target_pairs={{0,3},{1,2},{2,1},{3,0},{4,7},{5,6},{6,5},{7,4},{8,11},{9,10},{10,... | collective-permute-start | bytes 2359304 | tf_op jit(solution)/shard_map/ppermute | solution.py:332
  14.8 34.9 %collective-permute-start = (s32[1,96]{1,0:T(1,128)S(1)}, s32[1,96]{1,0:T(1,128)S(1)}, u32[]{:S(2)}, u32[]{:S(2)}) collective-permute-start(s32[1,96]{1,0:T(1,128)S(1)} %copy-done.26), channel_id=1, source_target_pairs={{0,2},{2,0},{1,3},{3,1},{4,6},{6,4},{5,7},{7,5},{8,10},{10,8},{9,1... | collective-permute-start | bytes 1160 | tf_op jit(solution)/shard_map/ppermute | solution.py:324
  16.3 41.9 %collective-permute-start.9 = (bf16[6,128,256]{2,1,0:T(8,128)(2,1)}, bf16[6,128,256]{2,1,0:T(8,128)(2,1)}, u32[]{:S(2)}, u32[]{:S(2)}) collective-permute-start(bf16[6,128,256]{2,1,0:T(8,128)(2,1)} %get-tuple-element.33.refs_5_), channel_id=1, source_target_pairs={{0,4},{4,8},{8,12},{12,0},{1,5},{5,9},{9,13},{13,1},{2,6},{6,10},{... | collective-permute-start | bytes 1179656 | tf_op jit(solution)/shard_map/ppermute | solution.py:324
  20.2 4.7 %copy-start.4 = (bf16[1,24,128,256]{3,2,1,0:T(8,128)(2,1)}, bf16[1,24,128,256]{3,2,1,0:T(8,128)(2,1)S(1)}, u32[]{:S(2)}) copy-start(bf16[1,24,128,256]{3,2,1,0:T(8,128)(2,1)S(1)} %collective-permute-done.3.refs_6_.refs_2_) | copy-start | bytes 4718596
  20.2 38.0 %collective-permute-start.10 = (bf16[6,128,256]{2,1,0:T(8,128)(2,1)}, bf16[6,128,256]{2,1,0:T(8,128)(2,1)}, u32[]{:S(2)}, u32[]{:S(2)}) collective-permute-start(bf16[6,128,256]{2,1,0:T(8,128)(2,1)} %shard_map.71.refs_5_), channel_id=1, source_target_pairs={{0,12},{4,0},{8,4},{12,8},{1,13},{5,1},{9,5},{13,9},{2,14},{6,2},{... | collective-permute-start | bytes 1179656 | tf_op jit(solution)/shard_map/ppermute | solution.py:324
  49.7 2.8 %copy-start.28 = (s32[1,96]{1,0:T(1,128)}, s32[1,96]{1,0:T(1,128)S(1)}, u32[]{:S(2)}) copy-start(s32[1,96]{1,0:T(1,128)S(1)} %collective-permute-done.partner) | copy-start | bytes 1156
  49.7 20.4 %collective-permute-start.11 = (bf16[6,128,256]{2,1,0:T(8,128)(2,1)}, bf16[6,128,256]{2,1,0:T(8,128)(2,1)}, u32[]{:S(2)}, u32[]{:S(2)}) collective-permute-start(bf16[6,128,256]{2,1,0:T(8,128)(2,1)} %shard_map.72.refs_5_), channel_id=1, source_target_pairs={{0,8},{4,12},{8,0},{12,4},{1,9},{5,13},{9,1},{13,5},{2,10},{6,14},... | collective-permute-start | bytes 1179656 | tf_op jit(solution)/shard_map/ppermute | solution.py:324
  53.9 2.5 %copy-start.1 = (bf16[24,64,256]{2,1,0:T(8,128)(2,1)S(1)}, bf16[24,64,256]{2,1,0:T(8,128)(2,1)}, u32[]{:S(2)}) copy-start(bf16[24,64,256]{2,1,0:T(8,128)(2,1)} %copy-done) | copy-start | bytes 2359300
  54.0 0.7 copy-start.23
  56.4 1.7 %copy-start.11 = (bf16[6,128,256]{2,1,0:T(8,128)(2,1)}, bf16[6,128,256]{2,1,0:T(8,128)(2,1)S(1)}, u32[]{:S(2)}) copy-start(bf16[6,128,256]{2,1,0:T(8,128)(2,1)S(1)} %shard_map.73.refs_5_.refs_0_) | copy-start | bytes 1179652
  70.1 2.7 %copy-start.2 = (bf16[24,64,256]{2,1,0:T(8,128)(2,1)S(1)}, bf16[24,64,256]{2,1,0:T(8,128)(2,1)}, u32[]{:S(2)}) copy-start(bf16[24,64,256]{2,1,0:T(8,128)(2,1)} %copy-done) | copy-start | bytes 2359300
  70.1 2.7 %copy-start.5 = (bf16[1,24,128,256]{3,2,1,0:T(8,128)(2,1)S(1)}, bf16[1,24,128,256]{3,2,1,0:T(8,128)(2,1)}, u32[]{:S(2)}) copy-start(bf16[1,24,128,256]{3,2,1,0:T(8,128)(2,1)} %copy-done.4) | copy-start | bytes 4718596
  70.1 2.7 %copy-start.8 = (bf16[1,24,128,256]{3,2,1,0:T(8,128)(2,1)S(1)}, bf16[1,24,128,256]{3,2,1,0:T(8,128)(2,1)}, u32[]{:S(2)}) copy-start(bf16[1,24,128,256]{3,2,1,0:T(8,128)(2,1)} %copy-done.7) | copy-start | bytes 4718596
  70.1 13.3 %collective-permute-start.12 = (bf16[6,128,256]{2,1,0:T(8,128)(2,1)}, bf16[6,128,256]{2,1,0:T(8,128)(2,1)S(1)}, u32[]{:S(2)}, u32[]{:S(2)}) collective-permute-start(bf16[6,128,256]{2,1,0:T(8,128)(2,1)} %shard_map.77), channel_id=1, source_target_pairs={{0,4},{4,8},{8,12},{12,0},{1,5},{5,9},{9,13},{13,1},{2,6},{6,10},{... | collective-permute-start | bytes 1179656 | tf_op jit(solution)/shard_map/ppermute | solution.py:324
  75.6 2.6 %copy-start.18 = (bf16[6,64,256]{2,1,0:T(8,128)(2,1)}, bf16[6,64,256]{2,1,0:T(8,128)(2,1)S(1)}, u32[]{:S(2)}) copy-start(bf16[6,64,256]{2,1,0:T(8,128)(2,1)S(1)} %get-tuple-element.34.refs_4_) | copy-start | bytes 589828
  78.3 15.8 %collective-permute-start.16 = (bf16[6,128,256]{2,1,0:T(8,128)(2,1)}, bf16[6,128,256]{2,1,0:T(8,128)(2,1)}, u32[]{:S(2)}, u32[]{:S(2)}) collective-permute-start(bf16[6,128,256]{2,1,0:T(8,128)(2,1)} %shard_map.78.refs_5_), channel_id=1, source_target_pairs={{0,12},{4,0},{8,4},{12,8},{1,13},{5,1},{9,5},{13,9},{2,14},{6,2},{... | collective-permute-start | bytes 1179656 | tf_op jit(solution)/shard_map/ppermute | solution.py:324
  81.5 8.4 %collective-permute-start.6 = (bf16[6,64,256]{2,1,0:T(8,128)(2,1)S(1)}, bf16[6,64,256]{2,1,0:T(8,128)(2,1)S(1)}, u32[]{:S(2)}, u32[]{:S(2)}) collective-permute-start(bf16[6,64,256]{2,1,0:T(8,128)(2,1)S(1)} %get-tuple-element.35), channel_id=1, source_target_pairs={{0,1},{1,0},{2,3},{3,2},{4,5},{5,4},{6,7},{7,6},{8,9},{9,8},{10,11... | collective-permute-start | bytes 589832 | tf_op jit(solution)/shard_map/ppermute | solution.py:332
  81.5 10.6 %collective-permute-start.7 = (bf16[6,64,256]{2,1,0:T(8,128)(2,1)S(1)}, bf16[6,64,256]{2,1,0:T(8,128)(2,1)S(1)}, u32[]{:S(2)}, u32[]{:S(2)}) collective-permute-start(bf16[6,64,256]{2,1,0:T(8,128)(2,1)S(1)} %get-tuple-element.36), channel_id=1, source_target_pairs={{0,2},{1,3},{2,0},{3,1},{4,6},{5,7},{6,4},{7,5},{8,10},{9,11},{10,... | collective-permute-start | bytes 589832 | tf_op jit(solution)/shard_map/ppermute | solution.py:332
  83.0 9.8 %collective-permute-start.8 = (bf16[6,64,256]{2,1,0:T(8,128)(2,1)}, bf16[6,64,256]{2,1,0:T(8,128)(2,1)}, u32[]{:S(2)}, u32[]{:S(2)}) collective-permute-start(bf16[6,64,256]{2,1,0:T(8,128)(2,1)} %get-tuple-element.37), channel_id=1, source_target_pairs={{0,3},{1,2},{2,1},{3,0},{4,7},{5,6},{6,5},{7,4},{8,11},{9,10},{10,... | collective-permute-start | bytes 589832 | tf_op jit(solution)/shard_map/ppermute | solution.py:332
  85.2 8.9 %copy-start.3 = (bf16[24,64,256]{2,1,0:T(8,128)(2,1)S(1)}, bf16[24,64,256]{2,1,0:T(8,128)(2,1)}, u32[]{:S(2)}) copy-start(bf16[24,64,256]{2,1,0:T(8,128)(2,1)} %copy-done) | copy-start | bytes 2359300
  85.2 8.9 %copy-start.6 = (bf16[1,24,128,256]{3,2,1,0:T(8,128)(2,1)S(1)}, bf16[1,24,128,256]{3,2,1,0:T(8,128)(2,1)}, u32[]{:S(2)}) copy-start(bf16[1,24,128,256]{3,2,1,0:T(8,128)(2,1)} %copy-done.4) | copy-start | bytes 4718596
  88.4 0.6 copy-start.20
  89.0 0.7 copy-start.27
  89.7 11.2 %collective-permute-start.13 = (bf16[6,64,256]{2,1,0:T(8,128)(2,1)}, bf16[6,64,256]{2,1,0:T(8,128)(2,1)S(1)}, u32[]{:S(2)}, u32[]{:S(2)}) collective-permute-start(bf16[6,64,256]{2,1,0:T(8,128)(2,1)} %get-tuple-element.40), channel_id=1, source_target_pairs={{0,1},{1,0},{2,3},{3,2},{4,5},{5,4},{6,7},{7,6},{8,9},{9,8},{10,11... | collective-permute-start | bytes 589832 | tf_op jit(solution)/shard_map/ppermute | solution.py:332
  89.9 0.7 copy-start.12
  90.6 10.9 %collective-permute-start.14 = (bf16[6,64,256]{2,1,0:T(8,128)(2,1)}, bf16[6,64,256]{2,1,0:T(8,128)(2,1)S(1)}, u32[]{:S(2)}, u32[]{:S(2)}) collective-permute-start(bf16[6,64,256]{2,1,0:T(8,128)(2,1)} %get-tuple-element.41), channel_id=1, source_target_pairs={{0,2},{1,3},{2,0},{3,1},{4,6},{5,7},{6,4},{7,5},{8,10},{9,11},{10,... | collective-permute-start | bytes 589832 | tf_op jit(solution)/shard_map/ppermute | solution.py:332
  92.1 0.7 copy-start.15
  92.8 19.2 %collective-permute-start.20 = (bf16[6,128,256]{2,1,0:T(8,128)(2,1)S(1)}, bf16[6,128,256]{2,1,0:T(8,128)(2,1)}, u32[]{:S(2)}, u32[]{:S(2)}) collective-permute-start(bf16[6,128,256]{2,1,0:T(8,128)(2,1)S(1)} %shard_map.79.refs_9_), channel_id=1, source_target_pairs={{0,8},{4,12},{8,0},{12,4},{1,9},{5,13},{9,1},{13,5},{2,10},{6,14},... | collective-permute-start | bytes 1179656 | tf_op jit(solution)/shard_map/ppermute | solution.py:324
  92.8 10.6 %collective-permute-start.15 = (bf16[6,64,256]{2,1,0:T(8,128)(2,1)}, bf16[6,64,256]{2,1,0:T(8,128)(2,1)S(1)}, u32[]{:S(2)}, u32[]{:S(2)}) collective-permute-start(bf16[6,64,256]{2,1,0:T(8,128)(2,1)} %copy-done.27), channel_id=1, source_target_pairs={{0,3},{1,2},{2,1},{3,0},{4,7},{5,6},{6,5},{7,4},{8,11},{9,10},{10,... | collective-permute-start | bytes 589832 | tf_op jit(solution)/shard_map/ppermute | solution.py:332
  94.1 1.4 %copy-start.9 = (bf16[1,24,128,256]{3,2,1,0:T(8,128)(2,1)S(1)}, bf16[1,24,128,256]{3,2,1,0:T(8,128)(2,1)}, u32[]{:S(2)}) copy-start(bf16[1,24,128,256]{3,2,1,0:T(8,128)(2,1)} %copy-done.7) | copy-start | bytes 4718596
  95.5 0.9 copy-start.13
  96.4 0.9 copy-start.16
  97.3 0.7 copy-start.21
  98.0 4.4 %copy-start.10 = (bf16[2,24,64,256]{3,2,1,0:T(8,128)(2,1)S(1)}, bf16[2,24,64,256]{3,2,1,0:T(8,128)(2,1)}, u32[]{:S(2)}) copy-start(bf16[2,24,64,256]{3,2,1,0:T(8,128)(2,1)} %refs_3_.1) | copy-start | bytes 4718596
  98.0 4.4 %copy-start.25 = (f32[24]{0:T(128)S(1)}, f32[24]{0:T(128)}, u32[]{:S(2)}) copy-start(f32[24]{0:T(128)} %refs_2_.1) | copy-start | bytes 292
  100.5 2.8 %collective-permute-start.17 = (bf16[6,64,256]{2,1,0:T(8,128)(2,1)S(1)}, bf16[6,64,256]{2,1,0:T(8,128)(2,1)S(1)}, u32[]{:S(2)}, u32[]{:S(2)}) collective-permute-start(bf16[6,64,256]{2,1,0:T(8,128)(2,1)S(1)} %get-tuple-element.45), channel_id=1, source_target_pairs={{0,1},{1,0},{2,3},{3,2},{4,5},{5,4},{6,7},{7,6},{8,9},{9,8},{10,11... | collective-permute-start | bytes 589832 | tf_op jit(solution)/shard_map/ppermute | solution.py:332
  100.9 7.7 %collective-permute-start.18 = (bf16[6,64,256]{2,1,0:T(8,128)(2,1)S(1)}, bf16[6,64,256]{2,1,0:T(8,128)(2,1)S(1)}, u32[]{:S(2)}, u32[]{:S(2)}) collective-permute-start(bf16[6,64,256]{2,1,0:T(8,128)(2,1)S(1)} %get-tuple-element.46), channel_id=1, source_target_pairs={{0,2},{1,3},{2,0},{3,1},{4,6},{5,7},{6,4},{7,5},{8,10},{9,11},{10,... | collective-permute-start | bytes 589832 | tf_op jit(solution)/shard_map/ppermute | solution.py:332
  101.5 9.9 %collective-permute-start.19 = (bf16[6,64,256]{2,1,0:T(8,128)(2,1)S(1)}, bf16[6,64,256]{2,1,0:T(8,128)(2,1)S(1)}, u32[]{:S(2)}, u32[]{:S(2)}) collective-permute-start(bf16[6,64,256]{2,1,0:T(8,128)(2,1)S(1)} %get-tuple-element.47), channel_id=1, source_target_pairs={{0,3},{1,2},{2,1},{3,0},{4,7},{5,6},{6,5},{7,4},{8,11},{9,10},{10,... | collective-permute-start | bytes 589832 | tf_op jit(solution)/shard_map/ppermute | solution.py:332
  111.9 4.4 %copy-start.22 = (f32[8,256]{1,0:T(8,128)S(1)}, f32[8,256]{1,0:T(8,128)}, u32[]{:S(2)}) copy-start(f32[8,256]{1,0:T(8,128)} %copy-done.20) | copy-start | bytes 24580
  111.9 6.2 %copy-start.14 = (bf16[6,64,256]{2,1,0:T(8,128)(2,1)S(1)}, bf16[6,64,256]{2,1,0:T(8,128)(2,1)}, u32[]{:S(2)}) copy-start(bf16[6,64,256]{2,1,0:T(8,128)(2,1)} %copy-done.12) | copy-start | bytes 589828
  111.9 6.2 %copy-start.17 = (bf16[6,64,256]{2,1,0:T(8,128)(2,1)S(1)}, bf16[6,64,256]{2,1,0:T(8,128)(2,1)}, u32[]{:S(2)}) copy-start(bf16[6,64,256]{2,1,0:T(8,128)(2,1)} %copy-done.15) | copy-start | bytes 589828
  111.9 6.2 %copy-start.19 = (bf16[6,64,256]{2,1,0:T(8,128)(2,1)S(1)}, bf16[6,64,256]{2,1,0:T(8,128)(2,1)}, u32[]{:S(2)}) copy-start(bf16[6,64,256]{2,1,0:T(8,128)(2,1)} %copy-done.18) | copy-start | bytes 589828
  112.0 6.2 %copy-start.24 = (s32[74]{0:T(128)S(1)}, s32[74]{0:T(128)}, u32[]{:S(2)}) copy-start(s32[74]{0:T(128)} %shard_map.69.refs_6_.refs_1_) | copy-start | bytes 892
  114.4 17.1 %collective-permute-start.21 = (bf16[6,64,256]{2,1,0:T(8,128)(2,1)S(1)}, bf16[6,64,256]{2,1,0:T(8,128)(2,1)S(1)}, u32[]{:S(2)}, u32[]{:S(2)}) collective-permute-start(bf16[6,64,256]{2,1,0:T(8,128)(2,1)S(1)} %get-tuple-element.51), channel_id=1, source_target_pairs={{0,1},{1,0},{2,3},{3,2},{4,5},{5,4},{6,7},{7,6},{8,9},{9,8},{10,11... | collective-permute-start | bytes 589832 | tf_op jit(solution)/shard_map/ppermute | solution.py:332
  114.6 16.9 %collective-permute-start.22 = (bf16[6,64,256]{2,1,0:T(8,128)(2,1)S(1)}, bf16[6,64,256]{2,1,0:T(8,128)(2,1)S(1)}, u32[]{:S(2)}, u32[]{:S(2)}) collective-permute-start(bf16[6,64,256]{2,1,0:T(8,128)(2,1)S(1)} %get-tuple-element.52), channel_id=1, source_target_pairs={{0,2},{1,3},{2,0},{3,1},{4,6},{5,7},{6,4},{7,5},{8,10},{9,11},{10,... | collective-permute-start | bytes 589832 | tf_op jit(solution)/shard_map/ppermute | solution.py:332
  115.2 16.4 %collective-permute-start.23 = (bf16[6,64,256]{2,1,0:T(8,128)(2,1)S(1)}, bf16[6,64,256]{2,1,0:T(8,128)(2,1)S(1)}, u32[]{:S(2)}, u32[]{:S(2)}) collective-permute-start(bf16[6,64,256]{2,1,0:T(8,128)(2,1)S(1)} %get-tuple-element.53), channel_id=1, source_target_pairs={{0,3},{1,2},{2,1},{3,0},{4,7},{5,6},{6,5},{7,4},{8,11},{9,10},{10,... | collective-permute-start | bytes 589832 | tf_op jit(solution)/shard_map/ppermute | solution.py:332
  117.6 3.6 %collective-permute-start.24 = (f32[2]{0:T(128)S(1)}, f32[2]{0:T(128)S(1)}, u32[]{:S(2)}, u32[]{:S(2)}) collective-permute-start(f32[2]{0:T(128)S(1)} %fusion.1), channel_id=1, source_target_pairs={{0,4},{4,0},{8,12},{12,8},{1,5},{5,1},{9,13},{13,9},{2,6},{6,2},{1... | collective-permute-start | bytes 32 | tf_op jit(solution)/shard_map/ppermute | solution.py:341
  121.9 4.5 %collective-permute-start.25 = (f32[2]{0:T(128)S(1)}, f32[2]{0:T(128)S(1)}, u32[]{:S(2)}, u32[]{:S(2)}) collective-permute-start(f32[2]{0:T(128)S(1)} %fusion.2), channel_id=1, source_target_pairs={{0,8},{4,12},{8,0},{12,4},{1,9},{5,13},{9,1},{13,5},{2,10},{6,14},... | collective-permute-start | bytes 32 | tf_op jit(solution)/shard_map/ppermute | solution.py:341
  126.4 3.5 %collective-permute-start.26 = (f32[2]{0:T(128)S(1)}, f32[2]{0:T(128)S(1)}, u32[]{:S(2)}, u32[]{:S(2)}) collective-permute-start(f32[2]{0:T(128)S(1)} %add.29), channel_id=1, source_target_pairs={{0,2},{2,0},{1,3},{3,1},{4,6},{6,4},{5,7},{7,5},{8,10},{10,8},{9,1... | collective-permute-start | bytes 32 | tf_op jit(solution)/shard_map/ppermute | solution.py:341
  129.9 1.1 collective-permute-start.27

commit v4 on v3

--- a/solution.py
+++ b/solution.py
@@ -11,7 +11,8 @@
 HBM = pl.BlockSpec(memory_space=pltpu.HBM)
 SMEM = pl.BlockSpec(memory_space=pltpu.SMEM)
 VMEM = pl.BlockSpec(memory_space=pltpu.VMEM)
-LIMIT = 40 * 1024 * 1024
+LIMIT = 12 * 1024 * 1024
+TAIL = 16
 BRIEF = pl.CostEstimate(flops=0, bytes_accessed=0, transcendentals=0)
 
 
@@ -66,14 +67,23 @@
     plan[z.chip] = lax.axis_index("env")
 
 
+def split_copy(source, target, slots, sem):
+    step = slots // 4 if slots % 4 == 0 else slots
+    copies = []
+    for i in range(slots // step):
+        part = pl.ds(i * step, step)
+        copies.append(pltpu.make_async_copy(source.at[part], target.at[part], sem.at[i]))
+    return copies
+
+
 def load_body(z, partner, vectors, right, plan, *refs):
     rows, block, count, sem = refs[: z.rep], refs[z.rep], refs[-2], refs[-1]
     core = lax.axis_index("rep")
-    copies = [pltpu.make_async_copy(right, block, sem.at[z.rep])]
+    copies = []
     for s, ref in enumerate(rows):
-        copies.append(
-            pltpu.make_async_copy(vectors.at[lax.rem(core + s, z.rep)], ref, sem.at[s])
-        )
+        mine = vectors.at[lax.rem(core + s, z.rep)]
+        copies += split_copy(mine, ref, z.slots, sem.at[s])
+    copies += split_copy(right.at[0], block.at[0], z.slots, sem.at[z.rep])
     for copy in copies:
         copy.start()
     write_plan(z, partner, plan, count)
@@ -90,7 +100,10 @@
         + [jax.ShapeDtypeStruct(right_env.shape, jnp.bfloat16)],
         in_specs=[SMEM, HBM, HBM],
         out_specs=[SMEM] + [VMEM] * (z.rep + 1),
-        scratch_shapes=[pltpu.SMEM((z.sector,), jnp.int32), pltpu.SemaphoreType.DMA((z.rep + 1,))],
+        scratch_shapes=[
+            pltpu.SMEM((z.sector,), jnp.int32),
+            pltpu.SemaphoreType.DMA((z.rep + 1, 4)),
+        ],
         compiler_params=pltpu.CompilerParams(vmem_limit_bytes=LIMIT),
         cost_estimate=BRIEF,
     )(
@@ -133,12 +146,12 @@
     return chosen
 
 
-def products_body(z, pieces, spans, copied, *refs):
+def line(ref, core, slot):
+    return ref[core, slot] if len(ref.shape) == 4 else ref[slot]
+
+
+def products_body(z, pieces, spans, *refs):
     refs = list(refs)
-    if copied:
-        sem = refs.pop()
-        copy = pltpu.make_async_copy(refs[1 + z.rep * (1 + pieces)], refs.pop(), sem)
-        copy.start()
     plan = refs.pop(0)
     right = [refs.pop(0) for _ in range(z.rep)]
     rows = [[refs.pop(0) for _ in range(z.rep)] for _ in range(pieces)]
@@ -148,7 +161,7 @@
         for i in range(count):
             slot = plan[z.source + first + i]
             halves = [ref[0, slot] for ref in right]
-            parts = [[ref[slot] for ref in piece] for piece in rows]
+            parts = [[line(ref, core, slot) for ref in piece] for piece in rows]
             block = jnp.concatenate([pick(z, core, k, halves) for k in range(z.rep)], axis=0)
             lines = jnp.concatenate(
                 [pick(z, core, k, part) for part in parts for k in range(z.rep)], axis=0
@@ -156,45 +169,38 @@
             out[i] = lax.dot_general(
                 lines, block, (((1,), (1,)), ((), ())), preferred_element_type=jnp.float32
             ).astype(jnp.bfloat16)
-    if copied:
-        copy.wait()
-
-
-def products(z, plan, right, rows, spans, after=(), copied=None):
+
+
+def products(z, plan, right, rows, spans, after=()):
     pieces = len(rows)
     flat = [ref for piece in rows for ref in piece]
     height = pieces * z.chip_rows
-    shapes = [(count, height, z.order) for _, count in spans]
-    scratch = []
-    if copied is not None:
-        shapes.append(copied.shape)
-        scratch = [pltpu.SemaphoreType.DMA]
-        after = (pltpu.with_memory_space_constraint(copied, pltpu.HBM), *after)
     return pl.pallas_call(
-        functools.partial(products_body, z, pieces, spans, copied is not None),
-        out_shape=[jax.ShapeDtypeStruct(shape, jnp.bfloat16) for shape in shapes],
-        in_specs=[SMEM]
-        + [VMEM] * (len(right) + len(flat))
-        + [HBM if copied is not None and i == 0 else ANY for i in range(len(after))],
-        out_specs=[VMEM] * len(shapes),
-        scratch_shapes=scratch,
+        functools.partial(products_body, z, pieces, spans),
+        out_shape=[
+            jax.ShapeDtypeStruct((count, height, z.order), jnp.bfloat16) for _, count in spans
+        ],
+        in_specs=[SMEM] + [VMEM] * (len(right) + len(flat)) + [ANY] * len(after),
+        out_specs=[VMEM] * len(spans),
         compiler_params=pltpu.CompilerParams(vmem_limit_bytes=LIMIT),
         cost_estimate=BRIEF,
     )(plan, *right, *flat, *after)
 
 
-def terms_body(z, spans, *refs):
+def terms_body(z, spans, chained, last, *refs):
     refs = list(refs)
     plan = refs.pop(0)
     left = [refs.pop(0) for _ in range(z.rep)]
     near = [refs.pop(0) for _ in spans]
     far = [refs.pop(0) for _ in spans]
     vec = [[refs.pop(0) for _ in range(z.rep)] for _ in range(z.env)]
+    so_far = refs.pop(0) if chained else None
+    own_sums = refs.pop(0) if last else None
     pbuf, tbuf = refs[-2:]
     dots = refs[-3]
     outs = refs[-3 - z.env * z.rep : -3]
     core, chip = plan[z.core], plan[z.chip]
-    total = jnp.zeros(dots.shape, jnp.float32)
+    total = so_far[...] if chained else jnp.zeros((8, z.order), jnp.float32)
     n = 0
     for d, (first, count, skip) in enumerate(spans):
         for i in range(count):
@@ -211,39 +217,68 @@
             tbuf[n] = jnp.dot(block, pbuf[n], preferred_element_type=jnp.float32).astype(
                 jnp.bfloat16
             )
-            folded = jnp.zeros(dots.shape, jnp.float32)
+            folded = jnp.zeros(total.shape, jnp.float32)
             for e in range(z.env):
                 for s in range(z.rep):
                     place = lax.rem(chip + e, z.env) * z.rep + lax.rem(core + s, z.rep)
                     term = tbuf[n, pl.ds(aligned(place, z.own_rows), z.own_rows)]
-                    outs[e * z.rep + s][n] = term
-                    lines = vec[(z.env - e) % z.env][(z.rep - s) % z.rep][slot]
+                    if last and e + s:
+                        outs[e * z.rep + s][n * z.own_rows : (n + 1) * z.own_rows] = term
+                    else:
+                        outs[e * z.rep + s][n] = term
+                    lines = line(vec[(z.env - e) % z.env][(z.rep - s) % z.rep], core, slot)
                     both = lines.astype(jnp.float32) * term.astype(jnp.float32)
-                    folded += jnp.sum(both.reshape(-1, *dots.shape), axis=0)
+                    folded += jnp.sum(both.reshape(-1, *total.shape), axis=0)
             if not z.full:
                 folded = jnp.where(plan[z.valid + first + i] == 1, folded, 0.0)
             total += folded
             n += 1
-    dots[...] = total
-
-
-def terms(z, plan, left, near, far, vec, spans, after=()):
+    if not last:
+        dots[...] = total
+        return
+    row = lax.broadcasted_iota(jnp.int32, dots.shape, 0)
+    column = lax.broadcasted_iota(jnp.int32, dots.shape, 1)
+    value = jnp.where(column == core, jnp.sum(total), 0.0)
+    for v in range(z.batch):
+        value += jnp.where(column == v, own_sums[v], 0.0)
+    split = jnp.zeros(dots.shape, jnp.float32)
+    for k in range(3):
+        piece = value.astype(jnp.bfloat16).astype(jnp.float32)
+        split = jnp.where(row == k, piece, split)
+        value = value - piece
+    split = split.astype(jnp.bfloat16)
+    dots[...] = split
+    for out in outs[1:]:
+        out[n * z.own_rows :] = split
+
+
+def terms(z, plan, left, near, far, vec, spans, so_far=None, own_sums=None, after=()):
     count = sum(span[1] for span in spans)
     flat = [ref for piece in vec for ref in piece]
     shapes = [(count, z.own_rows, z.order)] * (z.env * z.rep)
     whole = (count, z.order, z.order)
+    last = own_sums is not None
+    sums = jax.ShapeDtypeStruct((8, z.order), jnp.float32)
+    if last:
+        shapes[1:] = [(count * z.own_rows + TAIL, z.order)] * (z.env * z.rep - 1)
+        sums = jax.ShapeDtypeStruct((TAIL, z.order), jnp.bfloat16)
+    extra = [] if so_far is None else [so_far]
+    specs = [VMEM] * len(extra)
+    if last:
+        extra.append(own_sums)
+        specs.append(SMEM)
     *made, dots = pl.pallas_call(
-        functools.partial(terms_body, z, spans),
-        out_shape=[jax.ShapeDtypeStruct(shape, jnp.bfloat16) for shape in shapes]
-        + [jax.ShapeDtypeStruct((8, z.order), jnp.float32)],
+        functools.partial(terms_body, z, spans, so_far is not None, last),
+        out_shape=[jax.ShapeDtypeStruct(shape, jnp.bfloat16) for shape in shapes] + [sums],
         in_specs=[SMEM]
         + [VMEM] * (len(left) + len(near) + len(far) + len(flat))
+        + specs
         + [ANY] * len(after),
         out_specs=[VMEM] * (len(shapes) + 1),
         scratch_shapes=[pltpu.VMEM(whole, jnp.bfloat16), pltpu.VMEM(whole, jnp.bfloat16)],
         compiler_params=pltpu.CompilerParams(vmem_limit_bytes=LIMIT),
         cost_estimate=BRIEF,
-    )(plan, *left, *near, *far, *flat, *after)
+    )(plan, *left, *near, *far, *flat, *extra, *after)
     return made, dots
 
 
@@ -258,7 +293,12 @@
                     slot = plan[z.target + first + i]
                     for s in range(z.rep):
                         v = lax.rem(core + z.rep - s, z.rep)
-                        image[v, slot] += parts[e][s][n].astype(jnp.float32)
+                        ref = parts[e][s]
+                        if len(ref.shape) == 3:
+                            term = ref[n]
+                        else:
+                            term = ref[n * z.own_rows : (n + 1) * z.own_rows]
+                        image[v, slot] += term.astype(jnp.float32)
 
                 z.when_valid(plan, first + i, add)
             n += 1
@@ -296,7 +336,8 @@
     refs = list(refs)
     plans = [refs.pop(0) for _ in range(z.env)]
     so_far = refs.pop(0)
-    image = refs.pop()
+    token, image = refs.pop(), refs.pop()
+    token[...] = jnp.zeros_like(token)
     parts = [[refs.pop(0) for _ in range(z.rep)] for _ in range(z.env)]
 
     def start(j, carry):
@@ -312,12 +353,75 @@
     flat = [ref for piece in parts for ref in piece]
     return pl.pallas_call(
         functools.partial(image_body, z, spans),
-        out_shape=jax.ShapeDtypeStruct(so_far.shape, jnp.float32),
+        out_shape=[
+            jax.ShapeDtypeStruct(so_far.shape, jnp.float32),
+            jax.ShapeDtypeStruct((8, 128), jnp.float32),
+        ],
         in_specs=[SMEM] * z.env + [VMEM] * (1 + len(flat)),
+        out_specs=[VMEM, VMEM],
+        compiler_params=pltpu.CompilerParams(vmem_limit_bytes=LIMIT),
+        cost_estimate=BRIEF,
+    )(*plans, so_far, *flat)
+
+
+def in_order(parts, places, count):
+    total = 0.0
+    for place in range(count):
+        for part, at in zip(parts, places):
+            total = total + jnp.where(at == place, part, 0.0)
+    return total
+
+
+def chips_body(z, count, plan, own, *refs):
+    arrived, out = refs[:count], refs[-1]
+    core, chip = plan[z.core], plan[z.chip]
+    parts, places = [], []
+    for e in range(z.env):
+        for s in range(z.rep):
+            ref = arrived[e * z.rep + s - 1] if e + s else own
+            tail = ref[ref.shape[0] - TAIL :].astype(jnp.float32)
+            parts.append(tail[0:1] + tail[1:2] + tail[2:3])
+            at = lax.rem(chip + z.env - e, z.env) * z.rep + lax.rem(core + z.rep - s, z.rep)
+            places.append(at)
+    total = in_order(parts, places, z.env * z.rep)
+    out[...] = jnp.broadcast_to(total, out.shape)
+
+
+def chip_sums(z, plan, own, arrived, after):
+    return pl.pallas_call(
+        functools.partial(chips_body, z, len(arrived)),
+        out_shape=jax.ShapeDtypeStruct((8, z.order), jnp.float32),
+        in_specs=[SMEM] + [VMEM] * (1 + len(arrived)) + [ANY] * len(after),
         out_specs=VMEM,
-        compiler_params=pltpu.CompilerParams(vmem_limit_bytes=LIMIT),
-        cost_estimate=BRIEF,
-    )(*plans, so_far, *flat)
+        cost_estimate=BRIEF,
+    )(plan, own, *arrived, *after)
+
+
+def mean_body(z, count, scale, *refs):
+    out = refs[-1]
+    me = lax.axis_index("sector")
+    parts = [ref[0:1] for ref in refs[:count]]
+    total = parts[0]
+    if count > 1:
+        places = [lax.rem(me + z.sector - step, z.sector) for step in range(count)]
+        total = in_order(parts, places, count)
+    out[...] = total * scale
+
+
+def mean_over_sectors(z, array, entries, after):
+    held = [array]
+    if z.sector <= 4:
+        held += [shift(array, "sector", z.sector, step) for step in range(1, z.sector)]
+    else:
+        held = [total_over(array, "sector")]
+    made = pl.pallas_call(
+        functools.partial(mean_body, z, len(held), 1.0 / entries),
+        out_shape=jax.ShapeDtypeStruct((1, z.order), jnp.float32),
+        in_specs=[VMEM] * len(held) + [ANY] * len(after),
+        out_specs=VMEM,
+        cost_estimate=BRIEF,
+    )(*held, *after)
+    return made[0, : z.batch]
 
 
 def shift(array, axis, size, step):
@@ -348,11 +452,10 @@
     each = z.sector // 4
     span = z.capacity
 
-    def spans_of(g, low=0, count=span):
-        return [((g * each + d) * span + low, count, low) for d in range(each)]
-
-    def plain(spans):
-        return tuple(piece[:2] for piece in spans)
+    def spans_of(g):
+        return [((g * each + d) * span, span, 0) for d in range(each)]
+
+    chunks = {g: spans_of(g) for g in range(4)}
 
     def around(array):
         return [array] + [shift(array, "rep", z.rep, s) for s in range(1, z.rep)]
@@ -361,35 +464,37 @@
         steps = [g * each + d for d in range(each)]
         return [shift(a, "sector", z.sector, k) if k else a for a, k in zip(arrays, steps)]
 
+    partners = [shift(partner, "env", z.env, e) for e in range(1, z.env)]
+    vector_others = around(vectors)[1:]
     right_others = around(right_env)[1:]
+    left = around(left_env)
     plan, own, right_own = load(z, partner, vectors, right_env)
+    own = gate(own, partners)
     right = [right_own] + right_others
-    near_rows = [own[0]] + [shift(own[s], "rep", z.rep, s) for s in range(1, z.rep)]
+    near_rows = [own[0]] + vector_others
     vec = [near_rows]
     for e in range(1, z.env):
         vec.append([shift_both(z, own[s], e, s) for s in range(z.rep)])
-    plans = [plan]
-    for e in range(1, z.env):
-        plans.append(plan_only(z, shift(partner, "env", z.env, e)))
-
-    near = {}
-    *made, left_own = products(z, plan, right, [near_rows], plain(spans_of(1)), (), left_env)
-    near[1] = across(made, 1)
-    left = around(left_own)
-    made = products(z, plan, right, [near_rows], plain(spans_of(3)), made[:1])
-    near[3] = across(made, 3)
-    made = products(z, plan, right, [near_rows], plain(spans_of(2)), (made[0], *left[1:]))
+    plans = [plan] + [plan_only(z, other) for other in partners]
+
+    def near_products(g, after):
+        return products(z, plan, right, [near_rows], [c[:2] for c in chunks[g]], after)
+
+    def far_products(g, after):
+        return products(z, plan, right, vec[1:], [c[:2] for c in chunks[g]], after)
+
+    near, far, parts = {}, {}, {}
+    spans = [piece[:2] for g in (1, 3) for piece in chunks[g]]
+    made = products(z, plan, right, [near_rows], spans)
+    near[1], near[3] = across(made[:each], 1), across(made[each:], 3)
+    made = near_products(2, (made[0], *left[1:]))
     near[2] = across(made, 2)
-    chain = (made[0], *plans[1:])
-
-    chunks = {g: spans_of(g) for g in range(4)}
-    far, parts = {}, {}
-
-    def far_products(g, spans, after):
-        return products(z, plan, right, vec[1:], plain(spans), after)
-
-    def send_terms(g, after):
-        made, folded = terms(z, plan, left, near[g], far[g], vec, chunks[g], after)
+    sent = [array for g in (1, 3, 2) for array in near[g]]
+
+    def send_terms(g, so_far, own_sums, after):
+        made, folded = terms(
+            z, plan, left, near[g], far[g], vec, chunks[g], so_far, own_sums, after
+        )
         parts[g] = [
             [
                 shift_both(z, made[e * z.rep + s], e, s) if e + s else made[0]
@@ -402,19 +507,22 @@
     def arrived(g):
         return [part for piece in parts[g] for part in piece][1:]
 
-    made = far_products(1, chunks[1], chain)
-    sent = [array for g in (1, 3, 2) for array in near[g]]
-    far[1] = across(gate(made, sent), 1)
-    near[0] = products(z, plan, right, [near_rows], plain(chunks[0]), made[:1])
-    far[0] = far_products(0, chunks[0], near[0][:1])
-    dot0 = send_terms(0, ())
-    made = far_products(3, chunks[3], (dot0,))
-    far[3] = across(made, 3)
-    made = far_products(2, chunks[2], (made[0], far[1][0]))
+    far1 = far_products(1, (made[0], *plans[1:]))
+    far3 = far_products(3, far1[:1])
+    far2 = far_products(2, far3[:1])
+    near[0] = near_products(0, far2[:1])
+    far[0] = far_products(0, near[0][:1])
+    dots = send_terms(0, None, None, ())
+    made = gate([*far1, *far3], [dots, *sent])
+    far[1] = across(made[:each], 1)
+    far[3] = across(made[each:], 3)
+    made = gate(far2, far[1])
     far[2] = across(made, 2)
-    dot1 = send_terms(1, made[:1])
-    dot3 = send_terms(3, (dot1, *arrived(0)))
-    dot2 = send_terms(2, (dot3, *arrived(1), *arrived(3)))
+    dots = send_terms(1, dots, None, (*made, *arrived(0)))
+    dots = send_terms(3, dots, None, arrived(1))
+    own_block = vectors.astype(jnp.float32)
+    own_sums = jnp.sum(energy[None, :, None, None] * own_block * own_block, axis=(1, 2, 3))
+    dots = send_terms(2, dots, own_sums, arrived(3))
     early = (0, 1, 3)
     so_far = gather_terms(
         z,
@@ -423,18 +531,12 @@
         vectors,
         [parts[g] for g in early],
         [chunks[g] for g in early],
-        (dot2,),
+        (dots,),
     )
-    image = make_image(z, plans, so_far, parts[2], chunks[2])
-
-    own_block = vectors.astype(jnp.float32)
-    partial_sum = jnp.sum(energy[None, :, None, None] * own_block * own_block, axis=(1, 2, 3))
-    own_vector = (jnp.arange(z.batch) == lax.axis_index("rep")).astype(jnp.float32)
-    partial_sum = partial_sum + own_vector * jnp.sum(dot0 + dot1 + dot2 + dot3)
-    for axis in ("sector", "env", "rep"):
-        partial_sum = total_over(partial_sum, axis)
+    sums = chip_sums(z, plan, dots, arrived(2), (so_far,))
+    image, token = make_image(z, plans, so_far, parts[2], chunks[2])
     entries = z.slots * z.sector * z.order * z.order
-    return (image, partial_sum / entries)
+    return (image, mean_over_sectors(z, sums, entries, (token,)))
 
 
 def solution(mesh):

time: 135 us -> 149 us (1.10)
  local copies, waits for them, and re-layouts: 7.98 us -> 24.1 us
  starting transfers between devices: 27.3 us -> 34.3 us
  waiting for transfers between devices: 56.1 us -> 51.9 us
  Pallas kernels: 38.6 us -> 35.8 us
  other arithmetic: 3.31 us -> 0.85 us
    ppermute x14, waiting for transfers between devices: 8.09 us -> 37.8 us  [shift_both(): return lax.ppermute(array, ('env', 'rep'), perm)]
    ppermute x10 -> x13, waiting for transfers between devices: 39.7 us -> 14.2 us  [shift(): lax.ppermute(array, axis, [(i, (i + step) % size) for i in range(size)])]
    unnamed x58 -> x88, local copies, waits for them, and re-layouts: 7.98 us -> 22.9 us
    ppermute x10 -> x13, starting transfers between devices: 13 us -> 24.6 us  [shift(): lax.ppermute(array, axis, [(i, (i + step) % size) for i in range(size)])]
    ppermute x4 -> x0, waiting for transfers between devices: 8.25 us -> none  [total_over(): lax.ppermute(array, axis, [(i, i ^ step) for i in range(size)])]
    ppermute x4 -> x0, starting transfers between devices: 2.75 us -> none  [total_over(): lax.ppermute(array, axis, [(i, i ^ step) for i in range(size)])]
    pallas_call x13 -> x14, Pallas kernels: 31.9 us -> 29.8 us  [the longest x7 12.8 us: products(): pl.pallas_call(functools.partial(products_body, z, pieces, spans), out_sh...]
    ppermute x14, starting transfers between devices: 11.6 us -> 9.66 us  [shift_both(): return lax.ppermute(array, ('env', 'rep'), perm)]
  transfers between devices with their start and end apart: 28 -> 27, of which waited for: 10 -> 9; matrix products, arithmetic and copies ran while one was open for 2% -> 1% of each run, Pallas kernels for 22% -> 20%
where the time goes in v4:
time: 149 us; the launch traced here: 148 us
  waiting for transfers between devices  51.9 us (35%)
  Pallas kernels  35.8 us (24%)
  starting transfers between devices  34.3 us (23%)
  local copies, waits for them, and re-layouts  24.1 us (16%)
    ppermute x14, waiting for transfers between devices, shift_both(): return lax.ppermute(array, ('env', 'rep'), perm)  37.8 us
    ppermute x13, starting transfers between devices, shift(): lax.ppermute(array, axis, [(i, (i + step) % size) for i in range(size)])  24.6 us
    unnamed x88, local copies, waits for them, and re-layouts  22.9 us
    ppermute x13, waiting for transfers between devices, shift(): lax.ppermute(array, axis, [(i, (i + step) % size) for i in range(size)])  14.2 us
    pallas_call x7, Pallas kernels, products(): pl.pallas_call(functools.partial(products_body, z, pieces, spans), out_sh...  12.8 us
    pallas_call x4, Pallas kernels, terms(): pl.pallas_call(functools.partial(terms_body, z, spans, so_far is not None...  11.2 us
    ppermute x14, starting transfers between devices, shift_both(): return lax.ppermute(array, ('env', 'rep'), perm)  9.66 us
    pallas_call x1, Pallas kernels, load(): pl.pallas_call(functools.partial(load_body, z), out_shape=[jax.ShapeDtype...  3.3 us
  transfers between devices with their start and end apart: 27, of which 9 were waited for; matrix products, arithmetic and copies ran while one was open for 1% of the time, Pallas kernels for 20%

profile of v4, /device:TPU:0, one launch (start us, length us, event | category | flops | bytes accessed | tf_op | source)
XLA Modules:
  0.0 148.0 jit_solution(16799855312164039550)
XLA Ops:
  1.7 2.6 %collective-permute-start = (s32[1,96]{1,0:T(1,128)}, s32[1,96]{1,0:T(1,128)S(1)}, u32[]{:S(2)}, u32[]{:S(2)}) collective-permute-start(s32[1,96]{1,0:T(1,128)} %partner.1), channel_id=1, source_target_pairs={{0,2},{2,0},{1,3},{3,1},{4,6},{6,4},{5,7},{7,5},{8,10},{10,8},{9,1... | collective-permute-start | bytes 1160 | tf_op jit(solution)/shard_map/ppermute | solution.py:428
  4.2 0.7 copy-done.37
  4.9 3.3 %shard_map.68 = (s32[74]{0:T(128)S(1)}, bf16[24,64,256]{2,1,0:T(8,128)(2,1)S(1)}, bf16[24,64,256]{2,1,0:T(8,128)(2,1)S(1)}, bf16[1,24,128,256]{3,2,1,0:T(8,128)(2,1)S(1)}) custom-call(s32[1,96]{1,0:T(1,128)S(1)} %copy-done.37, bf16[2,24,64,256]{3,2,1,0:T(8,128)(2,1)} %refs_3_.1, bf16[1,24,128,256]{3,2,1,0:T(8,128)(2,1)} %right.1), custom_call_target="tpu_custom_call" | custom-call | tf_op jit(solution)/shard_map/pallas_call | solution.py:96
  8.2 1.1 copy-done
  9.4 0.9 copy-done.4
  10.3 0.9 copy-done.25
  11.8 1.5 %collective-permute-start.5 = (bf16[24,64,256]{2,1,0:T(8,128)(2,1)}, bf16[24,64,256]{2,1,0:T(8,128)(2,1)}, u32[]{:S(2)}, u32[]{:S(2)}) collective-permute-start(bf16[24,64,256]{2,1,0:T(8,128)(2,1)} %get-tuple-element.39), channel_id=1, source_target_pairs={{0,3},{1,2},{2,1},{3,0},{4,7},{5,6},{6,5},{7,4},{8,11},{9,10},{10,... | collective-permute-start | bytes 2359304 | tf_op jit(solution)/shard_map/ppermute | solution.py:436
  13.3 1.4 copy-done.1
  14.7 1.1 copy-done.5
  15.8 2.0 %shard_map.71 = (bf16[6,128,256]{2,1,0:T(8,128)(2,1)S(1)}, bf16[6,128,256]{2,1,0:T(8,128)(2,1)}) custom-call(s32[74]{0:T(128)S(1)} %get-tuple-element.34.refs_0_.plan, bf16[1,24,128,256]{3,2,1,0:T(8,128)(2,1)S(1)} %copy-done.1, bf16[1,24,128,256]{3,2,1,0:T(8,128)(2,1)S(1)} %collective-permute-done.2.refs_2_, bf16[24,64,256]{2,1,0:T(8,128)(2,1)S(1)} %copy-done.5, ...), custom_call_target="tpu_custom_call" | custom-call | tf_op jit(solution)/shard_map/pallas_call | solution.py:178
  17.8 1.6 %collective-permute-start.9 = (bf16[6,128,256]{2,1,0:T(8,128)(2,1)S(1)}, bf16[6,128,256]{2,1,0:T(8,128)(2,1)}, u32[]{:S(2)}, u32[]{:S(2)}) collective-permute-start(bf16[6,128,256]{2,1,0:T(8,128)(2,1)S(1)} %get-tuple-element.40.refs_5_), channel_id=1, source_target_pairs={{0,4},{4,8},{8,12},{12,0},{1,5},{5,9},{9,13},{13,1},{2,6},{6,10},{... | collective-permute-start | bytes 1179656 | tf_op jit(solution)/shard_map/ppermute | solution.py:428
  19.4 1.7 %shard_map.72.refs_5_ = bf16[6,128,256]{2,1,0:T(8,128)(2,1)} custom-call(s32[74]{0:T(128)S(1)} %get-tuple-element.34.refs_0_.plan, bf16[1,24,128,256]{3,2,1,0:T(8,128)(2,1)S(1)} %copy-done.1, bf16[1,24,128,256]{3,2,1,0:T(8,128)(2,1)S(1)} %collective-permute-done.2.refs_2_, bf16[24,64,256]{2,1,0:T(8,128)(2,1)S(1)} %copy-done.6, ...), custom_call_target="tpu_custom_call" | custom-call | tf_op jit(solution)/shard_map/pallas_call | solution.py:178
  21.1 2.6 %collective-permute-start.11 = (bf16[6,128,256]{2,1,0:T(8,128)(2,1)}, bf16[6,128,256]{2,1,0:T(8,128)(2,1)}, u32[]{:S(2)}, u32[]{:S(2)}) collective-permute-start(bf16[6,128,256]{2,1,0:T(8,128)(2,1)} %shard_map.72.refs_5_), channel_id=1, source_target_pairs={{0,8},{4,12},{8,0},{12,4},{1,9},{5,13},{9,1},{13,5},{2,10},{6,14},... | collective-permute-start | bytes 1179656 | tf_op jit(solution)/shard_map/ppermute | solution.py:428
  23.6 1.3 collective-permute-start.10
  25.0 1.4 shard_map.69.refs_6_.refs_1_
  26.4 6.1 %collective-permute-done.4.refs_3_.refs_7_ = bf16[24,64,256]{2,1,0:T(8,128)(2,1)} collective-permute-done((bf16[24,64,256]{2,1,0:T(8,128)(2,1)}, bf16[24,64,256]{2,1,0:T(8,128)(2,1)}, u32[]{:S(2)}, u32[]{:S(2)}) %collective-permute-start.4) | collective-permute-done | bytes 786464 | tf_op jit(solution)/shard_map/ppermute | solution.py:436
  32.5 15.3 %collective-permute-done.5.refs_4_.refs_8_ = bf16[24,64,256]{2,1,0:T(8,128)(2,1)} collective-permute-done((bf16[24,64,256]{2,1,0:T(8,128)(2,1)}, bf16[24,64,256]{2,1,0:T(8,128)(2,1)}, u32[]{:S(2)}, u32[]{:S(2)}) %collective-permute-start.5) | collective-permute-done | bytes 786464 | tf_op jit(solution)/shard_map/ppermute | solution.py:436
  47.8 1.4 copy-done.2
  49.2 0.6 copy-done.33
  49.8 1.8 %shard_map.73.refs_5_.refs_0_ = bf16[6,128,256]{2,1,0:T(8,128)(2,1)S(1)} custom-call(s32[74]{0:T(128)S(1)} %get-tuple-element.34.refs_0_.plan, bf16[1,24,128,256]{3,2,1,0:T(8,128)(2,1)S(1)} %copy-done.2, bf16[1,24,128,256]{3,2,1,0:T(8,128)(2,1)S(1)} %collective-permute-done.2.refs_2_, bf16[24,64,256]{2,1,0:T(8,128)(2,1)} %collective-permute-done.4.refs_3_.refs_7_, ...), custom_call_target="tpu_custom_call" | custom-call | tf_op jit(solution)/shard_map/pallas_call | solution.py:178
  51.6 1.9 %shard_map.74.refs_5_.refs_1_ = bf16[6,128,256]{2,1,0:T(8,128)(2,1)S(1)} custom-call(s32[74]{0:T(128)S(1)} %get-tuple-element.34.refs_0_.plan, bf16[1,24,128,256]{3,2,1,0:T(8,128)(2,1)S(1)} %copy-done.2, bf16[1,24,128,256]{3,2,1,0:T(8,128)(2,1)S(1)} %collective-permute-done.2.refs_2_, bf16[24,64,256]{2,1,0:T(8,128)(2,1)} %collective-permute-done.4.refs_3_.refs_7_, ...), custom_call_target="tpu_custom_call" | custom-call | tf_op jit(solution)/shard_map/pallas_call | solution.py:178
  53.6 2.7 %shard_map.75.refs_5_.refs_0_ = bf16[6,128,256]{2,1,0:T(8,128)(2,1)} custom-call(s32[74]{0:T(128)S(1)} %get-tuple-element.34.refs_0_.plan, bf16[1,24,128,256]{3,2,1,0:T(8,128)(2,1)S(1)} %copy-done.2, bf16[1,24,128,256]{3,2,1,0:T(8,128)(2,1)S(1)} %collective-permute-done.2.refs_2_, bf16[24,64,256]{2,1,0:T(8,128)(2,1)} %collective-permute-done.4.refs_3_.refs_7_, ...), custom_call_target="tpu_custom_call" | custom-call | tf_op jit(solution)/shard_map/pallas_call | solution.py:178
  56.2 0.8 copy-done.16
  57.0 0.9 shard_map.76.refs_5_.refs_3_
  58.0 1.9 %shard_map.77.refs_4_ = bf16[6,128,256]{2,1,0:T(8,128)(2,1)S(1)} custom-call(s32[74]{0:T(128)S(1)} %get-tuple-element.34.refs_0_.plan, bf16[1,24,128,256]{3,2,1,0:T(8,128)(2,1)S(1)} %copy-done.3, bf16[1,24,128,256]{3,2,1,0:T(8,128)(2,1)S(1)} %collective-permute-done.2.refs_2_, bf16[24,64,256]{2,1,0:T(8,128)(2,1)} %collective-permute-done.4.refs_3_.refs_7_, ...), custom_call_target="tpu_custom_call" | custom-call | tf_op jit(solution)/shard_map/pallas_call | solution.py:178
  59.9 3.2 %shard_map.78 = (bf16[6,64,256]{2,1,0:T(8,128)(2,1)S(1)}, bf16[6,64,256]{2,1,0:T(8,128)(2,1)}, bf16[6,64,256]{2,1,0:T(8,128)(2,1)}, bf16[6,64,256]{2,1,0:T(8,128)(2,1)S(1)}, f32[8,256]{1,0:T(8,128)S(1)}) custom-call(s32[74]{0:T(128)S(1)} %get-tuple-element.34.refs_0_.plan, bf16[1,24,128,256]{3,2,1,0:T(8,128)(2,1)S(1)} %copy-done.11, ...), custom_call_target="tpu_custom_call" | custom-call | tf_op jit(solution)/shard_map/pallas_call | solution.py:270
  63.1 0.7 copy-done.26
  64.3 0.7 copy-done.38
  65.1 1.6 %collective-permute-start.12 = (bf16[6,128,256]{2,1,0:T(8,128)(2,1)}, bf16[6,128,256]{2,1,0:T(8,128)(2,1)S(1)}, u32[]{:S(2)}, u32[]{:S(2)}) collective-permute-start(bf16[6,128,256]{2,1,0:T(8,128)(2,1)} %get-tuple-element.47), channel_id=1, source_target_pairs={{0,4},{4,8},{8,12},{12,0},{1,5},{5,9},{9,13},{13,1},{2,6},{6,10},{... | collective-permute-start | bytes 1179656 | tf_op jit(solution)/shard_map/ppermute | solution.py:428
  67.9 0.8 collective-permute-start.8
  68.7 2.5 %collective-permute-start.16 = (bf16[6,128,256]{2,1,0:T(8,128)(2,1)}, bf16[6,128,256]{2,1,0:T(8,128)(2,1)}, u32[]{:S(2)}, u32[]{:S(2)}) collective-permute-start(bf16[6,128,256]{2,1,0:T(8,128)(2,1)} %get-tuple-element.52), channel_id=1, source_target_pairs={{0,12},{4,0},{8,4},{12,8},{1,13},{5,1},{9,5},{13,9},{2,14},{6,2},{... | collective-permute-start | bytes 1179656 | tf_op jit(solution)/shard_map/ppermute | solution.py:428
  71.1 8.1 %collective-permute-done.12.refs_1_.refs_4_ = bf16[6,128,256]{2,1,0:T(8,128)(2,1)S(1)} collective-permute-done((bf16[6,128,256]{2,1,0:T(8,128)(2,1)}, bf16[6,128,256]{2,1,0:T(8,128)(2,1)S(1)}, u32[]{:S(2)}, u32[]{:S(2)}) %collective-permute-start.12) | collective-permute-done | bytes 393248 | tf_op jit(solution)/shard_map/ppermute | solution.py:428
  79.3 0.7 copy-done.17
  80.1 1.4 copy-done.12
  81.5 1.0 copy-done.18
  82.5 2.5 %shard_map.81 = (bf16[6,64,256]{2,1,0:T(8,128)(2,1)S(1)}, bf16[6,64,256]{2,1,0:T(8,128)(2,1)S(1)}, bf16[6,64,256]{2,1,0:T(8,128)(2,1)S(1)}, bf16[6,64,256]{2,1,0:T(8,128)(2,1)S(1)}, f32[8,256]{1,0:T(8,128)S(1)}) custom-call(s32[74]{0:T(128)S(1)} %get-tuple-element.34.refs_0_.plan, bf16[1,24,128,256]{3,2,1,0:T(8,128)(2,1)S(1)} %copy-done.12, ...), custom_call_target="tpu_custom_call" | custom-call | tf_op jit(solution)/shard_map/pallas_call | solution.py:270
  85.7 1.3 collective-permute-start.15
  87.0 0.9 collective-permute-start.20
  87.8 5.0 %collective-permute-done.14.refs_11_.refs_10_ = bf16[6,64,256]{2,1,0:T(8,128)(2,1)S(1)} collective-permute-done((bf16[6,64,256]{2,1,0:T(8,128)(2,1)S(1)}, bf16[6,64,256]{2,1,0:T(8,128)(2,1)S(1)}, u32[]{:S(2)}, u32[]{:S(2)}) %collective-permute-start.14) | collective-permute-done | bytes 196640 | tf_op jit(solution)/shard_map/ppermute | solution.py:436
  92.9 3.3 %collective-permute-done.15.refs_12_.refs_11_ = bf16[6,64,256]{2,1,0:T(8,128)(2,1)S(1)} collective-permute-done((bf16[6,64,256]{2,1,0:T(8,128)(2,1)S(1)}, bf16[6,64,256]{2,1,0:T(8,128)(2,1)S(1)}, u32[]{:S(2)}, u32[]{:S(2)}) %collective-permute-start.15) | collective-permute-done | bytes 196640 | tf_op jit(solution)/shard_map/ppermute | solution.py:436
  96.2 2.7 %shard_map.82 = (bf16[6,64,256]{2,1,0:T(8,128)(2,1)S(1)}, bf16[6,64,256]{2,1,0:T(8,128)(2,1)S(1)}, bf16[6,64,256]{2,1,0:T(8,128)(2,1)S(1)}, bf16[6,64,256]{2,1,0:T(8,128)(2,1)S(1)}, f32[8,256]{1,0:T(8,128)S(1)}) custom-call(s32[74]{0:T(128)S(1)} %get-tuple-element.34.refs_0_.plan, bf16[1,24,128,256]{3,2,1,0:T(8,128)(2,1)S(1)} %copy-done.12, ...), custom_call_target="tpu_custom_call" | custom-call | tf_op jit(solution)/shard_map/pallas_call | solution.py:270
  98.9 0.6 collective-permute-start.17
  100.1 0.9 collective-permute-start.19
  101.0 0.9 fusion.refs_10_
  101.8 6.0 %collective-permute-done.20.refs_4_ = bf16[6,128,256]{2,1,0:T(8,128)(2,1)S(1)} collective-permute-done((bf16[6,128,256]{2,1,0:T(8,128)(2,1)}, bf16[6,128,256]{2,1,0:T(8,128)(2,1)S(1)}, u32[]{:S(2)}, u32[]{:S(2)}) %collective-permute-start.20) | collective-permute-done | bytes 393248 | tf_op jit(solution)/shard_map/ppermute | solution.py:428
  107.9 1.9 %collective-permute-done.19.refs_13_.refs_15_ = bf16[6,64,256]{2,1,0:T(8,128)(2,1)S(1)} collective-permute-done((bf16[6,64,256]{2,1,0:T(8,128)(2,1)S(1)}, bf16[6,64,256]{2,1,0:T(8,128)(2,1)S(1)}, u32[]{:S(2)}, u32[]{:S(2)}) %collective-permute-start.19) | collective-permute-done | bytes 196640 | tf_op jit(solution)/shard_map/ppermute | solution.py:436
  109.8 2.7 %shard_map.83 = (bf16[6,64,256]{2,1,0:T(8,128)(2,1)S(1)}, bf16[400,256]{1,0:T(8,128)(2,1)S(1)}, bf16[400,256]{1,0:T(8,128)(2,1)S(1)}, bf16[400,256]{1,0:T(8,128)(2,1)S(1)}, bf16[16,256]{1,0:T(8,128)(2,1)S(1)}) custom-call(s32[74]{0:T(128)S(1)} %get-tuple-element.34.refs_0_.plan, bf16[1,24,128,256]{3,2,1,0:T(8,128)(2,1)S(1)} %copy-done.13, ...), custom_call_target="tpu_custom_call" | custom-call | tf_op jit(solution)/shard_map/pallas_call | solution.py:270
  112.5 0.8 collective-permute-start.21
  113.8 0.9 collective-permute-start.23
  114.7 1.4 shard_map.84.refs_2_.refs_3_
  116.1 1.7 %copy-done.9 = f32[2,24,64,256]{3,2,1,0:T(8,128)} copy-done((f32[2,24,64,256]{3,2,1,0:T(8,128)}, f32[2,24,64,256]{3,2,1,0:T(8,128)S(1)}, u32[]{:S(2)}) %copy-start.9) | copy-done | bytes 3145752
  117.8 3.4 %collective-permute-done.22.refs_5_.refs_1_ = bf16[400,256]{1,0:T(8,128)(2,1)S(1)} collective-permute-done((bf16[400,256]{1,0:T(8,128)(2,1)S(1)}, bf16[400,256]{1,0:T(8,128)(2,1)S(1)}, u32[]{:S(2)}, u32[]{:S(2)}) %collective-permute-start.22) | collective-permute-done | bytes 204832 | tf_op jit(solution)/shard_map/ppermute | solution.py:436
  121.2 2.6 %collective-permute-done.23.refs_6_.refs_2_ = bf16[400,256]{1,0:T(8,128)(2,1)S(1)} collective-permute-done((bf16[400,256]{1,0:T(8,128)(2,1)S(1)}, bf16[400,256]{1,0:T(8,128)(2,1)S(1)}, u32[]{:S(2)}, u32[]{:S(2)}) %collective-permute-start.23) | collective-permute-done | bytes 204832 | tf_op jit(solution)/shard_map/ppermute | solution.py:436
  123.9 0.7 copy-done.23
  124.5 1.8 %shard_map.86.refs_0_ = f32[8,256]{1,0:T(8,128)} custom-call(s32[74]{0:T(128)} %copy-done.28, bf16[16,256]{1,0:T(8,128)(2,1)} %copy-done.30, bf16[400,256]{1,0:T(8,128)(2,1)} %copy-done.19, bf16[400,256]{1,0:T(8,128)(2,1)} %copy-done.21, bf16[400,256]{1,0:T(8,128)(2,1)} %copy-done.23, f32[2,24,64,256]{3,2,1,0:T(8,128)} %copy-done.9), custom_call_target="tpu_custom_call" | custom-call | tf_op jit(solution)/shard_map/pallas_call | solution.py:391
  126.3 1.6 %collective-permute-start.24 = (f32[8,256]{1,0:T(8,128)}, f32[8,256]{1,0:T(8,128)S(1)}, u32[]{:S(2)}, u32[]{:S(2)}) collective-permute-start(f32[8,256]{1,0:T(8,128)} %shard_map.86.refs_0_), channel_id=1, source_target_pairs={{0,4},{4,8},{8,12},{12,0},{1,5},{5,9},{9,13},{13,1},{2,6},{6,10},{... | collective-permute-start | bytes 24584 | tf_op jit(solution)/shard_map/ppermute | solution.py:428
  127.9 9.0 %collective-permute-start.25 = (f32[8,256]{1,0:T(8,128)}, f32[8,256]{1,0:T(8,128)S(1)}, u32[]{:S(2)}, u32[]{:S(2)}) collective-permute-start(f32[8,256]{1,0:T(8,128)} %shard_map.86.refs_0_), channel_id=1, source_target_pairs={{0,8},{4,12},{8,0},{12,4},{1,9},{5,13},{9,1},{13,5},{2,10},{6,14},... | collective-permute-start | bytes 24584 | tf_op jit(solution)/shard_map/ppermute | solution.py:428
  136.9 1.9 %copy-done.10 = f32[2,24,64,256]{3,2,1,0:T(8,128)S(1)} copy-done((f32[2,24,64,256]{3,2,1,0:T(8,128)S(1)}, f32[2,24,64,256]{3,2,1,0:T(8,128)}, u32[]{:S(2)}) %copy-start.10) | copy-done | bytes 3145752
  138.8 0.9 copy-done.20
  139.7 0.9 copy-done.22
  140.7 0.9 copy-done.24
  141.6 2.6 %shard_map.85 = (f32[2,24,64,256]{3,2,1,0:T(8,128)}, f32[8,128]{1,0:T(8,128)S(1)}) custom-call(s32[74]{0:T(128)S(1)} %copy-done.29, s32[74]{0:T(128)S(1)} %copy-done.34, f32[2,24,64,256]{3,2,1,0:T(8,128)S(1)} %copy-done.10, bf16[6,64,256]{2,1,0:T(8,128)(2,1)S(1)} %get-tuple-element.60.refs_3_, bf16[400,256]{1,0:T(8,128)(2,1)S(1)} %copy-done.20, ...), custom_call_target="tpu_custom_call" | custom-call | tf_op jit(solution)/shard_map/pallas_call | solution.py:354
  145.4 1.3 shard_map.87
  146.8 1.2 slice_bitcast_fusion
  (100 shorter events, 6.5 us)
Async XLA Ops:
  0.6 12.7 %collective-permute-start.2 = (bf16[1,24,128,256]{3,2,1,0:T(8,128)(2,1)}, bf16[1,24,128,256]{3,2,1,0:T(8,128)(2,1)S(1)}, u32[]{:S(2)}, u32[]{:S(2)}) collective-permute-start(bf16[1,24,128,256]{3,2,1,0:T(8,128)(2,1)} %right.1), channel_id=1, source_target_pairs={{0,1},{1,0},{2,3},{3,2},{4,5},{5,4},{6,7},{7,6},{8,9},{9,8},{10,11... | collective-permute-start | bytes 4718600 | tf_op jit(solution)/shard_map/ppermute | solution.py:428
  1.1 12.1 %collective-permute-start.3 = (bf16[2,24,64,256]{3,2,1,0:T(8,128)(2,1)}, bf16[2,24,64,256]{3,2,1,0:T(8,128)(2,1)S(1)}, u32[]{:S(2)}, u32[]{:S(2)}) collective-permute-start(bf16[2,24,64,256]{3,2,1,0:T(8,128)(2,1)} %refs_3_.1), channel_id=1, source_target_pairs={{0,1},{1,0},{2,3},{3,2},{4,5},{5,4},{6,7},{7,6},{8,9},{9,8},{10,11... | collective-permute-start | bytes 4718600 | tf_op jit(solution)/shard_map/ppermute | solution.py:428
  1.2 18.2 %collective-permute-start.1 = (bf16[1,24,128,256]{3,2,1,0:T(8,128)(2,1)}, bf16[1,24,128,256]{3,2,1,0:T(8,128)(2,1)}, u32[]{:S(2)}, u32[]{:S(2)}) collective-permute-start(bf16[1,24,128,256]{3,2,1,0:T(8,128)(2,1)} %refs_1_.7), channel_id=1, source_target_pairs={{0,1},{1,0},{2,3},{3,2},{4,5},{5,4},{6,7},{7,6},{8,9},{9,8},{10,11... | collective-permute-start | bytes 4718600 | tf_op jit(solution)/shard_map/ppermute | solution.py:428
  1.7 9.5 %collective-permute-start = (s32[1,96]{1,0:T(1,128)}, s32[1,96]{1,0:T(1,128)S(1)}, u32[]{:S(2)}, u32[]{:S(2)}) collective-permute-start(s32[1,96]{1,0:T(1,128)} %partner.1), channel_id=1, source_target_pairs={{0,2},{2,0},{1,3},{3,1},{4,6},{6,4},{5,7},{7,5},{8,10},{10,8},{9,1... | collective-permute-start | bytes 1160 | tf_op jit(solution)/shard_map/ppermute | solution.py:428
  4.2 0.7 copy-start.37
  8.2 1.1 copy-start
  9.4 0.9 copy-start.4
  10.3 0.9 copy-start.25
  11.2 103.5 %copy-start.28 = (s32[74]{0:T(128)}, s32[74]{0:T(128)S(1)}, u32[]{:S(2)}) copy-start(s32[74]{0:T(128)S(1)} %get-tuple-element.34.refs_0_.plan) | copy-start | bytes 892
  11.8 20.7 %collective-permute-start.4 = (bf16[24,64,256]{2,1,0:T(8,128)(2,1)}, bf16[24,64,256]{2,1,0:T(8,128)(2,1)}, u32[]{:S(2)}, u32[]{:S(2)}) collective-permute-start(bf16[24,64,256]{2,1,0:T(8,128)(2,1)} %get-tuple-element.38.refs_3_.refs_5_), channel_id=1, source_target_pairs={{0,2},{1,3},{2,0},{3,1},{4,6},{5,7},{6,4},{7,5},{8,10},{9,11},{10,... | collective-permute-start | bytes 2359304 | tf_op jit(solution)/shard_map/ppermute | solution.py:436
  11.8 36.0 %collective-permute-start.5 = (bf16[24,64,256]{2,1,0:T(8,128)(2,1)}, bf16[24,64,256]{2,1,0:T(8,128)(2,1)}, u32[]{:S(2)}, u32[]{:S(2)}) collective-permute-start(bf16[24,64,256]{2,1,0:T(8,128)(2,1)} %get-tuple-element.39), channel_id=1, source_target_pairs={{0,3},{1,2},{2,1},{3,0},{4,7},{5,6},{6,5},{7,4},{8,11},{9,10},{10,... | collective-permute-start | bytes 2359304 | tf_op jit(solution)/shard_map/ppermute | solution.py:436
  13.3 1.4 copy-start.1
  14.7 1.1 copy-start.5
  15.8 3.5 %copy-start.6 = (bf16[24,64,256]{2,1,0:T(8,128)(2,1)S(1)}, bf16[24,64,256]{2,1,0:T(8,128)(2,1)}, u32[]{:S(2)}) copy-start(bf16[24,64,256]{2,1,0:T(8,128)(2,1)} %get-tuple-element.38.refs_3_.refs_5_) | copy-start | bytes 2359300
  17.8 47.2 %collective-permute-start.9 = (bf16[6,128,256]{2,1,0:T(8,128)(2,1)S(1)}, bf16[6,128,256]{2,1,0:T(8,128)(2,1)}, u32[]{:S(2)}, u32[]{:S(2)}) collective-permute-start(bf16[6,128,256]{2,1,0:T(8,128)(2,1)S(1)} %get-tuple-element.40.refs_5_), channel_id=1, source_target_pairs={{0,4},{4,8},{8,12},{12,0},{1,5},{5,9},{9,13},{13,1},{2,6},{6,10},{... | collective-permute-start | bytes 1179656 | tf_op jit(solution)/shard_map/ppermute | solution.py:428
  21.1 44.0 %collective-permute-start.11 = (bf16[6,128,256]{2,1,0:T(8,128)(2,1)}, bf16[6,128,256]{2,1,0:T(8,128)(2,1)}, u32[]{:S(2)}, u32[]{:S(2)}) collective-permute-start(bf16[6,128,256]{2,1,0:T(8,128)(2,1)} %shard_map.72.refs_5_), channel_id=1, source_target_pairs={{0,8},{4,12},{8,0},{12,4},{1,9},{5,13},{9,1},{13,5},{2,10},{6,14},... | collective-permute-start | bytes 1179656 | tf_op jit(solution)/shard_map/ppermute | solution.py:428
  23.6 41.4 %collective-permute-start.10 = (bf16[6,128,256]{2,1,0:T(8,128)(2,1)}, bf16[6,128,256]{2,1,0:T(8,128)(2,1)}, u32[]{:S(2)}, u32[]{:S(2)}) collective-permute-start(bf16[6,128,256]{2,1,0:T(8,128)(2,1)} %get-tuple-element.46), channel_id=1, source_target_pairs={{0,12},{4,0},{8,4},{12,8},{1,13},{5,1},{9,5},{13,9},{2,14},{6,2},{... | collective-permute-start | bytes 1179656 | tf_op jit(solution)/shard_map/ppermute | solution.py:428
  47.8 1.4 copy-start.2
  51.6 1.9 %copy-start.15 = (bf16[6,128,256]{2,1,0:T(8,128)(2,1)}, bf16[6,128,256]{2,1,0:T(8,128)(2,1)S(1)}, u32[]{:S(2)}) copy-start(bf16[6,128,256]{2,1,0:T(8,128)(2,1)S(1)} %shard_map.73.refs_5_.refs_0_) | copy-start | bytes 1179652
  53.5 3.5 %copy-start.3 = (bf16[1,24,128,256]{3,2,1,0:T(8,128)(2,1)S(1)}, bf16[1,24,128,256]{3,2,1,0:T(8,128)(2,1)}, u32[]{:S(2)}) copy-start(bf16[1,24,128,256]{3,2,1,0:T(8,128)(2,1)} %copy-done) | copy-start | bytes 4718596
  53.6 3.5 %copy-start.7 = (bf16[24,64,256]{2,1,0:T(8,128)(2,1)S(1)}, bf16[24,64,256]{2,1,0:T(8,128)(2,1)}, u32[]{:S(2)}) copy-start(bf16[24,64,256]{2,1,0:T(8,128)(2,1)} %get-tuple-element.38.refs_3_.refs_5_) | copy-start | bytes 2359300
  56.2 0.8 copy-start.16
  58.0 1.9 %copy-start.11 = (bf16[1,24,128,256]{3,2,1,0:T(8,128)(2,1)S(1)}, bf16[1,24,128,256]{3,2,1,0:T(8,128)(2,1)}, u32[]{:S(2)}) copy-start(bf16[1,24,128,256]{3,2,1,0:T(8,128)(2,1)} %refs_1_.7) | copy-start | bytes 4718596
  63.0 0.7 copy-start.26
  64.3 0.7 copy-start.38
  65.0 2.8 %copy-start.39 = (bf16[6,64,256]{2,1,0:T(8,128)(2,1)S(1)}, bf16[6,64,256]{2,1,0:T(8,128)(2,1)}, u32[]{:S(2)}) copy-start(bf16[6,64,256]{2,1,0:T(8,128)(2,1)} %copy-done.38) | copy-start | bytes 589828
  65.0 15.0 %copy-start.8 = (bf16[24,64,256]{2,1,0:T(8,128)(2,1)S(1)}, bf16[24,64,256]{2,1,0:T(8,128)(2,1)}, u32[]{:S(2)}) copy-start(bf16[24,64,256]{2,1,0:T(8,128)(2,1)} %get-tuple-element.38.refs_3_.refs_5_) | copy-start | bytes 2359300
  65.0 15.0 %copy-start.32 = (f32[8,256]{1,0:T(8,128)S(1)}, f32[8,256]{1,0:T(8,128)}, u32[]{:S(2)}) copy-start(f32[8,256]{1,0:T(8,128)} %copy-done.31) | copy-start | bytes 24580
  65.1 14.2 %collective-permute-start.12 = (bf16[6,128,256]{2,1,0:T(8,128)(2,1)}, bf16[6,128,256]{2,1,0:T(8,128)(2,1)S(1)}, u32[]{:S(2)}, u32[]{:S(2)}) collective-permute-start(bf16[6,128,256]{2,1,0:T(8,128)(2,1)} %get-tuple-element.47), channel_id=1, source_target_pairs={{0,4},{4,8},{8,12},{12,0},{1,5},{5,9},{9,13},{13,1},{2,6},{6,10},{... | collective-permute-start | bytes 1179656 | tf_op jit(solution)/shard_map/ppermute | solution.py:428
  66.7 13.3 %collective-permute-start.6 = (bf16[6,64,256]{2,1,0:T(8,128)(2,1)}, bf16[6,64,256]{2,1,0:T(8,128)(2,1)S(1)}, u32[]{:S(2)}, u32[]{:S(2)}) collective-permute-start(bf16[6,64,256]{2,1,0:T(8,128)(2,1)} %get-tuple-element.42), channel_id=1, source_target_pairs={{0,1},{1,0},{2,3},{3,2},{4,5},{5,4},{6,7},{7,6},{8,9},{9,8},{10,11... | collective-permute-start | bytes 589832 | tf_op jit(solution)/shard_map/ppermute | solution.py:436
  67.3 12.7 %collective-permute-start.7 = (bf16[6,64,256]{2,1,0:T(8,128)(2,1)}, bf16[6,64,256]{2,1,0:T(8,128)(2,1)S(1)}, u32[]{:S(2)}, u32[]{:S(2)}) collective-permute-start(bf16[6,64,256]{2,1,0:T(8,128)(2,1)} %get-tuple-element.43), channel_id=1, source_target_pairs={{0,2},{1,3},{2,0},{3,1},{4,6},{5,7},{6,4},{7,5},{8,10},{9,11},{10,... | collective-permute-start | bytes 589832 | tf_op jit(solution)/shard_map/ppermute | solution.py:436
  67.9 12.2 %collective-permute-start.8 = (bf16[6,64,256]{2,1,0:T(8,128)(2,1)S(1)}, bf16[6,64,256]{2,1,0:T(8,128)(2,1)S(1)}, u32[]{:S(2)}, u32[]{:S(2)}) collective-permute-start(bf16[6,64,256]{2,1,0:T(8,128)(2,1)S(1)} %copy-done.39), channel_id=1, source_target_pairs={{0,3},{1,2},{2,1},{3,0},{4,7},{5,6},{6,5},{7,4},{8,11},{9,10},{10,... | collective-permute-start | bytes 589832 | tf_op jit(solution)/shard_map/ppermute | solution.py:436
  68.7 19.2 %collective-permute-start.16 = (bf16[6,128,256]{2,1,0:T(8,128)(2,1)}, bf16[6,128,256]{2,1,0:T(8,128)(2,1)}, u32[]{:S(2)}, u32[]{:S(2)}) collective-permute-start(bf16[6,128,256]{2,1,0:T(8,128)(2,1)} %get-tuple-element.52), channel_id=1, source_target_pairs={{0,12},{4,0},{8,4},{12,8},{1,13},{5,1},{9,5},{13,9},{2,14},{6,2},{... | collective-permute-start | bytes 1179656 | tf_op jit(solution)/shard_map/ppermute | solution.py:428
  79.3 0.7 copy-start.17
  80.1 1.4 copy-start.12
  81.5 1.0 copy-start.18
  85.0 2.8 %collective-permute-start.13 = (bf16[6,64,256]{2,1,0:T(8,128)(2,1)S(1)}, bf16[6,64,256]{2,1,0:T(8,128)(2,1)S(1)}, u32[]{:S(2)}, u32[]{:S(2)}) collective-permute-start(bf16[6,64,256]{2,1,0:T(8,128)(2,1)S(1)} %get-tuple-element.49), channel_id=1, source_target_pairs={{0,1},{1,0},{2,3},{3,2},{4,5},{5,4},{6,7},{7,6},{8,9},{9,8},{10,11... | collective-permute-start | bytes 589832 | tf_op jit(solution)/shard_map/ppermute | solution.py:436
  85.1 7.8 %collective-permute-start.14 = (bf16[6,64,256]{2,1,0:T(8,128)(2,1)S(1)}, bf16[6,64,256]{2,1,0:T(8,128)(2,1)S(1)}, u32[]{:S(2)}, u32[]{:S(2)}) collective-permute-start(bf16[6,64,256]{2,1,0:T(8,128)(2,1)S(1)} %get-tuple-element.50), channel_id=1, source_target_pairs={{0,2},{1,3},{2,0},{3,1},{4,6},{5,7},{6,4},{7,5},{8,10},{9,11},{10,... | collective-permute-start | bytes 589832 | tf_op jit(solution)/shard_map/ppermute | solution.py:436
  85.7 10.5 %collective-permute-start.15 = (bf16[6,64,256]{2,1,0:T(8,128)(2,1)S(1)}, bf16[6,64,256]{2,1,0:T(8,128)(2,1)S(1)}, u32[]{:S(2)}, u32[]{:S(2)}) collective-permute-start(bf16[6,64,256]{2,1,0:T(8,128)(2,1)S(1)} %get-tuple-element.51), channel_id=1, source_target_pairs={{0,3},{1,2},{2,1},{3,0},{4,7},{5,6},{6,5},{7,4},{8,11},{9,10},{10,... | collective-permute-start | bytes 589832 | tf_op jit(solution)/shard_map/ppermute | solution.py:436
  87.0 20.9 %collective-permute-start.20 = (bf16[6,128,256]{2,1,0:T(8,128)(2,1)}, bf16[6,128,256]{2,1,0:T(8,128)(2,1)S(1)}, u32[]{:S(2)}, u32[]{:S(2)}) collective-permute-start(bf16[6,128,256]{2,1,0:T(8,128)(2,1)} %shard_map.80.refs_10_), channel_id=1, source_target_pairs={{0,8},{4,12},{8,0},{12,4},{1,9},{5,13},{9,1},{13,5},{2,10},{6,14},... | collective-permute-start | bytes 1179656 | tf_op jit(solution)/shard_map/ppermute | solution.py:428
  96.2 4.8 %copy-start.14 = (bf16[2,24,64,256]{3,2,1,0:T(8,128)(2,1)S(1)}, bf16[2,24,64,256]{3,2,1,0:T(8,128)(2,1)}, u32[]{:S(2)}) copy-start(bf16[2,24,64,256]{3,2,1,0:T(8,128)(2,1)} %refs_3_.1) | copy-start | bytes 4718596
  96.2 4.8 %copy-start.36 = (f32[24]{0:T(128)S(1)}, f32[24]{0:T(128)}, u32[]{:S(2)}) copy-start(f32[24]{0:T(128)} %refs_2_.1) | copy-start | bytes 292
  98.9 10.9 %copy-start.13 = (bf16[1,24,128,256]{3,2,1,0:T(8,128)(2,1)S(1)}, bf16[1,24,128,256]{3,2,1,0:T(8,128)(2,1)}, u32[]{:S(2)}) copy-start(bf16[1,24,128,256]{3,2,1,0:T(8,128)(2,1)} %refs_1_.7) | copy-start | bytes 4718596
  98.9 8.9 %collective-permute-start.17 = (bf16[6,64,256]{2,1,0:T(8,128)(2,1)S(1)}, bf16[6,64,256]{2,1,0:T(8,128)(2,1)S(1)}, u32[]{:S(2)}, u32[]{:S(2)}) collective-permute-start(bf16[6,64,256]{2,1,0:T(8,128)(2,1)S(1)} %get-tuple-element.55), channel_id=1, source_target_pairs={{0,1},{1,0},{2,3},{3,2},{4,5},{5,4},{6,7},{7,6},{8,9},{9,8},{10,11... | collective-permute-start | bytes 589832 | tf_op jit(solution)/shard_map/ppermute | solution.py:436
  99.6 8.3 %collective-permute-start.18 = (bf16[6,64,256]{2,1,0:T(8,128)(2,1)S(1)}, bf16[6,64,256]{2,1,0:T(8,128)(2,1)S(1)}, u32[]{:S(2)}, u32[]{:S(2)}) collective-permute-start(bf16[6,64,256]{2,1,0:T(8,128)(2,1)S(1)} %get-tuple-element.56), channel_id=1, source_target_pairs={{0,2},{1,3},{2,0},{3,1},{4,6},{5,7},{6,4},{7,5},{8,10},{9,11},{10,... | collective-permute-start | bytes 589832 | tf_op jit(solution)/shard_map/ppermute | solution.py:436
  100.1 9.7 %collective-permute-start.19 = (bf16[6,64,256]{2,1,0:T(8,128)(2,1)S(1)}, bf16[6,64,256]{2,1,0:T(8,128)(2,1)S(1)}, u32[]{:S(2)}, u32[]{:S(2)}) collective-permute-start(bf16[6,64,256]{2,1,0:T(8,128)(2,1)S(1)} %get-tuple-element.57), channel_id=1, source_target_pairs={{0,3},{1,2},{2,1},{3,0},{4,7},{5,6},{6,5},{7,4},{8,11},{9,10},{10,... | collective-permute-start | bytes 589832 | tf_op jit(solution)/shard_map/ppermute | solution.py:436
  109.8 4.9 %copy-start.27 = (bf16[6,64,256]{2,1,0:T(8,128)(2,1)S(1)}, bf16[6,64,256]{2,1,0:T(8,128)(2,1)}, u32[]{:S(2)}) copy-start(bf16[6,64,256]{2,1,0:T(8,128)(2,1)} %copy-done.26) | copy-start | bytes 589828
  109.8 4.9 %copy-start.34 = (s32[74]{0:T(128)S(1)}, s32[74]{0:T(128)}, u32[]{:S(2)}) copy-start(s32[74]{0:T(128)} %shard_map.69.refs_6_.refs_1_) | copy-start | bytes 892
  112.5 3.6 %copy-start.30 = (bf16[16,256]{1,0:T(8,128)(2,1)}, bf16[16,256]{1,0:T(8,128)(2,1)S(1)}, u32[]{:S(2)}) copy-start(bf16[16,256]{1,0:T(8,128)(2,1)S(1)} %get-tuple-element.59.refs_16_.own) | copy-start | bytes 24580
  112.5 5.2 %collective-permute-start.21 = (bf16[400,256]{1,0:T(8,128)(2,1)S(1)}, bf16[400,256]{1,0:T(8,128)(2,1)S(1)}, u32[]{:S(2)}, u32[]{:S(2)}) collective-permute-start(bf16[400,256]{1,0:T(8,128)(2,1)S(1)} %get-tuple-element.61), channel_id=1, source_target_pairs={{0,1},{1,0},{2,3},{3,2},{4,5},{5,4},{6,7},{7,6},{8,9},{9,8},{10,11... | collective-permute-start | bytes 614408 | tf_op jit(solution)/shard_map/ppermute | solution.py:436
  113.3 7.9 %collective-permute-start.22 = (bf16[400,256]{1,0:T(8,128)(2,1)S(1)}, bf16[400,256]{1,0:T(8,128)(2,1)S(1)}, u32[]{:S(2)}, u32[]{:S(2)}) collective-permute-start(bf16[400,256]{1,0:T(8,128)(2,1)S(1)} %get-tuple-element.62), channel_id=1, source_target_pairs={{0,2},{1,3},{2,0},{3,1},{4,6},{5,7},{6,4},{7,5},{8,10},{9,11},{10,... | collective-permute-start | bytes 614408 | tf_op jit(solution)/shard_map/ppermute | solution.py:436
  113.8 10.0 %collective-permute-start.23 = (bf16[400,256]{1,0:T(8,128)(2,1)S(1)}, bf16[400,256]{1,0:T(8,128)(2,1)S(1)}, u32[]{:S(2)}, u32[]{:S(2)}) collective-permute-start(bf16[400,256]{1,0:T(8,128)(2,1)S(1)} %get-tuple-element.63), channel_id=1, source_target_pairs={{0,3},{1,2},{2,1},{3,0},{4,7},{5,6},{6,5},{7,4},{8,11},{9,10},{10,... | collective-permute-start | bytes 614408 | tf_op jit(solution)/shard_map/ppermute | solution.py:436
  116.1 1.7 %copy-start.9 = (f32[2,24,64,256]{3,2,1,0:T(8,128)}, f32[2,24,64,256]{3,2,1,0:T(8,128)S(1)}, u32[]{:S(2)}) copy-start(f32[2,24,64,256]{3,2,1,0:T(8,128)S(1)} %shard_map.84.refs_2_.refs_3_) | copy-start | bytes 9437188
  117.8 19.1 %copy-start.29 = (s32[74]{0:T(128)S(1)}, s32[74]{0:T(128)}, u32[]{:S(2)}) copy-start(s32[74]{0:T(128)} %copy-done.28) | copy-start | bytes 892
  117.8 6.1 %copy-start.19 = (bf16[400,256]{1,0:T(8,128)(2,1)}, bf16[400,256]{1,0:T(8,128)(2,1)S(1)}, u32[]{:S(2)}) copy-start(bf16[400,256]{1,0:T(8,128)(2,1)S(1)} %collective-permute-done.21.refs_4_.refs_0_) | copy-start | bytes 614404
  121.2 2.6 %copy-start.21 = (bf16[400,256]{1,0:T(8,128)(2,1)}, bf16[400,256]{1,0:T(8,128)(2,1)S(1)}, u32[]{:S(2)}) copy-start(bf16[400,256]{1,0:T(8,128)(2,1)S(1)} %collective-permute-done.22.refs_5_.refs_1_) | copy-start | bytes 614404
  123.9 0.7 copy-start.23
  126.3 18.5 %collective-permute-start.24 = (f32[8,256]{1,0:T(8,128)}, f32[8,256]{1,0:T(8,128)S(1)}, u32[]{:S(2)}, u32[]{:S(2)}) collective-permute-start(f32[8,256]{1,0:T(8,128)} %shard_map.86.refs_0_), channel_id=1, source_target_pairs={{0,4},{4,8},{8,12},{12,0},{1,5},{5,9},{9,13},{13,1},{2,6},{6,10},{... | collective-permute-start | bytes 24584 | tf_op jit(solution)/shard_map/ppermute | solution.py:428
  127.9 16.9 %collective-permute-start.25 = (f32[8,256]{1,0:T(8,128)}, f32[8,256]{1,0:T(8,128)S(1)}, u32[]{:S(2)}, u32[]{:S(2)}) collective-permute-start(f32[8,256]{1,0:T(8,128)} %shard_map.86.refs_0_), channel_id=1, source_target_pairs={{0,8},{4,12},{8,0},{12,4},{1,9},{5,13},{9,1},{13,5},{2,10},{6,14},... | collective-permute-start | bytes 24584 | tf_op jit(solution)/shard_map/ppermute | solution.py:428
  136.9 7.9 %collective-permute-start.26 = (f32[8,256]{1,0:T(8,128)}, f32[8,256]{1,0:T(8,128)S(1)}, u32[]{:S(2)}, u32[]{:S(2)}) collective-permute-start(f32[8,256]{1,0:T(8,128)} %shard_map.86.refs_0_), channel_id=1, source_target_pairs={{0,12},{4,0},{8,4},{12,8},{1,13},{5,1},{9,5},{13,9},{2,14},{6,2},{... | collective-permute-start | bytes 24584 | tf_op jit(solution)/shard_map/ppermute | solution.py:428
  136.9 1.9 %copy-start.10 = (f32[2,24,64,256]{3,2,1,0:T(8,128)S(1)}, f32[2,24,64,256]{3,2,1,0:T(8,128)}, u32[]{:S(2)}) copy-start(f32[2,24,64,256]{3,2,1,0:T(8,128)} %copy-done.9) | copy-start | bytes 9437188
  138.8 0.9 copy-start.20
  139.7 0.9 copy-start.22
  140.7 0.9 copy-start.24
  (7 other events, 4.2 us)

commit v5 on v4

--- a/solution.py
+++ b/solution.py
@@ -12,6 +12,7 @@
 SMEM = pl.BlockSpec(memory_space=pltpu.SMEM)
 VMEM = pl.BlockSpec(memory_space=pltpu.VMEM)
 LIMIT = 12 * 1024 * 1024
+SMALL = 2 * 1024 * 1024
 TAIL = 16
 BRIEF = pl.CostEstimate(flops=0, bytes_accessed=0, transcendentals=0)
 
@@ -121,6 +122,7 @@
         in_specs=[SMEM],
         out_specs=SMEM,
         scratch_shapes=[pltpu.SMEM((z.sector,), jnp.int32)],
+        compiler_params=pltpu.CompilerParams(vmem_limit_bytes=SMALL),
         cost_estimate=BRIEF,
     )(partner)
 
@@ -135,6 +137,7 @@
         in_specs=[ANY] * (len(arrays) + len(after)),
         out_specs=[ANY] * len(arrays),
         input_output_aliases={i: i for i in range(len(arrays))},
+        compiler_params=pltpu.CompilerParams(vmem_limit_bytes=SMALL),
         cost_estimate=BRIEF,
     )(*arrays, *after)
 
@@ -393,6 +396,7 @@
         out_shape=jax.ShapeDtypeStruct((8, z.order), jnp.float32),
         in_specs=[SMEM] + [VMEM] * (1 + len(arrived)) + [ANY] * len(after),
         out_specs=VMEM,
+        compiler_params=pltpu.CompilerParams(vmem_limit_bytes=SMALL),
         cost_estimate=BRIEF,
     )(plan, own, *arrived, *after)
 
@@ -419,6 +423,7 @@
         out_shape=jax.ShapeDtypeStruct((1, z.order), jnp.float32),
         in_specs=[VMEM] * len(held) + [ANY] * len(after),
         out_specs=VMEM,
+        compiler_params=pltpu.CompilerParams(vmem_limit_bytes=SMALL),
         cost_estimate=BRIEF,
     )(*held, *after)
     return made[0, : z.batch]

time: 149 us -> 117 us (0.79)
  local copies, waits for them, and re-layouts: 24.1 us -> 1.67 us
  Pallas kernels: 35.8 us -> 20.5 us
  waiting for transfers between devices: 51.9 us -> 58.7 us
    unnamed x88 -> x8, local copies, waits for them, and re-layouts: 22.9 us -> 1.15 us
    ppermute x13, waiting for transfers between devices: 14.2 us -> 21.6 us  [shift(): lax.ppermute(array, axis, [(i, (i + step) % size) for i in range(size)])]
    pallas_call x4, Pallas kernels: 11.2 us -> 4.42 us  [terms(): pl.pallas_call(functools.partial(terms_body, z, spans, so_far is not None...]
    pallas_call x7, Pallas kernels: 12.8 us -> 6.84 us  [products(): pl.pallas_call(functools.partial(products_body, z, pieces, spans), out_sh...]
  transfers between devices with their start and end apart: 27 -> 27, of which waited for: 9 -> 10; matrix products, arithmetic and copies ran while one was open for 1% -> 1% of each run, Pallas kernels for 20% -> 16%
where the time goes in v5:
time: 117 us; the launch traced here: 116 us
  waiting for transfers between devices  58.7 us (50%)
  starting transfers between devices  33.8 us (29%)
  Pallas kernels  20.5 us (18%)
  local copies, waits for them, and re-layouts  1.67 us (1%)
    ppermute x14, waiting for transfers between devices, shift_both(): return lax.ppermute(array, ('env', 'rep'), perm)  37.2 us
    ppermute x13, starting transfers between devices, shift(): lax.ppermute(array, axis, [(i, (i + step) % size) for i in range(size)])  24.3 us
    ppermute x13, waiting for transfers between devices, shift(): lax.ppermute(array, axis, [(i, (i + step) % size) for i in range(size)])  21.6 us
    ppermute x14, starting transfers between devices, shift_both(): return lax.ppermute(array, ('env', 'rep'), perm)  9.48 us
    pallas_call x7, Pallas kernels, products(): pl.pallas_call(functools.partial(products_body, z, pieces, spans), out_sh...  6.84 us
    pallas_call x4, Pallas kernels, terms(): pl.pallas_call(functools.partial(terms_body, z, spans, so_far is not None...  4.42 us
    pallas_call x1, Pallas kernels, load(): pl.pallas_call(functools.partial(load_body, z), out_shape=[jax.ShapeDtype...  3.3 us
    pallas_call x1, Pallas kernels, make_image(): pl.pallas_call(functools.partial(image_body, z, spans), out_shape=[jax.Sh...  2.62 us
  transfers between devices with their start and end apart: 27, of which 10 were waited for; matrix products, arithmetic and copies ran while one was open for 1% of the time, Pallas kernels for 16%

profile of v5, /device:TPU:0, one launch (start us, length us, event | category | flops | bytes accessed | tf_op | source)
XLA Modules:
  0.0 116.4 jit_solution(1508505532307991493)
XLA Ops:
  0.6 0.5 collective-permute-start.2
  1.1 0.1 collective-permute-start.3
  1.2 0.4 collective-permute-start.1
  1.7 2.6 %collective-permute-start = (s32[1,96]{1,0:T(1,128)}, s32[1,96]{1,0:T(1,128)S(1)}, u32[]{:S(2)}, u32[]{:S(2)}) collective-permute-start(s32[1,96]{1,0:T(1,128)} %partner.1), channel_id=1, source_target_pairs={{0,2},{2,0},{1,3},{3,1},{4,6},{6,4},{5,7},{7,5},{8,10},{10,8},{9,1... | collective-permute-start | bytes 1160 | tf_op jit(solution)/shard_map/ppermute | solution.py:433
  4.2 0.7 copy-done.3
  4.9 3.3 %shard_map.68 = (s32[74]{0:T(128)S(1)}, bf16[24,64,256]{2,1,0:T(8,128)(2,1)S(1)}, bf16[24,64,256]{2,1,0:T(8,128)(2,1)S(1)}, bf16[1,24,128,256]{3,2,1,0:T(8,128)(2,1)S(1)}) custom-call(s32[1,96]{1,0:T(1,128)S(1)} %copy-done.3, bf16[2,24,64,256]{3,2,1,0:T(8,128)(2,1)} %refs_3_.1, bf16[1,24,128,256]{3,2,1,0:T(8,128)(2,1)} %right.1), custom_call_target="tpu_custom_call" | custom-call | tf_op jit(solution)/shard_map/pallas_call | solution.py:97
  8.2 0.1 collective-permute-start.4
  8.3 1.5 %collective-permute-start.5 = (bf16[24,64,256]{2,1,0:T(8,128)(2,1)S(1)}, bf16[24,64,256]{2,1,0:T(8,128)(2,1)S(1)}, u32[]{:S(2)}, u32[]{:S(2)}) collective-permute-start(bf16[24,64,256]{2,1,0:T(8,128)(2,1)S(1)} %get-tuple-element.39), channel_id=1, source_target_pairs={{0,3},{1,2},{2,1},{3,0},{4,7},{5,6},{6,5},{7,4},{8,11},{9,10},{10,... | collective-permute-start | bytes 2359304 | tf_op jit(solution)/shard_map/ppermute | solution.py:441
  9.8 0.0 collective-permute-done.2.refs_2_
  9.8 0.0 collective-permute-done.3.refs_4_.refs_6_
  9.8 1.2 %shard_map.71 = (bf16[6,128,256]{2,1,0:T(8,128)(2,1)S(1)}, bf16[6,128,256]{2,1,0:T(8,128)(2,1)S(1)}) custom-call(s32[74]{0:T(128)S(1)} %get-tuple-element.34.refs_0_.plan, bf16[1,24,128,256]{3,2,1,0:T(8,128)(2,1)S(1)} %get-tuple-element.35.refs_1_, bf16[1,24,128,256]{3,2,1,0:T(8,128)(2,1)S(1)} %collective-permute-done.2.refs_2_, ...), custom_call_target="tpu_custom_call" | custom-call | tf_op jit(solution)/shard_map/pallas_call | solution.py:181
  11.1 1.6 %collective-permute-start.9 = (bf16[6,128,256]{2,1,0:T(8,128)(2,1)S(1)}, bf16[6,128,256]{2,1,0:T(8,128)(2,1)S(1)}, u32[]{:S(2)}, u32[]{:S(2)}) collective-permute-start(bf16[6,128,256]{2,1,0:T(8,128)(2,1)S(1)} %get-tuple-element.40.refs_5_), channel_id=1, source_target_pairs={{0,4},{4,8},{8,12},{12,0},{1,5},{5,9},{9,13},{13,1},{2,6},{6,10},{... | collective-permute-start | bytes 1179656 | tf_op jit(solution)/shard_map/ppermute | solution.py:433
  12.7 0.0 collective-permute-done.1.refs_6_.refs_2_
  12.7 0.9 shard_map.72.refs_5_
  13.6 2.7 %collective-permute-start.11 = (bf16[6,128,256]{2,1,0:T(8,128)(2,1)S(1)}, bf16[6,128,256]{2,1,0:T(8,128)(2,1)S(1)}, u32[]{:S(2)}, u32[]{:S(2)}) collective-permute-start(bf16[6,128,256]{2,1,0:T(8,128)(2,1)S(1)} %shard_map.72.refs_5_), channel_id=1, source_target_pairs={{0,8},{4,12},{8,0},{12,4},{1,9},{5,13},{9,1},{13,5},{2,10},{6,14},... | collective-permute-start | bytes 1179656 | tf_op jit(solution)/shard_map/ppermute | solution.py:433
  16.3 1.4 %collective-permute-start.10 = (bf16[6,128,256]{2,1,0:T(8,128)(2,1)S(1)}, bf16[6,128,256]{2,1,0:T(8,128)(2,1)S(1)}, u32[]{:S(2)}, u32[]{:S(2)}) collective-permute-start(bf16[6,128,256]{2,1,0:T(8,128)(2,1)S(1)} %get-tuple-element.46), channel_id=1, source_target_pairs={{0,12},{4,0},{8,4},{12,8},{1,13},{5,1},{9,5},{13,9},{2,14},{6,2},{... | collective-permute-start | bytes 1179656 | tf_op jit(solution)/shard_map/ppermute | solution.py:433
  17.6 1.3 %shard_map.69.refs_6_.refs_1_ = s32[74]{0:T(128)S(1)} custom-call(s32[1,96]{1,0:T(1,128)S(1)} %collective-permute-done.partner.refs_2_), custom_call_target="tpu_custom_call" | custom-call | tf_op jit(solution)/shard_map/pallas_call | solution.py:119
  19.0 9.7 %collective-permute-done.4.refs_3_.refs_7_ = bf16[24,64,256]{2,1,0:T(8,128)(2,1)S(1)} collective-permute-done((bf16[24,64,256]{2,1,0:T(8,128)(2,1)S(1)}, bf16[24,64,256]{2,1,0:T(8,128)(2,1)S(1)}, u32[]{:S(2)}, u32[]{:S(2)}) %collective-permute-start.4) | collective-permute-done | bytes 786464 | tf_op jit(solution)/shard_map/ppermute | solution.py:441
  28.7 15.3 %collective-permute-done.5.refs_4_.refs_8_ = bf16[24,64,256]{2,1,0:T(8,128)(2,1)S(1)} collective-permute-done((bf16[24,64,256]{2,1,0:T(8,128)(2,1)S(1)}, bf16[24,64,256]{2,1,0:T(8,128)(2,1)S(1)}, u32[]{:S(2)}, u32[]{:S(2)}) %collective-permute-start.5) | collective-permute-done | bytes 786464 | tf_op jit(solution)/shard_map/ppermute | solution.py:441
  44.0 0.9 shard_map.73.refs_5_.refs_0_
  44.9 0.9 shard_map.74.refs_5_.refs_1_
  45.9 0.9 shard_map.75.refs_5_.refs_0_
  46.8 0.9 shard_map.76.refs_5_.refs_3_
  47.8 0.0 copy-start
  47.8 0.9 shard_map.77.refs_4_
  48.7 0.5 copy-done
  49.2 1.1 shard_map.78
  50.3 0.0 collective-permute-done.11.refs_5_.refs_3_
  50.3 0.0 collective-permute-done.9.refs_3_
  50.3 1.6 %collective-permute-start.12 = (bf16[6,128,256]{2,1,0:T(8,128)(2,1)S(1)}, bf16[6,128,256]{2,1,0:T(8,128)(2,1)S(1)}, u32[]{:S(2)}, u32[]{:S(2)}) collective-permute-start(bf16[6,128,256]{2,1,0:T(8,128)(2,1)S(1)} %get-tuple-element.47), channel_id=1, source_target_pairs={{0,4},{4,8},{8,12},{12,0},{1,5},{5,9},{9,13},{13,1},{2,6},{6,10},{... | collective-permute-start | bytes 1179656 | tf_op jit(solution)/shard_map/ppermute | solution.py:433
  51.9 0.6 collective-permute-start.6
  52.5 0.5 collective-permute-start.7
  53.1 0.8 collective-permute-start.8
  53.9 2.5 %collective-permute-start.16 = (bf16[6,128,256]{2,1,0:T(8,128)(2,1)S(1)}, bf16[6,128,256]{2,1,0:T(8,128)(2,1)S(1)}, u32[]{:S(2)}, u32[]{:S(2)}) collective-permute-start(bf16[6,128,256]{2,1,0:T(8,128)(2,1)S(1)} %get-tuple-element.52), channel_id=1, source_target_pairs={{0,12},{4,0},{8,4},{12,8},{1,13},{5,1},{9,5},{13,9},{2,14},{6,2},{... | collective-permute-start | bytes 1179656 | tf_op jit(solution)/shard_map/ppermute | solution.py:433
  56.4 7.9 %collective-permute-done.12.refs_1_.refs_4_ = bf16[6,128,256]{2,1,0:T(8,128)(2,1)S(1)} collective-permute-done((bf16[6,128,256]{2,1,0:T(8,128)(2,1)S(1)}, bf16[6,128,256]{2,1,0:T(8,128)(2,1)S(1)}, u32[]{:S(2)}, u32[]{:S(2)}) %collective-permute-start.12) | collective-permute-done | bytes 393248 | tf_op jit(solution)/shard_map/ppermute | solution.py:433
  64.3 0.0 collective-permute-done.6.refs_11_.refs_5_
  64.3 0.0 collective-permute-done.7.refs_12_.refs_6_
  64.3 1.1 shard_map.81
  65.4 0.1 collective-permute-start.13
  65.5 0.6 collective-permute-start.14
  66.1 1.2 %collective-permute-start.15 = (bf16[6,64,256]{2,1,0:T(8,128)(2,1)S(1)}, bf16[6,64,256]{2,1,0:T(8,128)(2,1)S(1)}, u32[]{:S(2)}, u32[]{:S(2)}) collective-permute-start(bf16[6,64,256]{2,1,0:T(8,128)(2,1)S(1)} %get-tuple-element.51), channel_id=1, source_target_pairs={{0,3},{1,2},{2,1},{3,0},{4,7},{5,6},{6,5},{7,4},{8,11},{9,10},{10,... | collective-permute-start | bytes 589832 | tf_op jit(solution)/shard_map/ppermute | solution.py:441
  67.3 1.5 %collective-permute-start.20 = (bf16[6,128,256]{2,1,0:T(8,128)(2,1)S(1)}, bf16[6,128,256]{2,1,0:T(8,128)(2,1)S(1)}, u32[]{:S(2)}, u32[]{:S(2)}) collective-permute-start(bf16[6,128,256]{2,1,0:T(8,128)(2,1)S(1)} %shard_map.80.refs_10_), channel_id=1, source_target_pairs={{0,8},{4,12},{8,0},{12,4},{1,9},{5,13},{9,1},{13,5},{2,10},{6,14},... | collective-permute-start | bytes 1179656 | tf_op jit(solution)/shard_map/ppermute | solution.py:433
  68.8 3.7 %collective-permute-done.16.refs_4_ = bf16[6,128,256]{2,1,0:T(8,128)(2,1)S(1)} collective-permute-done((bf16[6,128,256]{2,1,0:T(8,128)(2,1)S(1)}, bf16[6,128,256]{2,1,0:T(8,128)(2,1)S(1)}, u32[]{:S(2)}, u32[]{:S(2)}) %collective-permute-start.16) | collective-permute-done | bytes 393248 | tf_op jit(solution)/shard_map/ppermute | solution.py:433
  72.6 0.7 collective-permute-done.14.refs_11_.refs_10_
  73.2 3.3 %collective-permute-done.15.refs_12_.refs_11_ = bf16[6,64,256]{2,1,0:T(8,128)(2,1)S(1)} collective-permute-done((bf16[6,64,256]{2,1,0:T(8,128)(2,1)S(1)}, bf16[6,64,256]{2,1,0:T(8,128)(2,1)S(1)}, u32[]{:S(2)}, u32[]{:S(2)}) %collective-permute-start.15) | collective-permute-done | bytes 196640 | tf_op jit(solution)/shard_map/ppermute | solution.py:441
  76.5 1.1 shard_map.82
  77.6 0.6 collective-permute-start.17
  78.2 0.6 collective-permute-start.18
  78.8 0.9 collective-permute-start.19
  79.7 0.9 fusion.refs_10_
  80.6 8.9 %collective-permute-done.20.refs_4_ = bf16[6,128,256]{2,1,0:T(8,128)(2,1)S(1)} collective-permute-done((bf16[6,128,256]{2,1,0:T(8,128)(2,1)S(1)}, bf16[6,128,256]{2,1,0:T(8,128)(2,1)S(1)}, u32[]{:S(2)}, u32[]{:S(2)}) %collective-permute-start.20) | collective-permute-done | bytes 393248 | tf_op jit(solution)/shard_map/ppermute | solution.py:433
  89.4 1.2 %shard_map.83 = (bf16[6,64,256]{2,1,0:T(8,128)(2,1)S(1)}, bf16[400,256]{1,0:T(8,128)(2,1)S(1)}, bf16[400,256]{1,0:T(8,128)(2,1)S(1)}, bf16[400,256]{1,0:T(8,128)(2,1)S(1)}, bf16[16,256]{1,0:T(8,128)(2,1)S(1)}) custom-call(s32[74]{0:T(128)S(1)} %get-tuple-element.34.refs_0_.plan, bf16[1,24,128,256]{3,2,1,0:T(8,128)(2,1)S(1)} %copy-done, ...), custom_call_target="tpu_custom_call" | custom-call | tf_op jit(solution)/shard_map/pallas_call | solution.py:273
  90.7 0.2 collective-permute-start.21
  90.8 0.5 collective-permute-start.22
  91.4 1.2 %collective-permute-start.23 = (bf16[400,256]{1,0:T(8,128)(2,1)S(1)}, bf16[400,256]{1,0:T(8,128)(2,1)S(1)}, u32[]{:S(2)}, u32[]{:S(2)}) collective-permute-start(bf16[400,256]{1,0:T(8,128)(2,1)S(1)} %get-tuple-element.63), channel_id=1, source_target_pairs={{0,3},{1,2},{2,1},{3,0},{4,7},{5,6},{6,5},{7,4},{8,11},{9,10},{10,... | collective-permute-start | bytes 614408 | tf_op jit(solution)/shard_map/ppermute | solution.py:441
  92.6 1.3 %shard_map.84.refs_2_.refs_3_ = f32[2,24,64,256]{3,2,1,0:T(8,128)S(1)} custom-call(s32[74]{0:T(128)S(1)} %get-tuple-element.34.refs_0_.plan, s32[74]{0:T(128)S(1)} %shard_map.69.refs_6_.refs_1_, f32[24]{0:T(128)S(1)} %copy-done.2, bf16[2,24,64,256]{3,2,1,0:T(8,128)(2,1)S(1)} %copy-done.1, bf16[6,64,256]{2,1,0:T(8,128)(2,1)S(1)} %get-tuple-element.41.refs_4_, ...), custom_call_target="tpu_custom_call" | custom-call | tf_op jit(solution)/shard_map/pallas_call | solution.py:328
  94.0 4.7 %collective-permute-done.22.refs_5_.refs_1_ = bf16[400,256]{1,0:T(8,128)(2,1)S(1)} collective-permute-done((bf16[400,256]{1,0:T(8,128)(2,1)S(1)}, bf16[400,256]{1,0:T(8,128)(2,1)S(1)}, u32[]{:S(2)}, u32[]{:S(2)}) %collective-permute-start.22) | collective-permute-done | bytes 204832 | tf_op jit(solution)/shard_map/ppermute | solution.py:441
  98.7 3.4 %collective-permute-done.23.refs_6_.refs_2_ = bf16[400,256]{1,0:T(8,128)(2,1)S(1)} collective-permute-done((bf16[400,256]{1,0:T(8,128)(2,1)S(1)}, bf16[400,256]{1,0:T(8,128)(2,1)S(1)}, u32[]{:S(2)}, u32[]{:S(2)}) %collective-permute-start.23) | collective-permute-done | bytes 204832 | tf_op jit(solution)/shard_map/ppermute | solution.py:441
  102.1 0.6 shard_map.86.refs_0_
  102.7 0.6 collective-permute-start.24
  103.3 9.0 %collective-permute-start.25 = (f32[8,256]{1,0:T(8,128)S(1)}, f32[8,256]{1,0:T(8,128)S(1)}, u32[]{:S(2)}, u32[]{:S(2)}) collective-permute-start(f32[8,256]{1,0:T(8,128)S(1)} %shard_map.86.refs_0_), channel_id=1, source_target_pairs={{0,8},{4,12},{8,0},{12,4},{1,9},{5,13},{9,1},{13,5},{2,10},{6,14},... | collective-permute-start | bytes 24584 | tf_op jit(solution)/shard_map/ppermute | solution.py:433
  112.2 2.6 %shard_map.85 = (f32[2,24,64,256]{3,2,1,0:T(8,128)}, f32[8,128]{1,0:T(8,128)S(1)}) custom-call(s32[74]{0:T(128)S(1)} %get-tuple-element.34.refs_0_.plan, s32[74]{0:T(128)S(1)} %shard_map.69.refs_6_.refs_1_, f32[2,24,64,256]{3,2,1,0:T(8,128)S(1)} %shard_map.84.refs_2_.refs_3_, bf16[6,64,256]{2,1,0:T(8,128)(2,1)S(1)} %get-tuple-element.60.refs_3_, ...), custom_call_target="tpu_custom_call" | custom-call | tf_op jit(solution)/shard_map/pallas_call | solution.py:357
  114.9 1.0 collective-permute-done.26.refs_3_
  115.9 0.5 slice_bitcast_fusion
  (20 shorter events, 0.1 us)
Async XLA Ops:
  0.6 9.2 %collective-permute-start.2 = (bf16[1,24,128,256]{3,2,1,0:T(8,128)(2,1)}, bf16[1,24,128,256]{3,2,1,0:T(8,128)(2,1)S(1)}, u32[]{:S(2)}, u32[]{:S(2)}) collective-permute-start(bf16[1,24,128,256]{3,2,1,0:T(8,128)(2,1)} %right.1), channel_id=1, source_target_pairs={{0,1},{1,0},{2,3},{3,2},{4,5},{5,4},{6,7},{7,6},{8,9},{9,8},{10,11... | collective-permute-start | bytes 4718600 | tf_op jit(solution)/shard_map/ppermute | solution.py:433
  1.1 8.7 %collective-permute-start.3 = (bf16[2,24,64,256]{3,2,1,0:T(8,128)(2,1)}, bf16[2,24,64,256]{3,2,1,0:T(8,128)(2,1)S(1)}, u32[]{:S(2)}, u32[]{:S(2)}) collective-permute-start(bf16[2,24,64,256]{3,2,1,0:T(8,128)(2,1)} %refs_3_.1), channel_id=1, source_target_pairs={{0,1},{1,0},{2,3},{3,2},{4,5},{5,4},{6,7},{7,6},{8,9},{9,8},{10,11... | collective-permute-start | bytes 4718600 | tf_op jit(solution)/shard_map/ppermute | solution.py:433
  1.2 11.5 %collective-permute-start.1 = (bf16[1,24,128,256]{3,2,1,0:T(8,128)(2,1)}, bf16[1,24,128,256]{3,2,1,0:T(8,128)(2,1)S(1)}, u32[]{:S(2)}, u32[]{:S(2)}) collective-permute-start(bf16[1,24,128,256]{3,2,1,0:T(8,128)(2,1)} %refs_1_.7), channel_id=1, source_target_pairs={{0,1},{1,0},{2,3},{3,2},{4,5},{5,4},{6,7},{7,6},{8,9},{9,8},{10,11... | collective-permute-start | bytes 4718600 | tf_op jit(solution)/shard_map/ppermute | solution.py:433
  1.7 6.6 %collective-permute-start = (s32[1,96]{1,0:T(1,128)}, s32[1,96]{1,0:T(1,128)S(1)}, u32[]{:S(2)}, u32[]{:S(2)}) collective-permute-start(s32[1,96]{1,0:T(1,128)} %partner.1), channel_id=1, source_target_pairs={{0,2},{2,0},{1,3},{3,1},{4,6},{6,4},{5,7},{7,5},{8,10},{10,8},{9,1... | collective-permute-start | bytes 1160 | tf_op jit(solution)/shard_map/ppermute | solution.py:433
  4.2 0.7 copy-start.3
  8.2 20.5 %collective-permute-start.4 = (bf16[24,64,256]{2,1,0:T(8,128)(2,1)S(1)}, bf16[24,64,256]{2,1,0:T(8,128)(2,1)S(1)}, u32[]{:S(2)}, u32[]{:S(2)}) collective-permute-start(bf16[24,64,256]{2,1,0:T(8,128)(2,1)S(1)} %get-tuple-element.38.refs_3_.refs_5_), channel_id=1, source_target_pairs={{0,2},{1,3},{2,0},{3,1},{4,6},{5,7},{6,4},{7,5},{8,10},{9,11},{10,... | collective-permute-start | bytes 2359304 | tf_op jit(solution)/shard_map/ppermute | solution.py:441
  8.3 35.7 %collective-permute-start.5 = (bf16[24,64,256]{2,1,0:T(8,128)(2,1)S(1)}, bf16[24,64,256]{2,1,0:T(8,128)(2,1)S(1)}, u32[]{:S(2)}, u32[]{:S(2)}) collective-permute-start(bf16[24,64,256]{2,1,0:T(8,128)(2,1)S(1)} %get-tuple-element.39), channel_id=1, source_target_pairs={{0,3},{1,2},{2,1},{3,0},{4,7},{5,6},{6,5},{7,4},{8,11},{9,10},{10,... | collective-permute-start | bytes 2359304 | tf_op jit(solution)/shard_map/ppermute | solution.py:441
  11.1 39.2 %collective-permute-start.9 = (bf16[6,128,256]{2,1,0:T(8,128)(2,1)S(1)}, bf16[6,128,256]{2,1,0:T(8,128)(2,1)S(1)}, u32[]{:S(2)}, u32[]{:S(2)}) collective-permute-start(bf16[6,128,256]{2,1,0:T(8,128)(2,1)S(1)} %get-tuple-element.40.refs_5_), channel_id=1, source_target_pairs={{0,4},{4,8},{8,12},{12,0},{1,5},{5,9},{9,13},{13,1},{2,6},{6,10},{... | collective-permute-start | bytes 1179656 | tf_op jit(solution)/shard_map/ppermute | solution.py:433
  13.6 36.6 %collective-permute-start.11 = (bf16[6,128,256]{2,1,0:T(8,128)(2,1)S(1)}, bf16[6,128,256]{2,1,0:T(8,128)(2,1)S(1)}, u32[]{:S(2)}, u32[]{:S(2)}) collective-permute-start(bf16[6,128,256]{2,1,0:T(8,128)(2,1)S(1)} %shard_map.72.refs_5_), channel_id=1, source_target_pairs={{0,8},{4,12},{8,0},{12,4},{1,9},{5,13},{9,1},{13,5},{2,10},{6,14},... | collective-permute-start | bytes 1179656 | tf_op jit(solution)/shard_map/ppermute | solution.py:433
  16.3 34.0 %collective-permute-start.10 = (bf16[6,128,256]{2,1,0:T(8,128)(2,1)S(1)}, bf16[6,128,256]{2,1,0:T(8,128)(2,1)S(1)}, u32[]{:S(2)}, u32[]{:S(2)}) collective-permute-start(bf16[6,128,256]{2,1,0:T(8,128)(2,1)S(1)} %get-tuple-element.46), channel_id=1, source_target_pairs={{0,12},{4,0},{8,4},{12,8},{1,13},{5,1},{9,5},{13,9},{2,14},{6,2},{... | collective-permute-start | bytes 1179656 | tf_op jit(solution)/shard_map/ppermute | solution.py:433
  47.8 1.4 %copy-start = (bf16[1,24,128,256]{3,2,1,0:T(8,128)(2,1)S(1)}, bf16[1,24,128,256]{3,2,1,0:T(8,128)(2,1)}, u32[]{:S(2)}) copy-start(bf16[1,24,128,256]{3,2,1,0:T(8,128)(2,1)} %refs_1_.7) | copy-start | bytes 4718596
  50.3 14.0 %collective-permute-start.12 = (bf16[6,128,256]{2,1,0:T(8,128)(2,1)S(1)}, bf16[6,128,256]{2,1,0:T(8,128)(2,1)S(1)}, u32[]{:S(2)}, u32[]{:S(2)}) collective-permute-start(bf16[6,128,256]{2,1,0:T(8,128)(2,1)S(1)} %get-tuple-element.47), channel_id=1, source_target_pairs={{0,4},{4,8},{8,12},{12,0},{1,5},{5,9},{9,13},{13,1},{2,6},{6,10},{... | collective-permute-start | bytes 1179656 | tf_op jit(solution)/shard_map/ppermute | solution.py:433
  51.9 12.4 %collective-permute-start.6 = (bf16[6,64,256]{2,1,0:T(8,128)(2,1)S(1)}, bf16[6,64,256]{2,1,0:T(8,128)(2,1)S(1)}, u32[]{:S(2)}, u32[]{:S(2)}) collective-permute-start(bf16[6,64,256]{2,1,0:T(8,128)(2,1)S(1)} %get-tuple-element.42), channel_id=1, source_target_pairs={{0,1},{1,0},{2,3},{3,2},{4,5},{5,4},{6,7},{7,6},{8,9},{9,8},{10,11... | collective-permute-start | bytes 589832 | tf_op jit(solution)/shard_map/ppermute | solution.py:441
  52.5 11.8 %collective-permute-start.7 = (bf16[6,64,256]{2,1,0:T(8,128)(2,1)S(1)}, bf16[6,64,256]{2,1,0:T(8,128)(2,1)S(1)}, u32[]{:S(2)}, u32[]{:S(2)}) collective-permute-start(bf16[6,64,256]{2,1,0:T(8,128)(2,1)S(1)} %get-tuple-element.43), channel_id=1, source_target_pairs={{0,2},{1,3},{2,0},{3,1},{4,6},{5,7},{6,4},{7,5},{8,10},{9,11},{10,... | collective-permute-start | bytes 589832 | tf_op jit(solution)/shard_map/ppermute | solution.py:441
  53.1 11.2 %collective-permute-start.8 = (bf16[6,64,256]{2,1,0:T(8,128)(2,1)S(1)}, bf16[6,64,256]{2,1,0:T(8,128)(2,1)S(1)}, u32[]{:S(2)}, u32[]{:S(2)}) collective-permute-start(bf16[6,64,256]{2,1,0:T(8,128)(2,1)S(1)} %get-tuple-element.44), channel_id=1, source_target_pairs={{0,3},{1,2},{2,1},{3,0},{4,7},{5,6},{6,5},{7,4},{8,11},{9,10},{10,... | collective-permute-start | bytes 589832 | tf_op jit(solution)/shard_map/ppermute | solution.py:441
  53.9 18.7 %collective-permute-start.16 = (bf16[6,128,256]{2,1,0:T(8,128)(2,1)S(1)}, bf16[6,128,256]{2,1,0:T(8,128)(2,1)S(1)}, u32[]{:S(2)}, u32[]{:S(2)}) collective-permute-start(bf16[6,128,256]{2,1,0:T(8,128)(2,1)S(1)} %get-tuple-element.52), channel_id=1, source_target_pairs={{0,12},{4,0},{8,4},{12,8},{1,13},{5,1},{9,5},{13,9},{2,14},{6,2},{... | collective-permute-start | bytes 1179656 | tf_op jit(solution)/shard_map/ppermute | solution.py:433
  65.4 7.2 %collective-permute-start.13 = (bf16[6,64,256]{2,1,0:T(8,128)(2,1)S(1)}, bf16[6,64,256]{2,1,0:T(8,128)(2,1)S(1)}, u32[]{:S(2)}, u32[]{:S(2)}) collective-permute-start(bf16[6,64,256]{2,1,0:T(8,128)(2,1)S(1)} %get-tuple-element.49), channel_id=1, source_target_pairs={{0,1},{1,0},{2,3},{3,2},{4,5},{5,4},{6,7},{7,6},{8,9},{9,8},{10,11... | collective-permute-start | bytes 589832 | tf_op jit(solution)/shard_map/ppermute | solution.py:441
  65.5 7.8 %collective-permute-start.14 = (bf16[6,64,256]{2,1,0:T(8,128)(2,1)S(1)}, bf16[6,64,256]{2,1,0:T(8,128)(2,1)S(1)}, u32[]{:S(2)}, u32[]{:S(2)}) collective-permute-start(bf16[6,64,256]{2,1,0:T(8,128)(2,1)S(1)} %get-tuple-element.50), channel_id=1, source_target_pairs={{0,2},{1,3},{2,0},{3,1},{4,6},{5,7},{6,4},{7,5},{8,10},{9,11},{10,... | collective-permute-start | bytes 589832 | tf_op jit(solution)/shard_map/ppermute | solution.py:441
  66.1 10.5 %collective-permute-start.15 = (bf16[6,64,256]{2,1,0:T(8,128)(2,1)S(1)}, bf16[6,64,256]{2,1,0:T(8,128)(2,1)S(1)}, u32[]{:S(2)}, u32[]{:S(2)}) collective-permute-start(bf16[6,64,256]{2,1,0:T(8,128)(2,1)S(1)} %get-tuple-element.51), channel_id=1, source_target_pairs={{0,3},{1,2},{2,1},{3,0},{4,7},{5,6},{6,5},{7,4},{8,11},{9,10},{10,... | collective-permute-start | bytes 589832 | tf_op jit(solution)/shard_map/ppermute | solution.py:441
  67.3 22.1 %collective-permute-start.20 = (bf16[6,128,256]{2,1,0:T(8,128)(2,1)S(1)}, bf16[6,128,256]{2,1,0:T(8,128)(2,1)S(1)}, u32[]{:S(2)}, u32[]{:S(2)}) collective-permute-start(bf16[6,128,256]{2,1,0:T(8,128)(2,1)S(1)} %shard_map.80.refs_10_), channel_id=1, source_target_pairs={{0,8},{4,12},{8,0},{12,4},{1,9},{5,13},{9,1},{13,5},{2,10},{6,14},... | collective-permute-start | bytes 1179656 | tf_op jit(solution)/shard_map/ppermute | solution.py:433
  76.5 3.1 %copy-start.1 = (bf16[2,24,64,256]{3,2,1,0:T(8,128)(2,1)S(1)}, bf16[2,24,64,256]{3,2,1,0:T(8,128)(2,1)}, u32[]{:S(2)}) copy-start(bf16[2,24,64,256]{3,2,1,0:T(8,128)(2,1)} %refs_3_.1) | copy-start | bytes 4718596
  76.5 3.1 %copy-start.2 = (f32[24]{0:T(128)S(1)}, f32[24]{0:T(128)}, u32[]{:S(2)}) copy-start(f32[24]{0:T(128)} %refs_2_.1) | copy-start | bytes 292
  77.6 11.8 %collective-permute-start.17 = (bf16[6,64,256]{2,1,0:T(8,128)(2,1)S(1)}, bf16[6,64,256]{2,1,0:T(8,128)(2,1)S(1)}, u32[]{:S(2)}, u32[]{:S(2)}) collective-permute-start(bf16[6,64,256]{2,1,0:T(8,128)(2,1)S(1)} %get-tuple-element.55), channel_id=1, source_target_pairs={{0,1},{1,0},{2,3},{3,2},{4,5},{5,4},{6,7},{7,6},{8,9},{9,8},{10,11... | collective-permute-start | bytes 589832 | tf_op jit(solution)/shard_map/ppermute | solution.py:441
  78.2 11.2 %collective-permute-start.18 = (bf16[6,64,256]{2,1,0:T(8,128)(2,1)S(1)}, bf16[6,64,256]{2,1,0:T(8,128)(2,1)S(1)}, u32[]{:S(2)}, u32[]{:S(2)}) collective-permute-start(bf16[6,64,256]{2,1,0:T(8,128)(2,1)S(1)} %get-tuple-element.56), channel_id=1, source_target_pairs={{0,2},{1,3},{2,0},{3,1},{4,6},{5,7},{6,4},{7,5},{8,10},{9,11},{10,... | collective-permute-start | bytes 589832 | tf_op jit(solution)/shard_map/ppermute | solution.py:441
  78.8 10.6 %collective-permute-start.19 = (bf16[6,64,256]{2,1,0:T(8,128)(2,1)S(1)}, bf16[6,64,256]{2,1,0:T(8,128)(2,1)S(1)}, u32[]{:S(2)}, u32[]{:S(2)}) collective-permute-start(bf16[6,64,256]{2,1,0:T(8,128)(2,1)S(1)} %get-tuple-element.57), channel_id=1, source_target_pairs={{0,3},{1,2},{2,1},{3,0},{4,7},{5,6},{6,5},{7,4},{8,11},{9,10},{10,... | collective-permute-start | bytes 589832 | tf_op jit(solution)/shard_map/ppermute | solution.py:441
  90.7 3.3 %collective-permute-start.21 = (bf16[400,256]{1,0:T(8,128)(2,1)S(1)}, bf16[400,256]{1,0:T(8,128)(2,1)S(1)}, u32[]{:S(2)}, u32[]{:S(2)}) collective-permute-start(bf16[400,256]{1,0:T(8,128)(2,1)S(1)} %get-tuple-element.61), channel_id=1, source_target_pairs={{0,1},{1,0},{2,3},{3,2},{4,5},{5,4},{6,7},{7,6},{8,9},{9,8},{10,11... | collective-permute-start | bytes 614408 | tf_op jit(solution)/shard_map/ppermute | solution.py:441
  90.8 7.9 %collective-permute-start.22 = (bf16[400,256]{1,0:T(8,128)(2,1)S(1)}, bf16[400,256]{1,0:T(8,128)(2,1)S(1)}, u32[]{:S(2)}, u32[]{:S(2)}) collective-permute-start(bf16[400,256]{1,0:T(8,128)(2,1)S(1)} %get-tuple-element.62), channel_id=1, source_target_pairs={{0,2},{1,3},{2,0},{3,1},{4,6},{5,7},{6,4},{7,5},{8,10},{9,11},{10,... | collective-permute-start | bytes 614408 | tf_op jit(solution)/shard_map/ppermute | solution.py:441
  91.4 10.8 %collective-permute-start.23 = (bf16[400,256]{1,0:T(8,128)(2,1)S(1)}, bf16[400,256]{1,0:T(8,128)(2,1)S(1)}, u32[]{:S(2)}, u32[]{:S(2)}) collective-permute-start(bf16[400,256]{1,0:T(8,128)(2,1)S(1)} %get-tuple-element.63), channel_id=1, source_target_pairs={{0,3},{1,2},{2,1},{3,0},{4,7},{5,6},{6,5},{7,4},{8,11},{9,10},{10,... | collective-permute-start | bytes 614408 | tf_op jit(solution)/shard_map/ppermute | solution.py:441
  102.7 12.1 %collective-permute-start.24 = (f32[8,256]{1,0:T(8,128)S(1)}, f32[8,256]{1,0:T(8,128)S(1)}, u32[]{:S(2)}, u32[]{:S(2)}) collective-permute-start(f32[8,256]{1,0:T(8,128)S(1)} %shard_map.86.refs_0_), channel_id=1, source_target_pairs={{0,4},{4,8},{8,12},{12,0},{1,5},{5,9},{9,13},{13,1},{2,6},{6,10},{... | collective-permute-start | bytes 24584 | tf_op jit(solution)/shard_map/ppermute | solution.py:433
  103.3 11.6 %collective-permute-start.25 = (f32[8,256]{1,0:T(8,128)S(1)}, f32[8,256]{1,0:T(8,128)S(1)}, u32[]{:S(2)}, u32[]{:S(2)}) collective-permute-start(f32[8,256]{1,0:T(8,128)S(1)} %shard_map.86.refs_0_), channel_id=1, source_target_pairs={{0,8},{4,12},{8,0},{12,4},{1,9},{5,13},{9,1},{13,5},{2,10},{6,14},... | collective-permute-start | bytes 24584 | tf_op jit(solution)/shard_map/ppermute | solution.py:433
  112.2 3.7 %collective-permute-start.26 = (f32[8,256]{1,0:T(8,128)S(1)}, f32[8,256]{1,0:T(8,128)S(1)}, u32[]{:S(2)}, u32[]{:S(2)}) collective-permute-start(f32[8,256]{1,0:T(8,128)S(1)} %shard_map.86.refs_0_), channel_id=1, source_target_pairs={{0,12},{4,0},{8,4},{12,8},{1,13},{5,1},{9,5},{13,9},{2,14},{6,2},{... | collective-permute-start | bytes 24584 | tf_op jit(solution)/shard_map/ppermute | solution.py:433

commit v6 on v5

--- a/solution.py
+++ b/solution.py
@@ -53,11 +53,13 @@
         lax.fori_loop(0, 3 * z.flat, clear, 0)
     for d in range(z.sector):
         count[d] = 0
+    factor = -(-(1 << 16) // z.slots)
+    assert all(i * factor >> 16 == i // z.slots for i in range(z.sector * z.slots))
     for j in range(z.slots):
         sector = partner[0, j]
-        group = lax.div(sector, z.slots)
+        group = (sector * factor) >> 16
         slot = sector - group * z.slots
-        distance = lax.rem(z.sector - group, z.sector)
+        distance = jnp.where(group == 0, 0, z.sector - group)
         rank = count[distance]
         count[distance] = rank + 1
         index = distance * z.capacity + rank
@@ -285,51 +287,70 @@
     return made, dots
 
 
-def add_terms(z, plans, image, parts, spans):
-    core = plans[0][z.core]
+def for_terms(z, plans, parts, spans, action):
     n = 0
     for first, count, _ in spans:
         for i in range(count):
             for e, plan in enumerate(plans):
 
-                def add():
-                    slot = plan[z.target + first + i]
-                    for s in range(z.rep):
-                        v = lax.rem(core + z.rep - s, z.rep)
-                        ref = parts[e][s]
+                def act():
+                    blocks = []
+                    for ref in parts[e]:
                         if len(ref.shape) == 3:
-                            term = ref[n]
+                            blocks.append(lambda ref=ref: ref[n])
                         else:
-                            term = ref[n * z.own_rows : (n + 1) * z.own_rows]
-                        image[v, slot] += term.astype(jnp.float32)
-
-                z.when_valid(plan, first + i, add)
+                            rows = slice(n * z.own_rows, (n + 1) * z.own_rows)
+                            blocks.append(lambda ref=ref: ref[rows])
+                    action(plan[z.target + first + i], blocks)
+
+                z.when_valid(plan, first + i, act)
             n += 1
+
+
+def add_terms(z, plans, image, parts, spans):
+    core = plans[0][z.core]
+
+    def add(slot, blocks):
+        for s, block in enumerate(blocks):
+            v = lax.rem(core + z.rep - s, z.rep)
+            image[v, slot] += block().astype(jnp.float32)
+
+    for_terms(z, plans, parts, spans, add)
 
 
 def gather_body(z, chunks, *refs):
     refs = list(refs)
     plans = [refs.pop(0) for _ in range(z.env)]
-    energy, vectors, image = refs.pop(0), refs.pop(0), refs[-1]
+    energy, vectors = refs.pop(0), refs.pop(0)
+    so_far, image, sem = refs[-3:]
 
     def start(j, carry):
         for v in range(z.batch):
-            image[v, j] = energy[j] * vectors[v, j].astype(jnp.float32)
+            so_far[v, j] = energy[j] * vectors[v, j].astype(jnp.float32)
         return carry
 
     lax.fori_loop(0, z.slots, start, 0, unroll=2)
     for spans in chunks:
         parts = [[refs.pop(0) for _ in range(z.rep)] for _ in range(z.env)]
-        add_terms(z, plans, image, parts, spans)
+        add_terms(z, plans, so_far, parts, spans)
+    copies = []
+    for v in range(z.batch):
+        copies += split_copy(so_far.at[v], image.at[v], z.slots, sem.at[v])
+    for copy in copies:
+        copy.start()
+    for copy in copies:
+        copy.wait()
 
 
 def gather_terms(z, plans, energy, vectors, parts, chunks, after=()):
     flat = [ref for chunk in parts for piece in chunk for ref in piece]
+    shape = jax.ShapeDtypeStruct(vectors.shape, jnp.float32)
     return pl.pallas_call(
         functools.partial(gather_body, z, chunks),
-        out_shape=jax.ShapeDtypeStruct(vectors.shape, jnp.float32),
+        out_shape=[shape, pltpu.HBM(vectors.shape, jnp.float32)],
         in_specs=[SMEM] * (z.env + 1) + [VMEM] * (1 + len(flat)) + [ANY] * len(after),
-        out_specs=VMEM,
+        out_specs=[VMEM, HBM],
+        scratch_shapes=[pltpu.SemaphoreType.DMA((z.batch, 4))],
         compiler_params=pltpu.CompilerParams(vmem_limit_bytes=LIMIT),
         cost_estimate=BRIEF,
     )(*plans, energy, vectors, *flat, *after)
@@ -339,32 +360,52 @@
     refs = list(refs)
     plans = [refs.pop(0) for _ in range(z.env)]
     so_far = refs.pop(0)
-    token, image = refs.pop(), refs.pop()
+    parts = [[refs.pop(0) for _ in range(z.rep)] for _ in range(z.env)]
+    image, token, sums, sem = refs[-4:]
     token[...] = jnp.zeros_like(token)
-    parts = [[refs.pop(0) for _ in range(z.rep)] for _ in range(z.env)]
-
-    def start(j, carry):
+
+    def take(slot, blocks):
         for v in range(z.batch):
-            image[v, j] = so_far[v, j]
-        return carry
-
-    lax.fori_loop(0, z.slots, start, 0, unroll=2)
-    add_terms(z, plans, image, parts, spans)
-
-
-def make_image(z, plans, so_far, parts, spans):
+            sums[v, slot] = so_far[v, slot]
+
+    for_terms(z, plans, parts, spans, take)
+    add_terms(z, plans, sums, parts, spans)
+    for wait in (False, True):
+        used = []
+
+        def put(slot, blocks):
+            for v in range(z.batch):
+                copy = pltpu.make_async_copy(
+                    sums.at[v, slot], image.at[v, slot], sem.at[len(used), v]
+                )
+                if wait:
+                    copy.wait()
+                else:
+                    copy.start()
+            used.append(slot)
+
+        for_terms(z, plans, parts, spans, put)
+
+
+def make_image(z, plans, so_far, image, parts, spans):
     flat = [ref for piece in parts for ref in piece]
+    count = z.env * sum(span[1] for span in spans)
     return pl.pallas_call(
         functools.partial(image_body, z, spans),
         out_shape=[
-            jax.ShapeDtypeStruct(so_far.shape, jnp.float32),
+            pltpu.HBM(image.shape, jnp.float32),
             jax.ShapeDtypeStruct((8, 128), jnp.float32),
         ],
-        in_specs=[SMEM] * z.env + [VMEM] * (1 + len(flat)),
-        out_specs=[VMEM, VMEM],
+        in_specs=[SMEM] * z.env + [VMEM] * (1 + len(flat)) + [HBM],
+        out_specs=[HBM, VMEM],
+        input_output_aliases={z.env + 1 + len(flat): 0},
+        scratch_shapes=[
+            pltpu.VMEM(image.shape, jnp.float32),
+            pltpu.SemaphoreType.DMA((count, z.batch)),
+        ],
         compiler_params=pltpu.CompilerParams(vmem_limit_bytes=LIMIT),
         cost_estimate=BRIEF,
-    )(*plans, so_far, *flat)
+    )(*plans, so_far, *flat, image)
 
 
 def in_order(parts, places, count):
@@ -409,7 +450,7 @@
     if count > 1:
         places = [lax.rem(me + z.sector - step, z.sector) for step in range(count)]
         total = in_order(parts, places, count)
-    out[...] = total * scale
+    out[...] = total[:, : out.shape[1]] * scale
 
 
 def mean_over_sectors(z, array, entries, after):
@@ -420,13 +461,13 @@
         held = [total_over(array, "sector")]
     made = pl.pallas_call(
         functools.partial(mean_body, z, len(held), 1.0 / entries),
-        out_shape=jax.ShapeDtypeStruct((1, z.order), jnp.float32),
+        out_shape=jax.ShapeDtypeStruct((1, z.batch), jnp.float32),
         in_specs=[VMEM] * len(held) + [ANY] * len(after),
         out_specs=VMEM,
         compiler_params=pltpu.CompilerParams(vmem_limit_bytes=SMALL),
         cost_estimate=BRIEF,
     )(*held, *after)
-    return made[0, : z.batch]
+    return made.reshape(z.batch)
 
 
 def shift(array, axis, size, step):
@@ -457,10 +498,12 @@
     each = z.sector // 4
     span = z.capacity
 
-    def spans_of(g):
-        return [((g * each + d) * span, span, 0) for d in range(each)]
+    def spans_of(g, low=0, high=span):
+        return [((g * each + d) * span + low, high - low, low) for d in range(each)]
 
     chunks = {g: spans_of(g) for g in range(4)}
+    cut = 2 * span // 3
+    chunks[2], chunks[4] = spans_of(2, 0, cut), spans_of(2, cut, span)
 
     def around(array):
         return [array] + [shift(array, "rep", z.rep, s) for s in range(1, z.rep)]
@@ -483,7 +526,7 @@
     plans = [plan] + [plan_only(z, other) for other in partners]
 
     def near_products(g, after):
-        return products(z, plan, right, [near_rows], [c[:2] for c in chunks[g]], after)
+        return products(z, plan, right, [near_rows], [c[:2] for c in spans_of(g)], after)
 
     def far_products(g, after):
         return products(z, plan, right, vec[1:], [c[:2] for c in chunks[g]], after)
@@ -498,7 +541,7 @@
 
     def send_terms(g, so_far, own_sums, after):
         made, folded = terms(
-            z, plan, left, near[g], far[g], vec, chunks[g], so_far, own_sums, after
+            z, plan, left, near[2 if g == 4 else g], far[g], vec, chunks[g], so_far, own_sums, after
         )
         parts[g] = [
             [
@@ -515,21 +558,23 @@
     far1 = far_products(1, (made[0], *plans[1:]))
     far3 = far_products(3, far1[:1])
     far2 = far_products(2, far3[:1])
-    near[0] = near_products(0, far2[:1])
+    far4 = far_products(4, far2[:1])
+    near[0] = near_products(0, far4[:1])
     far[0] = far_products(0, near[0][:1])
     dots = send_terms(0, None, None, ())
-    made = gate([*far1, *far3], [dots, *sent])
-    far[1] = across(made[:each], 1)
-    far[3] = across(made[each:], 3)
-    made = gate(far2, far[1])
-    far[2] = across(made, 2)
-    dots = send_terms(1, dots, None, (*made, *arrived(0)))
-    dots = send_terms(3, dots, None, arrived(1))
+    far[1] = across(gate(far1, [dots, *sent]), 1)
+    far3 = gate(far3, [*far[1], *arrived(0)])
+    far[3] = across(far3, 3)
+    dots = send_terms(1, dots, None, far3[:1])
+    far2 = gate([*far2, *far4], far[3])
+    far[2], far[4] = across(far2[:each], 2), across(far2[each:], 2)
+    dots = send_terms(3, dots, None, (far2[0], *arrived(1)))
     own_block = vectors.astype(jnp.float32)
     own_sums = jnp.sum(energy[None, :, None, None] * own_block * own_block, axis=(1, 2, 3))
-    dots = send_terms(2, dots, own_sums, arrived(3))
-    early = (0, 1, 3)
-    so_far = gather_terms(
+    dots = send_terms(2, dots, None, arrived(3))
+    dots = send_terms(4, dots, own_sums, arrived(2))
+    early = (0, 1, 3, 2)
+    so_far, image = gather_terms(
         z,
         plans,
         energy,
@@ -538,8 +583,8 @@
         [chunks[g] for g in early],
         (dots,),
     )
-    sums = chip_sums(z, plan, dots, arrived(2), (so_far,))
-    image, token = make_image(z, plans, so_far, parts[2], chunks[2])
+    sums = chip_sums(z, plan, dots, arrived(4), (so_far,))
+    image, token = make_image(z, plans, so_far, image, parts[4], chunks[4])
     entries = z.slots * z.sector * z.order * z.order
     return (image, mean_over_sectors(z, sums, entries, (token,)))
 

time: 117 us -> 118 us (level)
  starting transfers between devices: 33.8 us -> 29.6 us
  waiting for transfers between devices: 58.7 us -> 61.9 us
  Pallas kernels: 20.5 us -> 23 us
    ppermute x14 -> x17, waiting for transfers between devices: 37.2 us -> 49.7 us  [shift_both(): return lax.ppermute(array, ('env', 'rep'), perm)]
    ppermute x13 -> x14, waiting for transfers between devices: 21.6 us -> 12.2 us  [shift(): lax.ppermute(array, axis, [(i, (i + step) % size) for i in range(size)])]
    ppermute x13 -> x14, starting transfers between devices: 24.3 us -> 18.3 us  [shift(): lax.ppermute(array, axis, [(i, (i + step) % size) for i in range(size)])]
    ppermute x14 -> x17, starting transfers between devices: 9.48 us -> 11.3 us  [shift_both(): return lax.ppermute(array, ('env', 'rep'), perm)]
    pallas_call x7 -> x8, Pallas kernels: 6.84 us -> 7.54 us  [products(): pl.pallas_call(functools.partial(products_body, z, pieces, spans), out_sh...]
    pallas_call x4 -> x5, Pallas kernels: 4.42 us -> 5.1 us  [terms(): pl.pallas_call(functools.partial(terms_body, z, spans, so_far is not None...]
  transfers between devices with their start and end apart: 27 -> 31, of which waited for: 10 -> 16; matrix products, arithmetic and copies ran while one was open for 1% -> 1% of each run, Pallas kernels for 16% -> 18%
where the time goes in v6:
time: 118 us; the launch traced here: 117 us
  waiting for transfers between devices  61.9 us (52%)
  starting transfers between devices  29.6 us (25%)
  Pallas kernels  23 us (19%)
    ppermute x17, waiting for transfers between devices, shift_both(): return lax.ppermute(array, ('env', 'rep'), perm)  49.7 us
    ppermute x14, starting transfers between devices, shift(): lax.ppermute(array, axis, [(i, (i + step) % size) for i in range(size)])  18.3 us
    ppermute x14, waiting for transfers between devices, shift(): lax.ppermute(array, axis, [(i, (i + step) % size) for i in range(size)])  12.2 us
    ppermute x17, starting transfers between devices, shift_both(): return lax.ppermute(array, ('env', 'rep'), perm)  11.3 us
    pallas_call x8, Pallas kernels, products(): pl.pallas_call(functools.partial(products_body, z, pieces, spans), out_sh...  7.54 us
    pallas_call x5, Pallas kernels, terms(): pl.pallas_call(functools.partial(terms_body, z, spans, so_far is not None...  5.1 us
    pallas_call x1, Pallas kernels, load(): pl.pallas_call(functools.partial(load_body, z), out_shape=[jax.ShapeDtype...  3.24 us
    pallas_call x1, Pallas kernels, gather_terms(): pl.pallas_call(functools.partial(gather_body, z, chunks), out_shape=[shap...  3.24 us
  transfers between devices with their start and end apart: 31, of which 16 were waited for; matrix products, arithmetic and copies ran while one was open for 1% of the time, Pallas kernels for 18%

profile of v6, /device:TPU:0, one launch (start us, length us, event | category | flops | bytes accessed | tf_op | source)
XLA Modules:
  0.0 117.4 jit_solution(12035407791380388672)
XLA Ops:
  0.6 0.5 collective-permute-start.2
  1.2 0.4 collective-permute-start.1
  1.7 2.6 %collective-permute-start = (s32[1,96]{1,0:T(1,128)}, s32[1,96]{1,0:T(1,128)S(1)}, u32[]{:S(2)}, u32[]{:S(2)}) collective-permute-start(s32[1,96]{1,0:T(1,128)} %partner.1), channel_id=1, source_target_pairs={{0,2},{2,0},{1,3},{3,1},{4,6},{6,4},{5,7},{7,5},{8,10},{10,8},{9,1... | collective-permute-start | bytes 1160 | tf_op jit(solution)/shard_map/ppermute | solution.py:474
  4.2 0.7 copy-done.3
  4.9 3.2 %shard_map.68 = (s32[74]{0:T(128)S(1)}, bf16[24,64,256]{2,1,0:T(8,128)(2,1)S(1)}, bf16[24,64,256]{2,1,0:T(8,128)(2,1)S(1)}, bf16[1,24,128,256]{3,2,1,0:T(8,128)(2,1)S(1)}) custom-call(s32[1,96]{1,0:T(1,128)S(1)} %copy-done.3, bf16[2,24,64,256]{3,2,1,0:T(8,128)(2,1)} %refs_3_.1, bf16[1,24,128,256]{3,2,1,0:T(8,128)(2,1)} %right.1), custom_call_target="tpu_custom_call" | custom-call | tf_op jit(solution)/shard_map/pallas_call | solution.py:99
  8.3 1.5 %collective-permute-start.5 = (bf16[24,64,256]{2,1,0:T(8,128)(2,1)S(1)}, bf16[24,64,256]{2,1,0:T(8,128)(2,1)S(1)}, u32[]{:S(2)}, u32[]{:S(2)}) collective-permute-start(bf16[24,64,256]{2,1,0:T(8,128)(2,1)S(1)} %get-tuple-element.46), channel_id=1, source_target_pairs={{0,3},{1,2},{2,1},{3,0},{4,7},{5,6},{6,5},{7,4},{8,11},{9,10},{10,... | collective-permute-start | bytes 2359304 | tf_op jit(solution)/shard_map/ppermute | solution.py:482
  9.8 1.2 %shard_map.71 = (bf16[6,128,256]{2,1,0:T(8,128)(2,1)S(1)}, bf16[6,128,256]{2,1,0:T(8,128)(2,1)S(1)}) custom-call(s32[74]{0:T(128)S(1)} %get-tuple-element.41.refs_0_.plan, bf16[1,24,128,256]{3,2,1,0:T(8,128)(2,1)S(1)} %get-tuple-element.42.refs_1_, bf16[1,24,128,256]{3,2,1,0:T(8,128)(2,1)S(1)} %collective-permute-done.2.refs_2_, ...), custom_call_target="tpu_custom_call" | custom-call | tf_op jit(solution)/shard_map/pallas_call | solution.py:183
  11.0 1.6 %collective-permute-start.9 = (bf16[6,128,256]{2,1,0:T(8,128)(2,1)S(1)}, bf16[6,128,256]{2,1,0:T(8,128)(2,1)S(1)}, u32[]{:S(2)}, u32[]{:S(2)}) collective-permute-start(bf16[6,128,256]{2,1,0:T(8,128)(2,1)S(1)} %get-tuple-element.47.refs_5_), channel_id=1, source_target_pairs={{0,4},{4,8},{8,12},{12,0},{1,5},{5,9},{9,13},{13,1},{2,6},{6,10},{... | collective-permute-start | bytes 1179656 | tf_op jit(solution)/shard_map/ppermute | solution.py:474
  12.6 0.9 shard_map.72.refs_5_
  13.6 2.7 %collective-permute-start.11 = (bf16[6,128,256]{2,1,0:T(8,128)(2,1)S(1)}, bf16[6,128,256]{2,1,0:T(8,128)(2,1)S(1)}, u32[]{:S(2)}, u32[]{:S(2)}) collective-permute-start(bf16[6,128,256]{2,1,0:T(8,128)(2,1)S(1)} %shard_map.72.refs_5_), channel_id=1, source_target_pairs={{0,8},{4,12},{8,0},{12,4},{1,9},{5,13},{9,1},{13,5},{2,10},{6,14},... | collective-permute-start | bytes 1179656 | tf_op jit(solution)/shard_map/ppermute | solution.py:474
  16.2 1.3 %collective-permute-start.10 = (bf16[6,128,256]{2,1,0:T(8,128)(2,1)S(1)}, bf16[6,128,256]{2,1,0:T(8,128)(2,1)S(1)}, u32[]{:S(2)}, u32[]{:S(2)}) collective-permute-start(bf16[6,128,256]{2,1,0:T(8,128)(2,1)S(1)} %get-tuple-element.53), channel_id=1, source_target_pairs={{0,12},{4,0},{8,4},{12,8},{1,13},{5,1},{9,5},{13,9},{2,14},{6,2},{... | collective-permute-start | bytes 1179656 | tf_op jit(solution)/shard_map/ppermute | solution.py:474
  17.6 1.3 %shard_map.69.refs_6_.refs_1_ = s32[74]{0:T(128)S(1)} custom-call(s32[1,96]{1,0:T(1,128)S(1)} %collective-permute-done.partner.refs_2_), custom_call_target="tpu_custom_call" | custom-call | tf_op jit(solution)/shard_map/pallas_call | solution.py:121
  18.9 9.8 %collective-permute-done.4.refs_3_.refs_7_ = bf16[24,64,256]{2,1,0:T(8,128)(2,1)S(1)} collective-permute-done((bf16[24,64,256]{2,1,0:T(8,128)(2,1)S(1)}, bf16[24,64,256]{2,1,0:T(8,128)(2,1)S(1)}, u32[]{:S(2)}, u32[]{:S(2)}) %collective-permute-start.4) | collective-permute-done | bytes 786464 | tf_op jit(solution)/shard_map/ppermute | solution.py:482
  28.6 15.3 %collective-permute-done.5.refs_4_.refs_8_ = bf16[24,64,256]{2,1,0:T(8,128)(2,1)S(1)} collective-permute-done((bf16[24,64,256]{2,1,0:T(8,128)(2,1)S(1)}, bf16[24,64,256]{2,1,0:T(8,128)(2,1)S(1)}, u32[]{:S(2)}, u32[]{:S(2)}) %collective-permute-start.5) | collective-permute-done | bytes 786464 | tf_op jit(solution)/shard_map/ppermute | solution.py:482
  43.9 0.9 shard_map.73.refs_5_.refs_0_
  44.9 0.9 shard_map.74.refs_5_.refs_0_
  45.8 0.9 shard_map.75.refs_5_.refs_0_
  46.7 0.8 shard_map.76.refs_5_.refs_1_
  47.5 0.9 shard_map.77.refs_5_.refs_3_
  48.4 0.9 shard_map.78.refs_4_
  49.4 0.5 copy-done
  49.8 1.1 shard_map.79
  51.0 1.6 %collective-permute-start.12 = (bf16[6,128,256]{2,1,0:T(8,128)(2,1)S(1)}, bf16[6,128,256]{2,1,0:T(8,128)(2,1)S(1)}, u32[]{:S(2)}, u32[]{:S(2)}) collective-permute-start(bf16[6,128,256]{2,1,0:T(8,128)(2,1)S(1)} %shard_map.80), channel_id=1, source_target_pairs={{0,4},{4,8},{8,12},{12,0},{1,5},{5,9},{9,13},{13,1},{2,6},{6,10},{... | collective-permute-start | bytes 1179656 | tf_op jit(solution)/shard_map/ppermute | solution.py:474
  52.6 0.6 collective-permute-start.6
  53.2 0.5 collective-permute-start.7
  53.7 0.8 collective-permute-start.8
  54.5 6.4 %collective-permute-done.7.refs_3_.refs_6_ = bf16[6,64,256]{2,1,0:T(8,128)(2,1)S(1)} collective-permute-done((bf16[6,64,256]{2,1,0:T(8,128)(2,1)S(1)}, bf16[6,64,256]{2,1,0:T(8,128)(2,1)S(1)}, u32[]{:S(2)}, u32[]{:S(2)}) %collective-permute-start.7) | collective-permute-done | bytes 196640 | tf_op jit(solution)/shard_map/ppermute | solution.py:482
  61.0 2.3 %collective-permute-done.8.refs_4_.refs_7_ = bf16[6,64,256]{2,1,0:T(8,128)(2,1)S(1)} collective-permute-done((bf16[6,64,256]{2,1,0:T(8,128)(2,1)S(1)}, bf16[6,64,256]{2,1,0:T(8,128)(2,1)S(1)}, u32[]{:S(2)}, u32[]{:S(2)}) %collective-permute-start.8) | collective-permute-done | bytes 196640 | tf_op jit(solution)/shard_map/ppermute | solution.py:482
  63.2 1.5 %collective-permute-done.12.refs_1_.refs_4_ = bf16[6,128,256]{2,1,0:T(8,128)(2,1)S(1)} collective-permute-done((bf16[6,128,256]{2,1,0:T(8,128)(2,1)S(1)}, bf16[6,128,256]{2,1,0:T(8,128)(2,1)S(1)}, u32[]{:S(2)}, u32[]{:S(2)}) %collective-permute-start.12) | collective-permute-done | bytes 393248 | tf_op jit(solution)/shard_map/ppermute | solution.py:474
  64.8 1.7 %collective-permute-start.16 = (bf16[6,128,256]{2,1,0:T(8,128)(2,1)S(1)}, bf16[6,128,256]{2,1,0:T(8,128)(2,1)S(1)}, u32[]{:S(2)}, u32[]{:S(2)}) collective-permute-start(bf16[6,128,256]{2,1,0:T(8,128)(2,1)S(1)} %shard_map.81.refs_10_), channel_id=1, source_target_pairs={{0,12},{4,0},{8,4},{12,8},{1,13},{5,1},{9,5},{13,9},{2,14},{6,2},{... | collective-permute-start | bytes 1179656 | tf_op jit(solution)/shard_map/ppermute | solution.py:474
  66.5 1.1 shard_map.82
  67.7 0.6 collective-permute-start.14
  68.3 1.2 %collective-permute-start.15 = (bf16[6,64,256]{2,1,0:T(8,128)(2,1)S(1)}, bf16[6,64,256]{2,1,0:T(8,128)(2,1)S(1)}, u32[]{:S(2)}, u32[]{:S(2)}) collective-permute-start(bf16[6,64,256]{2,1,0:T(8,128)(2,1)S(1)} %get-tuple-element.57), channel_id=1, source_target_pairs={{0,3},{1,2},{2,1},{3,0},{4,7},{5,6},{6,5},{7,4},{8,11},{9,10},{10,... | collective-permute-start | bytes 589832 | tf_op jit(solution)/shard_map/ppermute | solution.py:482
  69.5 6.4 %collective-permute-done.16.refs_2_.refs_4_ = bf16[6,128,256]{2,1,0:T(8,128)(2,1)S(1)} collective-permute-done((bf16[6,128,256]{2,1,0:T(8,128)(2,1)S(1)}, bf16[6,128,256]{2,1,0:T(8,128)(2,1)S(1)}, u32[]{:S(2)}, u32[]{:S(2)}) %collective-permute-start.16) | collective-permute-done | bytes 393248 | tf_op jit(solution)/shard_map/ppermute | solution.py:474
  75.9 1.8 %collective-permute-start.20 = (bf16[4,128,256]{2,1,0:T(8,128)(2,1)S(1)}, bf16[4,128,256]{2,1,0:T(8,128)(2,1)S(1)}, u32[]{:S(2)}, u32[]{:S(2)}) collective-permute-start(bf16[4,128,256]{2,1,0:T(8,128)(2,1)S(1)} %get-tuple-element.59.refs_10_), channel_id=1, source_target_pairs={{0,8},{4,12},{8,0},{12,4},{1,9},{5,13},{9,1},{13,5},{2,10},{6,14},... | collective-permute-start | bytes 786440 | tf_op jit(solution)/shard_map/ppermute | solution.py:474
  77.7 1.1 collective-permute-done.15.refs_13_.refs_11_
  78.7 1.1 shard_map.84
  79.8 0.3 collective-permute-start.17
  80.2 0.6 collective-permute-start.18
  80.7 1.0 collective-permute-start.19
  81.7 0.1 collective-permute-start.24
  81.9 6.0 %collective-permute-done.18.refs_11_.refs_14_ = bf16[6,64,256]{2,1,0:T(8,128)(2,1)S(1)} collective-permute-done((bf16[6,64,256]{2,1,0:T(8,128)(2,1)S(1)}, bf16[6,64,256]{2,1,0:T(8,128)(2,1)S(1)}, u32[]{:S(2)}, u32[]{:S(2)}) %collective-permute-start.18) | collective-permute-done | bytes 196640 | tf_op jit(solution)/shard_map/ppermute | solution.py:482
  87.9 2.8 %collective-permute-done.19.refs_12_.refs_15_ = bf16[6,64,256]{2,1,0:T(8,128)(2,1)S(1)} collective-permute-done((bf16[6,64,256]{2,1,0:T(8,128)(2,1)S(1)}, bf16[6,64,256]{2,1,0:T(8,128)(2,1)S(1)}, u32[]{:S(2)}, u32[]{:S(2)}) %collective-permute-start.19) | collective-permute-done | bytes 196640 | tf_op jit(solution)/shard_map/ppermute | solution.py:482
  90.7 3.1 %collective-permute-done.20.refs_4_ = bf16[4,128,256]{2,1,0:T(8,128)(2,1)S(1)} collective-permute-done((bf16[4,128,256]{2,1,0:T(8,128)(2,1)S(1)}, bf16[4,128,256]{2,1,0:T(8,128)(2,1)S(1)}, u32[]{:S(2)}, u32[]{:S(2)}) %collective-permute-start.20) | collective-permute-done | bytes 262176 | tf_op jit(solution)/shard_map/ppermute | solution.py:474
  93.8 0.9 shard_map.85
  94.8 0.6 collective-permute-start.22
  95.4 1.3 %collective-permute-start.23 = (bf16[4,64,256]{2,1,0:T(8,128)(2,1)S(1)}, bf16[4,64,256]{2,1,0:T(8,128)(2,1)S(1)}, u32[]{:S(2)}, u32[]{:S(2)}) collective-permute-start(bf16[4,64,256]{2,1,0:T(8,128)(2,1)S(1)} %get-tuple-element.68), channel_id=1, source_target_pairs={{0,3},{1,2},{2,1},{3,0},{4,7},{5,6},{6,5},{7,4},{8,11},{9,10},{10,... | collective-permute-start | bytes 393224 | tf_op jit(solution)/shard_map/ppermute | solution.py:482
  96.7 0.9 fusion.refs_10_
  97.6 3.6 %collective-permute-done.22.refs_12_.refs_18_ = bf16[4,64,256]{2,1,0:T(8,128)(2,1)S(1)} collective-permute-done((bf16[4,64,256]{2,1,0:T(8,128)(2,1)S(1)}, bf16[4,64,256]{2,1,0:T(8,128)(2,1)S(1)}, u32[]{:S(2)}, u32[]{:S(2)}) %collective-permute-start.22) | collective-permute-done | bytes 131104 | tf_op jit(solution)/shard_map/ppermute | solution.py:482
  101.2 1.9 %collective-permute-done.23.refs_13_.refs_19_ = bf16[4,64,256]{2,1,0:T(8,128)(2,1)S(1)} collective-permute-done((bf16[4,64,256]{2,1,0:T(8,128)(2,1)S(1)}, bf16[4,64,256]{2,1,0:T(8,128)(2,1)S(1)}, u32[]{:S(2)}, u32[]{:S(2)}) %collective-permute-start.23) | collective-permute-done | bytes 131104 | tf_op jit(solution)/shard_map/ppermute | solution.py:482
  103.1 1.0 shard_map.86
  104.1 0.3 collective-permute-start.25
  104.4 0.6 collective-permute-start.26
  105.0 1.0 collective-permute-start.27
  106.0 3.2 %shard_map.87 = (f32[2,24,64,256]{3,2,1,0:T(8,128)S(1)}, f32[2,24,64,256]{3,2,1,0:T(8,128)}) custom-call(s32[74]{0:T(128)S(1)} %get-tuple-element.41.refs_0_.plan, s32[74]{0:T(128)S(1)} %shard_map.69.refs_6_.refs_1_, f32[24]{0:T(128)S(1)} %copy-done.2, bf16[2,24,64,256]{3,2,1,0:T(8,128)(2,1)S(1)} %copy-done.1, ...), custom_call_target="tpu_custom_call" | custom-call | tf_op jit(solution)/shard_map/pallas_call | solution.py:348
  109.3 0.3 collective-permute-done.26.refs_5_.refs_1_
  109.5 0.2 collective-permute-done.27.refs_6_.refs_2_
  109.7 0.6 shard_map.89.refs_0_
  110.4 2.9 %collective-permute-start.29 = (f32[8,256]{1,0:T(8,128)S(1)}, f32[8,256]{1,0:T(8,128)S(1)}, u32[]{:S(2)}, u32[]{:S(2)}) collective-permute-start(f32[8,256]{1,0:T(8,128)S(1)} %shard_map.89.refs_0_), channel_id=1, source_target_pairs={{0,8},{4,12},{8,0},{12,4},{1,9},{5,13},{9,1},{13,5},{2,10},{6,14},... | collective-permute-start | bytes 24584 | tf_op jit(solution)/shard_map/ppermute | solution.py:474
  113.2 1.0 collective-permute-start.30
  114.2 1.5 %shard_map.88 = (f32[2,24,64,256]{3,2,1,0:T(8,128)}, f32[8,128]{1,0:T(8,128)S(1)}) custom-call(s32[74]{0:T(128)S(1)} %get-tuple-element.41.refs_0_.plan, s32[74]{0:T(128)S(1)} %shard_map.69.refs_6_.refs_1_, f32[2,24,64,256]{3,2,1,0:T(8,128)S(1)} %get-tuple-element.72.refs_2_.refs_3_, ...), custom_call_target="tpu_custom_call", output_to_operand_aliasing={{0}: (7, {})} | custom-call | tf_op jit(solution)/shard_map/pallas_call | solution.py:393
  115.7 0.1 collective-permute-done.28.refs_1_
  115.8 1.1 collective-permute-done.30.refs_3_
  116.9 0.5 shard_map.90
  (30 shorter events, 0.4 us)
Async XLA Ops:
  0.6 9.1 %collective-permute-start.2 = (bf16[1,24,128,256]{3,2,1,0:T(8,128)(2,1)}, bf16[1,24,128,256]{3,2,1,0:T(8,128)(2,1)S(1)}, u32[]{:S(2)}, u32[]{:S(2)}) collective-permute-start(bf16[1,24,128,256]{3,2,1,0:T(8,128)(2,1)} %right.1), channel_id=1, source_target_pairs={{0,1},{1,0},{2,3},{3,2},{4,5},{5,4},{6,7},{7,6},{8,9},{9,8},{10,11... | collective-permute-start | bytes 4718600 | tf_op jit(solution)/shard_map/ppermute | solution.py:474
  1.1 8.6 %collective-permute-start.3 = (bf16[2,24,64,256]{3,2,1,0:T(8,128)(2,1)}, bf16[2,24,64,256]{3,2,1,0:T(8,128)(2,1)S(1)}, u32[]{:S(2)}, u32[]{:S(2)}) collective-permute-start(bf16[2,24,64,256]{3,2,1,0:T(8,128)(2,1)} %refs_3_.1), channel_id=1, source_target_pairs={{0,1},{1,0},{2,3},{3,2},{4,5},{5,4},{6,7},{7,6},{8,9},{9,8},{10,11... | collective-permute-start | bytes 4718600 | tf_op jit(solution)/shard_map/ppermute | solution.py:474
  1.2 11.4 %collective-permute-start.1 = (bf16[1,24,128,256]{3,2,1,0:T(8,128)(2,1)}, bf16[1,24,128,256]{3,2,1,0:T(8,128)(2,1)S(1)}, u32[]{:S(2)}, u32[]{:S(2)}) collective-permute-start(bf16[1,24,128,256]{3,2,1,0:T(8,128)(2,1)} %refs_1_.9), channel_id=1, source_target_pairs={{0,1},{1,0},{2,3},{3,2},{4,5},{5,4},{6,7},{7,6},{8,9},{9,8},{10,11... | collective-permute-start | bytes 4718600 | tf_op jit(solution)/shard_map/ppermute | solution.py:474
  1.7 6.5 %collective-permute-start = (s32[1,96]{1,0:T(1,128)}, s32[1,96]{1,0:T(1,128)S(1)}, u32[]{:S(2)}, u32[]{:S(2)}) collective-permute-start(s32[1,96]{1,0:T(1,128)} %partner.1), channel_id=1, source_target_pairs={{0,2},{2,0},{1,3},{3,1},{4,6},{6,4},{5,7},{7,5},{8,10},{10,8},{9,1... | collective-permute-start | bytes 1160 | tf_op jit(solution)/shard_map/ppermute | solution.py:474
  4.2 0.7 copy-start.3
  8.2 20.5 %collective-permute-start.4 = (bf16[24,64,256]{2,1,0:T(8,128)(2,1)S(1)}, bf16[24,64,256]{2,1,0:T(8,128)(2,1)S(1)}, u32[]{:S(2)}, u32[]{:S(2)}) collective-permute-start(bf16[24,64,256]{2,1,0:T(8,128)(2,1)S(1)} %get-tuple-element.45.refs_3_.refs_5_), channel_id=1, source_target_pairs={{0,2},{1,3},{2,0},{3,1},{4,6},{5,7},{6,4},{7,5},{8,10},{9,11},{10,... | collective-permute-start | bytes 2359304 | tf_op jit(solution)/shard_map/ppermute | solution.py:482
  8.3 35.7 %collective-permute-start.5 = (bf16[24,64,256]{2,1,0:T(8,128)(2,1)S(1)}, bf16[24,64,256]{2,1,0:T(8,128)(2,1)S(1)}, u32[]{:S(2)}, u32[]{:S(2)}) collective-permute-start(bf16[24,64,256]{2,1,0:T(8,128)(2,1)S(1)} %get-tuple-element.46), channel_id=1, source_target_pairs={{0,3},{1,2},{2,1},{3,0},{4,7},{5,6},{6,5},{7,4},{8,11},{9,10},{10,... | collective-permute-start | bytes 2359304 | tf_op jit(solution)/shard_map/ppermute | solution.py:482
  11.0 39.9 %collective-permute-start.9 = (bf16[6,128,256]{2,1,0:T(8,128)(2,1)S(1)}, bf16[6,128,256]{2,1,0:T(8,128)(2,1)S(1)}, u32[]{:S(2)}, u32[]{:S(2)}) collective-permute-start(bf16[6,128,256]{2,1,0:T(8,128)(2,1)S(1)} %get-tuple-element.47.refs_5_), channel_id=1, source_target_pairs={{0,4},{4,8},{8,12},{12,0},{1,5},{5,9},{9,13},{13,1},{2,6},{6,10},{... | collective-permute-start | bytes 1179656 | tf_op jit(solution)/shard_map/ppermute | solution.py:474
  13.6 37.3 %collective-permute-start.11 = (bf16[6,128,256]{2,1,0:T(8,128)(2,1)S(1)}, bf16[6,128,256]{2,1,0:T(8,128)(2,1)S(1)}, u32[]{:S(2)}, u32[]{:S(2)}) collective-permute-start(bf16[6,128,256]{2,1,0:T(8,128)(2,1)S(1)} %shard_map.72.refs_5_), channel_id=1, source_target_pairs={{0,8},{4,12},{8,0},{12,4},{1,9},{5,13},{9,1},{13,5},{2,10},{6,14},... | collective-permute-start | bytes 1179656 | tf_op jit(solution)/shard_map/ppermute | solution.py:474
  16.2 34.7 %collective-permute-start.10 = (bf16[6,128,256]{2,1,0:T(8,128)(2,1)S(1)}, bf16[6,128,256]{2,1,0:T(8,128)(2,1)S(1)}, u32[]{:S(2)}, u32[]{:S(2)}) collective-permute-start(bf16[6,128,256]{2,1,0:T(8,128)(2,1)S(1)} %get-tuple-element.53), channel_id=1, source_target_pairs={{0,12},{4,0},{8,4},{12,8},{1,13},{5,1},{9,5},{13,9},{2,14},{6,2},{... | collective-permute-start | bytes 1179656 | tf_op jit(solution)/shard_map/ppermute | solution.py:474
  48.4 1.4 %copy-start = (bf16[1,24,128,256]{3,2,1,0:T(8,128)(2,1)S(1)}, bf16[1,24,128,256]{3,2,1,0:T(8,128)(2,1)}, u32[]{:S(2)}) copy-start(bf16[1,24,128,256]{3,2,1,0:T(8,128)(2,1)} %refs_1_.9) | copy-start | bytes 4718596
  51.0 13.8 %collective-permute-start.12 = (bf16[6,128,256]{2,1,0:T(8,128)(2,1)S(1)}, bf16[6,128,256]{2,1,0:T(8,128)(2,1)S(1)}, u32[]{:S(2)}, u32[]{:S(2)}) collective-permute-start(bf16[6,128,256]{2,1,0:T(8,128)(2,1)S(1)} %shard_map.80), channel_id=1, source_target_pairs={{0,4},{4,8},{8,12},{12,0},{1,5},{5,9},{9,13},{13,1},{2,6},{6,10},{... | collective-permute-start | bytes 1179656 | tf_op jit(solution)/shard_map/ppermute | solution.py:474
  52.6 2.0 %collective-permute-start.6 = (bf16[6,64,256]{2,1,0:T(8,128)(2,1)S(1)}, bf16[6,64,256]{2,1,0:T(8,128)(2,1)S(1)}, u32[]{:S(2)}, u32[]{:S(2)}) collective-permute-start(bf16[6,64,256]{2,1,0:T(8,128)(2,1)S(1)} %get-tuple-element.49), channel_id=1, source_target_pairs={{0,1},{1,0},{2,3},{3,2},{4,5},{5,4},{6,7},{7,6},{8,9},{9,8},{10,11... | collective-permute-start | bytes 589832 | tf_op jit(solution)/shard_map/ppermute | solution.py:482
  53.2 7.8 %collective-permute-start.7 = (bf16[6,64,256]{2,1,0:T(8,128)(2,1)S(1)}, bf16[6,64,256]{2,1,0:T(8,128)(2,1)S(1)}, u32[]{:S(2)}, u32[]{:S(2)}) collective-permute-start(bf16[6,64,256]{2,1,0:T(8,128)(2,1)S(1)} %get-tuple-element.50), channel_id=1, source_target_pairs={{0,2},{1,3},{2,0},{3,1},{4,6},{5,7},{6,4},{7,5},{8,10},{9,11},{10,... | collective-permute-start | bytes 589832 | tf_op jit(solution)/shard_map/ppermute | solution.py:482
  53.7 9.5 %collective-permute-start.8 = (bf16[6,64,256]{2,1,0:T(8,128)(2,1)S(1)}, bf16[6,64,256]{2,1,0:T(8,128)(2,1)S(1)}, u32[]{:S(2)}, u32[]{:S(2)}) collective-permute-start(bf16[6,64,256]{2,1,0:T(8,128)(2,1)S(1)} %get-tuple-element.51), channel_id=1, source_target_pairs={{0,3},{1,2},{2,1},{3,0},{4,7},{5,6},{6,5},{7,4},{8,11},{9,10},{10,... | collective-permute-start | bytes 589832 | tf_op jit(solution)/shard_map/ppermute | solution.py:482
  64.8 11.1 %collective-permute-start.16 = (bf16[6,128,256]{2,1,0:T(8,128)(2,1)S(1)}, bf16[6,128,256]{2,1,0:T(8,128)(2,1)S(1)}, u32[]{:S(2)}, u32[]{:S(2)}) collective-permute-start(bf16[6,128,256]{2,1,0:T(8,128)(2,1)S(1)} %shard_map.81.refs_10_), channel_id=1, source_target_pairs={{0,12},{4,0},{8,4},{12,8},{1,13},{5,1},{9,5},{13,9},{2,14},{6,2},{... | collective-permute-start | bytes 1179656 | tf_op jit(solution)/shard_map/ppermute | solution.py:474
  67.6 10.1 %collective-permute-start.13 = (bf16[6,64,256]{2,1,0:T(8,128)(2,1)S(1)}, bf16[6,64,256]{2,1,0:T(8,128)(2,1)S(1)}, u32[]{:S(2)}, u32[]{:S(2)}) collective-permute-start(bf16[6,64,256]{2,1,0:T(8,128)(2,1)S(1)} %get-tuple-element.55), channel_id=1, source_target_pairs={{0,1},{1,0},{2,3},{3,2},{4,5},{5,4},{6,7},{7,6},{8,9},{9,8},{10,11... | collective-permute-start | bytes 589832 | tf_op jit(solution)/shard_map/ppermute | solution.py:482
  67.7 10.0 %collective-permute-start.14 = (bf16[6,64,256]{2,1,0:T(8,128)(2,1)S(1)}, bf16[6,64,256]{2,1,0:T(8,128)(2,1)S(1)}, u32[]{:S(2)}, u32[]{:S(2)}) collective-permute-start(bf16[6,64,256]{2,1,0:T(8,128)(2,1)S(1)} %get-tuple-element.56), channel_id=1, source_target_pairs={{0,2},{1,3},{2,0},{3,1},{4,6},{5,7},{6,4},{7,5},{8,10},{9,11},{10,... | collective-permute-start | bytes 589832 | tf_op jit(solution)/shard_map/ppermute | solution.py:482
  68.3 10.5 %collective-permute-start.15 = (bf16[6,64,256]{2,1,0:T(8,128)(2,1)S(1)}, bf16[6,64,256]{2,1,0:T(8,128)(2,1)S(1)}, u32[]{:S(2)}, u32[]{:S(2)}) collective-permute-start(bf16[6,64,256]{2,1,0:T(8,128)(2,1)S(1)} %get-tuple-element.57), channel_id=1, source_target_pairs={{0,3},{1,2},{2,1},{3,0},{4,7},{5,6},{6,5},{7,4},{8,11},{9,10},{10,... | collective-permute-start | bytes 589832 | tf_op jit(solution)/shard_map/ppermute | solution.py:482
  75.9 17.9 %collective-permute-start.20 = (bf16[4,128,256]{2,1,0:T(8,128)(2,1)S(1)}, bf16[4,128,256]{2,1,0:T(8,128)(2,1)S(1)}, u32[]{:S(2)}, u32[]{:S(2)}) collective-permute-start(bf16[4,128,256]{2,1,0:T(8,128)(2,1)S(1)} %get-tuple-element.59.refs_10_), channel_id=1, source_target_pairs={{0,8},{4,12},{8,0},{12,4},{1,9},{5,13},{9,1},{13,5},{2,10},{6,14},... | collective-permute-start | bytes 786440 | tf_op jit(solution)/shard_map/ppermute | solution.py:474
  79.8 2.1 %collective-permute-start.17 = (bf16[6,64,256]{2,1,0:T(8,128)(2,1)S(1)}, bf16[6,64,256]{2,1,0:T(8,128)(2,1)S(1)}, u32[]{:S(2)}, u32[]{:S(2)}) collective-permute-start(bf16[6,64,256]{2,1,0:T(8,128)(2,1)S(1)} %get-tuple-element.61), channel_id=1, source_target_pairs={{0,1},{1,0},{2,3},{3,2},{4,5},{5,4},{6,7},{7,6},{8,9},{9,8},{10,11... | collective-permute-start | bytes 589832 | tf_op jit(solution)/shard_map/ppermute | solution.py:482
  80.2 7.7 %collective-permute-start.18 = (bf16[6,64,256]{2,1,0:T(8,128)(2,1)S(1)}, bf16[6,64,256]{2,1,0:T(8,128)(2,1)S(1)}, u32[]{:S(2)}, u32[]{:S(2)}) collective-permute-start(bf16[6,64,256]{2,1,0:T(8,128)(2,1)S(1)} %get-tuple-element.62), channel_id=1, source_target_pairs={{0,2},{1,3},{2,0},{3,1},{4,6},{5,7},{6,4},{7,5},{8,10},{9,11},{10,... | collective-permute-start | bytes 589832 | tf_op jit(solution)/shard_map/ppermute | solution.py:482
  80.7 10.0 %collective-permute-start.19 = (bf16[6,64,256]{2,1,0:T(8,128)(2,1)S(1)}, bf16[6,64,256]{2,1,0:T(8,128)(2,1)S(1)}, u32[]{:S(2)}, u32[]{:S(2)}) collective-permute-start(bf16[6,64,256]{2,1,0:T(8,128)(2,1)S(1)} %get-tuple-element.63), channel_id=1, source_target_pairs={{0,3},{1,2},{2,1},{3,0},{4,7},{5,6},{6,5},{7,4},{8,11},{9,10},{10,... | collective-permute-start | bytes 589832 | tf_op jit(solution)/shard_map/ppermute | solution.py:482
  81.7 15.8 %collective-permute-start.24 = (bf16[2,128,256]{2,1,0:T(8,128)(2,1)S(1)}, bf16[2,128,256]{2,1,0:T(8,128)(2,1)S(1)}, u32[]{:S(2)}, u32[]{:S(2)}) collective-permute-start(bf16[2,128,256]{2,1,0:T(8,128)(2,1)S(1)} %get-tuple-element.69), channel_id=1, source_target_pairs={{0,8},{4,12},{8,0},{12,4},{1,9},{5,13},{9,1},{13,5},{2,10},{6,14},... | collective-permute-start | bytes 393224 | tf_op jit(solution)/shard_map/ppermute | solution.py:474
  93.8 2.9 %copy-start.1 = (bf16[2,24,64,256]{3,2,1,0:T(8,128)(2,1)S(1)}, bf16[2,24,64,256]{3,2,1,0:T(8,128)(2,1)}, u32[]{:S(2)}) copy-start(bf16[2,24,64,256]{3,2,1,0:T(8,128)(2,1)} %refs_3_.1) | copy-start | bytes 4718596
  93.8 2.9 %copy-start.2 = (f32[24]{0:T(128)S(1)}, f32[24]{0:T(128)}, u32[]{:S(2)}) copy-start(f32[24]{0:T(128)} %refs_2_.1) | copy-start | bytes 292
  94.7 2.8 %collective-permute-start.21 = (bf16[4,64,256]{2,1,0:T(8,128)(2,1)S(1)}, bf16[4,64,256]{2,1,0:T(8,128)(2,1)S(1)}, u32[]{:S(2)}, u32[]{:S(2)}) collective-permute-start(bf16[4,64,256]{2,1,0:T(8,128)(2,1)S(1)} %get-tuple-element.66), channel_id=1, source_target_pairs={{0,1},{1,0},{2,3},{3,2},{4,5},{5,4},{6,7},{7,6},{8,9},{9,8},{10,11... | collective-permute-start | bytes 393224 | tf_op jit(solution)/shard_map/ppermute | solution.py:482
  94.8 6.4 %collective-permute-start.22 = (bf16[4,64,256]{2,1,0:T(8,128)(2,1)S(1)}, bf16[4,64,256]{2,1,0:T(8,128)(2,1)S(1)}, u32[]{:S(2)}, u32[]{:S(2)}) collective-permute-start(bf16[4,64,256]{2,1,0:T(8,128)(2,1)S(1)} %get-tuple-element.67), channel_id=1, source_target_pairs={{0,2},{1,3},{2,0},{3,1},{4,6},{5,7},{6,4},{7,5},{8,10},{9,11},{10,... | collective-permute-start | bytes 393224 | tf_op jit(solution)/shard_map/ppermute | solution.py:482
  95.4 7.7 %collective-permute-start.23 = (bf16[4,64,256]{2,1,0:T(8,128)(2,1)S(1)}, bf16[4,64,256]{2,1,0:T(8,128)(2,1)S(1)}, u32[]{:S(2)}, u32[]{:S(2)}) collective-permute-start(bf16[4,64,256]{2,1,0:T(8,128)(2,1)S(1)} %get-tuple-element.68), channel_id=1, source_target_pairs={{0,3},{1,2},{2,1},{3,0},{4,7},{5,6},{6,5},{7,4},{8,11},{9,10},{10,... | collective-permute-start | bytes 393224 | tf_op jit(solution)/shard_map/ppermute | solution.py:482
  104.1 5.2 %collective-permute-start.25 = (bf16[144,256]{1,0:T(8,128)(2,1)S(1)}, bf16[144,256]{1,0:T(8,128)(2,1)S(1)}, u32[]{:S(2)}, u32[]{:S(2)}) collective-permute-start(bf16[144,256]{1,0:T(8,128)(2,1)S(1)} %get-tuple-element.74), channel_id=1, source_target_pairs={{0,1},{1,0},{2,3},{3,2},{4,5},{5,4},{6,7},{7,6},{8,9},{9,8},{10,11... | collective-permute-start | bytes 221192 | tf_op jit(solution)/shard_map/ppermute | solution.py:482
  104.4 5.1 %collective-permute-start.26 = (bf16[144,256]{1,0:T(8,128)(2,1)S(1)}, bf16[144,256]{1,0:T(8,128)(2,1)S(1)}, u32[]{:S(2)}, u32[]{:S(2)}) collective-permute-start(bf16[144,256]{1,0:T(8,128)(2,1)S(1)} %get-tuple-element.75), channel_id=1, source_target_pairs={{0,2},{1,3},{2,0},{3,1},{4,6},{5,7},{6,4},{7,5},{8,10},{9,11},{10,... | collective-permute-start | bytes 221192 | tf_op jit(solution)/shard_map/ppermute | solution.py:482
  105.0 4.7 %collective-permute-start.27 = (bf16[144,256]{1,0:T(8,128)(2,1)S(1)}, bf16[144,256]{1,0:T(8,128)(2,1)S(1)}, u32[]{:S(2)}, u32[]{:S(2)}) collective-permute-start(bf16[144,256]{1,0:T(8,128)(2,1)S(1)} %get-tuple-element.76), channel_id=1, source_target_pairs={{0,3},{1,2},{2,1},{3,0},{4,7},{5,6},{6,5},{7,4},{8,11},{9,10},{10,... | collective-permute-start | bytes 221192 | tf_op jit(solution)/shard_map/ppermute | solution.py:482
  110.3 5.5 %collective-permute-start.28 = (f32[8,256]{1,0:T(8,128)S(1)}, f32[8,256]{1,0:T(8,128)S(1)}, u32[]{:S(2)}, u32[]{:S(2)}) collective-permute-start(f32[8,256]{1,0:T(8,128)S(1)} %shard_map.89.refs_0_), channel_id=1, source_target_pairs={{0,4},{4,8},{8,12},{12,0},{1,5},{5,9},{9,13},{13,1},{2,6},{6,10},{... | collective-permute-start | bytes 24584 | tf_op jit(solution)/shard_map/ppermute | solution.py:474
  110.4 5.4 %collective-permute-start.29 = (f32[8,256]{1,0:T(8,128)S(1)}, f32[8,256]{1,0:T(8,128)S(1)}, u32[]{:S(2)}, u32[]{:S(2)}) collective-permute-start(f32[8,256]{1,0:T(8,128)S(1)} %shard_map.89.refs_0_), channel_id=1, source_target_pairs={{0,8},{4,12},{8,0},{12,4},{1,9},{5,13},{9,1},{13,5},{2,10},{6,14},... | collective-permute-start | bytes 24584 | tf_op jit(solution)/shard_map/ppermute | solution.py:474
  113.2 3.7 %collective-permute-start.30 = (f32[8,256]{1,0:T(8,128)S(1)}, f32[8,256]{1,0:T(8,128)S(1)}, u32[]{:S(2)}, u32[]{:S(2)}) collective-permute-start(f32[8,256]{1,0:T(8,128)S(1)} %shard_map.89.refs_0_), channel_id=1, source_target_pairs={{0,12},{4,0},{8,4},{12,8},{1,13},{5,1},{9,5},{13,9},{2,14},{6,2},{... | collective-permute-start | bytes 24584 | tf_op jit(solution)/shard_map/ppermute | solution.py:474

commit v7 on v6

--- a/solution.py
+++ b/solution.py
@@ -537,7 +537,6 @@
     near[1], near[3] = across(made[:each], 1), across(made[each:], 3)
     made = near_products(2, (made[0], *left[1:]))
     near[2] = across(made, 2)
-    sent = [array for g in (1, 3, 2) for array in near[g]]
 
     def send_terms(g, so_far, own_sums, after):
         made, folded = terms(
@@ -556,19 +555,20 @@
         return [part for piece in parts[g] for part in piece][1:]
 
     far1 = far_products(1, (made[0], *plans[1:]))
-    far3 = far_products(3, far1[:1])
+    far1 = gate(far1, [*near[1], *near[3]])
+    far[1] = across(far1, 1)
+    near[0] = near_products(0, far1[:1])
+    far[0] = far_products(0, near[0][:1])
+    dots = send_terms(0, None, None, ())
+    far3 = far_products(3, (dots,))
     far2 = far_products(2, far3[:1])
     far4 = far_products(4, far2[:1])
-    near[0] = near_products(0, far4[:1])
-    far[0] = far_products(0, near[0][:1])
-    dots = send_terms(0, None, None, ())
-    far[1] = across(gate(far1, [dots, *sent]), 1)
-    far3 = gate(far3, [*far[1], *arrived(0)])
+    far3 = gate(far3, [far4[0], *near[2]])
     far[3] = across(far3, 3)
-    dots = send_terms(1, dots, None, far3[:1])
-    far2 = gate([*far2, *far4], far[3])
+    far2 = gate([*far2, *far4], [far3[0], *far[1]])
     far[2], far[4] = across(far2[:each], 2), across(far2[each:], 2)
-    dots = send_terms(3, dots, None, (far2[0], *arrived(1)))
+    dots = send_terms(1, dots, None, (far2[0], *arrived(0)))
+    dots = send_terms(3, dots, None, arrived(1))
     own_block = vectors.astype(jnp.float32)
     own_sums = jnp.sum(energy[None, :, None, None] * own_block * own_block, axis=(1, 2, 3))
     dots = send_terms(2, dots, None, arrived(3))

time: 118 us -> 110 us (0.932)
  waiting for transfers between devices: 61.9 us -> 48.7 us
  starting transfers between devices: 29.6 us -> 35.1 us
    ppermute x14, waiting for transfers between devices: 12.2 us -> 2.01 us  [shift(): lax.ppermute(array, axis, [(i, (i + step) % size) for i in range(size)])]
    ppermute x14, starting transfers between devices: 18.3 us -> 22.6 us  [shift(): lax.ppermute(array, axis, [(i, (i + step) % size) for i in range(size)])]
    ppermute x17, waiting for transfers between devices: 49.7 us -> 46.7 us  [shift_both(): return lax.ppermute(array, ('env', 'rep'), perm)]
    ppermute x17, starting transfers between devices: 11.3 us -> 12.5 us  [shift_both(): return lax.ppermute(array, ('env', 'rep'), perm)]
  transfers between devices with their start and end apart: 31 -> 31, of which waited for: 16 -> 13; matrix products, arithmetic and copies ran while one was open for 1% -> 1% of each run, Pallas kernels for 18% -> 19%
where the time goes in v7:
time: 110 us
  waiting for transfers between devices  48.7 us (44%)
  starting transfers between devices  35.1 us (32%)
  Pallas kernels  23 us (21%)
  local copies, waits for them, and re-layouts  1.15 us (1%)
    ppermute x17, waiting for transfers between devices, shift_both(): return lax.ppermute(array, ('env', 'rep'), perm)  46.7 us
    ppermute x14, starting transfers between devices, shift(): lax.ppermute(array, axis, [(i, (i + step) % size) for i in range(size)])  22.6 us
    ppermute x17, starting transfers between devices, shift_both(): return lax.ppermute(array, ('env', 'rep'), perm)  12.5 us
    pallas_call x8, Pallas kernels, products(): pl.pallas_call(functools.partial(products_body, z, pieces, spans), out_sh...  7.52 us
    pallas_call x5, Pallas kernels, terms(): pl.pallas_call(functools.partial(terms_body, z, spans, so_far is not None...  5.1 us
    pallas_call x1, Pallas kernels, load(): pl.pallas_call(functools.partial(load_body, z), out_shape=[jax.ShapeDtype...  3.24 us
    pallas_call x1, Pallas kernels, gather_terms(): pl.pallas_call(functools.partial(gather_body, z, chunks), out_shape=[shap...  3.24 us
  transfers between devices with their start and end apart: 31, of which 13 were waited for; matrix products, arithmetic and copies ran while one was open for 1% of the time, Pallas kernels for 19%

profile of v7, /device:TPU:0, one launch (start us, length us, event | category | flops | bytes accessed | tf_op | source)
XLA Modules:
  0.0 109.7 jit_solution(16234232466297218162)
XLA Ops:
  0.6 0.5 collective-permute-start.2
  1.1 0.1 collective-permute-start.3
  1.2 0.4 collective-permute-start.1
  1.7 2.6 %collective-permute-start = (s32[1,96]{1,0:T(1,128)}, s32[1,96]{1,0:T(1,128)S(1)}, u32[]{:S(2)}, u32[]{:S(2)}) collective-permute-start(s32[1,96]{1,0:T(1,128)} %partner.1), channel_id=1, source_target_pairs={{0,2},{2,0},{1,3},{3,1},{4,6},{6,4},{5,7},{7,5},{8,10},{10,8},{9,1... | collective-permute-start | bytes 1160 | tf_op jit(solution)/shard_map/ppermute | solution.py:474
  4.2 0.7 copy-done.3
  4.9 3.2 %shard_map.68 = (s32[74]{0:T(128)S(1)}, bf16[24,64,256]{2,1,0:T(8,128)(2,1)S(1)}, bf16[24,64,256]{2,1,0:T(8,128)(2,1)S(1)}, bf16[1,24,128,256]{3,2,1,0:T(8,128)(2,1)S(1)}) custom-call(s32[1,96]{1,0:T(1,128)S(1)} %copy-done.3, bf16[2,24,64,256]{3,2,1,0:T(8,128)(2,1)} %refs_3_.1, bf16[1,24,128,256]{3,2,1,0:T(8,128)(2,1)} %right.1), custom_call_target="tpu_custom_call" | custom-call | tf_op jit(solution)/shard_map/pallas_call | solution.py:99
  8.3 1.5 %collective-permute-start.5 = (bf16[24,64,256]{2,1,0:T(8,128)(2,1)S(1)}, bf16[24,64,256]{2,1,0:T(8,128)(2,1)S(1)}, u32[]{:S(2)}, u32[]{:S(2)}) collective-permute-start(bf16[24,64,256]{2,1,0:T(8,128)(2,1)S(1)} %get-tuple-element.46), channel_id=1, source_target_pairs={{0,3},{1,2},{2,1},{3,0},{4,7},{5,6},{6,5},{7,4},{8,11},{9,10},{10,... | collective-permute-start | bytes 2359304 | tf_op jit(solution)/shard_map/ppermute | solution.py:482
  9.8 1.2 %shard_map.71 = (bf16[6,128,256]{2,1,0:T(8,128)(2,1)S(1)}, bf16[6,128,256]{2,1,0:T(8,128)(2,1)S(1)}) custom-call(s32[74]{0:T(128)S(1)} %get-tuple-element.41.refs_0_.plan, bf16[1,24,128,256]{3,2,1,0:T(8,128)(2,1)S(1)} %get-tuple-element.42.refs_1_, bf16[1,24,128,256]{3,2,1,0:T(8,128)(2,1)S(1)} %collective-permute-done.2.refs_2_, ...), custom_call_target="tpu_custom_call" | custom-call | tf_op jit(solution)/shard_map/pallas_call | solution.py:183
  11.0 1.6 %collective-permute-start.6 = (bf16[6,128,256]{2,1,0:T(8,128)(2,1)S(1)}, bf16[6,128,256]{2,1,0:T(8,128)(2,1)S(1)}, u32[]{:S(2)}, u32[]{:S(2)}) collective-permute-start(bf16[6,128,256]{2,1,0:T(8,128)(2,1)S(1)} %get-tuple-element.47.refs_5_), channel_id=1, source_target_pairs={{0,4},{4,8},{8,12},{12,0},{1,5},{5,9},{9,13},{13,1},{2,6},{6,10},{... | collective-permute-start | bytes 1179656 | tf_op jit(solution)/shard_map/ppermute | solution.py:474
  12.6 2.3 %collective-permute-start.7 = (bf16[6,128,256]{2,1,0:T(8,128)(2,1)S(1)}, bf16[6,128,256]{2,1,0:T(8,128)(2,1)S(1)}, u32[]{:S(2)}, u32[]{:S(2)}) collective-permute-start(bf16[6,128,256]{2,1,0:T(8,128)(2,1)S(1)} %get-tuple-element.48), channel_id=1, source_target_pairs={{0,12},{4,0},{8,4},{12,8},{1,13},{5,1},{9,5},{13,9},{2,14},{6,2},{... | collective-permute-start | bytes 1179656 | tf_op jit(solution)/shard_map/ppermute | solution.py:474
  14.9 0.9 shard_map.72.refs_5_
  15.8 0.9 collective-permute-start.12
  16.7 1.3 %shard_map.69.refs_6_.refs_1_ = s32[74]{0:T(128)S(1)} custom-call(s32[1,96]{1,0:T(1,128)S(1)} %collective-permute-done.partner.refs_2_), custom_call_target="tpu_custom_call" | custom-call | tf_op jit(solution)/shard_map/pallas_call | solution.py:121
  18.0 10.7 %collective-permute-done.4.refs_3_.refs_7_ = bf16[24,64,256]{2,1,0:T(8,128)(2,1)S(1)} collective-permute-done((bf16[24,64,256]{2,1,0:T(8,128)(2,1)S(1)}, bf16[24,64,256]{2,1,0:T(8,128)(2,1)S(1)}, u32[]{:S(2)}, u32[]{:S(2)}) %collective-permute-start.4) | collective-permute-done | bytes 786464 | tf_op jit(solution)/shard_map/ppermute | solution.py:482
  28.6 15.3 %collective-permute-done.5.refs_4_.refs_8_ = bf16[24,64,256]{2,1,0:T(8,128)(2,1)S(1)} collective-permute-done((bf16[24,64,256]{2,1,0:T(8,128)(2,1)S(1)}, bf16[24,64,256]{2,1,0:T(8,128)(2,1)S(1)}, u32[]{:S(2)}, u32[]{:S(2)}) %collective-permute-start.5) | collective-permute-done | bytes 786464 | tf_op jit(solution)/shard_map/ppermute | solution.py:482
  43.9 0.9 shard_map.73.refs_0_
  44.9 1.6 %collective-permute-start.11 = (bf16[6,128,256]{2,1,0:T(8,128)(2,1)S(1)}, bf16[6,128,256]{2,1,0:T(8,128)(2,1)S(1)}, u32[]{:S(2)}, u32[]{:S(2)}) collective-permute-start(bf16[6,128,256]{2,1,0:T(8,128)(2,1)S(1)} %shard_map.74.refs_5_), channel_id=1, source_target_pairs={{0,4},{4,8},{8,12},{12,0},{1,5},{5,9},{9,13},{13,1},{2,6},{6,10},{... | collective-permute-start | bytes 1179656 | tf_op jit(solution)/shard_map/ppermute | solution.py:474
  46.5 0.9 shard_map.75.refs_5_.refs_3_
  47.5 0.9 shard_map.76.refs_4_
  48.4 0.5 copy-done
  48.9 1.1 shard_map.77
  50.0 0.5 collective-permute-start.10
  50.5 0.2 collective-permute-start.8
  50.7 1.5 %collective-permute-start.9 = (bf16[6,64,256]{2,1,0:T(8,128)(2,1)S(1)}, bf16[6,64,256]{2,1,0:T(8,128)(2,1)S(1)}, u32[]{:S(2)}, u32[]{:S(2)}) collective-permute-start(bf16[6,64,256]{2,1,0:T(8,128)(2,1)S(1)} %get-tuple-element.51), channel_id=1, source_target_pairs={{0,2},{1,3},{2,0},{3,1},{4,6},{5,7},{6,4},{7,5},{8,10},{9,11},{10,... | collective-permute-start | bytes 589832 | tf_op jit(solution)/shard_map/ppermute | solution.py:482
  52.2 0.9 shard_map.78.refs_5_.refs_0_
  53.1 0.9 shard_map.79.refs_5_.refs_0_
  54.0 0.8 shard_map.80.refs_1_
  54.8 2.5 %collective-permute-start.16 = (bf16[6,128,256]{2,1,0:T(8,128)(2,1)S(1)}, bf16[6,128,256]{2,1,0:T(8,128)(2,1)S(1)}, u32[]{:S(2)}, u32[]{:S(2)}) collective-permute-start(bf16[6,128,256]{2,1,0:T(8,128)(2,1)S(1)} %shard_map.81.refs_2_), channel_id=1, source_target_pairs={{0,12},{4,0},{8,4},{12,8},{1,13},{5,1},{9,5},{13,9},{2,14},{6,2},{... | collective-permute-start | bytes 1179656 | tf_op jit(solution)/shard_map/ppermute | solution.py:474
  57.3 1.6 %collective-permute-done.11.refs_3_.refs_4_ = bf16[6,128,256]{2,1,0:T(8,128)(2,1)S(1)} collective-permute-done((bf16[6,128,256]{2,1,0:T(8,128)(2,1)S(1)}, bf16[6,128,256]{2,1,0:T(8,128)(2,1)S(1)}, u32[]{:S(2)}, u32[]{:S(2)}) %collective-permute-start.11) | collective-permute-done | bytes 393248 | tf_op jit(solution)/shard_map/ppermute | solution.py:474
  58.9 2.6 %collective-permute-done.9.refs_12_.refs_6_ = bf16[6,64,256]{2,1,0:T(8,128)(2,1)S(1)} collective-permute-done((bf16[6,64,256]{2,1,0:T(8,128)(2,1)S(1)}, bf16[6,64,256]{2,1,0:T(8,128)(2,1)S(1)}, u32[]{:S(2)}, u32[]{:S(2)}) %collective-permute-start.9) | collective-permute-done | bytes 196640 | tf_op jit(solution)/shard_map/ppermute | solution.py:482
  61.5 1.1 shard_map.83
  62.6 0.6 collective-permute-start.14
  63.2 1.3 %collective-permute-start.15 = (bf16[6,64,256]{2,1,0:T(8,128)(2,1)S(1)}, bf16[6,64,256]{2,1,0:T(8,128)(2,1)S(1)}, u32[]{:S(2)}, u32[]{:S(2)}) collective-permute-start(bf16[6,64,256]{2,1,0:T(8,128)(2,1)S(1)} %get-tuple-element.58), channel_id=1, source_target_pairs={{0,3},{1,2},{2,1},{3,0},{4,7},{5,6},{6,5},{7,4},{8,11},{9,10},{10,... | collective-permute-start | bytes 589832 | tf_op jit(solution)/shard_map/ppermute | solution.py:482
  64.5 2.6 %collective-permute-start.20 = (bf16[4,128,256]{2,1,0:T(8,128)(2,1)S(1)}, bf16[4,128,256]{2,1,0:T(8,128)(2,1)S(1)}, u32[]{:S(2)}, u32[]{:S(2)}) collective-permute-start(bf16[4,128,256]{2,1,0:T(8,128)(2,1)S(1)} %get-tuple-element.54.refs_10_), channel_id=1, source_target_pairs={{0,8},{4,12},{8,0},{12,4},{1,9},{5,13},{9,1},{13,5},{2,10},{6,14},... | collective-permute-start | bytes 786440 | tf_op jit(solution)/shard_map/ppermute | solution.py:474
  67.0 0.1 collective-permute-done.16.refs_4_
  67.2 3.2 %collective-permute-done.14.refs_11_.refs_10_ = bf16[6,64,256]{2,1,0:T(8,128)(2,1)S(1)} collective-permute-done((bf16[6,64,256]{2,1,0:T(8,128)(2,1)S(1)}, bf16[6,64,256]{2,1,0:T(8,128)(2,1)S(1)}, u32[]{:S(2)}, u32[]{:S(2)}) %collective-permute-start.14) | collective-permute-done | bytes 196640 | tf_op jit(solution)/shard_map/ppermute | solution.py:482
  70.4 3.3 %collective-permute-done.15.refs_12_.refs_11_ = bf16[6,64,256]{2,1,0:T(8,128)(2,1)S(1)} collective-permute-done((bf16[6,64,256]{2,1,0:T(8,128)(2,1)S(1)}, bf16[6,64,256]{2,1,0:T(8,128)(2,1)S(1)}, u32[]{:S(2)}, u32[]{:S(2)}) %collective-permute-start.15) | collective-permute-done | bytes 196640 | tf_op jit(solution)/shard_map/ppermute | solution.py:482
  73.7 1.1 shard_map.84
  74.7 0.6 collective-permute-start.17
  75.4 0.5 collective-permute-start.18
  75.9 0.9 collective-permute-start.19
  76.8 2.4 %collective-permute-start.24 = (bf16[2,128,256]{2,1,0:T(8,128)(2,1)S(1)}, bf16[2,128,256]{2,1,0:T(8,128)(2,1)S(1)}, u32[]{:S(2)}, u32[]{:S(2)}) collective-permute-start(bf16[2,128,256]{2,1,0:T(8,128)(2,1)S(1)} %get-tuple-element.69), channel_id=1, source_target_pairs={{0,8},{4,12},{8,0},{12,4},{1,9},{5,13},{9,1},{13,5},{2,10},{6,14},... | collective-permute-start | bytes 393224 | tf_op jit(solution)/shard_map/ppermute | solution.py:474
  79.3 0.3 collective-permute-done.20.refs_4_
  79.5 3.6 %collective-permute-done.18.refs_11_.refs_14_ = bf16[6,64,256]{2,1,0:T(8,128)(2,1)S(1)} collective-permute-done((bf16[6,64,256]{2,1,0:T(8,128)(2,1)S(1)}, bf16[6,64,256]{2,1,0:T(8,128)(2,1)S(1)}, u32[]{:S(2)}, u32[]{:S(2)}) %collective-permute-start.18) | collective-permute-done | bytes 196640 | tf_op jit(solution)/shard_map/ppermute | solution.py:482
  83.1 2.5 %collective-permute-done.19.refs_12_.refs_15_ = bf16[6,64,256]{2,1,0:T(8,128)(2,1)S(1)} collective-permute-done((bf16[6,64,256]{2,1,0:T(8,128)(2,1)S(1)}, bf16[6,64,256]{2,1,0:T(8,128)(2,1)S(1)}, u32[]{:S(2)}, u32[]{:S(2)}) %collective-permute-start.19) | collective-permute-done | bytes 196640 | tf_op jit(solution)/shard_map/ppermute | solution.py:482
  85.6 0.9 shard_map.85
  86.5 1.1 collective-permute-start.21
  87.6 0.6 collective-permute-start.22
  88.2 0.9 collective-permute-start.23
  89.0 0.9 fusion.refs_10_
  89.9 4.0 %collective-permute-done.22.refs_12_.refs_18_ = bf16[4,64,256]{2,1,0:T(8,128)(2,1)S(1)} collective-permute-done((bf16[4,64,256]{2,1,0:T(8,128)(2,1)S(1)}, bf16[4,64,256]{2,1,0:T(8,128)(2,1)S(1)}, u32[]{:S(2)}, u32[]{:S(2)}) %collective-permute-start.22) | collective-permute-done | bytes 131104 | tf_op jit(solution)/shard_map/ppermute | solution.py:482
  94.0 1.1 collective-permute-done.23.refs_13_.refs_19_
  95.0 1.0 shard_map.86
  96.0 0.8 collective-permute-start.25
  96.8 0.6 collective-permute-start.26
  97.3 0.9 collective-permute-start.27
  98.2 3.2 %shard_map.87 = (f32[2,24,64,256]{3,2,1,0:T(8,128)S(1)}, f32[2,24,64,256]{3,2,1,0:T(8,128)}) custom-call(s32[74]{0:T(128)S(1)} %get-tuple-element.41.refs_0_.plan, s32[74]{0:T(128)S(1)} %shard_map.69.refs_6_.refs_1_, f32[24]{0:T(128)S(1)} %copy-done.2, bf16[2,24,64,256]{3,2,1,0:T(8,128)(2,1)S(1)} %copy-done.1, ...), custom_call_target="tpu_custom_call" | custom-call | tf_op jit(solution)/shard_map/pallas_call | solution.py:348
  101.4 0.4 collective-permute-done.26.refs_5_.refs_1_
  101.9 0.6 shard_map.89.refs_0_
  102.5 1.2 %collective-permute-start.28 = (f32[8,256]{1,0:T(8,128)S(1)}, f32[8,256]{1,0:T(8,128)S(1)}, u32[]{:S(2)}, u32[]{:S(2)}) collective-permute-start(f32[8,256]{1,0:T(8,128)S(1)} %shard_map.89.refs_0_), channel_id=1, source_target_pairs={{0,4},{4,8},{8,12},{12,0},{1,5},{5,9},{9,13},{13,1},{2,6},{6,10},{... | collective-permute-start | bytes 24584 | tf_op jit(solution)/shard_map/ppermute | solution.py:474
  103.7 1.7 %collective-permute-start.29 = (f32[8,256]{1,0:T(8,128)S(1)}, f32[8,256]{1,0:T(8,128)S(1)}, u32[]{:S(2)}, u32[]{:S(2)}) collective-permute-start(f32[8,256]{1,0:T(8,128)S(1)} %shard_map.89.refs_0_), channel_id=1, source_target_pairs={{0,8},{4,12},{8,0},{12,4},{1,9},{5,13},{9,1},{13,5},{2,10},{6,14},... | collective-permute-start | bytes 24584 | tf_op jit(solution)/shard_map/ppermute | solution.py:474
  105.4 2.2 %collective-permute-start.30 = (f32[8,256]{1,0:T(8,128)S(1)}, f32[8,256]{1,0:T(8,128)S(1)}, u32[]{:S(2)}, u32[]{:S(2)}) collective-permute-start(f32[8,256]{1,0:T(8,128)S(1)} %shard_map.89.refs_0_), channel_id=1, source_target_pairs={{0,12},{4,0},{8,4},{12,8},{1,13},{5,1},{9,5},{13,9},{2,14},{6,2},{... | collective-permute-start | bytes 24584 | tf_op jit(solution)/shard_map/ppermute | solution.py:474
  107.6 1.5 %shard_map.88 = (f32[2,24,64,256]{3,2,1,0:T(8,128)}, f32[8,128]{1,0:T(8,128)S(1)}) custom-call(s32[74]{0:T(128)S(1)} %get-tuple-element.41.refs_0_.plan, s32[74]{0:T(128)S(1)} %shard_map.69.refs_6_.refs_1_, f32[2,24,64,256]{3,2,1,0:T(8,128)S(1)} %get-tuple-element.72.refs_2_.refs_3_, ...), custom_call_target="tpu_custom_call", output_to_operand_aliasing={{0}: (7, {})} | custom-call | tf_op jit(solution)/shard_map/pallas_call | solution.py:393
  109.1 0.5 shard_map.90
  (30 shorter events, 0.2 us)
Async XLA Ops:
  0.6 9.1 %collective-permute-start.2 = (bf16[1,24,128,256]{3,2,1,0:T(8,128)(2,1)}, bf16[1,24,128,256]{3,2,1,0:T(8,128)(2,1)S(1)}, u32[]{:S(2)}, u32[]{:S(2)}) collective-permute-start(bf16[1,24,128,256]{3,2,1,0:T(8,128)(2,1)} %right.1), channel_id=1, source_target_pairs={{0,1},{1,0},{2,3},{3,2},{4,5},{5,4},{6,7},{7,6},{8,9},{9,8},{10,11... | collective-permute-start | bytes 4718600 | tf_op jit(solution)/shard_map/ppermute | solution.py:474
  1.1 8.6 %collective-permute-start.3 = (bf16[2,24,64,256]{3,2,1,0:T(8,128)(2,1)}, bf16[2,24,64,256]{3,2,1,0:T(8,128)(2,1)S(1)}, u32[]{:S(2)}, u32[]{:S(2)}) collective-permute-start(bf16[2,24,64,256]{3,2,1,0:T(8,128)(2,1)} %refs_3_.1), channel_id=1, source_target_pairs={{0,1},{1,0},{2,3},{3,2},{4,5},{5,4},{6,7},{7,6},{8,9},{9,8},{10,11... | collective-permute-start | bytes 4718600 | tf_op jit(solution)/shard_map/ppermute | solution.py:474
  1.2 13.7 %collective-permute-start.1 = (bf16[1,24,128,256]{3,2,1,0:T(8,128)(2,1)}, bf16[1,24,128,256]{3,2,1,0:T(8,128)(2,1)S(1)}, u32[]{:S(2)}, u32[]{:S(2)}) collective-permute-start(bf16[1,24,128,256]{3,2,1,0:T(8,128)(2,1)} %refs_1_.9), channel_id=1, source_target_pairs={{0,1},{1,0},{2,3},{3,2},{4,5},{5,4},{6,7},{7,6},{8,9},{9,8},{10,11... | collective-permute-start | bytes 4718600 | tf_op jit(solution)/shard_map/ppermute | solution.py:474
  1.7 6.5 %collective-permute-start = (s32[1,96]{1,0:T(1,128)}, s32[1,96]{1,0:T(1,128)S(1)}, u32[]{:S(2)}, u32[]{:S(2)}) collective-permute-start(s32[1,96]{1,0:T(1,128)} %partner.1), channel_id=1, source_target_pairs={{0,2},{2,0},{1,3},{3,1},{4,6},{6,4},{5,7},{7,5},{8,10},{10,8},{9,1... | collective-permute-start | bytes 1160 | tf_op jit(solution)/shard_map/ppermute | solution.py:474
  4.2 0.7 copy-start.3
  8.2 20.5 %collective-permute-start.4 = (bf16[24,64,256]{2,1,0:T(8,128)(2,1)S(1)}, bf16[24,64,256]{2,1,0:T(8,128)(2,1)S(1)}, u32[]{:S(2)}, u32[]{:S(2)}) collective-permute-start(bf16[24,64,256]{2,1,0:T(8,128)(2,1)S(1)} %get-tuple-element.45.refs_3_.refs_5_), channel_id=1, source_target_pairs={{0,2},{1,3},{2,0},{3,1},{4,6},{5,7},{6,4},{7,5},{8,10},{9,11},{10,... | collective-permute-start | bytes 2359304 | tf_op jit(solution)/shard_map/ppermute | solution.py:482
  8.3 35.7 %collective-permute-start.5 = (bf16[24,64,256]{2,1,0:T(8,128)(2,1)S(1)}, bf16[24,64,256]{2,1,0:T(8,128)(2,1)S(1)}, u32[]{:S(2)}, u32[]{:S(2)}) collective-permute-start(bf16[24,64,256]{2,1,0:T(8,128)(2,1)S(1)} %get-tuple-element.46), channel_id=1, source_target_pairs={{0,3},{1,2},{2,1},{3,0},{4,7},{5,6},{6,5},{7,4},{8,11},{9,10},{10,... | collective-permute-start | bytes 2359304 | tf_op jit(solution)/shard_map/ppermute | solution.py:482
  11.0 33.9 %collective-permute-start.6 = (bf16[6,128,256]{2,1,0:T(8,128)(2,1)S(1)}, bf16[6,128,256]{2,1,0:T(8,128)(2,1)S(1)}, u32[]{:S(2)}, u32[]{:S(2)}) collective-permute-start(bf16[6,128,256]{2,1,0:T(8,128)(2,1)S(1)} %get-tuple-element.47.refs_5_), channel_id=1, source_target_pairs={{0,4},{4,8},{8,12},{12,0},{1,5},{5,9},{9,13},{13,1},{2,6},{6,10},{... | collective-permute-start | bytes 1179656 | tf_op jit(solution)/shard_map/ppermute | solution.py:474
  12.6 32.3 %collective-permute-start.7 = (bf16[6,128,256]{2,1,0:T(8,128)(2,1)S(1)}, bf16[6,128,256]{2,1,0:T(8,128)(2,1)S(1)}, u32[]{:S(2)}, u32[]{:S(2)}) collective-permute-start(bf16[6,128,256]{2,1,0:T(8,128)(2,1)S(1)} %get-tuple-element.48), channel_id=1, source_target_pairs={{0,12},{4,0},{8,4},{12,8},{1,13},{5,1},{9,5},{13,9},{2,14},{6,2},{... | collective-permute-start | bytes 1179656 | tf_op jit(solution)/shard_map/ppermute | solution.py:474
  15.8 38.9 %collective-permute-start.12 = (bf16[6,128,256]{2,1,0:T(8,128)(2,1)S(1)}, bf16[6,128,256]{2,1,0:T(8,128)(2,1)S(1)}, u32[]{:S(2)}, u32[]{:S(2)}) collective-permute-start(bf16[6,128,256]{2,1,0:T(8,128)(2,1)S(1)} %shard_map.72.refs_5_), channel_id=1, source_target_pairs={{0,8},{4,12},{8,0},{12,4},{1,9},{5,13},{9,1},{13,5},{2,10},{6,14},... | collective-permute-start | bytes 1179656 | tf_op jit(solution)/shard_map/ppermute | solution.py:474
  44.9 13.9 %collective-permute-start.11 = (bf16[6,128,256]{2,1,0:T(8,128)(2,1)S(1)}, bf16[6,128,256]{2,1,0:T(8,128)(2,1)S(1)}, u32[]{:S(2)}, u32[]{:S(2)}) collective-permute-start(bf16[6,128,256]{2,1,0:T(8,128)(2,1)S(1)} %shard_map.74.refs_5_), channel_id=1, source_target_pairs={{0,4},{4,8},{8,12},{12,0},{1,5},{5,9},{9,13},{13,1},{2,6},{6,10},{... | collective-permute-start | bytes 1179656 | tf_op jit(solution)/shard_map/ppermute | solution.py:474
  47.5 1.4 %copy-start = (bf16[1,24,128,256]{3,2,1,0:T(8,128)(2,1)S(1)}, bf16[1,24,128,256]{3,2,1,0:T(8,128)(2,1)}, u32[]{:S(2)}) copy-start(bf16[1,24,128,256]{3,2,1,0:T(8,128)(2,1)} %refs_1_.9) | copy-start | bytes 4718596
  50.0 8.9 %collective-permute-start.10 = (bf16[6,64,256]{2,1,0:T(8,128)(2,1)S(1)}, bf16[6,64,256]{2,1,0:T(8,128)(2,1)S(1)}, u32[]{:S(2)}, u32[]{:S(2)}) collective-permute-start(bf16[6,64,256]{2,1,0:T(8,128)(2,1)S(1)} %get-tuple-element.52), channel_id=1, source_target_pairs={{0,3},{1,2},{2,1},{3,0},{4,7},{5,6},{6,5},{7,4},{8,11},{9,10},{10,... | collective-permute-start | bytes 589832 | tf_op jit(solution)/shard_map/ppermute | solution.py:482
  50.5 8.4 %collective-permute-start.8 = (bf16[6,64,256]{2,1,0:T(8,128)(2,1)S(1)}, bf16[6,64,256]{2,1,0:T(8,128)(2,1)S(1)}, u32[]{:S(2)}, u32[]{:S(2)}) collective-permute-start(bf16[6,64,256]{2,1,0:T(8,128)(2,1)S(1)} %get-tuple-element.50), channel_id=1, source_target_pairs={{0,1},{1,0},{2,3},{3,2},{4,5},{5,4},{6,7},{7,6},{8,9},{9,8},{10,11... | collective-permute-start | bytes 589832 | tf_op jit(solution)/shard_map/ppermute | solution.py:482
  50.7 10.8 %collective-permute-start.9 = (bf16[6,64,256]{2,1,0:T(8,128)(2,1)S(1)}, bf16[6,64,256]{2,1,0:T(8,128)(2,1)S(1)}, u32[]{:S(2)}, u32[]{:S(2)}) collective-permute-start(bf16[6,64,256]{2,1,0:T(8,128)(2,1)S(1)} %get-tuple-element.51), channel_id=1, source_target_pairs={{0,2},{1,3},{2,0},{3,1},{4,6},{5,7},{6,4},{7,5},{8,10},{9,11},{10,... | collective-permute-start | bytes 589832 | tf_op jit(solution)/shard_map/ppermute | solution.py:482
  54.8 12.4 %collective-permute-start.16 = (bf16[6,128,256]{2,1,0:T(8,128)(2,1)S(1)}, bf16[6,128,256]{2,1,0:T(8,128)(2,1)S(1)}, u32[]{:S(2)}, u32[]{:S(2)}) collective-permute-start(bf16[6,128,256]{2,1,0:T(8,128)(2,1)S(1)} %shard_map.81.refs_2_), channel_id=1, source_target_pairs={{0,12},{4,0},{8,4},{12,8},{1,13},{5,1},{9,5},{13,9},{2,14},{6,2},{... | collective-permute-start | bytes 1179656 | tf_op jit(solution)/shard_map/ppermute | solution.py:474
  62.5 4.7 %collective-permute-start.13 = (bf16[6,64,256]{2,1,0:T(8,128)(2,1)S(1)}, bf16[6,64,256]{2,1,0:T(8,128)(2,1)S(1)}, u32[]{:S(2)}, u32[]{:S(2)}) collective-permute-start(bf16[6,64,256]{2,1,0:T(8,128)(2,1)S(1)} %get-tuple-element.56), channel_id=1, source_target_pairs={{0,1},{1,0},{2,3},{3,2},{4,5},{5,4},{6,7},{7,6},{8,9},{9,8},{10,11... | collective-permute-start | bytes 589832 | tf_op jit(solution)/shard_map/ppermute | solution.py:482
  62.6 7.8 %collective-permute-start.14 = (bf16[6,64,256]{2,1,0:T(8,128)(2,1)S(1)}, bf16[6,64,256]{2,1,0:T(8,128)(2,1)S(1)}, u32[]{:S(2)}, u32[]{:S(2)}) collective-permute-start(bf16[6,64,256]{2,1,0:T(8,128)(2,1)S(1)} %get-tuple-element.57), channel_id=1, source_target_pairs={{0,2},{1,3},{2,0},{3,1},{4,6},{5,7},{6,4},{7,5},{8,10},{9,11},{10,... | collective-permute-start | bytes 589832 | tf_op jit(solution)/shard_map/ppermute | solution.py:482
  63.2 10.5 %collective-permute-start.15 = (bf16[6,64,256]{2,1,0:T(8,128)(2,1)S(1)}, bf16[6,64,256]{2,1,0:T(8,128)(2,1)S(1)}, u32[]{:S(2)}, u32[]{:S(2)}) collective-permute-start(bf16[6,64,256]{2,1,0:T(8,128)(2,1)S(1)} %get-tuple-element.58), channel_id=1, source_target_pairs={{0,3},{1,2},{2,1},{3,0},{4,7},{5,6},{6,5},{7,4},{8,11},{9,10},{10,... | collective-permute-start | bytes 589832 | tf_op jit(solution)/shard_map/ppermute | solution.py:482
  64.5 15.1 %collective-permute-start.20 = (bf16[4,128,256]{2,1,0:T(8,128)(2,1)S(1)}, bf16[4,128,256]{2,1,0:T(8,128)(2,1)S(1)}, u32[]{:S(2)}, u32[]{:S(2)}) collective-permute-start(bf16[4,128,256]{2,1,0:T(8,128)(2,1)S(1)} %get-tuple-element.54.refs_10_), channel_id=1, source_target_pairs={{0,8},{4,12},{8,0},{12,4},{1,9},{5,13},{9,1},{13,5},{2,10},{6,14},... | collective-permute-start | bytes 786440 | tf_op jit(solution)/shard_map/ppermute | solution.py:474
  74.7 4.8 %collective-permute-start.17 = (bf16[6,64,256]{2,1,0:T(8,128)(2,1)S(1)}, bf16[6,64,256]{2,1,0:T(8,128)(2,1)S(1)}, u32[]{:S(2)}, u32[]{:S(2)}) collective-permute-start(bf16[6,64,256]{2,1,0:T(8,128)(2,1)S(1)} %get-tuple-element.61), channel_id=1, source_target_pairs={{0,1},{1,0},{2,3},{3,2},{4,5},{5,4},{6,7},{7,6},{8,9},{9,8},{10,11... | collective-permute-start | bytes 589832 | tf_op jit(solution)/shard_map/ppermute | solution.py:482
  75.4 7.8 %collective-permute-start.18 = (bf16[6,64,256]{2,1,0:T(8,128)(2,1)S(1)}, bf16[6,64,256]{2,1,0:T(8,128)(2,1)S(1)}, u32[]{:S(2)}, u32[]{:S(2)}) collective-permute-start(bf16[6,64,256]{2,1,0:T(8,128)(2,1)S(1)} %get-tuple-element.62), channel_id=1, source_target_pairs={{0,2},{1,3},{2,0},{3,1},{4,6},{5,7},{6,4},{7,5},{8,10},{9,11},{10,... | collective-permute-start | bytes 589832 | tf_op jit(solution)/shard_map/ppermute | solution.py:482
  75.9 9.7 %collective-permute-start.19 = (bf16[6,64,256]{2,1,0:T(8,128)(2,1)S(1)}, bf16[6,64,256]{2,1,0:T(8,128)(2,1)S(1)}, u32[]{:S(2)}, u32[]{:S(2)}) collective-permute-start(bf16[6,64,256]{2,1,0:T(8,128)(2,1)S(1)} %get-tuple-element.63), channel_id=1, source_target_pairs={{0,3},{1,2},{2,1},{3,0},{4,7},{5,6},{6,5},{7,4},{8,11},{9,10},{10,... | collective-permute-start | bytes 589832 | tf_op jit(solution)/shard_map/ppermute | solution.py:482
  76.8 13.1 %collective-permute-start.24 = (bf16[2,128,256]{2,1,0:T(8,128)(2,1)S(1)}, bf16[2,128,256]{2,1,0:T(8,128)(2,1)S(1)}, u32[]{:S(2)}, u32[]{:S(2)}) collective-permute-start(bf16[2,128,256]{2,1,0:T(8,128)(2,1)S(1)} %get-tuple-element.69), channel_id=1, source_target_pairs={{0,8},{4,12},{8,0},{12,4},{1,9},{5,13},{9,1},{13,5},{2,10},{6,14},... | collective-permute-start | bytes 393224 | tf_op jit(solution)/shard_map/ppermute | solution.py:474
  85.6 3.4 %copy-start.1 = (bf16[2,24,64,256]{3,2,1,0:T(8,128)(2,1)S(1)}, bf16[2,24,64,256]{3,2,1,0:T(8,128)(2,1)}, u32[]{:S(2)}) copy-start(bf16[2,24,64,256]{3,2,1,0:T(8,128)(2,1)} %refs_3_.1) | copy-start | bytes 4718596
  85.6 3.4 %copy-start.2 = (f32[24]{0:T(128)S(1)}, f32[24]{0:T(128)}, u32[]{:S(2)}) copy-start(f32[24]{0:T(128)} %refs_2_.1) | copy-start | bytes 292
  86.5 3.4 %collective-permute-start.21 = (bf16[4,64,256]{2,1,0:T(8,128)(2,1)S(1)}, bf16[4,64,256]{2,1,0:T(8,128)(2,1)S(1)}, u32[]{:S(2)}, u32[]{:S(2)}) collective-permute-start(bf16[4,64,256]{2,1,0:T(8,128)(2,1)S(1)} %get-tuple-element.66), channel_id=1, source_target_pairs={{0,1},{1,0},{2,3},{3,2},{4,5},{5,4},{6,7},{7,6},{8,9},{9,8},{10,11... | collective-permute-start | bytes 393224 | tf_op jit(solution)/shard_map/ppermute | solution.py:482
  87.6 6.4 %collective-permute-start.22 = (bf16[4,64,256]{2,1,0:T(8,128)(2,1)S(1)}, bf16[4,64,256]{2,1,0:T(8,128)(2,1)S(1)}, u32[]{:S(2)}, u32[]{:S(2)}) collective-permute-start(bf16[4,64,256]{2,1,0:T(8,128)(2,1)S(1)} %get-tuple-element.67), channel_id=1, source_target_pairs={{0,2},{1,3},{2,0},{3,1},{4,6},{5,7},{6,4},{7,5},{8,10},{9,11},{10,... | collective-permute-start | bytes 393224 | tf_op jit(solution)/shard_map/ppermute | solution.py:482
  88.2 6.9 %collective-permute-start.23 = (bf16[4,64,256]{2,1,0:T(8,128)(2,1)S(1)}, bf16[4,64,256]{2,1,0:T(8,128)(2,1)S(1)}, u32[]{:S(2)}, u32[]{:S(2)}) collective-permute-start(bf16[4,64,256]{2,1,0:T(8,128)(2,1)S(1)} %get-tuple-element.68), channel_id=1, source_target_pairs={{0,3},{1,2},{2,1},{3,0},{4,7},{5,6},{6,5},{7,4},{8,11},{9,10},{10,... | collective-permute-start | bytes 393224 | tf_op jit(solution)/shard_map/ppermute | solution.py:482
  96.0 5.4 %collective-permute-start.25 = (bf16[144,256]{1,0:T(8,128)(2,1)S(1)}, bf16[144,256]{1,0:T(8,128)(2,1)S(1)}, u32[]{:S(2)}, u32[]{:S(2)}) collective-permute-start(bf16[144,256]{1,0:T(8,128)(2,1)S(1)} %get-tuple-element.74), channel_id=1, source_target_pairs={{0,1},{1,0},{2,3},{3,2},{4,5},{5,4},{6,7},{7,6},{8,9},{9,8},{10,11... | collective-permute-start | bytes 221192 | tf_op jit(solution)/shard_map/ppermute | solution.py:482
  96.8 5.1 %collective-permute-start.26 = (bf16[144,256]{1,0:T(8,128)(2,1)S(1)}, bf16[144,256]{1,0:T(8,128)(2,1)S(1)}, u32[]{:S(2)}, u32[]{:S(2)}) collective-permute-start(bf16[144,256]{1,0:T(8,128)(2,1)S(1)} %get-tuple-element.75), channel_id=1, source_target_pairs={{0,2},{1,3},{2,0},{3,1},{4,6},{5,7},{6,4},{7,5},{8,10},{9,11},{10,... | collective-permute-start | bytes 221192 | tf_op jit(solution)/shard_map/ppermute | solution.py:482
  97.3 4.6 %collective-permute-start.27 = (bf16[144,256]{1,0:T(8,128)(2,1)S(1)}, bf16[144,256]{1,0:T(8,128)(2,1)S(1)}, u32[]{:S(2)}, u32[]{:S(2)}) collective-permute-start(bf16[144,256]{1,0:T(8,128)(2,1)S(1)} %get-tuple-element.76), channel_id=1, source_target_pairs={{0,3},{1,2},{2,1},{3,0},{4,7},{5,6},{6,5},{7,4},{8,11},{9,10},{10,... | collective-permute-start | bytes 221192 | tf_op jit(solution)/shard_map/ppermute | solution.py:482
  102.5 6.6 %collective-permute-start.28 = (f32[8,256]{1,0:T(8,128)S(1)}, f32[8,256]{1,0:T(8,128)S(1)}, u32[]{:S(2)}, u32[]{:S(2)}) collective-permute-start(f32[8,256]{1,0:T(8,128)S(1)} %shard_map.89.refs_0_), channel_id=1, source_target_pairs={{0,4},{4,8},{8,12},{12,0},{1,5},{5,9},{9,13},{13,1},{2,6},{6,10},{... | collective-permute-start | bytes 24584 | tf_op jit(solution)/shard_map/ppermute | solution.py:474
  103.7 5.5 %collective-permute-start.29 = (f32[8,256]{1,0:T(8,128)S(1)}, f32[8,256]{1,0:T(8,128)S(1)}, u32[]{:S(2)}, u32[]{:S(2)}) collective-permute-start(f32[8,256]{1,0:T(8,128)S(1)} %shard_map.89.refs_0_), channel_id=1, source_target_pairs={{0,8},{4,12},{8,0},{12,4},{1,9},{5,13},{9,1},{13,5},{2,10},{6,14},... | collective-permute-start | bytes 24584 | tf_op jit(solution)/shard_map/ppermute | solution.py:474
  105.4 3.7 %collective-permute-start.30 = (f32[8,256]{1,0:T(8,128)S(1)}, f32[8,256]{1,0:T(8,128)S(1)}, u32[]{:S(2)}, u32[]{:S(2)}) collective-permute-start(f32[8,256]{1,0:T(8,128)S(1)} %shard_map.89.refs_0_), channel_id=1, source_target_pairs={{0,12},{4,0},{8,4},{12,8},{1,13},{5,1},{9,5},{13,9},{2,14},{6,2},{... | collective-permute-start | bytes 24584 | tf_op jit(solution)/shard_map/ppermute | solution.py:474

commit v8 on v7

--- a/solution.py
+++ b/solution.py
@@ -192,7 +192,7 @@
     )(plan, *right, *flat, *after)
 
 
-def terms_body(z, spans, chained, last, *refs):
+def terms_body(z, spans, chained, last, kept, *refs):
     refs = list(refs)
     plan = refs.pop(0)
     left = [refs.pop(0) for _ in range(z.rep)]
@@ -201,6 +201,7 @@
     vec = [[refs.pop(0) for _ in range(z.rep)] for _ in range(z.env)]
     so_far = refs.pop(0) if chained else None
     own_sums = refs.pop(0) if last else None
+    kept = [[refs.pop(0) for _ in range(z.rep - 1)] for _ in range(kept)]
     pbuf, tbuf = refs[-2:]
     dots = refs[-3]
     outs = refs[-3 - z.env * z.rep : -3]
@@ -253,11 +254,17 @@
         value = value - piece
     split = split.astype(jnp.bfloat16)
     dots[...] = split
+    at = n * z.own_rows
+    for blocks in kept:
+        for s, block in enumerate(blocks):
+            for i in range(block.shape[0]):
+                outs[1 + s][at + i * z.own_rows : at + (i + 1) * z.own_rows] = block[i]
+        at += blocks[0].shape[0] * z.own_rows
     for out in outs[1:]:
-        out[n * z.own_rows :] = split
-
-
-def terms(z, plan, left, near, far, vec, spans, so_far=None, own_sums=None, after=()):
+        out[out.shape[0] - TAIL :] = split
+
+
+def terms(z, plan, left, near, far, vec, spans, so_far=None, own_sums=None, kept=(), after=()):
     count = sum(span[1] for span in spans)
     flat = [ref for piece in vec for ref in piece]
     shapes = [(count, z.own_rows, z.order)] * (z.env * z.rep)
@@ -266,14 +273,18 @@
     sums = jax.ShapeDtypeStruct((8, z.order), jnp.float32)
     if last:
         shapes[1:] = [(count * z.own_rows + TAIL, z.order)] * (z.env * z.rep - 1)
+        more = sum(blocks[0].shape[0] for blocks in kept)
+        shapes[1 : z.rep] = [((count + more) * z.own_rows + TAIL, z.order)] * (z.rep - 1)
         sums = jax.ShapeDtypeStruct((TAIL, z.order), jnp.bfloat16)
     extra = [] if so_far is None else [so_far]
     specs = [VMEM] * len(extra)
     if last:
         extra.append(own_sums)
         specs.append(SMEM)
+    extra += [block for blocks in kept for block in blocks]
+    specs += [VMEM] * (len(extra) - len(specs))
     *made, dots = pl.pallas_call(
-        functools.partial(terms_body, z, spans, so_far is not None, last),
+        functools.partial(terms_body, z, spans, so_far is not None, last, len(kept)),
         out_shape=[jax.ShapeDtypeStruct(shape, jnp.bfloat16) for shape in shapes] + [sums],
         in_specs=[SMEM]
         + [VMEM] * (len(left) + len(near) + len(far) + len(flat))
@@ -295,12 +306,12 @@
 
                 def act():
                     blocks = []
-                    for ref in parts[e]:
+                    for ref, skip in parts[e]:
                         if len(ref.shape) == 3:
                             blocks.append(lambda ref=ref: ref[n])
                         else:
-                            rows = slice(n * z.own_rows, (n + 1) * z.own_rows)
-                            blocks.append(lambda ref=ref: ref[rows])
+                            rows = slice((skip + n) * z.own_rows, (skip + n + 1) * z.own_rows)
+                            blocks.append(lambda ref=ref, rows=rows: ref[rows])
                     action(plan[z.target + first + i], blocks)
 
                 z.when_valid(plan, first + i, act)
@@ -318,7 +329,7 @@
     for_terms(z, plans, parts, spans, add)
 
 
-def gather_body(z, chunks, *refs):
+def gather_body(z, chunks, skip, *refs):
     refs = list(refs)
     plans = [refs.pop(0) for _ in range(z.env)]
     energy, vectors = refs.pop(0), refs.pop(0)
@@ -330,9 +341,13 @@
         return carry
 
     lax.fori_loop(0, z.slots, start, 0, unroll=2)
+    joined = [refs.pop(0) for _ in range(z.rep - 1)]
     for spans in chunks:
-        parts = [[refs.pop(0) for _ in range(z.rep)] for _ in range(z.env)]
+        parts = [[(refs.pop(0), 0)] + [(ref, skip) for ref in joined]]
+        for _ in range(1, z.env):
+            parts.append([(refs.pop(0), 0) for _ in range(z.rep)])
         add_terms(z, plans, so_far, parts, spans)
+        skip += sum(span[1] for span in spans)
     copies = []
     for v in range(z.batch):
         copies += split_copy(so_far.at[v], image.at[v], z.slots, sem.at[v])
@@ -342,11 +357,13 @@
         copy.wait()
 
 
-def gather_terms(z, plans, energy, vectors, parts, chunks, after=()):
-    flat = [ref for chunk in parts for piece in chunk for ref in piece]
+def gather_terms(z, plans, energy, vectors, joined, skip, parts, chunks, after=()):
+    flat = [*joined]
+    for chunk in parts:
+        flat += [chunk[0][0]] + [ref for piece in chunk[1:] for ref in piece]
     shape = jax.ShapeDtypeStruct(vectors.shape, jnp.float32)
     return pl.pallas_call(
-        functools.partial(gather_body, z, chunks),
+        functools.partial(gather_body, z, chunks, skip),
         out_shape=[shape, pltpu.HBM(vectors.shape, jnp.float32)],
         in_specs=[SMEM] * (z.env + 1) + [VMEM] * (1 + len(flat)) + [ANY] * len(after),
         out_specs=[VMEM, HBM],
@@ -360,7 +377,7 @@
     refs = list(refs)
     plans = [refs.pop(0) for _ in range(z.env)]
     so_far = refs.pop(0)
-    parts = [[refs.pop(0) for _ in range(z.rep)] for _ in range(z.env)]
+    parts = [[(refs.pop(0), 0) for _ in range(z.rep)] for _ in range(z.env)]
     image, token, sums, sem = refs[-4:]
     token[...] = jnp.zeros_like(token)
 
@@ -538,28 +555,28 @@
     made = near_products(2, (made[0], *left[1:]))
     near[2] = across(made, 2)
 
-    def send_terms(g, so_far, own_sums, after):
+    def send_terms(g, so_far, own_sums, kept, after):
         made, folded = terms(
-            z, plan, left, near[2 if g == 4 else g], far[g], vec, chunks[g], so_far, own_sums, after
+            z, plan, left, near[2 if g == 4 else g], far[g], vec, chunks[g], so_far,
+            own_sums, kept, after
         )
-        parts[g] = [
-            [
-                shift_both(z, made[e * z.rep + s], e, s) if e + s else made[0]
-                for s in range(z.rep)
-            ]
-            for e in range(z.env)
-        ]
+        first = made[: z.rep]
+        if own_sums is not None:
+            first[1:] = [shift(first[s], "rep", z.rep, s) for s in range(1, z.rep)]
+        parts[g] = [first]
+        for e in range(1, z.env):
+            parts[g].append([shift_both(z, made[e * z.rep + s], e, s) for s in range(z.rep)])
         return folded
 
     def arrived(g):
-        return [part for piece in parts[g] for part in piece][1:]
-
-    far1 = far_products(1, (made[0], *plans[1:]))
+        return [part for piece in parts[g][1:] for part in piece]
+
+    near[0] = near_products(0, made[:1])
+    far1 = far_products(1, (near[0][0], *plans[1:]))
     far1 = gate(far1, [*near[1], *near[3]])
     far[1] = across(far1, 1)
-    near[0] = near_products(0, far1[:1])
-    far[0] = far_products(0, near[0][:1])
-    dots = send_terms(0, None, None, ())
+    far[0] = far_products(0, far1[:1])
+    dots = send_terms(0, None, None, (), ())
     far3 = far_products(3, (dots,))
     far2 = far_products(2, far3[:1])
     far4 = far_products(4, far2[:1])
@@ -567,23 +584,26 @@
     far[3] = across(far3, 3)
     far2 = gate([*far2, *far4], [far3[0], *far[1]])
     far[2], far[4] = across(far2[:each], 2), across(far2[each:], 2)
-    dots = send_terms(1, dots, None, (far2[0], *arrived(0)))
-    dots = send_terms(3, dots, None, arrived(1))
+    dots = send_terms(1, dots, None, (), (far2[0], *arrived(0)))
+    dots = send_terms(3, dots, None, (), arrived(1))
     own_block = vectors.astype(jnp.float32)
     own_sums = jnp.sum(energy[None, :, None, None] * own_block * own_block, axis=(1, 2, 3))
-    dots = send_terms(2, dots, None, arrived(3))
-    dots = send_terms(4, dots, own_sums, arrived(2))
+    dots = send_terms(2, dots, None, (), arrived(3))
     early = (0, 1, 3, 2)
+    kept = [parts[g][0][1:] for g in early]
+    dots = send_terms(4, dots, own_sums, kept, arrived(2)[:1])
     so_far, image = gather_terms(
         z,
         plans,
         energy,
         vectors,
+        parts[4][0][1:],
+        sum(piece[1] for piece in chunks[4]),
         [parts[g] for g in early],
         [chunks[g] for g in early],
         (dots,),
     )
-    sums = chip_sums(z, plan, dots, arrived(4), (so_far,))
+    sums = chip_sums(z, plan, dots, parts[4][0][1:] + arrived(4), (so_far,))
     image, token = make_image(z, plans, so_far, image, parts[4], chunks[4])
     entries = z.slots * z.sector * z.order * z.order
     return (image, mean_over_sectors(z, sums, entries, (token,)))

time: 110 us -> 115 us (1.045)
  starting transfers between devices: 35.1 us -> 38.4 us
  waiting for transfers between devices: 48.7 us -> 51 us
    ppermute x14 -> x15, starting transfers between devices: 22.6 us -> 28.4 us  [shift(): lax.ppermute(array, axis, [(i, (i + step) % size) for i in range(size)])]
    ppermute x14 -> x15, waiting for transfers between devices: 2.01 us -> 6.89 us  [shift(): lax.ppermute(array, axis, [(i, (i + step) % size) for i in range(size)])]
    ppermute x17 -> x12, waiting for transfers between devices: 46.7 us -> 44.1 us  [shift_both(): return lax.ppermute(array, ('env', 'rep'), perm)]
    ppermute x17 -> x12, starting transfers between devices: 12.5 us -> 10 us  [shift_both(): return lax.ppermute(array, ('env', 'rep'), perm)]
  transfers between devices with their start and end apart: 31 -> 27, of which waited for: 13 -> 13; matrix products, arithmetic and copies ran while one was open for 1% -> 1% of each run, Pallas kernels for 19% -> 18%
where the time goes in v8:
time: 115 us
  waiting for transfers between devices  51 us (44%)
  starting transfers between devices  38.4 us (33%)
  Pallas kernels  22.9 us (20%)
    ppermute x12, waiting for transfers between devices, shift_both(): return lax.ppermute(array, ('env', 'rep'), perm)  44.1 us
    ppermute x15, starting transfers between devices, shift(): lax.ppermute(array, axis, [(i, (i + step) % size) for i in range(size)])  28.4 us
    ppermute x12, starting transfers between devices, shift_both(): return lax.ppermute(array, ('env', 'rep'), perm)  10 us
    pallas_call x8, Pallas kernels, products(): pl.pallas_call(functools.partial(products_body, z, pieces, spans), out_sh...  7.49 us
    ppermute x15, waiting for transfers between devices, shift(): lax.ppermute(array, axis, [(i, (i + step) % size) for i in range(size)])  6.89 us
    pallas_call x5, Pallas kernels, terms(): pl.pallas_call(functools.partial(terms_body, z, spans, so_far is not None...  5.08 us
    pallas_call x1, Pallas kernels, load(): pl.pallas_call(functools.partial(load_body, z), out_shape=[jax.ShapeDtype...  3.24 us
    pallas_call x1, Pallas kernels, gather_terms(): pl.pallas_call(functools.partial(gather_body, z, chunks, skip), out_shape...  3.23 us
  transfers between devices with their start and end apart: 27, of which 13 were waited for; matrix products, arithmetic and copies ran while one was open for 1% of the time, Pallas kernels for 18%

profile of v8, /device:TPU:0, one launch (start us, length us, event | category | flops | bytes accessed | tf_op | source)
XLA Modules:
  0.0 114.8 jit_solution(1624363763279565839)
XLA Ops:
  0.6 0.5 collective-permute-start.2
  1.1 0.1 collective-permute-start.3
  1.2 0.4 collective-permute-start.1
  1.7 2.6 %collective-permute-start = (s32[1,96]{1,0:T(1,128)}, s32[1,96]{1,0:T(1,128)S(1)}, u32[]{:S(2)}, u32[]{:S(2)}) collective-permute-start(s32[1,96]{1,0:T(1,128)} %partner.1), channel_id=1, source_target_pairs={{0,2},{2,0},{1,3},{3,1},{4,6},{6,4},{5,7},{7,5},{8,10},{10,8},{9,1... | collective-permute-start | bytes 1160 | tf_op jit(solution)/shard_map/ppermute | solution.py:491
  4.2 0.7 copy-done.3
  4.9 3.2 %shard_map.68 = (s32[74]{0:T(128)S(1)}, bf16[24,64,256]{2,1,0:T(8,128)(2,1)S(1)}, bf16[24,64,256]{2,1,0:T(8,128)(2,1)S(1)}, bf16[1,24,128,256]{3,2,1,0:T(8,128)(2,1)S(1)}) custom-call(s32[1,96]{1,0:T(1,128)S(1)} %copy-done.3, bf16[2,24,64,256]{3,2,1,0:T(8,128)(2,1)} %refs_3_.1, bf16[1,24,128,256]{3,2,1,0:T(8,128)(2,1)} %right.1), custom_call_target="tpu_custom_call" | custom-call | tf_op jit(solution)/shard_map/pallas_call | solution.py:99
  8.2 0.0 collective-permute-done.partner.refs_2_
  8.2 0.1 collective-permute-start.5
  8.3 1.5 %collective-permute-start.6 = (bf16[24,64,256]{2,1,0:T(8,128)(2,1)S(1)}, bf16[24,64,256]{2,1,0:T(8,128)(2,1)S(1)}, u32[]{:S(2)}, u32[]{:S(2)}) collective-permute-start(bf16[24,64,256]{2,1,0:T(8,128)(2,1)S(1)} %get-tuple-element.47), channel_id=1, source_target_pairs={{0,3},{1,2},{2,1},{3,0},{4,7},{5,6},{6,5},{7,4},{8,11},{9,10},{10,... | collective-permute-start | bytes 2359304 | tf_op jit(solution)/shard_map/ppermute | solution.py:499
  9.8 0.0 collective-permute-done.2.refs_2_
  9.8 1.2 %shard_map.71 = (bf16[6,128,256]{2,1,0:T(8,128)(2,1)S(1)}, bf16[6,128,256]{2,1,0:T(8,128)(2,1)S(1)}) custom-call(s32[74]{0:T(128)S(1)} %get-tuple-element.41.refs_0_.plan, bf16[1,24,128,256]{3,2,1,0:T(8,128)(2,1)S(1)} %get-tuple-element.42.refs_1_, bf16[1,24,128,256]{3,2,1,0:T(8,128)(2,1)S(1)} %collective-permute-done.2.refs_2_, ...), custom_call_target="tpu_custom_call" | custom-call | tf_op jit(solution)/shard_map/pallas_call | solution.py:183
  11.0 1.6 %collective-permute-start.7 = (bf16[6,128,256]{2,1,0:T(8,128)(2,1)S(1)}, bf16[6,128,256]{2,1,0:T(8,128)(2,1)S(1)}, u32[]{:S(2)}, u32[]{:S(2)}) collective-permute-start(bf16[6,128,256]{2,1,0:T(8,128)(2,1)S(1)} %get-tuple-element.46.refs_5_), channel_id=1, source_target_pairs={{0,4},{4,8},{8,12},{12,0},{1,5},{5,9},{9,13},{13,1},{2,6},{6,10},{... | collective-permute-start | bytes 1179656 | tf_op jit(solution)/shard_map/ppermute | solution.py:491
  12.6 2.2 %collective-permute-start.8 = (bf16[6,128,256]{2,1,0:T(8,128)(2,1)S(1)}, bf16[6,128,256]{2,1,0:T(8,128)(2,1)S(1)}, u32[]{:S(2)}, u32[]{:S(2)}) collective-permute-start(bf16[6,128,256]{2,1,0:T(8,128)(2,1)S(1)} %get-tuple-element.48), channel_id=1, source_target_pairs={{0,12},{4,0},{8,4},{12,8},{1,13},{5,1},{9,5},{13,9},{2,14},{6,2},{... | collective-permute-start | bytes 1179656 | tf_op jit(solution)/shard_map/ppermute | solution.py:491
  14.9 0.9 shard_map.72.refs_5_
  15.8 0.9 collective-permute-start.4
  16.7 1.3 %shard_map.69.refs_6_.refs_1_ = s32[74]{0:T(128)S(1)} custom-call(s32[1,96]{1,0:T(1,128)S(1)} %collective-permute-done.partner.refs_2_), custom_call_target="tpu_custom_call" | custom-call | tf_op jit(solution)/shard_map/pallas_call | solution.py:121
  18.0 0.9 shard_map.73.refs_5_.refs_3_
  18.9 9.7 %collective-permute-done.5.refs_3_.refs_7_ = bf16[24,64,256]{2,1,0:T(8,128)(2,1)S(1)} collective-permute-done((bf16[24,64,256]{2,1,0:T(8,128)(2,1)S(1)}, bf16[24,64,256]{2,1,0:T(8,128)(2,1)S(1)}, u32[]{:S(2)}, u32[]{:S(2)}) %collective-permute-start.5) | collective-permute-done | bytes 786464 | tf_op jit(solution)/shard_map/ppermute | solution.py:499
  28.6 15.3 %collective-permute-done.6.refs_4_.refs_8_ = bf16[24,64,256]{2,1,0:T(8,128)(2,1)S(1)} collective-permute-done((bf16[24,64,256]{2,1,0:T(8,128)(2,1)S(1)}, bf16[24,64,256]{2,1,0:T(8,128)(2,1)S(1)}, u32[]{:S(2)}, u32[]{:S(2)}) %collective-permute-start.6) | collective-permute-done | bytes 786464 | tf_op jit(solution)/shard_map/ppermute | solution.py:499
  43.9 0.9 shard_map.74.refs_0_
  44.9 0.0 copy-start
  44.9 1.6 %collective-permute-start.9 = (bf16[6,128,256]{2,1,0:T(8,128)(2,1)S(1)}, bf16[6,128,256]{2,1,0:T(8,128)(2,1)S(1)}, u32[]{:S(2)}, u32[]{:S(2)}) collective-permute-start(bf16[6,128,256]{2,1,0:T(8,128)(2,1)S(1)} %shard_map.75.refs_5_), channel_id=1, source_target_pairs={{0,4},{4,8},{8,12},{12,0},{1,5},{5,9},{9,13},{13,1},{2,6},{6,10},{... | collective-permute-start | bytes 1179656 | tf_op jit(solution)/shard_map/ppermute | solution.py:491
  46.6 0.9 shard_map.76.refs_4_
  47.5 1.1 shard_map.77
  48.6 0.6 collective-permute-start.13
  49.2 1.1 collective-permute-start.14
  50.3 0.9 shard_map.78.refs_5_.refs_0_
  51.2 0.9 shard_map.79.refs_5_.refs_0_
  52.1 0.8 shard_map.80.refs_1_
  52.9 3.0 %collective-permute-start.12 = (bf16[6,128,256]{2,1,0:T(8,128)(2,1)S(1)}, bf16[6,128,256]{2,1,0:T(8,128)(2,1)S(1)}, u32[]{:S(2)}, u32[]{:S(2)}) collective-permute-start(bf16[6,128,256]{2,1,0:T(8,128)(2,1)S(1)} %shard_map.81.refs_2_), channel_id=1, source_target_pairs={{0,12},{4,0},{8,4},{12,8},{1,13},{5,1},{9,5},{13,9},{2,14},{6,2},{... | collective-permute-start | bytes 1179656 | tf_op jit(solution)/shard_map/ppermute | solution.py:491
  56.0 3.0 %collective-permute-done.9.refs_3_.refs_4_ = bf16[6,128,256]{2,1,0:T(8,128)(2,1)S(1)} collective-permute-done((bf16[6,128,256]{2,1,0:T(8,128)(2,1)S(1)}, bf16[6,128,256]{2,1,0:T(8,128)(2,1)S(1)}, u32[]{:S(2)}, u32[]{:S(2)}) %collective-permute-start.9) | collective-permute-done | bytes 393248 | tf_op jit(solution)/shard_map/ppermute | solution.py:491
  58.9 0.5 collective-permute-done.14.refs_12_.refs_7_
  59.4 1.1 shard_map.83
  60.4 0.6 collective-permute-start.15
  61.0 1.5 %collective-permute-start.16 = (bf16[6,64,256]{2,1,0:T(8,128)(2,1)S(1)}, bf16[6,64,256]{2,1,0:T(8,128)(2,1)S(1)}, u32[]{:S(2)}, u32[]{:S(2)}) collective-permute-start(bf16[6,64,256]{2,1,0:T(8,128)(2,1)S(1)} %get-tuple-element.56), channel_id=1, source_target_pairs={{0,3},{1,2},{2,1},{3,0},{4,7},{5,6},{6,5},{7,4},{8,11},{9,10},{10,... | collective-permute-start | bytes 589832 | tf_op jit(solution)/shard_map/ppermute | solution.py:499
  62.6 2.9 %collective-permute-start.11 = (bf16[4,128,256]{2,1,0:T(8,128)(2,1)S(1)}, bf16[4,128,256]{2,1,0:T(8,128)(2,1)S(1)}, u32[]{:S(2)}, u32[]{:S(2)}) collective-permute-start(bf16[4,128,256]{2,1,0:T(8,128)(2,1)S(1)} %get-tuple-element.51.refs_10_), channel_id=1, source_target_pairs={{0,8},{4,12},{8,0},{12,4},{1,9},{5,13},{9,1},{13,5},{2,10},{6,14},... | collective-permute-start | bytes 786440 | tf_op jit(solution)/shard_map/ppermute | solution.py:491
  65.5 1.8 %collective-permute-done.12.refs_4_ = bf16[6,128,256]{2,1,0:T(8,128)(2,1)S(1)} collective-permute-done((bf16[6,128,256]{2,1,0:T(8,128)(2,1)S(1)}, bf16[6,128,256]{2,1,0:T(8,128)(2,1)S(1)}, u32[]{:S(2)}, u32[]{:S(2)}) %collective-permute-start.12) | collective-permute-done | bytes 393248 | tf_op jit(solution)/shard_map/ppermute | solution.py:491
  67.2 1.0 collective-permute-done.15.refs_10_.refs_9_
  68.3 3.7 %collective-permute-done.16.refs_11_.refs_10_ = bf16[6,64,256]{2,1,0:T(8,128)(2,1)S(1)} collective-permute-done((bf16[6,64,256]{2,1,0:T(8,128)(2,1)S(1)}, bf16[6,64,256]{2,1,0:T(8,128)(2,1)S(1)}, u32[]{:S(2)}, u32[]{:S(2)}) %collective-permute-start.16) | collective-permute-done | bytes 196640 | tf_op jit(solution)/shard_map/ppermute | solution.py:499
  72.0 1.1 shard_map.84
  73.1 0.6 collective-permute-start.17
  73.7 1.2 %collective-permute-start.18 = (bf16[6,64,256]{2,1,0:T(8,128)(2,1)S(1)}, bf16[6,64,256]{2,1,0:T(8,128)(2,1)S(1)}, u32[]{:S(2)}, u32[]{:S(2)}) collective-permute-start(bf16[6,64,256]{2,1,0:T(8,128)(2,1)S(1)} %get-tuple-element.59), channel_id=1, source_target_pairs={{0,3},{1,2},{2,1},{3,0},{4,7},{5,6},{6,5},{7,4},{8,11},{9,10},{10,... | collective-permute-start | bytes 589832 | tf_op jit(solution)/shard_map/ppermute | solution.py:499
  74.8 2.8 %collective-permute-start.10 = (bf16[2,128,256]{2,1,0:T(8,128)(2,1)S(1)}, bf16[2,128,256]{2,1,0:T(8,128)(2,1)S(1)}, u32[]{:S(2)}, u32[]{:S(2)}) collective-permute-start(bf16[2,128,256]{2,1,0:T(8,128)(2,1)S(1)} %get-tuple-element.50), channel_id=1, source_target_pairs={{0,8},{4,12},{8,0},{12,4},{1,9},{5,13},{9,1},{13,5},{2,10},{6,14},... | collective-permute-start | bytes 393224 | tf_op jit(solution)/shard_map/ppermute | solution.py:491
  77.6 3.2 %collective-permute-done.17.refs_10_.refs_12_ = bf16[6,64,256]{2,1,0:T(8,128)(2,1)S(1)} collective-permute-done((bf16[6,64,256]{2,1,0:T(8,128)(2,1)S(1)}, bf16[6,64,256]{2,1,0:T(8,128)(2,1)S(1)}, u32[]{:S(2)}, u32[]{:S(2)}) %collective-permute-start.17) | collective-permute-done | bytes 196640 | tf_op jit(solution)/shard_map/ppermute | solution.py:499
  80.9 3.1 %collective-permute-done.18.refs_11_.refs_13_ = bf16[6,64,256]{2,1,0:T(8,128)(2,1)S(1)} collective-permute-done((bf16[6,64,256]{2,1,0:T(8,128)(2,1)S(1)}, bf16[6,64,256]{2,1,0:T(8,128)(2,1)S(1)}, u32[]{:S(2)}, u32[]{:S(2)}) %collective-permute-start.18) | collective-permute-done | bytes 196640 | tf_op jit(solution)/shard_map/ppermute | solution.py:499
  83.9 0.9 shard_map.85
  84.9 0.7 collective-permute-start.19
  85.5 0.9 fusion.refs_10_
  86.4 0.0 collective-permute-done.10.refs_4_
  86.4 4.3 %collective-permute-done.19.refs_15_ = bf16[4,64,256]{2,1,0:T(8,128)(2,1)S(1)} collective-permute-done((bf16[4,64,256]{2,1,0:T(8,128)(2,1)S(1)}, bf16[4,64,256]{2,1,0:T(8,128)(2,1)S(1)}, u32[]{:S(2)}, u32[]{:S(2)}) %collective-permute-start.19) | collective-permute-done | bytes 131104 | tf_op jit(solution)/shard_map/ppermute | solution.py:499
  90.7 1.0 shard_map.86
  91.7 0.1 collective-permute-start.20
  91.8 0.7 collective-permute-start.21
  92.5 1.5 %collective-permute-start.22 = (bf16[144,256]{1,0:T(8,128)(2,1)S(1)}, bf16[144,256]{1,0:T(8,128)(2,1)S(1)}, u32[]{:S(2)}, u32[]{:S(2)}) collective-permute-start(bf16[144,256]{1,0:T(8,128)(2,1)S(1)} %get-tuple-element.75), channel_id=1, source_target_pairs={{0,2},{1,3},{2,0},{3,1},{4,6},{5,7},{6,4},{7,5},{8,10},{9,11},{10,... | collective-permute-start | bytes 221192 | tf_op jit(solution)/shard_map/ppermute | solution.py:499
  93.9 3.1 %collective-permute-done.21.refs_16_ = bf16[4,64,256]{2,1,0:T(8,128)(2,1)S(1)} collective-permute-done((bf16[4,64,256]{2,1,0:T(8,128)(2,1)S(1)}, bf16[4,64,256]{2,1,0:T(8,128)(2,1)S(1)}, u32[]{:S(2)}, u32[]{:S(2)}) %collective-permute-start.21) | collective-permute-done | bytes 131104 | tf_op jit(solution)/shard_map/ppermute | solution.py:499
  97.1 3.2 %shard_map.87 = (f32[2,24,64,256]{3,2,1,0:T(8,128)S(1)}, f32[2,24,64,256]{3,2,1,0:T(8,128)}) custom-call(s32[74]{0:T(128)S(1)} %get-tuple-element.41.refs_0_.plan, s32[74]{0:T(128)S(1)} %shard_map.69.refs_6_.refs_1_, f32[24]{0:T(128)S(1)} %copy-done.2, bf16[2,24,64,256]{3,2,1,0:T(8,128)(2,1)S(1)} %copy-done.1, ...), custom_call_target="tpu_custom_call" | custom-call | tf_op jit(solution)/shard_map/pallas_call | solution.py:365
  100.3 0.0 collective-permute-done.22.refs_5_.refs_1_
  100.3 0.6 shard_map.89.refs_0_
  100.9 1.9 %collective-permute-start.24 = (f32[8,256]{1,0:T(8,128)S(1)}, f32[8,256]{1,0:T(8,128)S(1)}, u32[]{:S(2)}, u32[]{:S(2)}) collective-permute-start(f32[8,256]{1,0:T(8,128)S(1)} %shard_map.89.refs_0_), channel_id=1, source_target_pairs={{0,4},{4,8},{8,12},{12,0},{1,5},{5,9},{9,13},{13,1},{2,6},{6,10},{... | collective-permute-start | bytes 24584 | tf_op jit(solution)/shard_map/ppermute | solution.py:491
  102.9 7.7 %collective-permute-start.25 = (f32[8,256]{1,0:T(8,128)S(1)}, f32[8,256]{1,0:T(8,128)S(1)}, u32[]{:S(2)}, u32[]{:S(2)}) collective-permute-start(f32[8,256]{1,0:T(8,128)S(1)} %shard_map.89.refs_0_), channel_id=1, source_target_pairs={{0,8},{4,12},{8,0},{12,4},{1,9},{5,13},{9,1},{13,5},{2,10},{6,14},... | collective-permute-start | bytes 24584 | tf_op jit(solution)/shard_map/ppermute | solution.py:491
  110.6 1.5 %shard_map.88 = (f32[2,24,64,256]{3,2,1,0:T(8,128)}, f32[8,128]{1,0:T(8,128)S(1)}) custom-call(s32[74]{0:T(128)S(1)} %get-tuple-element.41.refs_0_.plan, s32[74]{0:T(128)S(1)} %shard_map.69.refs_6_.refs_1_, f32[2,24,64,256]{3,2,1,0:T(8,128)S(1)} %get-tuple-element.73.refs_2_.refs_3_, ...), custom_call_target="tpu_custom_call", output_to_operand_aliasing={{0}: (7, {})} | custom-call | tf_op jit(solution)/shard_map/pallas_call | solution.py:410
  112.1 0.2 collective-permute-done.25.refs_2_
  112.3 1.9 %collective-permute-done.26.refs_3_ = f32[8,256]{1,0:T(8,128)S(1)} collective-permute-done((f32[8,256]{1,0:T(8,128)S(1)}, f32[8,256]{1,0:T(8,128)S(1)}, u32[]{:S(2)}, u32[]{:S(2)}) %collective-permute-start.26) | collective-permute-done | bytes 8224 | tf_op jit(solution)/shard_map/ppermute | solution.py:491
  114.2 0.5 shard_map.90
  (22 shorter events, 0.0 us)
Async XLA Ops:
  0.6 9.1 %collective-permute-start.2 = (bf16[1,24,128,256]{3,2,1,0:T(8,128)(2,1)}, bf16[1,24,128,256]{3,2,1,0:T(8,128)(2,1)S(1)}, u32[]{:S(2)}, u32[]{:S(2)}) collective-permute-start(bf16[1,24,128,256]{3,2,1,0:T(8,128)(2,1)} %right.1), channel_id=1, source_target_pairs={{0,1},{1,0},{2,3},{3,2},{4,5},{5,4},{6,7},{7,6},{8,9},{9,8},{10,11... | collective-permute-start | bytes 4718600 | tf_op jit(solution)/shard_map/ppermute | solution.py:491
  1.1 8.6 %collective-permute-start.3 = (bf16[2,24,64,256]{3,2,1,0:T(8,128)(2,1)}, bf16[2,24,64,256]{3,2,1,0:T(8,128)(2,1)S(1)}, u32[]{:S(2)}, u32[]{:S(2)}) collective-permute-start(bf16[2,24,64,256]{3,2,1,0:T(8,128)(2,1)} %refs_3_.1), channel_id=1, source_target_pairs={{0,1},{1,0},{2,3},{3,2},{4,5},{5,4},{6,7},{7,6},{8,9},{9,8},{10,11... | collective-permute-start | bytes 4718600 | tf_op jit(solution)/shard_map/ppermute | solution.py:491
  1.2 13.6 %collective-permute-start.1 = (bf16[1,24,128,256]{3,2,1,0:T(8,128)(2,1)}, bf16[1,24,128,256]{3,2,1,0:T(8,128)(2,1)S(1)}, u32[]{:S(2)}, u32[]{:S(2)}) collective-permute-start(bf16[1,24,128,256]{3,2,1,0:T(8,128)(2,1)} %refs_1_.9), channel_id=1, source_target_pairs={{0,1},{1,0},{2,3},{3,2},{4,5},{5,4},{6,7},{7,6},{8,9},{9,8},{10,11... | collective-permute-start | bytes 4718600 | tf_op jit(solution)/shard_map/ppermute | solution.py:491
  1.7 6.5 %collective-permute-start = (s32[1,96]{1,0:T(1,128)}, s32[1,96]{1,0:T(1,128)S(1)}, u32[]{:S(2)}, u32[]{:S(2)}) collective-permute-start(s32[1,96]{1,0:T(1,128)} %partner.1), channel_id=1, source_target_pairs={{0,2},{2,0},{1,3},{3,1},{4,6},{6,4},{5,7},{7,5},{8,10},{10,8},{9,1... | collective-permute-start | bytes 1160 | tf_op jit(solution)/shard_map/ppermute | solution.py:491
  4.2 0.7 copy-start.3
  8.2 20.5 %collective-permute-start.5 = (bf16[24,64,256]{2,1,0:T(8,128)(2,1)S(1)}, bf16[24,64,256]{2,1,0:T(8,128)(2,1)S(1)}, u32[]{:S(2)}, u32[]{:S(2)}) collective-permute-start(bf16[24,64,256]{2,1,0:T(8,128)(2,1)S(1)} %get-tuple-element.45.refs_3_.refs_5_), channel_id=1, source_target_pairs={{0,2},{1,3},{2,0},{3,1},{4,6},{5,7},{6,4},{7,5},{8,10},{9,11},{10,... | collective-permute-start | bytes 2359304 | tf_op jit(solution)/shard_map/ppermute | solution.py:499
  8.3 35.7 %collective-permute-start.6 = (bf16[24,64,256]{2,1,0:T(8,128)(2,1)S(1)}, bf16[24,64,256]{2,1,0:T(8,128)(2,1)S(1)}, u32[]{:S(2)}, u32[]{:S(2)}) collective-permute-start(bf16[24,64,256]{2,1,0:T(8,128)(2,1)S(1)} %get-tuple-element.47), channel_id=1, source_target_pairs={{0,3},{1,2},{2,1},{3,0},{4,7},{5,6},{6,5},{7,4},{8,11},{9,10},{10,... | collective-permute-start | bytes 2359304 | tf_op jit(solution)/shard_map/ppermute | solution.py:499
  11.0 33.9 %collective-permute-start.7 = (bf16[6,128,256]{2,1,0:T(8,128)(2,1)S(1)}, bf16[6,128,256]{2,1,0:T(8,128)(2,1)S(1)}, u32[]{:S(2)}, u32[]{:S(2)}) collective-permute-start(bf16[6,128,256]{2,1,0:T(8,128)(2,1)S(1)} %get-tuple-element.46.refs_5_), channel_id=1, source_target_pairs={{0,4},{4,8},{8,12},{12,0},{1,5},{5,9},{9,13},{13,1},{2,6},{6,10},{... | collective-permute-start | bytes 1179656 | tf_op jit(solution)/shard_map/ppermute | solution.py:491
  12.6 32.3 %collective-permute-start.8 = (bf16[6,128,256]{2,1,0:T(8,128)(2,1)S(1)}, bf16[6,128,256]{2,1,0:T(8,128)(2,1)S(1)}, u32[]{:S(2)}, u32[]{:S(2)}) collective-permute-start(bf16[6,128,256]{2,1,0:T(8,128)(2,1)S(1)} %get-tuple-element.48), channel_id=1, source_target_pairs={{0,12},{4,0},{8,4},{12,8},{1,13},{5,1},{9,5},{13,9},{2,14},{6,2},{... | collective-permute-start | bytes 1179656 | tf_op jit(solution)/shard_map/ppermute | solution.py:491
  15.8 37.1 %collective-permute-start.4 = (bf16[6,128,256]{2,1,0:T(8,128)(2,1)S(1)}, bf16[6,128,256]{2,1,0:T(8,128)(2,1)S(1)}, u32[]{:S(2)}, u32[]{:S(2)}) collective-permute-start(bf16[6,128,256]{2,1,0:T(8,128)(2,1)S(1)} %shard_map.72.refs_5_), channel_id=1, source_target_pairs={{0,8},{4,12},{8,0},{12,4},{1,9},{5,13},{9,1},{13,5},{2,10},{6,14},... | collective-permute-start | bytes 1179656 | tf_op jit(solution)/shard_map/ppermute | solution.py:491
  44.9 2.6 %copy-start = (bf16[1,24,128,256]{3,2,1,0:T(8,128)(2,1)S(1)}, bf16[1,24,128,256]{3,2,1,0:T(8,128)(2,1)}, u32[]{:S(2)}) copy-start(bf16[1,24,128,256]{3,2,1,0:T(8,128)(2,1)} %refs_1_.9) | copy-start | bytes 4718596
  44.9 14.0 %collective-permute-start.9 = (bf16[6,128,256]{2,1,0:T(8,128)(2,1)S(1)}, bf16[6,128,256]{2,1,0:T(8,128)(2,1)S(1)}, u32[]{:S(2)}, u32[]{:S(2)}) collective-permute-start(bf16[6,128,256]{2,1,0:T(8,128)(2,1)S(1)} %shard_map.75.refs_5_), channel_id=1, source_target_pairs={{0,4},{4,8},{8,12},{12,0},{1,5},{5,9},{9,13},{13,1},{2,6},{6,10},{... | collective-permute-start | bytes 1179656 | tf_op jit(solution)/shard_map/ppermute | solution.py:491
  48.6 10.3 %collective-permute-start.13 = (bf16[6,64,256]{2,1,0:T(8,128)(2,1)S(1)}, bf16[6,64,256]{2,1,0:T(8,128)(2,1)S(1)}, u32[]{:S(2)}, u32[]{:S(2)}) collective-permute-start(bf16[6,64,256]{2,1,0:T(8,128)(2,1)S(1)} %get-tuple-element.52), channel_id=1, source_target_pairs={{0,2},{1,3},{2,0},{3,1},{4,6},{5,7},{6,4},{7,5},{8,10},{9,11},{10,... | collective-permute-start | bytes 589832 | tf_op jit(solution)/shard_map/ppermute | solution.py:499
  49.2 10.2 %collective-permute-start.14 = (bf16[6,64,256]{2,1,0:T(8,128)(2,1)S(1)}, bf16[6,64,256]{2,1,0:T(8,128)(2,1)S(1)}, u32[]{:S(2)}, u32[]{:S(2)}) collective-permute-start(bf16[6,64,256]{2,1,0:T(8,128)(2,1)S(1)} %get-tuple-element.53), channel_id=1, source_target_pairs={{0,3},{1,2},{2,1},{3,0},{4,7},{5,6},{6,5},{7,4},{8,11},{9,10},{10,... | collective-permute-start | bytes 589832 | tf_op jit(solution)/shard_map/ppermute | solution.py:499
  52.9 14.3 %collective-permute-start.12 = (bf16[6,128,256]{2,1,0:T(8,128)(2,1)S(1)}, bf16[6,128,256]{2,1,0:T(8,128)(2,1)S(1)}, u32[]{:S(2)}, u32[]{:S(2)}) collective-permute-start(bf16[6,128,256]{2,1,0:T(8,128)(2,1)S(1)} %shard_map.81.refs_2_), channel_id=1, source_target_pairs={{0,12},{4,0},{8,4},{12,8},{1,13},{5,1},{9,5},{13,9},{2,14},{6,2},{... | collective-permute-start | bytes 1179656 | tf_op jit(solution)/shard_map/ppermute | solution.py:491
  60.4 7.8 %collective-permute-start.15 = (bf16[6,64,256]{2,1,0:T(8,128)(2,1)S(1)}, bf16[6,64,256]{2,1,0:T(8,128)(2,1)S(1)}, u32[]{:S(2)}, u32[]{:S(2)}) collective-permute-start(bf16[6,64,256]{2,1,0:T(8,128)(2,1)S(1)} %get-tuple-element.55), channel_id=1, source_target_pairs={{0,2},{1,3},{2,0},{3,1},{4,6},{5,7},{6,4},{7,5},{8,10},{9,11},{10,... | collective-permute-start | bytes 589832 | tf_op jit(solution)/shard_map/ppermute | solution.py:499
  61.0 10.9 %collective-permute-start.16 = (bf16[6,64,256]{2,1,0:T(8,128)(2,1)S(1)}, bf16[6,64,256]{2,1,0:T(8,128)(2,1)S(1)}, u32[]{:S(2)}, u32[]{:S(2)}) collective-permute-start(bf16[6,64,256]{2,1,0:T(8,128)(2,1)S(1)} %get-tuple-element.56), channel_id=1, source_target_pairs={{0,3},{1,2},{2,1},{3,0},{4,7},{5,6},{6,5},{7,4},{8,11},{9,10},{10,... | collective-permute-start | bytes 589832 | tf_op jit(solution)/shard_map/ppermute | solution.py:499
  62.6 15.0 %collective-permute-start.11 = (bf16[4,128,256]{2,1,0:T(8,128)(2,1)S(1)}, bf16[4,128,256]{2,1,0:T(8,128)(2,1)S(1)}, u32[]{:S(2)}, u32[]{:S(2)}) collective-permute-start(bf16[4,128,256]{2,1,0:T(8,128)(2,1)S(1)} %get-tuple-element.51.refs_10_), channel_id=1, source_target_pairs={{0,8},{4,12},{8,0},{12,4},{1,9},{5,13},{9,1},{13,5},{2,10},{6,14},... | collective-permute-start | bytes 786440 | tf_op jit(solution)/shard_map/ppermute | solution.py:491
  73.1 7.8 %collective-permute-start.17 = (bf16[6,64,256]{2,1,0:T(8,128)(2,1)S(1)}, bf16[6,64,256]{2,1,0:T(8,128)(2,1)S(1)}, u32[]{:S(2)}, u32[]{:S(2)}) collective-permute-start(bf16[6,64,256]{2,1,0:T(8,128)(2,1)S(1)} %get-tuple-element.58), channel_id=1, source_target_pairs={{0,2},{1,3},{2,0},{3,1},{4,6},{5,7},{6,4},{7,5},{8,10},{9,11},{10,... | collective-permute-start | bytes 589832 | tf_op jit(solution)/shard_map/ppermute | solution.py:499
  73.7 10.3 %collective-permute-start.18 = (bf16[6,64,256]{2,1,0:T(8,128)(2,1)S(1)}, bf16[6,64,256]{2,1,0:T(8,128)(2,1)S(1)}, u32[]{:S(2)}, u32[]{:S(2)}) collective-permute-start(bf16[6,64,256]{2,1,0:T(8,128)(2,1)S(1)} %get-tuple-element.59), channel_id=1, source_target_pairs={{0,3},{1,2},{2,1},{3,0},{4,7},{5,6},{6,5},{7,4},{8,11},{9,10},{10,... | collective-permute-start | bytes 589832 | tf_op jit(solution)/shard_map/ppermute | solution.py:499
  74.8 11.6 %collective-permute-start.10 = (bf16[2,128,256]{2,1,0:T(8,128)(2,1)S(1)}, bf16[2,128,256]{2,1,0:T(8,128)(2,1)S(1)}, u32[]{:S(2)}, u32[]{:S(2)}) collective-permute-start(bf16[2,128,256]{2,1,0:T(8,128)(2,1)S(1)} %get-tuple-element.50), channel_id=1, source_target_pairs={{0,8},{4,12},{8,0},{12,4},{1,9},{5,13},{9,1},{13,5},{2,10},{6,14},... | collective-permute-start | bytes 393224 | tf_op jit(solution)/shard_map/ppermute | solution.py:491
  83.9 1.6 %copy-start.1 = (bf16[2,24,64,256]{3,2,1,0:T(8,128)(2,1)S(1)}, bf16[2,24,64,256]{3,2,1,0:T(8,128)(2,1)}, u32[]{:S(2)}) copy-start(bf16[2,24,64,256]{3,2,1,0:T(8,128)(2,1)} %refs_3_.1) | copy-start | bytes 4718596
  83.9 1.6 %copy-start.2 = (f32[24]{0:T(128)S(1)}, f32[24]{0:T(128)}, u32[]{:S(2)}) copy-start(f32[24]{0:T(128)} %refs_2_.1) | copy-start | bytes 292
  84.9 5.9 %collective-permute-start.19 = (bf16[4,64,256]{2,1,0:T(8,128)(2,1)S(1)}, bf16[4,64,256]{2,1,0:T(8,128)(2,1)S(1)}, u32[]{:S(2)}, u32[]{:S(2)}) collective-permute-start(bf16[4,64,256]{2,1,0:T(8,128)(2,1)S(1)} %get-tuple-element.65), channel_id=1, source_target_pairs={{0,2},{1,3},{2,0},{3,1},{4,6},{5,7},{6,4},{7,5},{8,10},{9,11},{10,... | collective-permute-start | bytes 393224 | tf_op jit(solution)/shard_map/ppermute | solution.py:499
  91.7 5.4 %collective-permute-start.20 = (bf16[1552,256]{1,0:T(8,128)(2,1)S(1)}, bf16[1552,256]{1,0:T(8,128)(2,1)S(1)}, u32[]{:S(2)}, u32[]{:S(2)}) collective-permute-start(bf16[1552,256]{1,0:T(8,128)(2,1)S(1)} %get-tuple-element.66), channel_id=1, source_target_pairs={{0,1},{1,0},{2,3},{3,2},{4,5},{5,4},{6,7},{7,6},{8,9},{9,8},{10,11... | collective-permute-start | bytes 2383880 | tf_op jit(solution)/shard_map/ppermute | solution.py:491
  91.8 5.3 %collective-permute-start.21 = (bf16[4,64,256]{2,1,0:T(8,128)(2,1)S(1)}, bf16[4,64,256]{2,1,0:T(8,128)(2,1)S(1)}, u32[]{:S(2)}, u32[]{:S(2)}) collective-permute-start(bf16[4,64,256]{2,1,0:T(8,128)(2,1)S(1)} %get-tuple-element.71), channel_id=1, source_target_pairs={{0,3},{1,2},{2,1},{3,0},{4,7},{5,6},{6,5},{7,4},{8,11},{9,10},{10,... | collective-permute-start | bytes 393224 | tf_op jit(solution)/shard_map/ppermute | solution.py:499
  92.5 7.9 %collective-permute-start.22 = (bf16[144,256]{1,0:T(8,128)(2,1)S(1)}, bf16[144,256]{1,0:T(8,128)(2,1)S(1)}, u32[]{:S(2)}, u32[]{:S(2)}) collective-permute-start(bf16[144,256]{1,0:T(8,128)(2,1)S(1)} %get-tuple-element.75), channel_id=1, source_target_pairs={{0,2},{1,3},{2,0},{3,1},{4,6},{5,7},{6,4},{7,5},{8,10},{9,11},{10,... | collective-permute-start | bytes 221192 | tf_op jit(solution)/shard_map/ppermute | solution.py:499
  93.9 6.4 %collective-permute-start.23 = (bf16[144,256]{1,0:T(8,128)(2,1)S(1)}, bf16[144,256]{1,0:T(8,128)(2,1)S(1)}, u32[]{:S(2)}, u32[]{:S(2)}) collective-permute-start(bf16[144,256]{1,0:T(8,128)(2,1)S(1)} %get-tuple-element.76), channel_id=1, source_target_pairs={{0,3},{1,2},{2,1},{3,0},{4,7},{5,6},{6,5},{7,4},{8,11},{9,10},{10,... | collective-permute-start | bytes 221192 | tf_op jit(solution)/shard_map/ppermute | solution.py:499
  100.9 11.2 %collective-permute-start.24 = (f32[8,256]{1,0:T(8,128)S(1)}, f32[8,256]{1,0:T(8,128)S(1)}, u32[]{:S(2)}, u32[]{:S(2)}) collective-permute-start(f32[8,256]{1,0:T(8,128)S(1)} %shard_map.89.refs_0_), channel_id=1, source_target_pairs={{0,4},{4,8},{8,12},{12,0},{1,5},{5,9},{9,13},{13,1},{2,6},{6,10},{... | collective-permute-start | bytes 24584 | tf_op jit(solution)/shard_map/ppermute | solution.py:491
  102.9 9.4 %collective-permute-start.25 = (f32[8,256]{1,0:T(8,128)S(1)}, f32[8,256]{1,0:T(8,128)S(1)}, u32[]{:S(2)}, u32[]{:S(2)}) collective-permute-start(f32[8,256]{1,0:T(8,128)S(1)} %shard_map.89.refs_0_), channel_id=1, source_target_pairs={{0,8},{4,12},{8,0},{12,4},{1,9},{5,13},{9,1},{13,5},{2,10},{6,14},... | collective-permute-start | bytes 24584 | tf_op jit(solution)/shard_map/ppermute | solution.py:491
  110.6 3.7 %collective-permute-start.26 = (f32[8,256]{1,0:T(8,128)S(1)}, f32[8,256]{1,0:T(8,128)S(1)}, u32[]{:S(2)}, u32[]{:S(2)}) collective-permute-start(f32[8,256]{1,0:T(8,128)S(1)} %shard_map.89.refs_0_), channel_id=1, source_target_pairs={{0,12},{4,0},{8,4},{12,8},{1,13},{5,1},{9,5},{13,9},{2,14},{6,2},{... | collective-permute-start | bytes 24584 | tf_op jit(solution)/shard_map/ppermute | solution.py:491

commit v9 on v8

--- a/solution.py
+++ b/solution.py
@@ -580,18 +580,18 @@
     far3 = far_products(3, (dots,))
     far2 = far_products(2, far3[:1])
     far4 = far_products(4, far2[:1])
-    far3 = gate(far3, [far4[0], *near[2]])
+    far3 = gate(far3, [far4[0], *near[2], *arrived(0)[:1]])
     far[3] = across(far3, 3)
     far2 = gate([*far2, *far4], [far3[0], *far[1]])
     far[2], far[4] = across(far2[:each], 2), across(far2[each:], 2)
-    dots = send_terms(1, dots, None, (), (far2[0], *arrived(0)))
-    dots = send_terms(3, dots, None, (), arrived(1))
+    dots = send_terms(1, dots, None, (), (far2[0], *arrived(0)[1:]))
+    dots = send_terms(3, dots, None, (), arrived(1)[:1])
     own_block = vectors.astype(jnp.float32)
     own_sums = jnp.sum(energy[None, :, None, None] * own_block * own_block, axis=(1, 2, 3))
-    dots = send_terms(2, dots, None, (), arrived(3))
+    dots = send_terms(2, dots, None, (), arrived(1)[1:] + arrived(3)[:1])
     early = (0, 1, 3, 2)
     kept = [parts[g][0][1:] for g in early]
-    dots = send_terms(4, dots, own_sums, kept, arrived(2)[:1])
+    dots = send_terms(4, dots, own_sums, kept, arrived(3)[1:] + arrived(2)[:1])
     so_far, image = gather_terms(
         z,
         plans,

time: 115 us -> 107 us (0.930)
  waiting for transfers between devices: 51 us -> 44.3 us
    ppermute x12, waiting for transfers between devices: 44.1 us -> 38.4 us  [shift_both(): return lax.ppermute(array, ('env', 'rep'), perm)]
    ppermute x12, starting transfers between devices: 10 us -> 8.17 us  [shift_both(): return lax.ppermute(array, ('env', 'rep'), perm)]
  transfers between devices with their start and end apart: 27 -> 27, of which waited for: 13 -> 11; matrix products, arithmetic and copies ran while one was open for 1% -> 1% of each run, Pallas kernels for 18% -> 20%
where the time goes in v9:
time: 107 us
  waiting for transfers between devices  44.3 us (41%)
  starting transfers between devices  37.4 us (35%)
  Pallas kernels  23 us (21%)
    ppermute x12, waiting for transfers between devices, shift_both(): return lax.ppermute(array, ('env', 'rep'), perm)  38.4 us
    ppermute x15, starting transfers between devices, shift(): lax.ppermute(array, axis, [(i, (i + step) % size) for i in range(size)])  29.2 us
    ppermute x12, starting transfers between devices, shift_both(): return lax.ppermute(array, ('env', 'rep'), perm)  8.17 us
    pallas_call x8, Pallas kernels, products(): pl.pallas_call(functools.partial(products_body, z, pieces, spans), out_sh...  7.53 us
    ppermute x15, waiting for transfers between devices, shift(): lax.ppermute(array, axis, [(i, (i + step) % size) for i in range(size)])  5.97 us
    pallas_call x5, Pallas kernels, terms(): pl.pallas_call(functools.partial(terms_body, z, spans, so_far is not None...  5.13 us
    pallas_call x1, Pallas kernels, load(): pl.pallas_call(functools.partial(load_body, z), out_shape=[jax.ShapeDtype...  3.24 us
    pallas_call x1, Pallas kernels, gather_terms(): pl.pallas_call(functools.partial(gather_body, z, chunks, skip), out_shape...  3.23 us
  transfers between devices with their start and end apart: 27, of which 11 were waited for; matrix products, arithmetic and copies ran while one was open for 1% of the time, Pallas kernels for 20%

profile of v9, /device:TPU:0, one launch (start us, length us, event | category | flops | bytes accessed | tf_op | source)
XLA Modules:
  0.0 107.2 jit_solution(2784908561559131471)
XLA Ops:
  0.6 0.5 collective-permute-start.2
  1.1 0.1 collective-permute-start.3
  1.2 0.4 collective-permute-start.1
  1.7 2.6 %collective-permute-start = (s32[1,96]{1,0:T(1,128)}, s32[1,96]{1,0:T(1,128)S(1)}, u32[]{:S(2)}, u32[]{:S(2)}) collective-permute-start(s32[1,96]{1,0:T(1,128)} %partner.1), channel_id=1, source_target_pairs={{0,2},{2,0},{1,3},{3,1},{4,6},{6,4},{5,7},{7,5},{8,10},{10,8},{9,1... | collective-permute-start | bytes 1160 | tf_op jit(solution)/shard_map/ppermute | solution.py:491
  4.2 0.7 copy-done.3
  4.9 3.2 %shard_map.68 = (s32[74]{0:T(128)S(1)}, bf16[24,64,256]{2,1,0:T(8,128)(2,1)S(1)}, bf16[24,64,256]{2,1,0:T(8,128)(2,1)S(1)}, bf16[1,24,128,256]{3,2,1,0:T(8,128)(2,1)S(1)}) custom-call(s32[1,96]{1,0:T(1,128)S(1)} %copy-done.3, bf16[2,24,64,256]{3,2,1,0:T(8,128)(2,1)} %refs_3_.1, bf16[1,24,128,256]{3,2,1,0:T(8,128)(2,1)} %right.1), custom_call_target="tpu_custom_call" | custom-call | tf_op jit(solution)/shard_map/pallas_call | solution.py:99
  8.2 0.1 collective-permute-start.5
  8.3 1.5 %collective-permute-start.6 = (bf16[24,64,256]{2,1,0:T(8,128)(2,1)S(1)}, bf16[24,64,256]{2,1,0:T(8,128)(2,1)S(1)}, u32[]{:S(2)}, u32[]{:S(2)}) collective-permute-start(bf16[24,64,256]{2,1,0:T(8,128)(2,1)S(1)} %get-tuple-element.47), channel_id=1, source_target_pairs={{0,3},{1,2},{2,1},{3,0},{4,7},{5,6},{6,5},{7,4},{8,11},{9,10},{10,... | collective-permute-start | bytes 2359304 | tf_op jit(solution)/shard_map/ppermute | solution.py:499
  9.8 0.0 collective-permute-done.2.refs_2_
  9.8 0.0 collective-permute-done.3.refs_4_.refs_6_
  9.8 1.2 %shard_map.71 = (bf16[6,128,256]{2,1,0:T(8,128)(2,1)S(1)}, bf16[6,128,256]{2,1,0:T(8,128)(2,1)S(1)}) custom-call(s32[74]{0:T(128)S(1)} %get-tuple-element.41.refs_0_.plan, bf16[1,24,128,256]{3,2,1,0:T(8,128)(2,1)S(1)} %get-tuple-element.42.refs_1_, bf16[1,24,128,256]{3,2,1,0:T(8,128)(2,1)S(1)} %collective-permute-done.2.refs_2_, ...), custom_call_target="tpu_custom_call" | custom-call | tf_op jit(solution)/shard_map/pallas_call | solution.py:183
  11.0 1.6 %collective-permute-start.7 = (bf16[6,128,256]{2,1,0:T(8,128)(2,1)S(1)}, bf16[6,128,256]{2,1,0:T(8,128)(2,1)S(1)}, u32[]{:S(2)}, u32[]{:S(2)}) collective-permute-start(bf16[6,128,256]{2,1,0:T(8,128)(2,1)S(1)} %get-tuple-element.46.refs_5_), channel_id=1, source_target_pairs={{0,4},{4,8},{8,12},{12,0},{1,5},{5,9},{9,13},{13,1},{2,6},{6,10},{... | collective-permute-start | bytes 1179656 | tf_op jit(solution)/shard_map/ppermute | solution.py:491
  12.6 2.2 %collective-permute-start.8 = (bf16[6,128,256]{2,1,0:T(8,128)(2,1)S(1)}, bf16[6,128,256]{2,1,0:T(8,128)(2,1)S(1)}, u32[]{:S(2)}, u32[]{:S(2)}) collective-permute-start(bf16[6,128,256]{2,1,0:T(8,128)(2,1)S(1)} %get-tuple-element.48), channel_id=1, source_target_pairs={{0,12},{4,0},{8,4},{12,8},{1,13},{5,1},{9,5},{13,9},{2,14},{6,2},{... | collective-permute-start | bytes 1179656 | tf_op jit(solution)/shard_map/ppermute | solution.py:491
  14.9 0.9 shard_map.72.refs_5_
  15.8 0.9 collective-permute-start.4
  16.7 1.3 %shard_map.69.refs_6_.refs_1_ = s32[74]{0:T(128)S(1)} custom-call(s32[1,96]{1,0:T(1,128)S(1)} %collective-permute-done.partner.refs_2_), custom_call_target="tpu_custom_call" | custom-call | tf_op jit(solution)/shard_map/pallas_call | solution.py:121
  18.0 0.9 shard_map.73.refs_5_.refs_3_
  18.9 9.7 %collective-permute-done.5.refs_3_.refs_7_ = bf16[24,64,256]{2,1,0:T(8,128)(2,1)S(1)} collective-permute-done((bf16[24,64,256]{2,1,0:T(8,128)(2,1)S(1)}, bf16[24,64,256]{2,1,0:T(8,128)(2,1)S(1)}, u32[]{:S(2)}, u32[]{:S(2)}) %collective-permute-start.5) | collective-permute-done | bytes 786464 | tf_op jit(solution)/shard_map/ppermute | solution.py:499
  28.6 15.3 %collective-permute-done.6.refs_4_.refs_8_ = bf16[24,64,256]{2,1,0:T(8,128)(2,1)S(1)} collective-permute-done((bf16[24,64,256]{2,1,0:T(8,128)(2,1)S(1)}, bf16[24,64,256]{2,1,0:T(8,128)(2,1)S(1)}, u32[]{:S(2)}, u32[]{:S(2)}) %collective-permute-start.6) | collective-permute-done | bytes 786464 | tf_op jit(solution)/shard_map/ppermute | solution.py:499
  43.9 0.9 shard_map.74.refs_0_
  44.9 0.0 collective-permute-done.8.refs_2_.refs_3_
  44.9 0.0 copy-start
  44.9 1.6 %collective-permute-start.10 = (bf16[6,128,256]{2,1,0:T(8,128)(2,1)S(1)}, bf16[6,128,256]{2,1,0:T(8,128)(2,1)S(1)}, u32[]{:S(2)}, u32[]{:S(2)}) collective-permute-start(bf16[6,128,256]{2,1,0:T(8,128)(2,1)S(1)} %shard_map.75.refs_5_), channel_id=1, source_target_pairs={{0,4},{4,8},{8,12},{12,0},{1,5},{5,9},{9,13},{13,1},{2,6},{6,10},{... | collective-permute-start | bytes 1179656 | tf_op jit(solution)/shard_map/ppermute | solution.py:491
  46.6 0.9 shard_map.76.refs_4_
  47.5 1.1 shard_map.77
  48.6 0.6 collective-permute-start.9
  49.2 1.1 %collective-permute-start.14 = (bf16[6,64,256]{2,1,0:T(8,128)(2,1)S(1)}, bf16[6,64,256]{2,1,0:T(8,128)(2,1)S(1)}, u32[]{:S(2)}, u32[]{:S(2)}) collective-permute-start(bf16[6,64,256]{2,1,0:T(8,128)(2,1)S(1)} %get-tuple-element.53), channel_id=1, source_target_pairs={{0,3},{1,2},{2,1},{3,0},{4,7},{5,6},{6,5},{7,4},{8,11},{9,10},{10,... | collective-permute-start | bytes 589832 | tf_op jit(solution)/shard_map/ppermute | solution.py:499
  50.3 0.9 shard_map.78.refs_5_.refs_0_
  51.3 0.9 shard_map.79.refs_5_.refs_0_
  52.1 0.8 shard_map.80.refs_1_
  52.9 0.0 collective-permute-done.4.refs_2_.refs_3_
  52.9 3.5 %collective-permute-done.9.refs_3_.refs_6_ = bf16[6,64,256]{2,1,0:T(8,128)(2,1)S(1)} collective-permute-done((bf16[6,64,256]{2,1,0:T(8,128)(2,1)S(1)}, bf16[6,64,256]{2,1,0:T(8,128)(2,1)S(1)}, u32[]{:S(2)}, u32[]{:S(2)}) %collective-permute-start.9) | collective-permute-done | bytes 196640 | tf_op jit(solution)/shard_map/ppermute | solution.py:499
  56.4 2.5 %collective-permute-start.13 = (bf16[6,128,256]{2,1,0:T(8,128)(2,1)S(1)}, bf16[6,128,256]{2,1,0:T(8,128)(2,1)S(1)}, u32[]{:S(2)}, u32[]{:S(2)}) collective-permute-start(bf16[6,128,256]{2,1,0:T(8,128)(2,1)S(1)} %shard_map.81.refs_2_), channel_id=1, source_target_pairs={{0,12},{4,0},{8,4},{12,8},{1,13},{5,1},{9,5},{13,9},{2,14},{6,2},{... | collective-permute-start | bytes 1179656 | tf_op jit(solution)/shard_map/ppermute | solution.py:491
  58.8 0.0 collective-permute-done.10.refs_3_.refs_4_
  58.8 0.5 collective-permute-done.14.refs_11_.refs_7_
  59.4 1.1 shard_map.83
  60.5 0.6 collective-permute-start.15
  61.1 3.2 %collective-permute-start.12 = (bf16[4,128,256]{2,1,0:T(8,128)(2,1)S(1)}, bf16[4,128,256]{2,1,0:T(8,128)(2,1)S(1)}, u32[]{:S(2)}, u32[]{:S(2)}) collective-permute-start(bf16[4,128,256]{2,1,0:T(8,128)(2,1)S(1)} %get-tuple-element.52.refs_10_), channel_id=1, source_target_pairs={{0,8},{4,12},{8,0},{12,4},{1,9},{5,13},{9,1},{13,5},{2,10},{6,14},... | collective-permute-start | bytes 786440 | tf_op jit(solution)/shard_map/ppermute | solution.py:491
  64.3 0.9 collective-permute-start.16
  65.2 3.0 %collective-permute-done.15.refs_10_.refs_9_ = bf16[6,64,256]{2,1,0:T(8,128)(2,1)S(1)} collective-permute-done((bf16[6,64,256]{2,1,0:T(8,128)(2,1)S(1)}, bf16[6,64,256]{2,1,0:T(8,128)(2,1)S(1)}, u32[]{:S(2)}, u32[]{:S(2)}) %collective-permute-start.15) | collective-permute-done | bytes 196640 | tf_op jit(solution)/shard_map/ppermute | solution.py:499
  68.2 0.2 collective-permute-done.13.refs_4_
  68.4 1.1 shard_map.84
  69.5 0.6 collective-permute-start.17
  70.1 7.0 %collective-permute-start.11 = (bf16[2,128,256]{2,1,0:T(8,128)(2,1)S(1)}, bf16[2,128,256]{2,1,0:T(8,128)(2,1)S(1)}, u32[]{:S(2)}, u32[]{:S(2)}) collective-permute-start(bf16[2,128,256]{2,1,0:T(8,128)(2,1)S(1)} %get-tuple-element.51), channel_id=1, source_target_pairs={{0,8},{4,12},{8,0},{12,4},{1,9},{5,13},{9,1},{13,5},{2,10},{6,14},... | collective-permute-start | bytes 393224 | tf_op jit(solution)/shard_map/ppermute | solution.py:491
  77.1 4.7 %collective-permute-done.12.refs_4_ = bf16[4,128,256]{2,1,0:T(8,128)(2,1)S(1)} collective-permute-done((bf16[4,128,256]{2,1,0:T(8,128)(2,1)S(1)}, bf16[4,128,256]{2,1,0:T(8,128)(2,1)S(1)}, u32[]{:S(2)}, u32[]{:S(2)}) %collective-permute-start.12) | collective-permute-done | bytes 262176 | tf_op jit(solution)/shard_map/ppermute | solution.py:491
  81.8 0.9 shard_map.85
  82.8 0.6 collective-permute-start.19
  83.4 0.9 fusion.refs_10_
  84.3 0.4 collective-permute-done.11.refs_4_
  84.6 0.0 collective-permute-done.18.refs_15_.refs_13_
  84.7 3.2 %collective-permute-done.19.refs_16_.refs_15_ = bf16[4,64,256]{2,1,0:T(8,128)(2,1)S(1)} collective-permute-done((bf16[4,64,256]{2,1,0:T(8,128)(2,1)S(1)}, bf16[4,64,256]{2,1,0:T(8,128)(2,1)S(1)}, u32[]{:S(2)}, u32[]{:S(2)}) %collective-permute-start.19) | collective-permute-done | bytes 131104 | tf_op jit(solution)/shard_map/ppermute | solution.py:499
  87.8 1.0 shard_map.86
  88.8 0.1 collective-permute-start.20
  88.9 0.7 collective-permute-start.21
  89.6 1.5 %collective-permute-start.22 = (bf16[144,256]{1,0:T(8,128)(2,1)S(1)}, bf16[144,256]{1,0:T(8,128)(2,1)S(1)}, u32[]{:S(2)}, u32[]{:S(2)}) collective-permute-start(bf16[144,256]{1,0:T(8,128)(2,1)S(1)} %get-tuple-element.75), channel_id=1, source_target_pairs={{0,2},{1,3},{2,0},{3,1},{4,6},{5,7},{6,4},{7,5},{8,10},{9,11},{10,... | collective-permute-start | bytes 221192 | tf_op jit(solution)/shard_map/ppermute | solution.py:499
  91.0 3.1 %collective-permute-done.21.refs_16_ = bf16[4,64,256]{2,1,0:T(8,128)(2,1)S(1)} collective-permute-done((bf16[4,64,256]{2,1,0:T(8,128)(2,1)S(1)}, bf16[4,64,256]{2,1,0:T(8,128)(2,1)S(1)}, u32[]{:S(2)}, u32[]{:S(2)}) %collective-permute-start.21) | collective-permute-done | bytes 131104 | tf_op jit(solution)/shard_map/ppermute | solution.py:499
  94.2 3.2 %shard_map.87 = (f32[2,24,64,256]{3,2,1,0:T(8,128)S(1)}, f32[2,24,64,256]{3,2,1,0:T(8,128)}) custom-call(s32[74]{0:T(128)S(1)} %get-tuple-element.41.refs_0_.plan, s32[74]{0:T(128)S(1)} %shard_map.69.refs_6_.refs_1_, f32[24]{0:T(128)S(1)} %copy-done.2, bf16[2,24,64,256]{3,2,1,0:T(8,128)(2,1)S(1)} %copy-done.1, ...), custom_call_target="tpu_custom_call" | custom-call | tf_op jit(solution)/shard_map/pallas_call | solution.py:365
  97.5 0.6 shard_map.89.refs_0_
  98.0 4.0 %collective-permute-start.24 = (f32[8,256]{1,0:T(8,128)S(1)}, f32[8,256]{1,0:T(8,128)S(1)}, u32[]{:S(2)}, u32[]{:S(2)}) collective-permute-start(f32[8,256]{1,0:T(8,128)S(1)} %shard_map.89.refs_0_), channel_id=1, source_target_pairs={{0,4},{4,8},{8,12},{12,0},{1,5},{5,9},{9,13},{13,1},{2,6},{6,10},{... | collective-permute-start | bytes 24584 | tf_op jit(solution)/shard_map/ppermute | solution.py:491
  102.1 0.9 collective-permute-start.25
  102.9 1.6 %collective-permute-start.26 = (f32[8,256]{1,0:T(8,128)S(1)}, f32[8,256]{1,0:T(8,128)S(1)}, u32[]{:S(2)}, u32[]{:S(2)}) collective-permute-start(f32[8,256]{1,0:T(8,128)S(1)} %shard_map.89.refs_0_), channel_id=1, source_target_pairs={{0,12},{4,0},{8,4},{12,8},{1,13},{5,1},{9,5},{13,9},{2,14},{6,2},{... | collective-permute-start | bytes 24584 | tf_op jit(solution)/shard_map/ppermute | solution.py:491
  104.5 1.5 %shard_map.88 = (f32[2,24,64,256]{3,2,1,0:T(8,128)}, f32[8,128]{1,0:T(8,128)S(1)}) custom-call(s32[74]{0:T(128)S(1)} %get-tuple-element.41.refs_0_.plan, s32[74]{0:T(128)S(1)} %shard_map.69.refs_6_.refs_1_, f32[2,24,64,256]{3,2,1,0:T(8,128)S(1)} %get-tuple-element.73.refs_2_.refs_3_, ...), custom_call_target="tpu_custom_call", output_to_operand_aliasing={{0}: (7, {})} | custom-call | tf_op jit(solution)/shard_map/pallas_call | solution.py:410
  106.0 0.7 collective-permute-done.25.refs_2_
  106.7 0.5 shard_map.90
  (22 shorter events, 0.0 us)
Async XLA Ops:
  0.6 9.1 %collective-permute-start.2 = (bf16[1,24,128,256]{3,2,1,0:T(8,128)(2,1)}, bf16[1,24,128,256]{3,2,1,0:T(8,128)(2,1)S(1)}, u32[]{:S(2)}, u32[]{:S(2)}) collective-permute-start(bf16[1,24,128,256]{3,2,1,0:T(8,128)(2,1)} %right.1), channel_id=1, source_target_pairs={{0,1},{1,0},{2,3},{3,2},{4,5},{5,4},{6,7},{7,6},{8,9},{9,8},{10,11... | collective-permute-start | bytes 4718600 | tf_op jit(solution)/shard_map/ppermute | solution.py:491
  1.1 8.6 %collective-permute-start.3 = (bf16[2,24,64,256]{3,2,1,0:T(8,128)(2,1)}, bf16[2,24,64,256]{3,2,1,0:T(8,128)(2,1)S(1)}, u32[]{:S(2)}, u32[]{:S(2)}) collective-permute-start(bf16[2,24,64,256]{3,2,1,0:T(8,128)(2,1)} %refs_3_.1), channel_id=1, source_target_pairs={{0,1},{1,0},{2,3},{3,2},{4,5},{5,4},{6,7},{7,6},{8,9},{9,8},{10,11... | collective-permute-start | bytes 4718600 | tf_op jit(solution)/shard_map/ppermute | solution.py:491
  1.2 13.6 %collective-permute-start.1 = (bf16[1,24,128,256]{3,2,1,0:T(8,128)(2,1)}, bf16[1,24,128,256]{3,2,1,0:T(8,128)(2,1)S(1)}, u32[]{:S(2)}, u32[]{:S(2)}) collective-permute-start(bf16[1,24,128,256]{3,2,1,0:T(8,128)(2,1)} %refs_1_.9), channel_id=1, source_target_pairs={{0,1},{1,0},{2,3},{3,2},{4,5},{5,4},{6,7},{7,6},{8,9},{9,8},{10,11... | collective-permute-start | bytes 4718600 | tf_op jit(solution)/shard_map/ppermute | solution.py:491
  1.7 6.5 %collective-permute-start = (s32[1,96]{1,0:T(1,128)}, s32[1,96]{1,0:T(1,128)S(1)}, u32[]{:S(2)}, u32[]{:S(2)}) collective-permute-start(s32[1,96]{1,0:T(1,128)} %partner.1), channel_id=1, source_target_pairs={{0,2},{2,0},{1,3},{3,1},{4,6},{6,4},{5,7},{7,5},{8,10},{10,8},{9,1... | collective-permute-start | bytes 1160 | tf_op jit(solution)/shard_map/ppermute | solution.py:491
  4.2 0.7 copy-start.3
  8.2 20.5 %collective-permute-start.5 = (bf16[24,64,256]{2,1,0:T(8,128)(2,1)S(1)}, bf16[24,64,256]{2,1,0:T(8,128)(2,1)S(1)}, u32[]{:S(2)}, u32[]{:S(2)}) collective-permute-start(bf16[24,64,256]{2,1,0:T(8,128)(2,1)S(1)} %get-tuple-element.45.refs_3_.refs_5_), channel_id=1, source_target_pairs={{0,2},{1,3},{2,0},{3,1},{4,6},{5,7},{6,4},{7,5},{8,10},{9,11},{10,... | collective-permute-start | bytes 2359304 | tf_op jit(solution)/shard_map/ppermute | solution.py:499
  8.3 35.7 %collective-permute-start.6 = (bf16[24,64,256]{2,1,0:T(8,128)(2,1)S(1)}, bf16[24,64,256]{2,1,0:T(8,128)(2,1)S(1)}, u32[]{:S(2)}, u32[]{:S(2)}) collective-permute-start(bf16[24,64,256]{2,1,0:T(8,128)(2,1)S(1)} %get-tuple-element.47), channel_id=1, source_target_pairs={{0,3},{1,2},{2,1},{3,0},{4,7},{5,6},{6,5},{7,4},{8,11},{9,10},{10,... | collective-permute-start | bytes 2359304 | tf_op jit(solution)/shard_map/ppermute | solution.py:499
  11.0 33.9 %collective-permute-start.7 = (bf16[6,128,256]{2,1,0:T(8,128)(2,1)S(1)}, bf16[6,128,256]{2,1,0:T(8,128)(2,1)S(1)}, u32[]{:S(2)}, u32[]{:S(2)}) collective-permute-start(bf16[6,128,256]{2,1,0:T(8,128)(2,1)S(1)} %get-tuple-element.46.refs_5_), channel_id=1, source_target_pairs={{0,4},{4,8},{8,12},{12,0},{1,5},{5,9},{9,13},{13,1},{2,6},{6,10},{... | collective-permute-start | bytes 1179656 | tf_op jit(solution)/shard_map/ppermute | solution.py:491
  12.6 32.3 %collective-permute-start.8 = (bf16[6,128,256]{2,1,0:T(8,128)(2,1)S(1)}, bf16[6,128,256]{2,1,0:T(8,128)(2,1)S(1)}, u32[]{:S(2)}, u32[]{:S(2)}) collective-permute-start(bf16[6,128,256]{2,1,0:T(8,128)(2,1)S(1)} %get-tuple-element.48), channel_id=1, source_target_pairs={{0,12},{4,0},{8,4},{12,8},{1,13},{5,1},{9,5},{13,9},{2,14},{6,2},{... | collective-permute-start | bytes 1179656 | tf_op jit(solution)/shard_map/ppermute | solution.py:491
  15.8 37.1 %collective-permute-start.4 = (bf16[6,128,256]{2,1,0:T(8,128)(2,1)S(1)}, bf16[6,128,256]{2,1,0:T(8,128)(2,1)S(1)}, u32[]{:S(2)}, u32[]{:S(2)}) collective-permute-start(bf16[6,128,256]{2,1,0:T(8,128)(2,1)S(1)} %shard_map.72.refs_5_), channel_id=1, source_target_pairs={{0,8},{4,12},{8,0},{12,4},{1,9},{5,13},{9,1},{13,5},{2,10},{6,14},... | collective-permute-start | bytes 1179656 | tf_op jit(solution)/shard_map/ppermute | solution.py:491
  44.9 2.6 %copy-start = (bf16[1,24,128,256]{3,2,1,0:T(8,128)(2,1)S(1)}, bf16[1,24,128,256]{3,2,1,0:T(8,128)(2,1)}, u32[]{:S(2)}) copy-start(bf16[1,24,128,256]{3,2,1,0:T(8,128)(2,1)} %refs_1_.9) | copy-start | bytes 4718596
  44.9 13.9 %collective-permute-start.10 = (bf16[6,128,256]{2,1,0:T(8,128)(2,1)S(1)}, bf16[6,128,256]{2,1,0:T(8,128)(2,1)S(1)}, u32[]{:S(2)}, u32[]{:S(2)}) collective-permute-start(bf16[6,128,256]{2,1,0:T(8,128)(2,1)S(1)} %shard_map.75.refs_5_), channel_id=1, source_target_pairs={{0,4},{4,8},{8,12},{12,0},{1,5},{5,9},{9,13},{13,1},{2,6},{6,10},{... | collective-permute-start | bytes 1179656 | tf_op jit(solution)/shard_map/ppermute | solution.py:491
  48.6 7.8 %collective-permute-start.9 = (bf16[6,64,256]{2,1,0:T(8,128)(2,1)S(1)}, bf16[6,64,256]{2,1,0:T(8,128)(2,1)S(1)}, u32[]{:S(2)}, u32[]{:S(2)}) collective-permute-start(bf16[6,64,256]{2,1,0:T(8,128)(2,1)S(1)} %get-tuple-element.50), channel_id=1, source_target_pairs={{0,2},{1,3},{2,0},{3,1},{4,6},{5,7},{6,4},{7,5},{8,10},{9,11},{10,... | collective-permute-start | bytes 589832 | tf_op jit(solution)/shard_map/ppermute | solution.py:499
  49.2 10.2 %collective-permute-start.14 = (bf16[6,64,256]{2,1,0:T(8,128)(2,1)S(1)}, bf16[6,64,256]{2,1,0:T(8,128)(2,1)S(1)}, u32[]{:S(2)}, u32[]{:S(2)}) collective-permute-start(bf16[6,64,256]{2,1,0:T(8,128)(2,1)S(1)} %get-tuple-element.53), channel_id=1, source_target_pairs={{0,3},{1,2},{2,1},{3,0},{4,7},{5,6},{6,5},{7,4},{8,11},{9,10},{10,... | collective-permute-start | bytes 589832 | tf_op jit(solution)/shard_map/ppermute | solution.py:499
  56.4 12.0 %collective-permute-start.13 = (bf16[6,128,256]{2,1,0:T(8,128)(2,1)S(1)}, bf16[6,128,256]{2,1,0:T(8,128)(2,1)S(1)}, u32[]{:S(2)}, u32[]{:S(2)}) collective-permute-start(bf16[6,128,256]{2,1,0:T(8,128)(2,1)S(1)} %shard_map.81.refs_2_), channel_id=1, source_target_pairs={{0,12},{4,0},{8,4},{12,8},{1,13},{5,1},{9,5},{13,9},{2,14},{6,2},{... | collective-permute-start | bytes 1179656 | tf_op jit(solution)/shard_map/ppermute | solution.py:491
  60.5 7.8 %collective-permute-start.15 = (bf16[6,64,256]{2,1,0:T(8,128)(2,1)S(1)}, bf16[6,64,256]{2,1,0:T(8,128)(2,1)S(1)}, u32[]{:S(2)}, u32[]{:S(2)}) collective-permute-start(bf16[6,64,256]{2,1,0:T(8,128)(2,1)S(1)} %get-tuple-element.55), channel_id=1, source_target_pairs={{0,2},{1,3},{2,0},{3,1},{4,6},{5,7},{6,4},{7,5},{8,10},{9,11},{10,... | collective-permute-start | bytes 589832 | tf_op jit(solution)/shard_map/ppermute | solution.py:499
  61.1 20.8 %collective-permute-start.12 = (bf16[4,128,256]{2,1,0:T(8,128)(2,1)S(1)}, bf16[4,128,256]{2,1,0:T(8,128)(2,1)S(1)}, u32[]{:S(2)}, u32[]{:S(2)}) collective-permute-start(bf16[4,128,256]{2,1,0:T(8,128)(2,1)S(1)} %get-tuple-element.52.refs_10_), channel_id=1, source_target_pairs={{0,8},{4,12},{8,0},{12,4},{1,9},{5,13},{9,1},{13,5},{2,10},{6,14},... | collective-permute-start | bytes 786440 | tf_op jit(solution)/shard_map/ppermute | solution.py:491
  64.3 12.8 %collective-permute-start.16 = (bf16[6,64,256]{2,1,0:T(8,128)(2,1)S(1)}, bf16[6,64,256]{2,1,0:T(8,128)(2,1)S(1)}, u32[]{:S(2)}, u32[]{:S(2)}) collective-permute-start(bf16[6,64,256]{2,1,0:T(8,128)(2,1)S(1)} %get-tuple-element.57), channel_id=1, source_target_pairs={{0,3},{1,2},{2,1},{3,0},{4,7},{5,6},{6,5},{7,4},{8,11},{9,10},{10,... | collective-permute-start | bytes 589832 | tf_op jit(solution)/shard_map/ppermute | solution.py:499
  69.5 12.4 %collective-permute-start.17 = (bf16[6,64,256]{2,1,0:T(8,128)(2,1)S(1)}, bf16[6,64,256]{2,1,0:T(8,128)(2,1)S(1)}, u32[]{:S(2)}, u32[]{:S(2)}) collective-permute-start(bf16[6,64,256]{2,1,0:T(8,128)(2,1)S(1)} %get-tuple-element.58), channel_id=1, source_target_pairs={{0,2},{1,3},{2,0},{3,1},{4,6},{5,7},{6,4},{7,5},{8,10},{9,11},{10,... | collective-permute-start | bytes 589832 | tf_op jit(solution)/shard_map/ppermute | solution.py:499
  70.1 14.6 %collective-permute-start.11 = (bf16[2,128,256]{2,1,0:T(8,128)(2,1)S(1)}, bf16[2,128,256]{2,1,0:T(8,128)(2,1)S(1)}, u32[]{:S(2)}, u32[]{:S(2)}) collective-permute-start(bf16[2,128,256]{2,1,0:T(8,128)(2,1)S(1)} %get-tuple-element.51), channel_id=1, source_target_pairs={{0,8},{4,12},{8,0},{12,4},{1,9},{5,13},{9,1},{13,5},{2,10},{6,14},... | collective-permute-start | bytes 393224 | tf_op jit(solution)/shard_map/ppermute | solution.py:491
  77.1 7.6 %collective-permute-start.18 = (bf16[6,64,256]{2,1,0:T(8,128)(2,1)S(1)}, bf16[6,64,256]{2,1,0:T(8,128)(2,1)S(1)}, u32[]{:S(2)}, u32[]{:S(2)}) collective-permute-start(bf16[6,64,256]{2,1,0:T(8,128)(2,1)S(1)} %get-tuple-element.64), channel_id=1, source_target_pairs={{0,3},{1,2},{2,1},{3,0},{4,7},{5,6},{6,5},{7,4},{8,11},{9,10},{10,... | collective-permute-start | bytes 589832 | tf_op jit(solution)/shard_map/ppermute | solution.py:499
  81.8 1.6 %copy-start.1 = (bf16[2,24,64,256]{3,2,1,0:T(8,128)(2,1)S(1)}, bf16[2,24,64,256]{3,2,1,0:T(8,128)(2,1)}, u32[]{:S(2)}) copy-start(bf16[2,24,64,256]{3,2,1,0:T(8,128)(2,1)} %refs_3_.1) | copy-start | bytes 4718596
  81.8 1.6 %copy-start.2 = (f32[24]{0:T(128)S(1)}, f32[24]{0:T(128)}, u32[]{:S(2)}) copy-start(f32[24]{0:T(128)} %refs_2_.1) | copy-start | bytes 292
  82.8 5.0 %collective-permute-start.19 = (bf16[4,64,256]{2,1,0:T(8,128)(2,1)S(1)}, bf16[4,64,256]{2,1,0:T(8,128)(2,1)S(1)}, u32[]{:S(2)}, u32[]{:S(2)}) collective-permute-start(bf16[4,64,256]{2,1,0:T(8,128)(2,1)S(1)} %get-tuple-element.65), channel_id=1, source_target_pairs={{0,2},{1,3},{2,0},{3,1},{4,6},{5,7},{6,4},{7,5},{8,10},{9,11},{10,... | collective-permute-start | bytes 393224 | tf_op jit(solution)/shard_map/ppermute | solution.py:499
  88.8 5.4 %collective-permute-start.20 = (bf16[1552,256]{1,0:T(8,128)(2,1)S(1)}, bf16[1552,256]{1,0:T(8,128)(2,1)S(1)}, u32[]{:S(2)}, u32[]{:S(2)}) collective-permute-start(bf16[1552,256]{1,0:T(8,128)(2,1)S(1)} %get-tuple-element.66), channel_id=1, source_target_pairs={{0,1},{1,0},{2,3},{3,2},{4,5},{5,4},{6,7},{7,6},{8,9},{9,8},{10,11... | collective-permute-start | bytes 2383880 | tf_op jit(solution)/shard_map/ppermute | solution.py:491
  88.9 5.3 %collective-permute-start.21 = (bf16[4,64,256]{2,1,0:T(8,128)(2,1)S(1)}, bf16[4,64,256]{2,1,0:T(8,128)(2,1)S(1)}, u32[]{:S(2)}, u32[]{:S(2)}) collective-permute-start(bf16[4,64,256]{2,1,0:T(8,128)(2,1)S(1)} %get-tuple-element.71), channel_id=1, source_target_pairs={{0,3},{1,2},{2,1},{3,0},{4,7},{5,6},{6,5},{7,4},{8,11},{9,10},{10,... | collective-permute-start | bytes 393224 | tf_op jit(solution)/shard_map/ppermute | solution.py:499
  89.6 7.9 %collective-permute-start.22 = (bf16[144,256]{1,0:T(8,128)(2,1)S(1)}, bf16[144,256]{1,0:T(8,128)(2,1)S(1)}, u32[]{:S(2)}, u32[]{:S(2)}) collective-permute-start(bf16[144,256]{1,0:T(8,128)(2,1)S(1)} %get-tuple-element.75), channel_id=1, source_target_pairs={{0,2},{1,3},{2,0},{3,1},{4,6},{5,7},{6,4},{7,5},{8,10},{9,11},{10,... | collective-permute-start | bytes 221192 | tf_op jit(solution)/shard_map/ppermute | solution.py:499
  91.0 6.4 %collective-permute-start.23 = (bf16[144,256]{1,0:T(8,128)(2,1)S(1)}, bf16[144,256]{1,0:T(8,128)(2,1)S(1)}, u32[]{:S(2)}, u32[]{:S(2)}) collective-permute-start(bf16[144,256]{1,0:T(8,128)(2,1)S(1)} %get-tuple-element.76), channel_id=1, source_target_pairs={{0,3},{1,2},{2,1},{3,0},{4,7},{5,6},{6,5},{7,4},{8,11},{9,10},{10,... | collective-permute-start | bytes 221192 | tf_op jit(solution)/shard_map/ppermute | solution.py:499
  98.0 8.0 %collective-permute-start.24 = (f32[8,256]{1,0:T(8,128)S(1)}, f32[8,256]{1,0:T(8,128)S(1)}, u32[]{:S(2)}, u32[]{:S(2)}) collective-permute-start(f32[8,256]{1,0:T(8,128)S(1)} %shard_map.89.refs_0_), channel_id=1, source_target_pairs={{0,4},{4,8},{8,12},{12,0},{1,5},{5,9},{9,13},{13,1},{2,6},{6,10},{... | collective-permute-start | bytes 24584 | tf_op jit(solution)/shard_map/ppermute | solution.py:491
  102.1 4.6 %collective-permute-start.25 = (f32[8,256]{1,0:T(8,128)S(1)}, f32[8,256]{1,0:T(8,128)S(1)}, u32[]{:S(2)}, u32[]{:S(2)}) collective-permute-start(f32[8,256]{1,0:T(8,128)S(1)} %shard_map.89.refs_0_), channel_id=1, source_target_pairs={{0,8},{4,12},{8,0},{12,4},{1,9},{5,13},{9,1},{13,5},{2,10},{6,14},... | collective-permute-start | bytes 24584 | tf_op jit(solution)/shard_map/ppermute | solution.py:491
  102.9 3.7 %collective-permute-start.26 = (f32[8,256]{1,0:T(8,128)S(1)}, f32[8,256]{1,0:T(8,128)S(1)}, u32[]{:S(2)}, u32[]{:S(2)}) collective-permute-start(f32[8,256]{1,0:T(8,128)S(1)} %shard_map.89.refs_0_), channel_id=1, source_target_pairs={{0,12},{4,0},{8,4},{12,8},{1,13},{5,1},{9,5},{13,9},{2,14},{6,2},{... | collective-permute-start | bytes 24584 | tf_op jit(solution)/shard_map/ppermute | solution.py:491

commit v10 on v9

--- a/solution.py
+++ b/solution.py
@@ -79,7 +79,7 @@
     return copies
 
 
-def load_body(z, partner, vectors, right, plan, *refs):
+def load_body(z, partner, lane, vectors, right, plan, to_send, *refs):
     rows, block, count, sem = refs[: z.rep], refs[z.rep], refs[-2], refs[-1]
     core = lax.axis_index("rep")
     copies = []
@@ -90,19 +90,23 @@
     for copy in copies:
         copy.start()
     write_plan(z, partner, plan, count)
+    to_send[...] = lane[...]
     for copy in copies:
         copy.wait()
 
 
 def load(z, partner, vectors, right_env):
     row = jax.ShapeDtypeStruct(vectors.shape[1:], jnp.bfloat16)
-    plan, *made = pl.pallas_call(
+    plan, to_send, *made = pl.pallas_call(
         functools.partial(load_body, z),
-        out_shape=[jax.ShapeDtypeStruct((3 * z.flat + 2,), jnp.int32)]
+        out_shape=[
+            jax.ShapeDtypeStruct((3 * z.flat + 2,), jnp.int32),
+            jax.ShapeDtypeStruct(partner.shape, jnp.int32),
+        ]
         + [row] * z.rep
         + [jax.ShapeDtypeStruct(right_env.shape, jnp.bfloat16)],
-        in_specs=[SMEM, HBM, HBM],
-        out_specs=[SMEM] + [VMEM] * (z.rep + 1),
+        in_specs=[SMEM, VMEM, HBM, HBM],
+        out_specs=[SMEM] + [VMEM] * (z.rep + 2),
         scratch_shapes=[
             pltpu.SMEM((z.sector,), jnp.int32),
             pltpu.SemaphoreType.DMA((z.rep + 1, 4)),
@@ -111,10 +115,11 @@
         cost_estimate=BRIEF,
     )(
         partner,
+        partner,
         pltpu.with_memory_space_constraint(vectors, pltpu.HBM),
         pltpu.with_memory_space_constraint(right_env, pltpu.HBM),
     )
-    return plan, made[: z.rep], made[z.rep]
+    return plan, to_send, made[: z.rep], made[z.rep]
 
 
 def plan_only(z, partner):
@@ -208,13 +213,13 @@
     core, chip = plan[z.core], plan[z.chip]
     total = so_far[...] if chained else jnp.zeros((8, z.order), jnp.float32)
     n = 0
-    for d, (first, count, skip) in enumerate(spans):
+    for d, (first, count) in enumerate(spans):
         for i in range(count):
             slot = plan[z.target + first + i]
             for e in range(z.env):
                 place = lax.rem(chip + z.env - e, z.env)
                 if e == 0:
-                    lines = near[d][skip + i]
+                    lines = near[d][i]
                 else:
                     lines = far[d][i, (e - 1) * z.chip_rows : e * z.chip_rows]
                 pbuf[n, pl.ds(aligned(place, z.chip_rows), z.chip_rows)] = lines
@@ -300,7 +305,7 @@
 
 def for_terms(z, plans, parts, spans, action):
     n = 0
-    for first, count, _ in spans:
+    for first, count in spans:
         for i in range(count):
             for e, plan in enumerate(plans):
 
@@ -515,12 +520,10 @@
     each = z.sector // 4
     span = z.capacity
 
-    def spans_of(g, low=0, high=span):
-        return [((g * each + d) * span + low, high - low, low) for d in range(each)]
+    def spans_of(g):
+        return [((g * each + d) * span, span) for d in range(each)]
 
     chunks = {g: spans_of(g) for g in range(4)}
-    cut = 2 * span // 3
-    chunks[2], chunks[4] = spans_of(2, 0, cut), spans_of(2, cut, span)
 
     def around(array):
         return [array] + [shift(array, "rep", z.rep, s) for s in range(1, z.rep)]
@@ -529,11 +532,11 @@
         steps = [g * each + d for d in range(each)]
         return [shift(a, "sector", z.sector, k) if k else a for a, k in zip(arrays, steps)]
 
-    partners = [shift(partner, "env", z.env, e) for e in range(1, z.env)]
     vector_others = around(vectors)[1:]
     right_others = around(right_env)[1:]
     left = around(left_env)
-    plan, own, right_own = load(z, partner, vectors, right_env)
+    plan, to_send, own, right_own = load(z, partner, vectors, right_env)
+    partners = [shift(to_send, "env", z.env, e) for e in range(1, z.env)]
     own = gate(own, partners)
     right = [right_own] + right_others
     near_rows = [own[0]] + vector_others
@@ -543,13 +546,13 @@
     plans = [plan] + [plan_only(z, other) for other in partners]
 
     def near_products(g, after):
-        return products(z, plan, right, [near_rows], [c[:2] for c in spans_of(g)], after)
+        return products(z, plan, right, [near_rows], chunks[g], after)
 
     def far_products(g, after):
-        return products(z, plan, right, vec[1:], [c[:2] for c in chunks[g]], after)
+        return products(z, plan, right, vec[1:], chunks[g], after)
 
     near, far, parts = {}, {}, {}
-    spans = [piece[:2] for g in (1, 3) for piece in chunks[g]]
+    spans = chunks[1] + chunks[3]
     made = products(z, plan, right, [near_rows], spans)
     near[1], near[3] = across(made[:each], 1), across(made[each:], 3)
     made = near_products(2, (made[0], *left[1:]))
@@ -557,7 +560,7 @@
 
     def send_terms(g, so_far, own_sums, kept, after):
         made, folded = terms(
-            z, plan, left, near[2 if g == 4 else g], far[g], vec, chunks[g], so_far,
+            z, plan, left, near[g], far[g], vec, chunks[g], so_far,
             own_sums, kept, after
         )
         first = made[: z.rep]
@@ -579,32 +582,30 @@
     dots = send_terms(0, None, None, (), ())
     far3 = far_products(3, (dots,))
     far2 = far_products(2, far3[:1])
-    far4 = far_products(4, far2[:1])
-    far3 = gate(far3, [far4[0], *near[2], *arrived(0)[:1]])
+    far3 = gate(far3, [far2[0], *near[2], *arrived(0)[:1]])
     far[3] = across(far3, 3)
-    far2 = gate([*far2, *far4], [far3[0], *far[1]])
-    far[2], far[4] = across(far2[:each], 2), across(far2[each:], 2)
+    far2 = gate(far2, [far3[0], *far[1]])
+    far[2] = across(far2, 2)
     dots = send_terms(1, dots, None, (), (far2[0], *arrived(0)[1:]))
     dots = send_terms(3, dots, None, (), arrived(1)[:1])
     own_block = vectors.astype(jnp.float32)
     own_sums = jnp.sum(energy[None, :, None, None] * own_block * own_block, axis=(1, 2, 3))
-    dots = send_terms(2, dots, None, (), arrived(1)[1:] + arrived(3)[:1])
-    early = (0, 1, 3, 2)
+    early = (0, 1, 3)
     kept = [parts[g][0][1:] for g in early]
-    dots = send_terms(4, dots, own_sums, kept, arrived(3)[1:] + arrived(2)[:1])
+    dots = send_terms(2, dots, own_sums, kept, arrived(1)[1:] + arrived(3))
     so_far, image = gather_terms(
         z,
         plans,
         energy,
         vectors,
-        parts[4][0][1:],
-        sum(piece[1] for piece in chunks[4]),
+        parts[2][0][1:],
+        sum(piece[1] for piece in chunks[2]),
         [parts[g] for g in early],
         [chunks[g] for g in early],
         (dots,),
     )
-    sums = chip_sums(z, plan, dots, parts[4][0][1:] + arrived(4), (so_far,))
-    image, token = make_image(z, plans, so_far, image, parts[4], chunks[4])
+    sums = chip_sums(z, plan, dots, parts[2][0][1:] + arrived(2), (so_far,))
+    image, token = make_image(z, plans, so_far, image, parts[2], chunks[2])
     entries = z.slots * z.sector * z.order * z.order
     return (image, mean_over_sectors(z, sums, entries, (token,)))
 

time: 107 us -> 109 us (1.019)
  waiting for transfers between devices: 44.3 us -> 57.5 us
  starting transfers between devices: 37.4 us -> 26.4 us
    ppermute x15 -> x14, waiting for transfers between devices: 5.97 us -> 24.4 us  [shift(): lax.ppermute(array, axis, [(i, (i + step) % size) for i in range(size)])]
    ppermute x15 -> x14, starting transfers between devices: 29.2 us -> 17.7 us  [shift(): lax.ppermute(array, axis, [(i, (i + step) % size) for i in range(size)])]
    ppermute x12 -> x10, waiting for transfers between devices: 38.4 us -> 33 us  [shift_both(): return lax.ppermute(array, ('env', 'rep'), perm)]
    pallas_call x5 -> x4, Pallas kernels: 5.13 us -> 4.37 us  [terms(): pl.pallas_call(functools.partial(terms_body, z, spans, so_far is not None...]
    pallas_call x8 -> x7, Pallas kernels: 7.53 us -> 6.86 us  [products(): pl.pallas_call(functools.partial(products_body, z, pieces, spans), out_sh...]
    ppermute x12 -> x10, starting transfers between devices: 8.17 us -> 8.72 us  [shift_both(): return lax.ppermute(array, ('env', 'rep'), perm)]
  transfers between devices with their start and end apart: 27 -> 24, of which waited for: 11 -> 12; matrix products, arithmetic and copies ran while one was open for 1% -> 1% of each run, Pallas kernels for 20% -> 18%
where the time goes in v10:
time: 109 us; the launch traced here: 108 us
  waiting for transfers between devices  57.5 us (53%)
  starting transfers between devices  26.4 us (24%)
  Pallas kernels  22.1 us (20%)
    ppermute x10, waiting for transfers between devices, shift_both(): return lax.ppermute(array, ('env', 'rep'), perm)  33 us
    ppermute x14, waiting for transfers between devices, shift(): lax.ppermute(array, axis, [(i, (i + step) % size) for i in range(size)])  24.4 us
    ppermute x14, starting transfers between devices, shift(): lax.ppermute(array, axis, [(i, (i + step) % size) for i in range(size)])  17.7 us
    ppermute x10, starting transfers between devices, shift_both(): return lax.ppermute(array, ('env', 'rep'), perm)  8.72 us
    pallas_call x7, Pallas kernels, products(): pl.pallas_call(functools.partial(products_body, z, pieces, spans), out_sh...  6.86 us
    pallas_call x4, Pallas kernels, terms(): pl.pallas_call(functools.partial(terms_body, z, spans, so_far is not None...  4.37 us
    pallas_call x1, Pallas kernels, load(): pl.pallas_call(functools.partial(load_body, z), out_shape=[jax.ShapeDtype...  3.24 us
    pallas_call x1, Pallas kernels, gather_terms(): pl.pallas_call(functools.partial(gather_body, z, chunks, skip), out_shape...  3.07 us
  transfers between devices with their start and end apart: 24, of which 12 were waited for; matrix products, arithmetic and copies ran while one was open for 1% of the time, Pallas kernels for 18%

profile of v10, /device:TPU:0, one launch (start us, length us, event | category | flops | bytes accessed | tf_op | source)
XLA Modules:
  0.0 108.4 jit_solution(11074461622327958376)
XLA Ops:
  0.6 0.5 collective-permute-start.2
  1.1 0.1 collective-permute-start.3
  1.2 0.4 collective-permute-start.1
  1.7 0.7 copy-done.2
  2.3 3.2 %shard_map.68 = (s32[74]{0:T(128)S(1)}, s32[1,96]{1,0:T(1,128)S(1)}, bf16[24,64,256]{2,1,0:T(8,128)(2,1)S(1)}, bf16[24,64,256]{2,1,0:T(8,128)(2,1)S(1)}, bf16[1,24,128,256]{3,2,1,0:T(8,128)(2,1)S(1)}) custom-call(s32[1,96]{1,0:T(1,128)S(1)} %copy-done.2, s32[1,96]{1,0:T(1,128)S(1)} %copy-done.2, bf16[2,24,64,256]{3,2,1,0:T(8,128)(2,1)} %refs_3_.1, ...), custom_call_target="tpu_custom_call" | custom-call | tf_op jit(solution)/shard_map/pallas_call | solution.py:100
  5.6 2.6 %collective-permute-start = (s32[1,96]{1,0:T(1,128)S(1)}, s32[1,96]{1,0:T(1,128)S(1)}, u32[]{:S(2)}, u32[]{:S(2)}) collective-permute-start(s32[1,96]{1,0:T(1,128)S(1)} %get-tuple-element.36), channel_id=1, source_target_pairs={{0,2},{2,0},{1,3},{3,1},{4,6},{6,4},{5,7},{7,5},{8,10},{10,8},{9,1... | collective-permute-start | bytes 1160 | tf_op jit(solution)/shard_map/ppermute | solution.py:496
  8.2 1.5 %collective-permute-done.partner.refs_2_ = s32[1,96]{1,0:T(1,128)S(1)} collective-permute-done((s32[1,96]{1,0:T(1,128)S(1)}, s32[1,96]{1,0:T(1,128)S(1)}, u32[]{:S(2)}, u32[]{:S(2)}) %collective-permute-start) | collective-permute-done | bytes 416 | tf_op jit(solution)/shard_map/ppermute | solution.py:496
  9.7 2.0 %collective-permute-start.5 = (bf16[24,64,256]{2,1,0:T(8,128)(2,1)S(1)}, bf16[24,64,256]{2,1,0:T(8,128)(2,1)S(1)}, u32[]{:S(2)}, u32[]{:S(2)}) collective-permute-start(bf16[24,64,256]{2,1,0:T(8,128)(2,1)S(1)} %get-tuple-element.40.refs_3_.refs_5_), channel_id=1, source_target_pairs={{0,2},{1,3},{2,0},{3,1},{4,6},{5,7},{6,4},{7,5},{8,10},{9,11},{10,... | collective-permute-start | bytes 2359304 | tf_op jit(solution)/shard_map/ppermute | solution.py:504
  11.7 0.0 collective-permute-start.6
  11.7 0.0 collective-permute-done.2.refs_2_
  11.7 0.0 collective-permute-done.3.refs_4_.refs_6_
  11.8 1.2 %shard_map.71 = (bf16[6,128,256]{2,1,0:T(8,128)(2,1)S(1)}, bf16[6,128,256]{2,1,0:T(8,128)(2,1)S(1)}) custom-call(s32[74]{0:T(128)S(1)} %get-tuple-element.35.refs_0_.plan, bf16[1,24,128,256]{3,2,1,0:T(8,128)(2,1)S(1)} %get-tuple-element.37.refs_1_, bf16[1,24,128,256]{3,2,1,0:T(8,128)(2,1)S(1)} %collective-permute-done.2.refs_2_, ...), custom_call_target="tpu_custom_call" | custom-call | tf_op jit(solution)/shard_map/pallas_call | solution.py:188
  13.0 1.6 %collective-permute-start.7 = (bf16[6,128,256]{2,1,0:T(8,128)(2,1)S(1)}, bf16[6,128,256]{2,1,0:T(8,128)(2,1)S(1)}, u32[]{:S(2)}, u32[]{:S(2)}) collective-permute-start(bf16[6,128,256]{2,1,0:T(8,128)(2,1)S(1)} %get-tuple-element.41.refs_5_), channel_id=1, source_target_pairs={{0,4},{4,8},{8,12},{12,0},{1,5},{5,9},{9,13},{13,1},{2,6},{6,10},{... | collective-permute-start | bytes 1179656 | tf_op jit(solution)/shard_map/ppermute | solution.py:496
  14.6 2.3 %collective-permute-start.8 = (bf16[6,128,256]{2,1,0:T(8,128)(2,1)S(1)}, bf16[6,128,256]{2,1,0:T(8,128)(2,1)S(1)}, u32[]{:S(2)}, u32[]{:S(2)}) collective-permute-start(bf16[6,128,256]{2,1,0:T(8,128)(2,1)S(1)} %get-tuple-element.43), channel_id=1, source_target_pairs={{0,12},{4,0},{8,4},{12,8},{1,13},{5,1},{9,5},{13,9},{2,14},{6,2},{... | collective-permute-start | bytes 1179656 | tf_op jit(solution)/shard_map/ppermute | solution.py:496
  16.9 0.0 collective-permute-done.1.refs_6_.refs_2_
  16.9 0.9 shard_map.72.refs_5_
  17.8 0.9 collective-permute-start.4
  18.7 1.3 %shard_map.69.refs_6_.refs_1_ = s32[74]{0:T(128)S(1)} custom-call(s32[1,96]{1,0:T(1,128)S(1)} %collective-permute-done.partner.refs_2_), custom_call_target="tpu_custom_call" | custom-call | tf_op jit(solution)/shard_map/pallas_call | solution.py:126
  20.0 0.9 shard_map.73.refs_5_.refs_3_
  20.9 9.3 %collective-permute-done.5.refs_3_.refs_7_ = bf16[24,64,256]{2,1,0:T(8,128)(2,1)S(1)} collective-permute-done((bf16[24,64,256]{2,1,0:T(8,128)(2,1)S(1)}, bf16[24,64,256]{2,1,0:T(8,128)(2,1)S(1)}, u32[]{:S(2)}, u32[]{:S(2)}) %collective-permute-start.5) | collective-permute-done | bytes 786464 | tf_op jit(solution)/shard_map/ppermute | solution.py:504
  30.2 14.7 %collective-permute-done.6.refs_4_.refs_8_ = bf16[24,64,256]{2,1,0:T(8,128)(2,1)S(1)} collective-permute-done((bf16[24,64,256]{2,1,0:T(8,128)(2,1)S(1)}, bf16[24,64,256]{2,1,0:T(8,128)(2,1)S(1)}, u32[]{:S(2)}, u32[]{:S(2)}) %collective-permute-start.6) | collective-permute-done | bytes 786464 | tf_op jit(solution)/shard_map/ppermute | solution.py:504
  44.9 0.9 shard_map.74.refs_0_
  45.8 0.0 collective-permute-done.7.refs_1_.refs_3_
  45.8 0.0 collective-permute-done.8.refs_2_.refs_3_
  45.8 0.0 copy-start
  45.8 1.6 %collective-permute-start.10 = (bf16[6,128,256]{2,1,0:T(8,128)(2,1)S(1)}, bf16[6,128,256]{2,1,0:T(8,128)(2,1)S(1)}, u32[]{:S(2)}, u32[]{:S(2)}) collective-permute-start(bf16[6,128,256]{2,1,0:T(8,128)(2,1)S(1)} %shard_map.75.refs_5_), channel_id=1, source_target_pairs={{0,4},{4,8},{8,12},{12,0},{1,5},{5,9},{9,13},{13,1},{2,6},{6,10},{... | collective-permute-start | bytes 1179656 | tf_op jit(solution)/shard_map/ppermute | solution.py:496
  47.5 0.9 shard_map.76.refs_4_
  48.4 1.1 shard_map.77
  49.5 0.8 collective-permute-start.9
  50.3 1.1 %collective-permute-start.13 = (bf16[6,64,256]{2,1,0:T(8,128)(2,1)S(1)}, bf16[6,64,256]{2,1,0:T(8,128)(2,1)S(1)}, u32[]{:S(2)}, u32[]{:S(2)}) collective-permute-start(bf16[6,64,256]{2,1,0:T(8,128)(2,1)S(1)} %get-tuple-element.46), channel_id=1, source_target_pairs={{0,3},{1,2},{2,1},{3,0},{4,7},{5,6},{6,5},{7,4},{8,11},{9,10},{10,... | collective-permute-start | bytes 589832 | tf_op jit(solution)/shard_map/ppermute | solution.py:504
  51.4 0.9 shard_map.78.refs_5_.refs_0_
  52.4 0.9 shard_map.79.refs_1_.refs_0_
  53.3 6.9 %collective-permute-done.4.refs_2_.refs_3_ = bf16[6,128,256]{2,1,0:T(8,128)(2,1)S(1)} collective-permute-done((bf16[6,128,256]{2,1,0:T(8,128)(2,1)S(1)}, bf16[6,128,256]{2,1,0:T(8,128)(2,1)S(1)}, u32[]{:S(2)}, u32[]{:S(2)}) %collective-permute-start.4) | collective-permute-done | bytes 393248 | tf_op jit(solution)/shard_map/ppermute | solution.py:496
  60.3 0.0 collective-permute-done.9.refs_3_.refs_6_
  60.3 0.0 collective-permute-done.10.refs_2_.refs_4_
  60.3 0.5 collective-permute-done.13.refs_11_.refs_7_
  60.8 1.1 shard_map.82
  61.8 1.6 %collective-permute-start.14 = (bf16[6,64,256]{2,1,0:T(8,128)(2,1)S(1)}, bf16[6,64,256]{2,1,0:T(8,128)(2,1)S(1)}, u32[]{:S(2)}, u32[]{:S(2)}) collective-permute-start(bf16[6,64,256]{2,1,0:T(8,128)(2,1)S(1)} %get-tuple-element.48), channel_id=1, source_target_pairs={{0,2},{1,3},{2,0},{3,1},{4,6},{5,7},{6,4},{7,5},{8,10},{9,11},{10,... | collective-permute-start | bytes 589832 | tf_op jit(solution)/shard_map/ppermute | solution.py:504
  63.4 2.6 %collective-permute-start.11 = (bf16[6,128,256]{2,1,0:T(8,128)(2,1)S(1)}, bf16[6,128,256]{2,1,0:T(8,128)(2,1)S(1)}, u32[]{:S(2)}, u32[]{:S(2)}) collective-permute-start(bf16[6,128,256]{2,1,0:T(8,128)(2,1)S(1)} %shard_map.81.refs_10_), channel_id=1, source_target_pairs={{0,8},{4,12},{8,0},{12,4},{1,9},{5,13},{9,1},{13,5},{2,10},{6,14},... | collective-permute-start | bytes 1179656 | tf_op jit(solution)/shard_map/ppermute | solution.py:496
  66.0 0.3 collective-permute-start.15
  66.3 2.6 %collective-permute-done.14.refs_10_.refs_9_ = bf16[6,64,256]{2,1,0:T(8,128)(2,1)S(1)} collective-permute-done((bf16[6,64,256]{2,1,0:T(8,128)(2,1)S(1)}, bf16[6,64,256]{2,1,0:T(8,128)(2,1)S(1)}, u32[]{:S(2)}, u32[]{:S(2)}) %collective-permute-start.14) | collective-permute-done | bytes 196640 | tf_op jit(solution)/shard_map/ppermute | solution.py:504
  68.9 3.7 %collective-permute-done.12.refs_4_ = bf16[6,128,256]{2,1,0:T(8,128)(2,1)S(1)} collective-permute-done((bf16[6,128,256]{2,1,0:T(8,128)(2,1)S(1)}, bf16[6,128,256]{2,1,0:T(8,128)(2,1)S(1)}, u32[]{:S(2)}, u32[]{:S(2)}) %collective-permute-start.12) | collective-permute-done | bytes 393248 | tf_op jit(solution)/shard_map/ppermute | solution.py:496
  72.6 1.1 shard_map.83
  73.7 1.0 collective-permute-start.16
  74.7 0.0 collective-permute-start.17
  74.7 0.9 fusion.refs_10_
  75.5 0.0 collective-permute-done.15.refs_14_.refs_10_
  75.5 10.3 %collective-permute-done.11.refs_4_ = bf16[6,128,256]{2,1,0:T(8,128)(2,1)S(1)} collective-permute-done((bf16[6,128,256]{2,1,0:T(8,128)(2,1)S(1)}, bf16[6,128,256]{2,1,0:T(8,128)(2,1)S(1)}, u32[]{:S(2)}, u32[]{:S(2)}) %collective-permute-start.11) | collective-permute-done | bytes 393248 | tf_op jit(solution)/shard_map/ppermute | solution.py:496
  85.9 0.0 collective-permute-done.16.refs_15_.refs_12_
  85.9 0.0 collective-permute-done.17.refs_16_.refs_13_
  85.9 1.2 %shard_map.84 = (bf16[6,64,256]{2,1,0:T(8,128)(2,1)S(1)}, bf16[1552,256]{1,0:T(8,128)(2,1)S(1)}, bf16[400,256]{1,0:T(8,128)(2,1)S(1)}, bf16[400,256]{1,0:T(8,128)(2,1)S(1)}, bf16[16,256]{1,0:T(8,128)(2,1)S(1)}) custom-call(s32[74]{0:T(128)S(1)} %get-tuple-element.35.refs_0_.plan, bf16[1,24,128,256]{3,2,1,0:T(8,128)(2,1)S(1)} %copy-done, ...), custom_call_target="tpu_custom_call" | custom-call | tf_op jit(solution)/shard_map/pallas_call | solution.py:291
  87.1 0.1 collective-permute-start.18
  87.2 1.7 %collective-permute-start.19 = (bf16[400,256]{1,0:T(8,128)(2,1)S(1)}, bf16[400,256]{1,0:T(8,128)(2,1)S(1)}, u32[]{:S(2)}, u32[]{:S(2)}) collective-permute-start(bf16[400,256]{1,0:T(8,128)(2,1)S(1)} %get-tuple-element.63), channel_id=1, source_target_pairs={{0,2},{1,3},{2,0},{3,1},{4,6},{5,7},{6,4},{7,5},{8,10},{9,11},{10,... | collective-permute-start | bytes 614408 | tf_op jit(solution)/shard_map/ppermute | solution.py:504
  88.8 0.2 collective-permute-start.20
  89.0 0.4 collective-permute-done.18.refs_4_.refs_0_
  89.5 3.1 %shard_map.85 = (f32[2,24,64,256]{3,2,1,0:T(8,128)S(1)}, f32[2,24,64,256]{3,2,1,0:T(8,128)}) custom-call(s32[74]{0:T(128)S(1)} %get-tuple-element.35.refs_0_.plan, s32[74]{0:T(128)S(1)} %shard_map.69.refs_6_.refs_1_, f32[24]{0:T(128)S(1)} %copy-done.3, bf16[2,24,64,256]{3,2,1,0:T(8,128)(2,1)S(1)} %copy-done.1, ...), custom_call_target="tpu_custom_call" | custom-call | tf_op jit(solution)/shard_map/pallas_call | solution.py:370
  92.5 2.6 %collective-permute-done.19.refs_5_.refs_1_ = bf16[400,256]{1,0:T(8,128)(2,1)S(1)} collective-permute-done((bf16[400,256]{1,0:T(8,128)(2,1)S(1)}, bf16[400,256]{1,0:T(8,128)(2,1)S(1)}, u32[]{:S(2)}, u32[]{:S(2)}) %collective-permute-start.19) | collective-permute-done | bytes 204832 | tf_op jit(solution)/shard_map/ppermute | solution.py:504
  95.1 3.5 %collective-permute-done.20.refs_6_.refs_2_ = bf16[400,256]{1,0:T(8,128)(2,1)S(1)} collective-permute-done((bf16[400,256]{1,0:T(8,128)(2,1)S(1)}, bf16[400,256]{1,0:T(8,128)(2,1)S(1)}, u32[]{:S(2)}, u32[]{:S(2)}) %collective-permute-start.20) | collective-permute-done | bytes 204832 | tf_op jit(solution)/shard_map/ppermute | solution.py:504
  98.6 0.6 shard_map.87.refs_0_
  99.2 1.6 %collective-permute-start.21 = (f32[8,256]{1,0:T(8,128)S(1)}, f32[8,256]{1,0:T(8,128)S(1)}, u32[]{:S(2)}, u32[]{:S(2)}) collective-permute-start(f32[8,256]{1,0:T(8,128)S(1)} %shard_map.87.refs_0_), channel_id=1, source_target_pairs={{0,4},{4,8},{8,12},{12,0},{1,5},{5,9},{9,13},{13,1},{2,6},{6,10},{... | collective-permute-start | bytes 24584 | tf_op jit(solution)/shard_map/ppermute | solution.py:496
  100.8 3.4 %collective-permute-start.22 = (f32[8,256]{1,0:T(8,128)S(1)}, f32[8,256]{1,0:T(8,128)S(1)}, u32[]{:S(2)}, u32[]{:S(2)}) collective-permute-start(f32[8,256]{1,0:T(8,128)S(1)} %shard_map.87.refs_0_), channel_id=1, source_target_pairs={{0,8},{4,12},{8,0},{12,4},{1,9},{5,13},{9,1},{13,5},{2,10},{6,14},... | collective-permute-start | bytes 24584 | tf_op jit(solution)/shard_map/ppermute | solution.py:496
  104.2 2.2 %shard_map.86 = (f32[2,24,64,256]{3,2,1,0:T(8,128)}, f32[8,128]{1,0:T(8,128)S(1)}) custom-call(s32[74]{0:T(128)S(1)} %get-tuple-element.35.refs_0_.plan, s32[74]{0:T(128)S(1)} %shard_map.69.refs_6_.refs_1_, f32[2,24,64,256]{3,2,1,0:T(8,128)S(1)} %get-tuple-element.61.refs_2_.refs_3_, ...), custom_call_target="tpu_custom_call", output_to_operand_aliasing={{0}: (7, {})} | custom-call | tf_op jit(solution)/shard_map/pallas_call | solution.py:415
  106.4 1.4 %collective-permute-done.23.refs_3_ = f32[8,256]{1,0:T(8,128)S(1)} collective-permute-done((f32[8,256]{1,0:T(8,128)S(1)}, f32[8,256]{1,0:T(8,128)S(1)}, u32[]{:S(2)}, u32[]{:S(2)}) %collective-permute-start.23) | collective-permute-done | bytes 8224 | tf_op jit(solution)/shard_map/ppermute | solution.py:496
  107.8 0.5 shard_map.88
  (14 shorter events, 0.0 us)
Async XLA Ops:
  0.6 11.1 %collective-permute-start.2 = (bf16[1,24,128,256]{3,2,1,0:T(8,128)(2,1)}, bf16[1,24,128,256]{3,2,1,0:T(8,128)(2,1)S(1)}, u32[]{:S(2)}, u32[]{:S(2)}) collective-permute-start(bf16[1,24,128,256]{3,2,1,0:T(8,128)(2,1)} %right.1), channel_id=1, source_target_pairs={{0,1},{1,0},{2,3},{3,2},{4,5},{5,4},{6,7},{7,6},{8,9},{9,8},{10,11... | collective-permute-start | bytes 4718600 | tf_op jit(solution)/shard_map/ppermute | solution.py:496
  1.1 10.6 %collective-permute-start.3 = (bf16[2,24,64,256]{3,2,1,0:T(8,128)(2,1)}, bf16[2,24,64,256]{3,2,1,0:T(8,128)(2,1)S(1)}, u32[]{:S(2)}, u32[]{:S(2)}) collective-permute-start(bf16[2,24,64,256]{3,2,1,0:T(8,128)(2,1)} %refs_3_.1), channel_id=1, source_target_pairs={{0,1},{1,0},{2,3},{3,2},{4,5},{5,4},{6,7},{7,6},{8,9},{9,8},{10,11... | collective-permute-start | bytes 4718600 | tf_op jit(solution)/shard_map/ppermute | solution.py:496
  1.2 15.6 %collective-permute-start.1 = (bf16[1,24,128,256]{3,2,1,0:T(8,128)(2,1)}, bf16[1,24,128,256]{3,2,1,0:T(8,128)(2,1)S(1)}, u32[]{:S(2)}, u32[]{:S(2)}) collective-permute-start(bf16[1,24,128,256]{3,2,1,0:T(8,128)(2,1)} %refs_1_.7), channel_id=1, source_target_pairs={{0,1},{1,0},{2,3},{3,2},{4,5},{5,4},{6,7},{7,6},{8,9},{9,8},{10,11... | collective-permute-start | bytes 4718600 | tf_op jit(solution)/shard_map/ppermute | solution.py:496
  1.7 0.7 copy-start.2
  5.6 4.1 %collective-permute-start = (s32[1,96]{1,0:T(1,128)S(1)}, s32[1,96]{1,0:T(1,128)S(1)}, u32[]{:S(2)}, u32[]{:S(2)}) collective-permute-start(s32[1,96]{1,0:T(1,128)S(1)} %get-tuple-element.36), channel_id=1, source_target_pairs={{0,2},{2,0},{1,3},{3,1},{4,6},{6,4},{5,7},{7,5},{8,10},{10,8},{9,1... | collective-permute-start | bytes 1160 | tf_op jit(solution)/shard_map/ppermute | solution.py:496
  9.7 20.5 %collective-permute-start.5 = (bf16[24,64,256]{2,1,0:T(8,128)(2,1)S(1)}, bf16[24,64,256]{2,1,0:T(8,128)(2,1)S(1)}, u32[]{:S(2)}, u32[]{:S(2)}) collective-permute-start(bf16[24,64,256]{2,1,0:T(8,128)(2,1)S(1)} %get-tuple-element.40.refs_3_.refs_5_), channel_id=1, source_target_pairs={{0,2},{1,3},{2,0},{3,1},{4,6},{5,7},{6,4},{7,5},{8,10},{9,11},{10,... | collective-permute-start | bytes 2359304 | tf_op jit(solution)/shard_map/ppermute | solution.py:504
  11.7 33.1 %collective-permute-start.6 = (bf16[24,64,256]{2,1,0:T(8,128)(2,1)S(1)}, bf16[24,64,256]{2,1,0:T(8,128)(2,1)S(1)}, u32[]{:S(2)}, u32[]{:S(2)}) collective-permute-start(bf16[24,64,256]{2,1,0:T(8,128)(2,1)S(1)} %get-tuple-element.42), channel_id=1, source_target_pairs={{0,3},{1,2},{2,1},{3,0},{4,7},{5,6},{6,5},{7,4},{8,11},{9,10},{10,... | collective-permute-start | bytes 2359304 | tf_op jit(solution)/shard_map/ppermute | solution.py:504
  13.0 32.8 %collective-permute-start.7 = (bf16[6,128,256]{2,1,0:T(8,128)(2,1)S(1)}, bf16[6,128,256]{2,1,0:T(8,128)(2,1)S(1)}, u32[]{:S(2)}, u32[]{:S(2)}) collective-permute-start(bf16[6,128,256]{2,1,0:T(8,128)(2,1)S(1)} %get-tuple-element.41.refs_5_), channel_id=1, source_target_pairs={{0,4},{4,8},{8,12},{12,0},{1,5},{5,9},{9,13},{13,1},{2,6},{6,10},{... | collective-permute-start | bytes 1179656 | tf_op jit(solution)/shard_map/ppermute | solution.py:496
  14.6 31.2 %collective-permute-start.8 = (bf16[6,128,256]{2,1,0:T(8,128)(2,1)S(1)}, bf16[6,128,256]{2,1,0:T(8,128)(2,1)S(1)}, u32[]{:S(2)}, u32[]{:S(2)}) collective-permute-start(bf16[6,128,256]{2,1,0:T(8,128)(2,1)S(1)} %get-tuple-element.43), channel_id=1, source_target_pairs={{0,12},{4,0},{8,4},{12,8},{1,13},{5,1},{9,5},{13,9},{2,14},{6,2},{... | collective-permute-start | bytes 1179656 | tf_op jit(solution)/shard_map/ppermute | solution.py:496
  17.8 42.5 %collective-permute-start.4 = (bf16[6,128,256]{2,1,0:T(8,128)(2,1)S(1)}, bf16[6,128,256]{2,1,0:T(8,128)(2,1)S(1)}, u32[]{:S(2)}, u32[]{:S(2)}) collective-permute-start(bf16[6,128,256]{2,1,0:T(8,128)(2,1)S(1)} %shard_map.72.refs_5_), channel_id=1, source_target_pairs={{0,8},{4,12},{8,0},{12,4},{1,9},{5,13},{9,1},{13,5},{2,10},{6,14},... | collective-permute-start | bytes 1179656 | tf_op jit(solution)/shard_map/ppermute | solution.py:496
  45.8 2.6 %copy-start = (bf16[1,24,128,256]{3,2,1,0:T(8,128)(2,1)S(1)}, bf16[1,24,128,256]{3,2,1,0:T(8,128)(2,1)}, u32[]{:S(2)}) copy-start(bf16[1,24,128,256]{3,2,1,0:T(8,128)(2,1)} %refs_1_.7) | copy-start | bytes 4718596
  45.8 14.4 %collective-permute-start.10 = (bf16[6,128,256]{2,1,0:T(8,128)(2,1)S(1)}, bf16[6,128,256]{2,1,0:T(8,128)(2,1)S(1)}, u32[]{:S(2)}, u32[]{:S(2)}) collective-permute-start(bf16[6,128,256]{2,1,0:T(8,128)(2,1)S(1)} %shard_map.75.refs_5_), channel_id=1, source_target_pairs={{0,4},{4,8},{8,12},{12,0},{1,5},{5,9},{9,13},{13,1},{2,6},{6,10},{... | collective-permute-start | bytes 1179656 | tf_op jit(solution)/shard_map/ppermute | solution.py:496
  49.5 10.8 %collective-permute-start.9 = (bf16[6,64,256]{2,1,0:T(8,128)(2,1)S(1)}, bf16[6,64,256]{2,1,0:T(8,128)(2,1)S(1)}, u32[]{:S(2)}, u32[]{:S(2)}) collective-permute-start(bf16[6,64,256]{2,1,0:T(8,128)(2,1)S(1)} %get-tuple-element.45), channel_id=1, source_target_pairs={{0,2},{1,3},{2,0},{3,1},{4,6},{5,7},{6,4},{7,5},{8,10},{9,11},{10,... | collective-permute-start | bytes 589832 | tf_op jit(solution)/shard_map/ppermute | solution.py:504
  50.3 10.5 %collective-permute-start.13 = (bf16[6,64,256]{2,1,0:T(8,128)(2,1)S(1)}, bf16[6,64,256]{2,1,0:T(8,128)(2,1)S(1)}, u32[]{:S(2)}, u32[]{:S(2)}) collective-permute-start(bf16[6,64,256]{2,1,0:T(8,128)(2,1)S(1)} %get-tuple-element.46), channel_id=1, source_target_pairs={{0,3},{1,2},{2,1},{3,0},{4,7},{5,6},{6,5},{7,4},{8,11},{9,10},{10,... | collective-permute-start | bytes 589832 | tf_op jit(solution)/shard_map/ppermute | solution.py:504
  60.3 12.4 %collective-permute-start.12 = (bf16[6,128,256]{2,1,0:T(8,128)(2,1)S(1)}, bf16[6,128,256]{2,1,0:T(8,128)(2,1)S(1)}, u32[]{:S(2)}, u32[]{:S(2)}) collective-permute-start(bf16[6,128,256]{2,1,0:T(8,128)(2,1)S(1)} %shard_map.80.refs_1_), channel_id=1, source_target_pairs={{0,12},{4,0},{8,4},{12,8},{1,13},{5,1},{9,5},{13,9},{2,14},{6,2},{... | collective-permute-start | bytes 1179656 | tf_op jit(solution)/shard_map/ppermute | solution.py:496
  61.8 7.0 %collective-permute-start.14 = (bf16[6,64,256]{2,1,0:T(8,128)(2,1)S(1)}, bf16[6,64,256]{2,1,0:T(8,128)(2,1)S(1)}, u32[]{:S(2)}, u32[]{:S(2)}) collective-permute-start(bf16[6,64,256]{2,1,0:T(8,128)(2,1)S(1)} %get-tuple-element.48), channel_id=1, source_target_pairs={{0,2},{1,3},{2,0},{3,1},{4,6},{5,7},{6,4},{7,5},{8,10},{9,11},{10,... | collective-permute-start | bytes 589832 | tf_op jit(solution)/shard_map/ppermute | solution.py:504
  63.4 22.5 %collective-permute-start.11 = (bf16[6,128,256]{2,1,0:T(8,128)(2,1)S(1)}, bf16[6,128,256]{2,1,0:T(8,128)(2,1)S(1)}, u32[]{:S(2)}, u32[]{:S(2)}) collective-permute-start(bf16[6,128,256]{2,1,0:T(8,128)(2,1)S(1)} %shard_map.81.refs_10_), channel_id=1, source_target_pairs={{0,8},{4,12},{8,0},{12,4},{1,9},{5,13},{9,1},{13,5},{2,10},{6,14},... | collective-permute-start | bytes 1179656 | tf_op jit(solution)/shard_map/ppermute | solution.py:496
  66.0 9.5 %collective-permute-start.15 = (bf16[6,64,256]{2,1,0:T(8,128)(2,1)S(1)}, bf16[6,64,256]{2,1,0:T(8,128)(2,1)S(1)}, u32[]{:S(2)}, u32[]{:S(2)}) collective-permute-start(bf16[6,64,256]{2,1,0:T(8,128)(2,1)S(1)} %get-tuple-element.53), channel_id=1, source_target_pairs={{0,3},{1,2},{2,1},{3,0},{4,7},{5,6},{6,5},{7,4},{8,11},{9,10},{10,... | collective-permute-start | bytes 589832 | tf_op jit(solution)/shard_map/ppermute | solution.py:504
  72.6 2.1 %copy-start.1 = (bf16[2,24,64,256]{3,2,1,0:T(8,128)(2,1)S(1)}, bf16[2,24,64,256]{3,2,1,0:T(8,128)(2,1)}, u32[]{:S(2)}) copy-start(bf16[2,24,64,256]{3,2,1,0:T(8,128)(2,1)} %refs_3_.1) | copy-start | bytes 4718596
  72.6 2.1 %copy-start.3 = (f32[24]{0:T(128)S(1)}, f32[24]{0:T(128)}, u32[]{:S(2)}) copy-start(f32[24]{0:T(128)} %refs_2_.1) | copy-start | bytes 292
  73.7 12.2 %collective-permute-start.16 = (bf16[6,64,256]{2,1,0:T(8,128)(2,1)S(1)}, bf16[6,64,256]{2,1,0:T(8,128)(2,1)S(1)}, u32[]{:S(2)}, u32[]{:S(2)}) collective-permute-start(bf16[6,64,256]{2,1,0:T(8,128)(2,1)S(1)} %get-tuple-element.54), channel_id=1, source_target_pairs={{0,2},{1,3},{2,0},{3,1},{4,6},{5,7},{6,4},{7,5},{8,10},{9,11},{10,... | collective-permute-start | bytes 589832 | tf_op jit(solution)/shard_map/ppermute | solution.py:504
  74.7 11.2 %collective-permute-start.17 = (bf16[6,64,256]{2,1,0:T(8,128)(2,1)S(1)}, bf16[6,64,256]{2,1,0:T(8,128)(2,1)S(1)}, u32[]{:S(2)}, u32[]{:S(2)}) collective-permute-start(bf16[6,64,256]{2,1,0:T(8,128)(2,1)S(1)} %get-tuple-element.55), channel_id=1, source_target_pairs={{0,3},{1,2},{2,1},{3,0},{4,7},{5,6},{6,5},{7,4},{8,11},{9,10},{10,... | collective-permute-start | bytes 589832 | tf_op jit(solution)/shard_map/ppermute | solution.py:504
  87.1 2.4 %collective-permute-start.18 = (bf16[1552,256]{1,0:T(8,128)(2,1)S(1)}, bf16[1552,256]{1,0:T(8,128)(2,1)S(1)}, u32[]{:S(2)}, u32[]{:S(2)}) collective-permute-start(bf16[1552,256]{1,0:T(8,128)(2,1)S(1)} %get-tuple-element.56), channel_id=1, source_target_pairs={{0,1},{1,0},{2,3},{3,2},{4,5},{5,4},{6,7},{7,6},{8,9},{9,8},{10,11... | collective-permute-start | bytes 2383880 | tf_op jit(solution)/shard_map/ppermute | solution.py:496
  87.2 7.9 %collective-permute-start.19 = (bf16[400,256]{1,0:T(8,128)(2,1)S(1)}, bf16[400,256]{1,0:T(8,128)(2,1)S(1)}, u32[]{:S(2)}, u32[]{:S(2)}) collective-permute-start(bf16[400,256]{1,0:T(8,128)(2,1)S(1)} %get-tuple-element.63), channel_id=1, source_target_pairs={{0,2},{1,3},{2,0},{3,1},{4,6},{5,7},{6,4},{7,5},{8,10},{9,11},{10,... | collective-permute-start | bytes 614408 | tf_op jit(solution)/shard_map/ppermute | solution.py:504
  88.8 9.8 %collective-permute-start.20 = (bf16[400,256]{1,0:T(8,128)(2,1)S(1)}, bf16[400,256]{1,0:T(8,128)(2,1)S(1)}, u32[]{:S(2)}, u32[]{:S(2)}) collective-permute-start(bf16[400,256]{1,0:T(8,128)(2,1)S(1)} %get-tuple-element.64), channel_id=1, source_target_pairs={{0,3},{1,2},{2,1},{3,0},{4,7},{5,6},{6,5},{7,4},{8,11},{9,10},{10,... | collective-permute-start | bytes 614408 | tf_op jit(solution)/shard_map/ppermute | solution.py:504
  99.2 7.2 %collective-permute-start.21 = (f32[8,256]{1,0:T(8,128)S(1)}, f32[8,256]{1,0:T(8,128)S(1)}, u32[]{:S(2)}, u32[]{:S(2)}) collective-permute-start(f32[8,256]{1,0:T(8,128)S(1)} %shard_map.87.refs_0_), channel_id=1, source_target_pairs={{0,4},{4,8},{8,12},{12,0},{1,5},{5,9},{9,13},{13,1},{2,6},{6,10},{... | collective-permute-start | bytes 24584 | tf_op jit(solution)/shard_map/ppermute | solution.py:496
  100.8 5.6 %collective-permute-start.22 = (f32[8,256]{1,0:T(8,128)S(1)}, f32[8,256]{1,0:T(8,128)S(1)}, u32[]{:S(2)}, u32[]{:S(2)}) collective-permute-start(f32[8,256]{1,0:T(8,128)S(1)} %shard_map.87.refs_0_), channel_id=1, source_target_pairs={{0,8},{4,12},{8,0},{12,4},{1,9},{5,13},{9,1},{13,5},{2,10},{6,14},... | collective-permute-start | bytes 24584 | tf_op jit(solution)/shard_map/ppermute | solution.py:496
  104.2 3.7 %collective-permute-start.23 = (f32[8,256]{1,0:T(8,128)S(1)}, f32[8,256]{1,0:T(8,128)S(1)}, u32[]{:S(2)}, u32[]{:S(2)}) collective-permute-start(f32[8,256]{1,0:T(8,128)S(1)} %shard_map.87.refs_0_), channel_id=1, source_target_pairs={{0,12},{4,0},{8,4},{12,8},{1,13},{5,1},{9,5},{13,9},{2,14},{6,2},{... | collective-permute-start | bytes 24584 | tf_op jit(solution)/shard_map/ppermute | solution.py:496

commit v11 on v9

--- a/solution.py
+++ b/solution.py
@@ -529,19 +529,15 @@
         steps = [g * each + d for d in range(each)]
         return [shift(a, "sector", z.sector, k) if k else a for a, k in zip(arrays, steps)]
 
-    partners = [shift(partner, "env", z.env, e) for e in range(1, z.env)]
     vector_others = around(vectors)[1:]
     right_others = around(right_env)[1:]
     left = around(left_env)
     plan, own, right_own = load(z, partner, vectors, right_env)
-    own = gate(own, partners)
     right = [right_own] + right_others
     near_rows = [own[0]] + vector_others
     vec = [near_rows]
     for e in range(1, z.env):
         vec.append([shift_both(z, own[s], e, s) for s in range(z.rep)])
-    plans = [plan] + [plan_only(z, other) for other in partners]
-
     def near_products(g, after):
         return products(z, plan, right, [near_rows], [c[:2] for c in spans_of(g)], after)
 
@@ -572,23 +568,27 @@
         return [part for piece in parts[g][1:] for part in piece]
 
     near[0] = near_products(0, made[:1])
-    far1 = far_products(1, (near[0][0], *plans[1:]))
+    far1 = far_products(1, near[0][:1])
     far1 = gate(far1, [*near[1], *near[3]])
     far[1] = across(far1, 1)
     far[0] = far_products(0, far1[:1])
-    dots = send_terms(0, None, None, (), ())
+    partners = [shift(partner, "env", z.env, e) for e in range(1, z.env)]
+    plans = [plan] + [plan_only(z, other) for other in partners]
+    dots = send_terms(0, None, None, (), plans[1:])
     far3 = far_products(3, (dots,))
     far2 = far_products(2, far3[:1])
     far4 = far_products(4, far2[:1])
-    far3 = gate(far3, [far4[0], *near[2], *arrived(0)[:1]])
+    far3 = gate(far3, [far4[0], *near[2]])
     far[3] = across(far3, 3)
-    far2 = gate([*far2, *far4], [far3[0], *far[1]])
-    far[2], far[4] = across(far2[:each], 2), across(far2[each:], 2)
-    dots = send_terms(1, dots, None, (), (far2[0], *arrived(0)[1:]))
+    far2 = gate(far2, [far3[0], *far[1]])
+    far[2] = across(far2, 2)
+    far4 = gate(far4, far[2])
+    far[4] = across(far4, 2)
+    dots = send_terms(1, dots, None, (), (far2[0], *arrived(0)))
     dots = send_terms(3, dots, None, (), arrived(1)[:1])
     own_block = vectors.astype(jnp.float32)
     own_sums = jnp.sum(energy[None, :, None, None] * own_block * own_block, axis=(1, 2, 3))
-    dots = send_terms(2, dots, None, (), arrived(1)[1:] + arrived(3)[:1])
+    dots = send_terms(2, dots, None, (), [far4[0]] + arrived(1)[1:] + arrived(3)[:1])
     early = (0, 1, 3, 2)
     kept = [parts[g][0][1:] for g in early]
     dots = send_terms(4, dots, own_sums, kept, arrived(3)[1:] + arrived(2)[:1])

time: 107 us -> 107 us (level)
  starting transfers between devices: 37.4 us -> 29.3 us
  waiting for transfers between devices: 44.3 us -> 51.6 us
    ppermute x15, waiting for transfers between devices: 5.97 us -> 17.2 us  [shift(): lax.ppermute(array, axis, [(i, (i + step) % size) for i in range(size)])]
    ppermute x15, starting transfers between devices: 29.2 us -> 18.6 us  [shift(): lax.ppermute(array, axis, [(i, (i + step) % size) for i in range(size)])]
    ppermute x12, waiting for transfers between devices: 38.4 us -> 34.4 us  [shift_both(): return lax.ppermute(array, ('env', 'rep'), perm)]
    ppermute x12, starting transfers between devices: 8.17 us -> 10.7 us  [shift_both(): return lax.ppermute(array, ('env', 'rep'), perm)]
  transfers between devices with their start and end apart: 27 -> 27, of which waited for: 11 -> 12; matrix products, arithmetic and copies ran while one was open for 1% -> 1% of each run, Pallas kernels for 20% -> 20%
where the time goes in v11:
time: 107 us
  waiting for transfers between devices  51.6 us (48%)
  starting transfers between devices  29.3 us (27%)
  Pallas kernels  23 us (21%)
  local copies, waits for them, and re-layouts  1.22 us (1%)
    ppermute x12, waiting for transfers between devices, shift_both(): return lax.ppermute(array, ('env', 'rep'), perm)  34.4 us
    ppermute x15, starting transfers between devices, shift(): lax.ppermute(array, axis, [(i, (i + step) % size) for i in range(size)])  18.6 us
    ppermute x15, waiting for transfers between devices, shift(): lax.ppermute(array, axis, [(i, (i + step) % size) for i in range(size)])  17.2 us
    ppermute x12, starting transfers between devices, shift_both(): return lax.ppermute(array, ('env', 'rep'), perm)  10.7 us
    pallas_call x8, Pallas kernels, products(): pl.pallas_call(functools.partial(products_body, z, pieces, spans), out_sh...  7.49 us
    pallas_call x5, Pallas kernels, terms(): pl.pallas_call(functools.partial(terms_body, z, spans, so_far is not None...  5.1 us
    pallas_call x1, Pallas kernels, load(): pl.pallas_call(functools.partial(load_body, z), out_shape=[jax.ShapeDtype...  3.24 us
    pallas_call x1, Pallas kernels, gather_terms(): pl.pallas_call(functools.partial(gather_body, z, chunks, skip), out_shape...  3.23 us
  transfers between devices with their start and end apart: 27, of which 12 were waited for; matrix products, arithmetic and copies ran while one was open for 1% of the time, Pallas kernels for 20%

profile of v11, /device:TPU:0, one launch (start us, length us, event | category | flops | bytes accessed | tf_op | source)
XLA Modules:
  0.0 106.8 jit_solution(12095100270661688880)
XLA Ops:
  0.6 0.5 collective-permute-start.2
  1.1 0.1 collective-permute-start.3
  1.2 0.4 collective-permute-start.1
  1.7 0.7 copy-done.3
  2.3 3.2 %shard_map.68 = (s32[74]{0:T(128)S(1)}, bf16[24,64,256]{2,1,0:T(8,128)(2,1)S(1)}, bf16[24,64,256]{2,1,0:T(8,128)(2,1)S(1)}, bf16[1,24,128,256]{3,2,1,0:T(8,128)(2,1)S(1)}) custom-call(s32[1,96]{1,0:T(1,128)S(1)} %copy-done.3, bf16[2,24,64,256]{3,2,1,0:T(8,128)(2,1)} %refs_3_.1, bf16[1,24,128,256]{3,2,1,0:T(8,128)(2,1)} %right.1), custom_call_target="tpu_custom_call" | custom-call | tf_op jit(solution)/shard_map/pallas_call | solution.py:99
  5.6 2.6 %collective-permute-start.5 = (bf16[24,64,256]{2,1,0:T(8,128)(2,1)S(1)}, bf16[24,64,256]{2,1,0:T(8,128)(2,1)S(1)}, u32[]{:S(2)}, u32[]{:S(2)}) collective-permute-start(bf16[24,64,256]{2,1,0:T(8,128)(2,1)S(1)} %get-tuple-element.39.refs_3_.refs_5_), channel_id=1, source_target_pairs={{0,2},{1,3},{2,0},{3,1},{4,6},{5,7},{6,4},{7,5},{8,10},{9,11},{10,... | collective-permute-start | bytes 2359304 | tf_op jit(solution)/shard_map/ppermute | solution.py:499
  8.2 0.1 collective-permute-start.6
  8.3 0.0 collective-permute-done.3.refs_4_.refs_6_
  8.3 1.2 %shard_map.70 = (bf16[6,128,256]{2,1,0:T(8,128)(2,1)S(1)}, bf16[6,128,256]{2,1,0:T(8,128)(2,1)S(1)}) custom-call(s32[74]{0:T(128)S(1)} %get-tuple-element.37.refs_0_.plan, bf16[1,24,128,256]{3,2,1,0:T(8,128)(2,1)S(1)} %get-tuple-element.38.refs_1_, bf16[1,24,128,256]{3,2,1,0:T(8,128)(2,1)S(1)} %collective-permute-done.2.refs_2_, ...), custom_call_target="tpu_custom_call" | custom-call | tf_op jit(solution)/shard_map/pallas_call | solution.py:183
  9.5 1.8 %collective-permute-start.7 = (bf16[6,128,256]{2,1,0:T(8,128)(2,1)S(1)}, bf16[6,128,256]{2,1,0:T(8,128)(2,1)S(1)}, u32[]{:S(2)}, u32[]{:S(2)}) collective-permute-start(bf16[6,128,256]{2,1,0:T(8,128)(2,1)S(1)} %get-tuple-element.40.refs_5_), channel_id=1, source_target_pairs={{0,4},{4,8},{8,12},{12,0},{1,5},{5,9},{9,13},{13,1},{2,6},{6,10},{... | collective-permute-start | bytes 1179656 | tf_op jit(solution)/shard_map/ppermute | solution.py:491
  11.3 2.1 %collective-permute-start.8 = (bf16[6,128,256]{2,1,0:T(8,128)(2,1)S(1)}, bf16[6,128,256]{2,1,0:T(8,128)(2,1)S(1)}, u32[]{:S(2)}, u32[]{:S(2)}) collective-permute-start(bf16[6,128,256]{2,1,0:T(8,128)(2,1)S(1)} %get-tuple-element.42), channel_id=1, source_target_pairs={{0,12},{4,0},{8,4},{12,8},{1,13},{5,1},{9,5},{13,9},{2,14},{6,2},{... | collective-permute-start | bytes 1179656 | tf_op jit(solution)/shard_map/ppermute | solution.py:491
  13.4 0.9 shard_map.71.refs_5_
  14.4 1.0 collective-permute-start.4
  15.4 0.9 shard_map.72.refs_5_.refs_3_
  16.3 10.3 %collective-permute-done.5.refs_3_.refs_7_ = bf16[24,64,256]{2,1,0:T(8,128)(2,1)S(1)} collective-permute-done((bf16[24,64,256]{2,1,0:T(8,128)(2,1)S(1)}, bf16[24,64,256]{2,1,0:T(8,128)(2,1)S(1)}, u32[]{:S(2)}, u32[]{:S(2)}) %collective-permute-start.5) | collective-permute-done | bytes 786464 | tf_op jit(solution)/shard_map/ppermute | solution.py:499
  26.6 16.3 %collective-permute-done.6.refs_4_.refs_8_ = bf16[24,64,256]{2,1,0:T(8,128)(2,1)S(1)} collective-permute-done((bf16[24,64,256]{2,1,0:T(8,128)(2,1)S(1)}, bf16[24,64,256]{2,1,0:T(8,128)(2,1)S(1)}, u32[]{:S(2)}, u32[]{:S(2)}) %collective-permute-start.6) | collective-permute-done | bytes 786464 | tf_op jit(solution)/shard_map/ppermute | solution.py:499
  42.9 0.9 shard_map.73.refs_0_
  43.9 1.7 %collective-permute-start.9 = (bf16[6,128,256]{2,1,0:T(8,128)(2,1)S(1)}, bf16[6,128,256]{2,1,0:T(8,128)(2,1)S(1)}, u32[]{:S(2)}, u32[]{:S(2)}) collective-permute-start(bf16[6,128,256]{2,1,0:T(8,128)(2,1)S(1)} %shard_map.74.refs_5_), channel_id=1, source_target_pairs={{0,4},{4,8},{8,12},{12,0},{1,5},{5,9},{9,13},{13,1},{2,6},{6,10},{... | collective-permute-start | bytes 1179656 | tf_op jit(solution)/shard_map/ppermute | solution.py:491
  45.6 1.5 %collective-permute-start = (s32[1,96]{1,0:T(1,128)S(1)}, s32[1,96]{1,0:T(1,128)S(1)}, u32[]{:S(2)}, u32[]{:S(2)}) collective-permute-start(s32[1,96]{1,0:T(1,128)S(1)} %copy-done.3), channel_id=1, source_target_pairs={{0,2},{2,0},{1,3},{3,1},{4,6},{6,4},{5,7},{7,5},{8,10},{10,8},{9,1... | collective-permute-start | bytes 1160 | tf_op jit(solution)/shard_map/ppermute | solution.py:491
  47.1 2.1 %collective-permute-done.partner = s32[1,96]{1,0:T(1,128)S(1)} collective-permute-done((s32[1,96]{1,0:T(1,128)S(1)}, s32[1,96]{1,0:T(1,128)S(1)}, u32[]{:S(2)}, u32[]{:S(2)}) %collective-permute-start) | collective-permute-done | bytes 416 | tf_op jit(solution)/shard_map/ppermute | solution.py:491
  49.1 1.3 %shard_map.69.refs_9_.refs_1_ = s32[74]{0:T(128)S(1)} custom-call(s32[1,96]{1,0:T(1,128)S(1)} %collective-permute-done.partner), custom_call_target="tpu_custom_call" | custom-call | tf_op jit(solution)/shard_map/pallas_call | solution.py:121
  50.4 0.0 copy-start
  50.4 0.9 shard_map.75.refs_4_
  51.4 0.5 copy-done
  51.8 1.1 shard_map.76
  52.9 1.6 %collective-permute-start.13 = (bf16[6,64,256]{2,1,0:T(8,128)(2,1)S(1)}, bf16[6,64,256]{2,1,0:T(8,128)(2,1)S(1)}, u32[]{:S(2)}, u32[]{:S(2)}) collective-permute-start(bf16[6,64,256]{2,1,0:T(8,128)(2,1)S(1)} %get-tuple-element.44), channel_id=1, source_target_pairs={{0,2},{1,3},{2,0},{3,1},{4,6},{5,7},{6,4},{7,5},{8,10},{9,11},{10,... | collective-permute-start | bytes 589832 | tf_op jit(solution)/shard_map/ppermute | solution.py:499
  54.5 0.9 shard_map.77.refs_5_.refs_0_
  55.4 0.9 shard_map.78.refs_5_.refs_0_
  56.3 0.8 shard_map.79.refs_1_.refs_0_
  57.1 2.3 %collective-permute-start.12 = (bf16[6,128,256]{2,1,0:T(8,128)(2,1)S(1)}, bf16[6,128,256]{2,1,0:T(8,128)(2,1)S(1)}, u32[]{:S(2)}, u32[]{:S(2)}) collective-permute-start(bf16[6,128,256]{2,1,0:T(8,128)(2,1)S(1)} %shard_map.80.refs_1_), channel_id=1, source_target_pairs={{0,12},{4,0},{8,4},{12,8},{1,13},{5,1},{9,5},{13,9},{2,14},{6,2},{... | collective-permute-start | bytes 1179656 | tf_op jit(solution)/shard_map/ppermute | solution.py:491
  59.4 1.0 collective-permute-done.13.refs_11_.refs_6_
  60.4 1.8 %collective-permute-done.14.refs_12_.refs_7_ = bf16[6,64,256]{2,1,0:T(8,128)(2,1)S(1)} collective-permute-done((bf16[6,64,256]{2,1,0:T(8,128)(2,1)S(1)}, bf16[6,64,256]{2,1,0:T(8,128)(2,1)S(1)}, u32[]{:S(2)}, u32[]{:S(2)}) %collective-permute-start.14) | collective-permute-done | bytes 196640 | tf_op jit(solution)/shard_map/ppermute | solution.py:499
  62.1 1.1 shard_map.83
  63.2 0.7 collective-permute-start.15
  63.9 3.2 %collective-permute-start.10 = (bf16[4,128,256]{2,1,0:T(8,128)(2,1)S(1)}, bf16[4,128,256]{2,1,0:T(8,128)(2,1)S(1)}, u32[]{:S(2)}, u32[]{:S(2)}) collective-permute-start(bf16[4,128,256]{2,1,0:T(8,128)(2,1)S(1)} %shard_map.81.refs_10_), channel_id=1, source_target_pairs={{0,8},{4,12},{8,0},{12,4},{1,9},{5,13},{9,1},{13,5},{2,10},{6,14},... | collective-permute-start | bytes 786440 | tf_op jit(solution)/shard_map/ppermute | solution.py:491
  67.0 1.3 %collective-permute-start.16 = (bf16[6,64,256]{2,1,0:T(8,128)(2,1)S(1)}, bf16[6,64,256]{2,1,0:T(8,128)(2,1)S(1)}, u32[]{:S(2)}, u32[]{:S(2)}) collective-permute-start(bf16[6,64,256]{2,1,0:T(8,128)(2,1)S(1)} %get-tuple-element.49), channel_id=1, source_target_pairs={{0,3},{1,2},{2,1},{3,0},{4,7},{5,6},{6,5},{7,4},{8,11},{9,10},{10,... | collective-permute-start | bytes 589832 | tf_op jit(solution)/shard_map/ppermute | solution.py:499
  68.3 0.5 collective-permute-done.12.refs_4_
  68.8 2.1 %collective-permute-done.15.refs_10_.refs_9_ = bf16[6,64,256]{2,1,0:T(8,128)(2,1)S(1)} collective-permute-done((bf16[6,64,256]{2,1,0:T(8,128)(2,1)S(1)}, bf16[6,64,256]{2,1,0:T(8,128)(2,1)S(1)}, u32[]{:S(2)}, u32[]{:S(2)}) %collective-permute-start.15) | collective-permute-done | bytes 196640 | tf_op jit(solution)/shard_map/ppermute | solution.py:499
  70.9 1.1 shard_map.84
  72.0 0.1 collective-permute-start.17
  72.1 1.6 %collective-permute-start.18 = (bf16[6,64,256]{2,1,0:T(8,128)(2,1)S(1)}, bf16[6,64,256]{2,1,0:T(8,128)(2,1)S(1)}, u32[]{:S(2)}, u32[]{:S(2)}) collective-permute-start(bf16[6,64,256]{2,1,0:T(8,128)(2,1)S(1)} %get-tuple-element.56), channel_id=1, source_target_pairs={{0,3},{1,2},{2,1},{3,0},{4,7},{5,6},{6,5},{7,4},{8,11},{9,10},{10,... | collective-permute-start | bytes 589832 | tf_op jit(solution)/shard_map/ppermute | solution.py:499
  73.7 7.4 %collective-permute-done.10.refs_1_.refs_4_ = bf16[4,128,256]{2,1,0:T(8,128)(2,1)S(1)} collective-permute-done((bf16[4,128,256]{2,1,0:T(8,128)(2,1)S(1)}, bf16[4,128,256]{2,1,0:T(8,128)(2,1)S(1)}, u32[]{:S(2)}, u32[]{:S(2)}) %collective-permute-start.10) | collective-permute-done | bytes 262176 | tf_op jit(solution)/shard_map/ppermute | solution.py:491
  81.1 0.0 copy-start.1
  81.1 0.0 copy-start.2
  81.1 0.9 shard_map.85
  82.0 0.3 collective-permute-start.19
  82.4 0.1 copy-done.1
  82.5 0.9 fusion.refs_10_
  83.3 6.6 %collective-permute-done.11.refs_4_ = bf16[2,128,256]{2,1,0:T(8,128)(2,1)S(1)} collective-permute-done((bf16[2,128,256]{2,1,0:T(8,128)(2,1)S(1)}, bf16[2,128,256]{2,1,0:T(8,128)(2,1)S(1)}, u32[]{:S(2)}, u32[]{:S(2)}) %collective-permute-start.11) | collective-permute-done | bytes 131104 | tf_op jit(solution)/shard_map/ppermute | solution.py:491
  90.0 1.0 shard_map.86
  91.0 0.1 collective-permute-start.20
  91.0 1.0 collective-permute-start.21
  92.1 1.1 %collective-permute-start.22 = (bf16[144,256]{1,0:T(8,128)(2,1)S(1)}, bf16[144,256]{1,0:T(8,128)(2,1)S(1)}, u32[]{:S(2)}, u32[]{:S(2)}) collective-permute-start(bf16[144,256]{1,0:T(8,128)(2,1)S(1)} %get-tuple-element.67), channel_id=1, source_target_pairs={{0,2},{1,3},{2,0},{3,1},{4,6},{5,7},{6,4},{7,5},{8,10},{9,11},{10,... | collective-permute-start | bytes 221192 | tf_op jit(solution)/shard_map/ppermute | solution.py:499
  93.2 0.3 collective-permute-start.23
  93.5 2.9 %collective-permute-done.21.refs_16_ = bf16[4,64,256]{2,1,0:T(8,128)(2,1)S(1)} collective-permute-done((bf16[4,64,256]{2,1,0:T(8,128)(2,1)S(1)}, bf16[4,64,256]{2,1,0:T(8,128)(2,1)S(1)}, u32[]{:S(2)}, u32[]{:S(2)}) %collective-permute-start.21) | collective-permute-done | bytes 131104 | tf_op jit(solution)/shard_map/ppermute | solution.py:499
  96.3 3.2 %shard_map.87 = (f32[2,24,64,256]{3,2,1,0:T(8,128)S(1)}, f32[2,24,64,256]{3,2,1,0:T(8,128)}) custom-call(s32[74]{0:T(128)S(1)} %get-tuple-element.37.refs_0_.plan, s32[74]{0:T(128)S(1)} %shard_map.69.refs_9_.refs_1_, f32[24]{0:T(128)S(1)} %copy-done.2, bf16[2,24,64,256]{3,2,1,0:T(8,128)(2,1)S(1)} %copy-done.1, ...), custom_call_target="tpu_custom_call" | custom-call | tf_op jit(solution)/shard_map/pallas_call | solution.py:365
  99.6 0.6 shard_map.89.refs_0_
  100.2 0.9 collective-permute-start.24
  101.1 0.9 collective-permute-start.25
  102.0 2.1 %collective-permute-start.26 = (f32[8,256]{1,0:T(8,128)S(1)}, f32[8,256]{1,0:T(8,128)S(1)}, u32[]{:S(2)}, u32[]{:S(2)}) collective-permute-start(f32[8,256]{1,0:T(8,128)S(1)} %shard_map.89.refs_0_), channel_id=1, source_target_pairs={{0,12},{4,0},{8,4},{12,8},{1,13},{5,1},{9,5},{13,9},{2,14},{6,2},{... | collective-permute-start | bytes 24584 | tf_op jit(solution)/shard_map/ppermute | solution.py:491
  104.1 1.5 %shard_map.88 = (f32[2,24,64,256]{3,2,1,0:T(8,128)}, f32[8,128]{1,0:T(8,128)S(1)}) custom-call(s32[74]{0:T(128)S(1)} %get-tuple-element.37.refs_0_.plan, s32[74]{0:T(128)S(1)} %shard_map.69.refs_9_.refs_1_, f32[2,24,64,256]{3,2,1,0:T(8,128)S(1)} %get-tuple-element.65.refs_2_.refs_3_, ...), custom_call_target="tpu_custom_call", output_to_operand_aliasing={{0}: (7, {})} | custom-call | tf_op jit(solution)/shard_map/pallas_call | solution.py:410
  105.6 0.2 collective-permute-done.24.refs_1_
  105.8 0.4 collective-permute-done.26.refs_3_
  106.2 0.5 shard_map.90
  (22 shorter events, 0.1 us)
Async XLA Ops:
  0.6 7.7 %collective-permute-start.2 = (bf16[1,24,128,256]{3,2,1,0:T(8,128)(2,1)}, bf16[1,24,128,256]{3,2,1,0:T(8,128)(2,1)S(1)}, u32[]{:S(2)}, u32[]{:S(2)}) collective-permute-start(bf16[1,24,128,256]{3,2,1,0:T(8,128)(2,1)} %right.1), channel_id=1, source_target_pairs={{0,1},{1,0},{2,3},{3,2},{4,5},{5,4},{6,7},{7,6},{8,9},{9,8},{10,11... | collective-permute-start | bytes 4718600 | tf_op jit(solution)/shard_map/ppermute | solution.py:491
  1.1 7.2 %collective-permute-start.3 = (bf16[2,24,64,256]{3,2,1,0:T(8,128)(2,1)}, bf16[2,24,64,256]{3,2,1,0:T(8,128)(2,1)S(1)}, u32[]{:S(2)}, u32[]{:S(2)}) collective-permute-start(bf16[2,24,64,256]{3,2,1,0:T(8,128)(2,1)} %refs_3_.1), channel_id=1, source_target_pairs={{0,1},{1,0},{2,3},{3,2},{4,5},{5,4},{6,7},{7,6},{8,9},{9,8},{10,11... | collective-permute-start | bytes 4718600 | tf_op jit(solution)/shard_map/ppermute | solution.py:491
  1.2 12.2 %collective-permute-start.1 = (bf16[1,24,128,256]{3,2,1,0:T(8,128)(2,1)}, bf16[1,24,128,256]{3,2,1,0:T(8,128)(2,1)S(1)}, u32[]{:S(2)}, u32[]{:S(2)}) collective-permute-start(bf16[1,24,128,256]{3,2,1,0:T(8,128)(2,1)} %refs_1_.9), channel_id=1, source_target_pairs={{0,1},{1,0},{2,3},{3,2},{4,5},{5,4},{6,7},{7,6},{8,9},{9,8},{10,11... | collective-permute-start | bytes 4718600 | tf_op jit(solution)/shard_map/ppermute | solution.py:491
  1.7 0.7 copy-start.3
  5.6 21.0 %collective-permute-start.5 = (bf16[24,64,256]{2,1,0:T(8,128)(2,1)S(1)}, bf16[24,64,256]{2,1,0:T(8,128)(2,1)S(1)}, u32[]{:S(2)}, u32[]{:S(2)}) collective-permute-start(bf16[24,64,256]{2,1,0:T(8,128)(2,1)S(1)} %get-tuple-element.39.refs_3_.refs_5_), channel_id=1, source_target_pairs={{0,2},{1,3},{2,0},{3,1},{4,6},{5,7},{6,4},{7,5},{8,10},{9,11},{10,... | collective-permute-start | bytes 2359304 | tf_op jit(solution)/shard_map/ppermute | solution.py:499
  8.2 34.7 %collective-permute-start.6 = (bf16[24,64,256]{2,1,0:T(8,128)(2,1)S(1)}, bf16[24,64,256]{2,1,0:T(8,128)(2,1)S(1)}, u32[]{:S(2)}, u32[]{:S(2)}) collective-permute-start(bf16[24,64,256]{2,1,0:T(8,128)(2,1)S(1)} %get-tuple-element.41), channel_id=1, source_target_pairs={{0,3},{1,2},{2,1},{3,0},{4,7},{5,6},{6,5},{7,4},{8,11},{9,10},{10,... | collective-permute-start | bytes 2359304 | tf_op jit(solution)/shard_map/ppermute | solution.py:499
  9.5 34.3 %collective-permute-start.7 = (bf16[6,128,256]{2,1,0:T(8,128)(2,1)S(1)}, bf16[6,128,256]{2,1,0:T(8,128)(2,1)S(1)}, u32[]{:S(2)}, u32[]{:S(2)}) collective-permute-start(bf16[6,128,256]{2,1,0:T(8,128)(2,1)S(1)} %get-tuple-element.40.refs_5_), channel_id=1, source_target_pairs={{0,4},{4,8},{8,12},{12,0},{1,5},{5,9},{9,13},{13,1},{2,6},{6,10},{... | collective-permute-start | bytes 1179656 | tf_op jit(solution)/shard_map/ppermute | solution.py:491
  11.3 32.5 %collective-permute-start.8 = (bf16[6,128,256]{2,1,0:T(8,128)(2,1)S(1)}, bf16[6,128,256]{2,1,0:T(8,128)(2,1)S(1)}, u32[]{:S(2)}, u32[]{:S(2)}) collective-permute-start(bf16[6,128,256]{2,1,0:T(8,128)(2,1)S(1)} %get-tuple-element.42), channel_id=1, source_target_pairs={{0,12},{4,0},{8,4},{12,8},{1,13},{5,1},{9,5},{13,9},{2,14},{6,2},{... | collective-permute-start | bytes 1179656 | tf_op jit(solution)/shard_map/ppermute | solution.py:491
  14.4 42.7 %collective-permute-start.4 = (bf16[6,128,256]{2,1,0:T(8,128)(2,1)S(1)}, bf16[6,128,256]{2,1,0:T(8,128)(2,1)S(1)}, u32[]{:S(2)}, u32[]{:S(2)}) collective-permute-start(bf16[6,128,256]{2,1,0:T(8,128)(2,1)S(1)} %shard_map.71.refs_5_), channel_id=1, source_target_pairs={{0,8},{4,12},{8,0},{12,4},{1,9},{5,13},{9,1},{13,5},{2,10},{6,14},... | collective-permute-start | bytes 1179656 | tf_op jit(solution)/shard_map/ppermute | solution.py:491
  43.9 15.5 %collective-permute-start.9 = (bf16[6,128,256]{2,1,0:T(8,128)(2,1)S(1)}, bf16[6,128,256]{2,1,0:T(8,128)(2,1)S(1)}, u32[]{:S(2)}, u32[]{:S(2)}) collective-permute-start(bf16[6,128,256]{2,1,0:T(8,128)(2,1)S(1)} %shard_map.74.refs_5_), channel_id=1, source_target_pairs={{0,4},{4,8},{8,12},{12,0},{1,5},{5,9},{9,13},{13,1},{2,6},{6,10},{... | collective-permute-start | bytes 1179656 | tf_op jit(solution)/shard_map/ppermute | solution.py:491
  45.6 3.5 %collective-permute-start = (s32[1,96]{1,0:T(1,128)S(1)}, s32[1,96]{1,0:T(1,128)S(1)}, u32[]{:S(2)}, u32[]{:S(2)}) collective-permute-start(s32[1,96]{1,0:T(1,128)S(1)} %copy-done.3), channel_id=1, source_target_pairs={{0,2},{2,0},{1,3},{3,1},{4,6},{6,4},{5,7},{7,5},{8,10},{10,8},{9,1... | collective-permute-start | bytes 1160 | tf_op jit(solution)/shard_map/ppermute | solution.py:491
  50.4 1.4 %copy-start = (bf16[1,24,128,256]{3,2,1,0:T(8,128)(2,1)S(1)}, bf16[1,24,128,256]{3,2,1,0:T(8,128)(2,1)}, u32[]{:S(2)}) copy-start(bf16[1,24,128,256]{3,2,1,0:T(8,128)(2,1)} %refs_1_.9) | copy-start | bytes 4718596
  52.9 7.5 %collective-permute-start.13 = (bf16[6,64,256]{2,1,0:T(8,128)(2,1)S(1)}, bf16[6,64,256]{2,1,0:T(8,128)(2,1)S(1)}, u32[]{:S(2)}, u32[]{:S(2)}) collective-permute-start(bf16[6,64,256]{2,1,0:T(8,128)(2,1)S(1)} %get-tuple-element.44), channel_id=1, source_target_pairs={{0,2},{1,3},{2,0},{3,1},{4,6},{5,7},{6,4},{7,5},{8,10},{9,11},{10,... | collective-permute-start | bytes 589832 | tf_op jit(solution)/shard_map/ppermute | solution.py:499
  54.5 7.7 %collective-permute-start.14 = (bf16[6,64,256]{2,1,0:T(8,128)(2,1)S(1)}, bf16[6,64,256]{2,1,0:T(8,128)(2,1)S(1)}, u32[]{:S(2)}, u32[]{:S(2)}) collective-permute-start(bf16[6,64,256]{2,1,0:T(8,128)(2,1)S(1)} %get-tuple-element.45), channel_id=1, source_target_pairs={{0,3},{1,2},{2,1},{3,0},{4,7},{5,6},{6,5},{7,4},{8,11},{9,10},{10,... | collective-permute-start | bytes 589832 | tf_op jit(solution)/shard_map/ppermute | solution.py:499
  57.1 11.7 %collective-permute-start.12 = (bf16[6,128,256]{2,1,0:T(8,128)(2,1)S(1)}, bf16[6,128,256]{2,1,0:T(8,128)(2,1)S(1)}, u32[]{:S(2)}, u32[]{:S(2)}) collective-permute-start(bf16[6,128,256]{2,1,0:T(8,128)(2,1)S(1)} %shard_map.80.refs_1_), channel_id=1, source_target_pairs={{0,12},{4,0},{8,4},{12,8},{1,13},{5,1},{9,5},{13,9},{2,14},{6,2},{... | collective-permute-start | bytes 1179656 | tf_op jit(solution)/shard_map/ppermute | solution.py:491
  63.2 7.7 %collective-permute-start.15 = (bf16[6,64,256]{2,1,0:T(8,128)(2,1)S(1)}, bf16[6,64,256]{2,1,0:T(8,128)(2,1)S(1)}, u32[]{:S(2)}, u32[]{:S(2)}) collective-permute-start(bf16[6,64,256]{2,1,0:T(8,128)(2,1)S(1)} %get-tuple-element.47), channel_id=1, source_target_pairs={{0,2},{1,3},{2,0},{3,1},{4,6},{5,7},{6,4},{7,5},{8,10},{9,11},{10,... | collective-permute-start | bytes 589832 | tf_op jit(solution)/shard_map/ppermute | solution.py:499
  63.9 17.2 %collective-permute-start.10 = (bf16[4,128,256]{2,1,0:T(8,128)(2,1)S(1)}, bf16[4,128,256]{2,1,0:T(8,128)(2,1)S(1)}, u32[]{:S(2)}, u32[]{:S(2)}) collective-permute-start(bf16[4,128,256]{2,1,0:T(8,128)(2,1)S(1)} %shard_map.81.refs_10_), channel_id=1, source_target_pairs={{0,8},{4,12},{8,0},{12,4},{1,9},{5,13},{9,1},{13,5},{2,10},{6,14},... | collective-permute-start | bytes 786440 | tf_op jit(solution)/shard_map/ppermute | solution.py:491
  67.0 14.0 %collective-permute-start.16 = (bf16[6,64,256]{2,1,0:T(8,128)(2,1)S(1)}, bf16[6,64,256]{2,1,0:T(8,128)(2,1)S(1)}, u32[]{:S(2)}, u32[]{:S(2)}) collective-permute-start(bf16[6,64,256]{2,1,0:T(8,128)(2,1)S(1)} %get-tuple-element.49), channel_id=1, source_target_pairs={{0,3},{1,2},{2,1},{3,0},{4,7},{5,6},{6,5},{7,4},{8,11},{9,10},{10,... | collective-permute-start | bytes 589832 | tf_op jit(solution)/shard_map/ppermute | solution.py:499
  72.0 9.1 %collective-permute-start.17 = (bf16[6,64,256]{2,1,0:T(8,128)(2,1)S(1)}, bf16[6,64,256]{2,1,0:T(8,128)(2,1)S(1)}, u32[]{:S(2)}, u32[]{:S(2)}) collective-permute-start(bf16[6,64,256]{2,1,0:T(8,128)(2,1)S(1)} %get-tuple-element.50), channel_id=1, source_target_pairs={{0,2},{1,3},{2,0},{3,1},{4,6},{5,7},{6,4},{7,5},{8,10},{9,11},{10,... | collective-permute-start | bytes 589832 | tf_op jit(solution)/shard_map/ppermute | solution.py:499
  72.1 17.9 %collective-permute-start.18 = (bf16[6,64,256]{2,1,0:T(8,128)(2,1)S(1)}, bf16[6,64,256]{2,1,0:T(8,128)(2,1)S(1)}, u32[]{:S(2)}, u32[]{:S(2)}) collective-permute-start(bf16[6,64,256]{2,1,0:T(8,128)(2,1)S(1)} %get-tuple-element.56), channel_id=1, source_target_pairs={{0,3},{1,2},{2,1},{3,0},{4,7},{5,6},{6,5},{7,4},{8,11},{9,10},{10,... | collective-permute-start | bytes 589832 | tf_op jit(solution)/shard_map/ppermute | solution.py:499
  81.1 8.9 %collective-permute-start.11 = (bf16[2,128,256]{2,1,0:T(8,128)(2,1)S(1)}, bf16[2,128,256]{2,1,0:T(8,128)(2,1)S(1)}, u32[]{:S(2)}, u32[]{:S(2)}) collective-permute-start(bf16[2,128,256]{2,1,0:T(8,128)(2,1)S(1)} %shard_map.82.refs_10_), channel_id=1, source_target_pairs={{0,8},{4,12},{8,0},{12,4},{1,9},{5,13},{9,1},{13,5},{2,10},{6,14},... | collective-permute-start | bytes 393224 | tf_op jit(solution)/shard_map/ppermute | solution.py:491
  81.1 1.4 %copy-start.1 = (bf16[2,24,64,256]{3,2,1,0:T(8,128)(2,1)S(1)}, bf16[2,24,64,256]{3,2,1,0:T(8,128)(2,1)}, u32[]{:S(2)}) copy-start(bf16[2,24,64,256]{3,2,1,0:T(8,128)(2,1)} %refs_3_.1) | copy-start | bytes 4718596
  81.1 1.4 %copy-start.2 = (f32[24]{0:T(128)S(1)}, f32[24]{0:T(128)}, u32[]{:S(2)}) copy-start(f32[24]{0:T(128)} %refs_2_.1) | copy-start | bytes 292
  82.0 7.9 %collective-permute-start.19 = (bf16[4,64,256]{2,1,0:T(8,128)(2,1)S(1)}, bf16[4,64,256]{2,1,0:T(8,128)(2,1)S(1)}, u32[]{:S(2)}, u32[]{:S(2)}) collective-permute-start(bf16[4,64,256]{2,1,0:T(8,128)(2,1)S(1)} %get-tuple-element.57), channel_id=1, source_target_pairs={{0,2},{1,3},{2,0},{3,1},{4,6},{5,7},{6,4},{7,5},{8,10},{9,11},{10,... | collective-permute-start | bytes 393224 | tf_op jit(solution)/shard_map/ppermute | solution.py:499
  91.0 5.4 %collective-permute-start.20 = (bf16[1552,256]{1,0:T(8,128)(2,1)S(1)}, bf16[1552,256]{1,0:T(8,128)(2,1)S(1)}, u32[]{:S(2)}, u32[]{:S(2)}) collective-permute-start(bf16[1552,256]{1,0:T(8,128)(2,1)S(1)} %get-tuple-element.58), channel_id=1, source_target_pairs={{0,1},{1,0},{2,3},{3,2},{4,5},{5,4},{6,7},{7,6},{8,9},{9,8},{10,11... | collective-permute-start | bytes 2383880 | tf_op jit(solution)/shard_map/ppermute | solution.py:491
  91.0 5.3 %collective-permute-start.21 = (bf16[4,64,256]{2,1,0:T(8,128)(2,1)S(1)}, bf16[4,64,256]{2,1,0:T(8,128)(2,1)S(1)}, u32[]{:S(2)}, u32[]{:S(2)}) collective-permute-start(bf16[4,64,256]{2,1,0:T(8,128)(2,1)S(1)} %get-tuple-element.63), channel_id=1, source_target_pairs={{0,3},{1,2},{2,1},{3,0},{4,7},{5,6},{6,5},{7,4},{8,11},{9,10},{10,... | collective-permute-start | bytes 393224 | tf_op jit(solution)/shard_map/ppermute | solution.py:499
  92.1 7.5 %collective-permute-start.22 = (bf16[144,256]{1,0:T(8,128)(2,1)S(1)}, bf16[144,256]{1,0:T(8,128)(2,1)S(1)}, u32[]{:S(2)}, u32[]{:S(2)}) collective-permute-start(bf16[144,256]{1,0:T(8,128)(2,1)S(1)} %get-tuple-element.67), channel_id=1, source_target_pairs={{0,2},{1,3},{2,0},{3,1},{4,6},{5,7},{6,4},{7,5},{8,10},{9,11},{10,... | collective-permute-start | bytes 221192 | tf_op jit(solution)/shard_map/ppermute | solution.py:499
  93.2 6.4 %collective-permute-start.23 = (bf16[144,256]{1,0:T(8,128)(2,1)S(1)}, bf16[144,256]{1,0:T(8,128)(2,1)S(1)}, u32[]{:S(2)}, u32[]{:S(2)}) collective-permute-start(bf16[144,256]{1,0:T(8,128)(2,1)S(1)} %get-tuple-element.68), channel_id=1, source_target_pairs={{0,3},{1,2},{2,1},{3,0},{4,7},{5,6},{6,5},{7,4},{8,11},{9,10},{10,... | collective-permute-start | bytes 221192 | tf_op jit(solution)/shard_map/ppermute | solution.py:499
  100.2 5.6 %collective-permute-start.24 = (f32[8,256]{1,0:T(8,128)S(1)}, f32[8,256]{1,0:T(8,128)S(1)}, u32[]{:S(2)}, u32[]{:S(2)}) collective-permute-start(f32[8,256]{1,0:T(8,128)S(1)} %shard_map.89.refs_0_), channel_id=1, source_target_pairs={{0,4},{4,8},{8,12},{12,0},{1,5},{5,9},{9,13},{13,1},{2,6},{6,10},{... | collective-permute-start | bytes 24584 | tf_op jit(solution)/shard_map/ppermute | solution.py:491
  101.1 4.7 %collective-permute-start.25 = (f32[8,256]{1,0:T(8,128)S(1)}, f32[8,256]{1,0:T(8,128)S(1)}, u32[]{:S(2)}, u32[]{:S(2)}) collective-permute-start(f32[8,256]{1,0:T(8,128)S(1)} %shard_map.89.refs_0_), channel_id=1, source_target_pairs={{0,8},{4,12},{8,0},{12,4},{1,9},{5,13},{9,1},{13,5},{2,10},{6,14},... | collective-permute-start | bytes 24584 | tf_op jit(solution)/shard_map/ppermute | solution.py:491
  102.0 4.3 %collective-permute-start.26 = (f32[8,256]{1,0:T(8,128)S(1)}, f32[8,256]{1,0:T(8,128)S(1)}, u32[]{:S(2)}, u32[]{:S(2)}) collective-permute-start(f32[8,256]{1,0:T(8,128)S(1)} %shard_map.89.refs_0_), channel_id=1, source_target_pairs={{0,12},{4,0},{8,4},{12,8},{1,13},{5,1},{9,5},{13,9},{2,14},{6,2},{... | collective-permute-start | bytes 24584 | tf_op jit(solution)/shard_map/ppermute | solution.py:491

commit v12 on v11

--- a/solution.py
+++ b/solution.py
@@ -529,10 +529,13 @@
         steps = [g * each + d for d in range(each)]
         return [shift(a, "sector", z.sector, k) if k else a for a, k in zip(arrays, steps)]
 
+    partners = [shift(partner, "env", z.env, e) for e in range(1, z.env)]
     vector_others = around(vectors)[1:]
     right_others = around(right_env)[1:]
     left = around(left_env)
     plan, own, right_own = load(z, partner, vectors, right_env)
+    own = gate(own, partners)
+    plans = [plan] + [plan_only(z, other) for other in partners]
     right = [right_own] + right_others
     near_rows = [own[0]] + vector_others
     vec = [near_rows]
@@ -568,17 +571,15 @@
         return [part for piece in parts[g][1:] for part in piece]
 
     near[0] = near_products(0, made[:1])
-    far1 = far_products(1, near[0][:1])
+    far1 = far_products(1, (near[0][0], *plans[1:]))
     far1 = gate(far1, [*near[1], *near[3]])
     far[1] = across(far1, 1)
     far[0] = far_products(0, far1[:1])
-    partners = [shift(partner, "env", z.env, e) for e in range(1, z.env)]
-    plans = [plan] + [plan_only(z, other) for other in partners]
-    dots = send_terms(0, None, None, (), plans[1:])
+    dots = send_terms(0, None, None, (), ())
     far3 = far_products(3, (dots,))
     far2 = far_products(2, far3[:1])
     far4 = far_products(4, far2[:1])
-    far3 = gate(far3, [far4[0], *near[2]])
+    far3 = gate(far3, [far4[0], *near[2], *arrived(0)[:1]])
     far[3] = across(far3, 3)
     far2 = gate(far2, [far3[0], *far[1]])
     far[2] = across(far2, 2)
@@ -591,7 +592,7 @@
     dots = send_terms(2, dots, None, (), [far4[0]] + arrived(1)[1:] + arrived(3)[:1])
     early = (0, 1, 3, 2)
     kept = [parts[g][0][1:] for g in early]
-    dots = send_terms(4, dots, own_sums, kept, arrived(3)[1:] + arrived(2)[:1])
+    dots = send_terms(4, dots, own_sums, kept, arrived(3)[1:] + arrived(2))
     so_far, image = gather_terms(
         z,
         plans,

time: 107 us -> 106 us (level)
  waiting for transfers between devices: 51.6 us -> 47.2 us
  starting transfers between devices: 29.3 us -> 32.9 us
    ppermute x15, starting transfers between devices: 18.6 us -> 25.4 us  [shift(): lax.ppermute(array, axis, [(i, (i + step) % size) for i in range(size)])]
    ppermute x15, waiting for transfers between devices: 17.2 us -> 13.7 us  [shift(): lax.ppermute(array, axis, [(i, (i + step) % size) for i in range(size)])]
    ppermute x12, starting transfers between devices: 10.7 us -> 7.46 us  [shift_both(): return lax.ppermute(array, ('env', 'rep'), perm)]
  transfers between devices with their start and end apart: 27 -> 27, of which waited for: 12 -> 11; matrix products, arithmetic and copies ran while one was open for 1% -> 1% of each run, Pallas kernels for 20% -> 20%
where the time goes in v12:
time: 106 us
  waiting for transfers between devices  47.2 us (45%)
  starting transfers between devices  32.9 us (31%)
  Pallas kernels  23 us (22%)
    ppermute x12, waiting for transfers between devices, shift_both(): return lax.ppermute(array, ('env', 'rep'), perm)  33.6 us
    ppermute x15, starting transfers between devices, shift(): lax.ppermute(array, axis, [(i, (i + step) % size) for i in range(size)])  25.4 us
    ppermute x15, waiting for transfers between devices, shift(): lax.ppermute(array, axis, [(i, (i + step) % size) for i in range(size)])  13.7 us
    pallas_call x8, Pallas kernels, products(): pl.pallas_call(functools.partial(products_body, z, pieces, spans), out_sh...  7.53 us
    ppermute x12, starting transfers between devices, shift_both(): return lax.ppermute(array, ('env', 'rep'), perm)  7.46 us
    pallas_call x5, Pallas kernels, terms(): pl.pallas_call(functools.partial(terms_body, z, spans, so_far is not None...  5.13 us
    pallas_call x1, Pallas kernels, load(): pl.pallas_call(functools.partial(load_body, z), out_shape=[jax.ShapeDtype...  3.24 us
    pallas_call x1, Pallas kernels, gather_terms(): pl.pallas_call(functools.partial(gather_body, z, chunks, skip), out_shape...  3.23 us
  transfers between devices with their start and end apart: 27, of which 11 were waited for; matrix products, arithmetic and copies ran while one was open for 1% of the time, Pallas kernels for 20%

profile of v12, /device:TPU:0, one launch (start us, length us, event | category | flops | bytes accessed | tf_op | source)
XLA Modules:
  0.0 105.6 jit_solution(7765895372492066362)
XLA Ops:
  0.6 0.5 collective-permute-start.2
  1.1 0.1 collective-permute-start.3
  1.2 0.4 collective-permute-start.1
  1.7 2.6 %collective-permute-start = (s32[1,96]{1,0:T(1,128)}, s32[1,96]{1,0:T(1,128)S(1)}, u32[]{:S(2)}, u32[]{:S(2)}) collective-permute-start(s32[1,96]{1,0:T(1,128)} %partner.1), channel_id=1, source_target_pairs={{0,2},{2,0},{1,3},{3,1},{4,6},{6,4},{5,7},{7,5},{8,10},{10,8},{9,1... | collective-permute-start | bytes 1160 | tf_op jit(solution)/shard_map/ppermute | solution.py:491
  4.2 0.7 copy-done.3
  4.9 3.2 %shard_map.68 = (s32[74]{0:T(128)S(1)}, bf16[24,64,256]{2,1,0:T(8,128)(2,1)S(1)}, bf16[24,64,256]{2,1,0:T(8,128)(2,1)S(1)}, bf16[1,24,128,256]{3,2,1,0:T(8,128)(2,1)S(1)}) custom-call(s32[1,96]{1,0:T(1,128)S(1)} %copy-done.3, bf16[2,24,64,256]{3,2,1,0:T(8,128)(2,1)} %refs_3_.1, bf16[1,24,128,256]{3,2,1,0:T(8,128)(2,1)} %right.1), custom_call_target="tpu_custom_call" | custom-call | tf_op jit(solution)/shard_map/pallas_call | solution.py:99
  8.2 0.0 collective-permute-done.partner.refs_2_
  8.2 0.1 collective-permute-start.5
  8.3 1.5 %collective-permute-start.6 = (bf16[24,64,256]{2,1,0:T(8,128)(2,1)S(1)}, bf16[24,64,256]{2,1,0:T(8,128)(2,1)S(1)}, u32[]{:S(2)}, u32[]{:S(2)}) collective-permute-start(bf16[24,64,256]{2,1,0:T(8,128)(2,1)S(1)} %get-tuple-element.45), channel_id=1, source_target_pairs={{0,3},{1,2},{2,1},{3,0},{4,7},{5,6},{6,5},{7,4},{8,11},{9,10},{10,... | collective-permute-start | bytes 2359304 | tf_op jit(solution)/shard_map/ppermute | solution.py:499
  9.8 1.2 %shard_map.71 = (bf16[6,128,256]{2,1,0:T(8,128)(2,1)S(1)}, bf16[6,128,256]{2,1,0:T(8,128)(2,1)S(1)}) custom-call(s32[74]{0:T(128)S(1)} %get-tuple-element.39.refs_0_.plan, bf16[1,24,128,256]{3,2,1,0:T(8,128)(2,1)S(1)} %get-tuple-element.40.refs_1_, bf16[1,24,128,256]{3,2,1,0:T(8,128)(2,1)S(1)} %collective-permute-done.2.refs_2_, ...), custom_call_target="tpu_custom_call" | custom-call | tf_op jit(solution)/shard_map/pallas_call | solution.py:183
  11.0 1.6 %collective-permute-start.7 = (bf16[6,128,256]{2,1,0:T(8,128)(2,1)S(1)}, bf16[6,128,256]{2,1,0:T(8,128)(2,1)S(1)}, u32[]{:S(2)}, u32[]{:S(2)}) collective-permute-start(bf16[6,128,256]{2,1,0:T(8,128)(2,1)S(1)} %get-tuple-element.44.refs_5_), channel_id=1, source_target_pairs={{0,4},{4,8},{8,12},{12,0},{1,5},{5,9},{9,13},{13,1},{2,6},{6,10},{... | collective-permute-start | bytes 1179656 | tf_op jit(solution)/shard_map/ppermute | solution.py:491
  12.6 2.2 %collective-permute-start.8 = (bf16[6,128,256]{2,1,0:T(8,128)(2,1)S(1)}, bf16[6,128,256]{2,1,0:T(8,128)(2,1)S(1)}, u32[]{:S(2)}, u32[]{:S(2)}) collective-permute-start(bf16[6,128,256]{2,1,0:T(8,128)(2,1)S(1)} %get-tuple-element.46), channel_id=1, source_target_pairs={{0,12},{4,0},{8,4},{12,8},{1,13},{5,1},{9,5},{13,9},{2,14},{6,2},{... | collective-permute-start | bytes 1179656 | tf_op jit(solution)/shard_map/ppermute | solution.py:491
  14.9 0.0 collective-permute-done.1.refs_6_.refs_2_
  14.9 0.9 shard_map.72.refs_5_
  15.8 0.9 collective-permute-start.4
  16.7 1.3 %shard_map.69.refs_6_.refs_1_ = s32[74]{0:T(128)S(1)} custom-call(s32[1,96]{1,0:T(1,128)S(1)} %collective-permute-done.partner.refs_2_), custom_call_target="tpu_custom_call" | custom-call | tf_op jit(solution)/shard_map/pallas_call | solution.py:121
  18.0 0.9 shard_map.73.refs_5_.refs_3_
  18.9 9.7 %collective-permute-done.5.refs_3_.refs_7_ = bf16[24,64,256]{2,1,0:T(8,128)(2,1)S(1)} collective-permute-done((bf16[24,64,256]{2,1,0:T(8,128)(2,1)S(1)}, bf16[24,64,256]{2,1,0:T(8,128)(2,1)S(1)}, u32[]{:S(2)}, u32[]{:S(2)}) %collective-permute-start.5) | collective-permute-done | bytes 786464 | tf_op jit(solution)/shard_map/ppermute | solution.py:499
  28.6 15.3 %collective-permute-done.6.refs_4_.refs_8_ = bf16[24,64,256]{2,1,0:T(8,128)(2,1)S(1)} collective-permute-done((bf16[24,64,256]{2,1,0:T(8,128)(2,1)S(1)}, bf16[24,64,256]{2,1,0:T(8,128)(2,1)S(1)}, u32[]{:S(2)}, u32[]{:S(2)}) %collective-permute-start.6) | collective-permute-done | bytes 786464 | tf_op jit(solution)/shard_map/ppermute | solution.py:499
  43.9 0.9 shard_map.74.refs_0_
  44.9 0.0 collective-permute-done.7.refs_1_.refs_3_
  44.9 0.0 copy-start
  44.9 1.6 %collective-permute-start.10 = (bf16[6,128,256]{2,1,0:T(8,128)(2,1)S(1)}, bf16[6,128,256]{2,1,0:T(8,128)(2,1)S(1)}, u32[]{:S(2)}, u32[]{:S(2)}) collective-permute-start(bf16[6,128,256]{2,1,0:T(8,128)(2,1)S(1)} %shard_map.75.refs_5_), channel_id=1, source_target_pairs={{0,4},{4,8},{8,12},{12,0},{1,5},{5,9},{9,13},{13,1},{2,6},{6,10},{... | collective-permute-start | bytes 1179656 | tf_op jit(solution)/shard_map/ppermute | solution.py:491
  46.6 0.9 shard_map.76.refs_4_
  47.5 1.1 %shard_map.77 = (bf16[6,64,256]{2,1,0:T(8,128)(2,1)S(1)}, bf16[6,64,256]{2,1,0:T(8,128)(2,1)S(1)}, bf16[6,64,256]{2,1,0:T(8,128)(2,1)S(1)}, bf16[6,64,256]{2,1,0:T(8,128)(2,1)S(1)}, f32[8,256]{1,0:T(8,128)S(1)}) custom-call(s32[74]{0:T(128)S(1)} %get-tuple-element.39.refs_0_.plan, bf16[1,24,128,256]{3,2,1,0:T(8,128)(2,1)S(1)} %copy-done, ...), custom_call_target="tpu_custom_call" | custom-call | tf_op jit(solution)/shard_map/pallas_call | solution.py:286
  48.6 0.6 collective-permute-start.9
  49.2 1.1 %collective-permute-start.14 = (bf16[6,64,256]{2,1,0:T(8,128)(2,1)S(1)}, bf16[6,64,256]{2,1,0:T(8,128)(2,1)S(1)}, u32[]{:S(2)}, u32[]{:S(2)}) collective-permute-start(bf16[6,64,256]{2,1,0:T(8,128)(2,1)S(1)} %get-tuple-element.49), channel_id=1, source_target_pairs={{0,3},{1,2},{2,1},{3,0},{4,7},{5,6},{6,5},{7,4},{8,11},{9,10},{10,... | collective-permute-start | bytes 589832 | tf_op jit(solution)/shard_map/ppermute | solution.py:499
  50.3 0.9 shard_map.78.refs_5_.refs_0_
  51.3 0.9 shard_map.79.refs_5_.refs_0_
  52.1 0.8 shard_map.80.refs_1_.refs_0_
  52.9 0.0 collective-permute-done.4.refs_2_.refs_3_
  52.9 3.5 %collective-permute-done.9.refs_3_.refs_11_.refs_6_ = bf16[6,64,256]{2,1,0:T(8,128)(2,1)S(1)} collective-permute-done((bf16[6,64,256]{2,1,0:T(8,128)(2,1)S(1)}, bf16[6,64,256]{2,1,0:T(8,128)(2,1)S(1)}, u32[]{:S(2)}, u32[]{:S(2)}) %collective-permute-start.9) | collective-permute-done | bytes 196640 | tf_op jit(solution)/shard_map/ppermute | solution.py:499
  56.4 2.5 %collective-permute-start.13 = (bf16[6,128,256]{2,1,0:T(8,128)(2,1)S(1)}, bf16[6,128,256]{2,1,0:T(8,128)(2,1)S(1)}, u32[]{:S(2)}, u32[]{:S(2)}) collective-permute-start(bf16[6,128,256]{2,1,0:T(8,128)(2,1)S(1)} %shard_map.81.refs_1_), channel_id=1, source_target_pairs={{0,12},{4,0},{8,4},{12,8},{1,13},{5,1},{9,5},{13,9},{2,14},{6,2},{... | collective-permute-start | bytes 1179656 | tf_op jit(solution)/shard_map/ppermute | solution.py:491
  58.8 0.0 collective-permute-done.10.refs_2_.refs_4_
  58.8 0.5 collective-permute-done.14.refs_12_.refs_7_
  59.4 1.1 %shard_map.84 = (bf16[6,64,256]{2,1,0:T(8,128)(2,1)S(1)}, bf16[6,64,256]{2,1,0:T(8,128)(2,1)S(1)}, bf16[6,64,256]{2,1,0:T(8,128)(2,1)S(1)}, bf16[6,64,256]{2,1,0:T(8,128)(2,1)S(1)}, f32[8,256]{1,0:T(8,128)S(1)}) custom-call(s32[74]{0:T(128)S(1)} %get-tuple-element.39.refs_0_.plan, bf16[1,24,128,256]{3,2,1,0:T(8,128)(2,1)S(1)} %copy-done, ...), custom_call_target="tpu_custom_call" | custom-call | tf_op jit(solution)/shard_map/pallas_call | solution.py:286
  60.5 0.6 collective-permute-start.15
  61.1 3.2 %collective-permute-start.11 = (bf16[4,128,256]{2,1,0:T(8,128)(2,1)S(1)}, bf16[4,128,256]{2,1,0:T(8,128)(2,1)S(1)}, u32[]{:S(2)}, u32[]{:S(2)}) collective-permute-start(bf16[4,128,256]{2,1,0:T(8,128)(2,1)S(1)} %shard_map.82.refs_10_), channel_id=1, source_target_pairs={{0,8},{4,12},{8,0},{12,4},{1,9},{5,13},{9,1},{13,5},{2,10},{6,14},... | collective-permute-start | bytes 786440 | tf_op jit(solution)/shard_map/ppermute | solution.py:491
  64.3 0.9 collective-permute-start.16
  65.2 3.0 %collective-permute-done.15.refs_10_.refs_9_ = bf16[6,64,256]{2,1,0:T(8,128)(2,1)S(1)} collective-permute-done((bf16[6,64,256]{2,1,0:T(8,128)(2,1)S(1)}, bf16[6,64,256]{2,1,0:T(8,128)(2,1)S(1)}, u32[]{:S(2)}, u32[]{:S(2)}) %collective-permute-start.15) | collective-permute-done | bytes 196640 | tf_op jit(solution)/shard_map/ppermute | solution.py:499
  68.2 0.2 collective-permute-done.13.refs_4_
  68.4 1.1 %shard_map.85 = (bf16[6,64,256]{2,1,0:T(8,128)(2,1)S(1)}, bf16[6,64,256]{2,1,0:T(8,128)(2,1)S(1)}, bf16[6,64,256]{2,1,0:T(8,128)(2,1)S(1)}, bf16[6,64,256]{2,1,0:T(8,128)(2,1)S(1)}, f32[8,256]{1,0:T(8,128)S(1)}) custom-call(s32[74]{0:T(128)S(1)} %get-tuple-element.39.refs_0_.plan, bf16[1,24,128,256]{3,2,1,0:T(8,128)(2,1)S(1)} %copy-done, ...), custom_call_target="tpu_custom_call" | custom-call | tf_op jit(solution)/shard_map/pallas_call | solution.py:286
  69.5 0.6 collective-permute-start.17
  70.1 9.0 %collective-permute-done.11.refs_1_.refs_4_ = bf16[4,128,256]{2,1,0:T(8,128)(2,1)S(1)} collective-permute-done((bf16[4,128,256]{2,1,0:T(8,128)(2,1)S(1)}, bf16[4,128,256]{2,1,0:T(8,128)(2,1)S(1)}, u32[]{:S(2)}, u32[]{:S(2)}) %collective-permute-start.11) | collective-permute-done | bytes 262176 | tf_op jit(solution)/shard_map/ppermute | solution.py:491
  79.0 0.0 copy-start.1
  79.1 0.0 copy-start.2
  79.1 0.9 shard_map.86
  80.0 0.6 collective-permute-start.19
  80.6 0.9 fusion.refs_10_
  81.5 3.4 %collective-permute-done.12.refs_4_ = bf16[2,128,256]{2,1,0:T(8,128)(2,1)S(1)} collective-permute-done((bf16[2,128,256]{2,1,0:T(8,128)(2,1)S(1)}, bf16[2,128,256]{2,1,0:T(8,128)(2,1)S(1)}, u32[]{:S(2)}, u32[]{:S(2)}) %collective-permute-start.12) | collective-permute-done | bytes 131104 | tf_op jit(solution)/shard_map/ppermute | solution.py:491
  84.9 1.5 %collective-permute-done.19.refs_16_.refs_15_ = bf16[4,64,256]{2,1,0:T(8,128)(2,1)S(1)} collective-permute-done((bf16[4,64,256]{2,1,0:T(8,128)(2,1)S(1)}, bf16[4,64,256]{2,1,0:T(8,128)(2,1)S(1)}, u32[]{:S(2)}, u32[]{:S(2)}) %collective-permute-start.19) | collective-permute-done | bytes 131104 | tf_op jit(solution)/shard_map/ppermute | solution.py:499
  86.4 1.0 shard_map.87
  87.4 1.3 %collective-permute-start.21 = (bf16[1552,256]{1,0:T(8,128)(2,1)S(1)}, bf16[1552,256]{1,0:T(8,128)(2,1)S(1)}, u32[]{:S(2)}, u32[]{:S(2)}) collective-permute-start(bf16[1552,256]{1,0:T(8,128)(2,1)S(1)} %get-tuple-element.63), channel_id=1, source_target_pairs={{0,1},{1,0},{2,3},{3,2},{4,5},{5,4},{6,7},{7,6},{8,9},{9,8},{10,11... | collective-permute-start | bytes 2383880 | tf_op jit(solution)/shard_map/ppermute | solution.py:491
  88.7 0.6 collective-permute-start.22
  89.3 0.8 collective-permute-start.23
  90.1 0.5 collective-permute-done.21.refs_4_.refs_0_
  90.6 3.2 %shard_map.88 = (f32[2,24,64,256]{3,2,1,0:T(8,128)S(1)}, f32[2,24,64,256]{3,2,1,0:T(8,128)}) custom-call(s32[74]{0:T(128)S(1)} %get-tuple-element.39.refs_0_.plan, s32[74]{0:T(128)S(1)} %shard_map.69.refs_6_.refs_1_, f32[24]{0:T(128)S(1)} %copy-done.2, bf16[2,24,64,256]{3,2,1,0:T(8,128)(2,1)S(1)} %copy-done.1, ...), custom_call_target="tpu_custom_call" | custom-call | tf_op jit(solution)/shard_map/pallas_call | solution.py:365
  93.9 0.6 shard_map.90.refs_0_
  94.5 6.0 %collective-permute-start.24 = (f32[8,256]{1,0:T(8,128)S(1)}, f32[8,256]{1,0:T(8,128)S(1)}, u32[]{:S(2)}, u32[]{:S(2)}) collective-permute-start(f32[8,256]{1,0:T(8,128)S(1)} %shard_map.90.refs_0_), channel_id=1, source_target_pairs={{0,4},{4,8},{8,12},{12,0},{1,5},{5,9},{9,13},{13,1},{2,6},{6,10},{... | collective-permute-start | bytes 24584 | tf_op jit(solution)/shard_map/ppermute | solution.py:491
  100.5 0.3 collective-permute-start.25
  100.8 2.1 %collective-permute-start.26 = (f32[8,256]{1,0:T(8,128)S(1)}, f32[8,256]{1,0:T(8,128)S(1)}, u32[]{:S(2)}, u32[]{:S(2)}) collective-permute-start(f32[8,256]{1,0:T(8,128)S(1)} %shard_map.90.refs_0_), channel_id=1, source_target_pairs={{0,12},{4,0},{8,4},{12,8},{1,13},{5,1},{9,5},{13,9},{2,14},{6,2},{... | collective-permute-start | bytes 24584 | tf_op jit(solution)/shard_map/ppermute | solution.py:491
  103.0 1.5 %shard_map.89 = (f32[2,24,64,256]{3,2,1,0:T(8,128)}, f32[8,128]{1,0:T(8,128)S(1)}) custom-call(s32[74]{0:T(128)S(1)} %get-tuple-element.39.refs_0_.plan, s32[74]{0:T(128)S(1)} %shard_map.69.refs_6_.refs_1_, f32[2,24,64,256]{3,2,1,0:T(8,128)S(1)} %get-tuple-element.69.refs_2_.refs_3_, ...), custom_call_target="tpu_custom_call", output_to_operand_aliasing={{0}: (7, {})} | custom-call | tf_op jit(solution)/shard_map/pallas_call | solution.py:410
  104.5 0.6 collective-permute-done.25.refs_2_
  105.1 0.5 shard_map.91
  (23 shorter events, 0.1 us)
Async XLA Ops:
  0.6 9.1 %collective-permute-start.2 = (bf16[1,24,128,256]{3,2,1,0:T(8,128)(2,1)}, bf16[1,24,128,256]{3,2,1,0:T(8,128)(2,1)S(1)}, u32[]{:S(2)}, u32[]{:S(2)}) collective-permute-start(bf16[1,24,128,256]{3,2,1,0:T(8,128)(2,1)} %right.1), channel_id=1, source_target_pairs={{0,1},{1,0},{2,3},{3,2},{4,5},{5,4},{6,7},{7,6},{8,9},{9,8},{10,11... | collective-permute-start | bytes 4718600 | tf_op jit(solution)/shard_map/ppermute | solution.py:491
  1.1 8.6 %collective-permute-start.3 = (bf16[2,24,64,256]{3,2,1,0:T(8,128)(2,1)}, bf16[2,24,64,256]{3,2,1,0:T(8,128)(2,1)S(1)}, u32[]{:S(2)}, u32[]{:S(2)}) collective-permute-start(bf16[2,24,64,256]{3,2,1,0:T(8,128)(2,1)} %refs_3_.1), channel_id=1, source_target_pairs={{0,1},{1,0},{2,3},{3,2},{4,5},{5,4},{6,7},{7,6},{8,9},{9,8},{10,11... | collective-permute-start | bytes 4718600 | tf_op jit(solution)/shard_map/ppermute | solution.py:491
  1.2 13.6 %collective-permute-start.1 = (bf16[1,24,128,256]{3,2,1,0:T(8,128)(2,1)}, bf16[1,24,128,256]{3,2,1,0:T(8,128)(2,1)S(1)}, u32[]{:S(2)}, u32[]{:S(2)}) collective-permute-start(bf16[1,24,128,256]{3,2,1,0:T(8,128)(2,1)} %refs_1_.9), channel_id=1, source_target_pairs={{0,1},{1,0},{2,3},{3,2},{4,5},{5,4},{6,7},{7,6},{8,9},{9,8},{10,11... | collective-permute-start | bytes 4718600 | tf_op jit(solution)/shard_map/ppermute | solution.py:491
  1.7 6.5 %collective-permute-start = (s32[1,96]{1,0:T(1,128)}, s32[1,96]{1,0:T(1,128)S(1)}, u32[]{:S(2)}, u32[]{:S(2)}) collective-permute-start(s32[1,96]{1,0:T(1,128)} %partner.1), channel_id=1, source_target_pairs={{0,2},{2,0},{1,3},{3,1},{4,6},{6,4},{5,7},{7,5},{8,10},{10,8},{9,1... | collective-permute-start | bytes 1160 | tf_op jit(solution)/shard_map/ppermute | solution.py:491
  4.2 0.7 copy-start.3
  8.2 20.5 %collective-permute-start.5 = (bf16[24,64,256]{2,1,0:T(8,128)(2,1)S(1)}, bf16[24,64,256]{2,1,0:T(8,128)(2,1)S(1)}, u32[]{:S(2)}, u32[]{:S(2)}) collective-permute-start(bf16[24,64,256]{2,1,0:T(8,128)(2,1)S(1)} %get-tuple-element.43.refs_3_.refs_5_), channel_id=1, source_target_pairs={{0,2},{1,3},{2,0},{3,1},{4,6},{5,7},{6,4},{7,5},{8,10},{9,11},{10,... | collective-permute-start | bytes 2359304 | tf_op jit(solution)/shard_map/ppermute | solution.py:499
  8.3 35.7 %collective-permute-start.6 = (bf16[24,64,256]{2,1,0:T(8,128)(2,1)S(1)}, bf16[24,64,256]{2,1,0:T(8,128)(2,1)S(1)}, u32[]{:S(2)}, u32[]{:S(2)}) collective-permute-start(bf16[24,64,256]{2,1,0:T(8,128)(2,1)S(1)} %get-tuple-element.45), channel_id=1, source_target_pairs={{0,3},{1,2},{2,1},{3,0},{4,7},{5,6},{6,5},{7,4},{8,11},{9,10},{10,... | collective-permute-start | bytes 2359304 | tf_op jit(solution)/shard_map/ppermute | solution.py:499
  11.0 33.9 %collective-permute-start.7 = (bf16[6,128,256]{2,1,0:T(8,128)(2,1)S(1)}, bf16[6,128,256]{2,1,0:T(8,128)(2,1)S(1)}, u32[]{:S(2)}, u32[]{:S(2)}) collective-permute-start(bf16[6,128,256]{2,1,0:T(8,128)(2,1)S(1)} %get-tuple-element.44.refs_5_), channel_id=1, source_target_pairs={{0,4},{4,8},{8,12},{12,0},{1,5},{5,9},{9,13},{13,1},{2,6},{6,10},{... | collective-permute-start | bytes 1179656 | tf_op jit(solution)/shard_map/ppermute | solution.py:491
  12.6 32.3 %collective-permute-start.8 = (bf16[6,128,256]{2,1,0:T(8,128)(2,1)S(1)}, bf16[6,128,256]{2,1,0:T(8,128)(2,1)S(1)}, u32[]{:S(2)}, u32[]{:S(2)}) collective-permute-start(bf16[6,128,256]{2,1,0:T(8,128)(2,1)S(1)} %get-tuple-element.46), channel_id=1, source_target_pairs={{0,12},{4,0},{8,4},{12,8},{1,13},{5,1},{9,5},{13,9},{2,14},{6,2},{... | collective-permute-start | bytes 1179656 | tf_op jit(solution)/shard_map/ppermute | solution.py:491
  15.8 37.1 %collective-permute-start.4 = (bf16[6,128,256]{2,1,0:T(8,128)(2,1)S(1)}, bf16[6,128,256]{2,1,0:T(8,128)(2,1)S(1)}, u32[]{:S(2)}, u32[]{:S(2)}) collective-permute-start(bf16[6,128,256]{2,1,0:T(8,128)(2,1)S(1)} %shard_map.72.refs_5_), channel_id=1, source_target_pairs={{0,8},{4,12},{8,0},{12,4},{1,9},{5,13},{9,1},{13,5},{2,10},{6,14},... | collective-permute-start | bytes 1179656 | tf_op jit(solution)/shard_map/ppermute | solution.py:491
  44.9 2.6 %copy-start = (bf16[1,24,128,256]{3,2,1,0:T(8,128)(2,1)S(1)}, bf16[1,24,128,256]{3,2,1,0:T(8,128)(2,1)}, u32[]{:S(2)}) copy-start(bf16[1,24,128,256]{3,2,1,0:T(8,128)(2,1)} %refs_1_.9) | copy-start | bytes 4718596
  44.9 13.9 %collective-permute-start.10 = (bf16[6,128,256]{2,1,0:T(8,128)(2,1)S(1)}, bf16[6,128,256]{2,1,0:T(8,128)(2,1)S(1)}, u32[]{:S(2)}, u32[]{:S(2)}) collective-permute-start(bf16[6,128,256]{2,1,0:T(8,128)(2,1)S(1)} %shard_map.75.refs_5_), channel_id=1, source_target_pairs={{0,4},{4,8},{8,12},{12,0},{1,5},{5,9},{9,13},{13,1},{2,6},{6,10},{... | collective-permute-start | bytes 1179656 | tf_op jit(solution)/shard_map/ppermute | solution.py:491
  48.6 7.8 %collective-permute-start.9 = (bf16[6,64,256]{2,1,0:T(8,128)(2,1)S(1)}, bf16[6,64,256]{2,1,0:T(8,128)(2,1)S(1)}, u32[]{:S(2)}, u32[]{:S(2)}) collective-permute-start(bf16[6,64,256]{2,1,0:T(8,128)(2,1)S(1)} %get-tuple-element.48), channel_id=1, source_target_pairs={{0,2},{1,3},{2,0},{3,1},{4,6},{5,7},{6,4},{7,5},{8,10},{9,11},{10,... | collective-permute-start | bytes 589832 | tf_op jit(solution)/shard_map/ppermute | solution.py:499
  49.2 10.2 %collective-permute-start.14 = (bf16[6,64,256]{2,1,0:T(8,128)(2,1)S(1)}, bf16[6,64,256]{2,1,0:T(8,128)(2,1)S(1)}, u32[]{:S(2)}, u32[]{:S(2)}) collective-permute-start(bf16[6,64,256]{2,1,0:T(8,128)(2,1)S(1)} %get-tuple-element.49), channel_id=1, source_target_pairs={{0,3},{1,2},{2,1},{3,0},{4,7},{5,6},{6,5},{7,4},{8,11},{9,10},{10,... | collective-permute-start | bytes 589832 | tf_op jit(solution)/shard_map/ppermute | solution.py:499
  56.4 12.0 %collective-permute-start.13 = (bf16[6,128,256]{2,1,0:T(8,128)(2,1)S(1)}, bf16[6,128,256]{2,1,0:T(8,128)(2,1)S(1)}, u32[]{:S(2)}, u32[]{:S(2)}) collective-permute-start(bf16[6,128,256]{2,1,0:T(8,128)(2,1)S(1)} %shard_map.81.refs_1_), channel_id=1, source_target_pairs={{0,12},{4,0},{8,4},{12,8},{1,13},{5,1},{9,5},{13,9},{2,14},{6,2},{... | collective-permute-start | bytes 1179656 | tf_op jit(solution)/shard_map/ppermute | solution.py:491
  60.5 7.8 %collective-permute-start.15 = (bf16[6,64,256]{2,1,0:T(8,128)(2,1)S(1)}, bf16[6,64,256]{2,1,0:T(8,128)(2,1)S(1)}, u32[]{:S(2)}, u32[]{:S(2)}) collective-permute-start(bf16[6,64,256]{2,1,0:T(8,128)(2,1)S(1)} %get-tuple-element.51), channel_id=1, source_target_pairs={{0,2},{1,3},{2,0},{3,1},{4,6},{5,7},{6,4},{7,5},{8,10},{9,11},{10,... | collective-permute-start | bytes 589832 | tf_op jit(solution)/shard_map/ppermute | solution.py:499
  61.1 18.0 %collective-permute-start.11 = (bf16[4,128,256]{2,1,0:T(8,128)(2,1)S(1)}, bf16[4,128,256]{2,1,0:T(8,128)(2,1)S(1)}, u32[]{:S(2)}, u32[]{:S(2)}) collective-permute-start(bf16[4,128,256]{2,1,0:T(8,128)(2,1)S(1)} %shard_map.82.refs_10_), channel_id=1, source_target_pairs={{0,8},{4,12},{8,0},{12,4},{1,9},{5,13},{9,1},{13,5},{2,10},{6,14},... | collective-permute-start | bytes 786440 | tf_op jit(solution)/shard_map/ppermute | solution.py:491
  64.3 14.7 %collective-permute-start.16 = (bf16[6,64,256]{2,1,0:T(8,128)(2,1)S(1)}, bf16[6,64,256]{2,1,0:T(8,128)(2,1)S(1)}, u32[]{:S(2)}, u32[]{:S(2)}) collective-permute-start(bf16[6,64,256]{2,1,0:T(8,128)(2,1)S(1)} %get-tuple-element.53), channel_id=1, source_target_pairs={{0,3},{1,2},{2,1},{3,0},{4,7},{5,6},{6,5},{7,4},{8,11},{9,10},{10,... | collective-permute-start | bytes 589832 | tf_op jit(solution)/shard_map/ppermute | solution.py:499
  69.5 9.6 %collective-permute-start.17 = (bf16[6,64,256]{2,1,0:T(8,128)(2,1)S(1)}, bf16[6,64,256]{2,1,0:T(8,128)(2,1)S(1)}, u32[]{:S(2)}, u32[]{:S(2)}) collective-permute-start(bf16[6,64,256]{2,1,0:T(8,128)(2,1)S(1)} %get-tuple-element.54), channel_id=1, source_target_pairs={{0,2},{1,3},{2,0},{3,1},{4,6},{5,7},{6,4},{7,5},{8,10},{9,11},{10,... | collective-permute-start | bytes 589832 | tf_op jit(solution)/shard_map/ppermute | solution.py:499
  70.1 14.8 %collective-permute-start.18 = (bf16[6,64,256]{2,1,0:T(8,128)(2,1)S(1)}, bf16[6,64,256]{2,1,0:T(8,128)(2,1)S(1)}, u32[]{:S(2)}, u32[]{:S(2)}) collective-permute-start(bf16[6,64,256]{2,1,0:T(8,128)(2,1)S(1)} %get-tuple-element.60), channel_id=1, source_target_pairs={{0,3},{1,2},{2,1},{3,0},{4,7},{5,6},{6,5},{7,4},{8,11},{9,10},{10,... | collective-permute-start | bytes 589832 | tf_op jit(solution)/shard_map/ppermute | solution.py:499
  79.0 5.9 %collective-permute-start.12 = (bf16[2,128,256]{2,1,0:T(8,128)(2,1)S(1)}, bf16[2,128,256]{2,1,0:T(8,128)(2,1)S(1)}, u32[]{:S(2)}, u32[]{:S(2)}) collective-permute-start(bf16[2,128,256]{2,1,0:T(8,128)(2,1)S(1)} %shard_map.83.refs_10_), channel_id=1, source_target_pairs={{0,8},{4,12},{8,0},{12,4},{1,9},{5,13},{9,1},{13,5},{2,10},{6,14},... | collective-permute-start | bytes 393224 | tf_op jit(solution)/shard_map/ppermute | solution.py:491
  79.0 1.6 %copy-start.1 = (bf16[2,24,64,256]{3,2,1,0:T(8,128)(2,1)S(1)}, bf16[2,24,64,256]{3,2,1,0:T(8,128)(2,1)}, u32[]{:S(2)}) copy-start(bf16[2,24,64,256]{3,2,1,0:T(8,128)(2,1)} %refs_3_.1) | copy-start | bytes 4718596
  79.1 1.6 %copy-start.2 = (f32[24]{0:T(128)S(1)}, f32[24]{0:T(128)}, u32[]{:S(2)}) copy-start(f32[24]{0:T(128)} %refs_2_.1) | copy-start | bytes 292
  80.0 6.4 %collective-permute-start.19 = (bf16[4,64,256]{2,1,0:T(8,128)(2,1)S(1)}, bf16[4,64,256]{2,1,0:T(8,128)(2,1)S(1)}, u32[]{:S(2)}, u32[]{:S(2)}) collective-permute-start(bf16[4,64,256]{2,1,0:T(8,128)(2,1)S(1)} %get-tuple-element.61), channel_id=1, source_target_pairs={{0,2},{1,3},{2,0},{3,1},{4,6},{5,7},{6,4},{7,5},{8,10},{9,11},{10,... | collective-permute-start | bytes 393224 | tf_op jit(solution)/shard_map/ppermute | solution.py:499
  80.6 5.8 %collective-permute-start.20 = (bf16[4,64,256]{2,1,0:T(8,128)(2,1)S(1)}, bf16[4,64,256]{2,1,0:T(8,128)(2,1)S(1)}, u32[]{:S(2)}, u32[]{:S(2)}) collective-permute-start(bf16[4,64,256]{2,1,0:T(8,128)(2,1)S(1)} %get-tuple-element.62), channel_id=1, source_target_pairs={{0,3},{1,2},{2,1},{3,0},{4,7},{5,6},{6,5},{7,4},{8,11},{9,10},{10,... | collective-permute-start | bytes 393224 | tf_op jit(solution)/shard_map/ppermute | solution.py:499
  87.4 3.2 %collective-permute-start.21 = (bf16[1552,256]{1,0:T(8,128)(2,1)S(1)}, bf16[1552,256]{1,0:T(8,128)(2,1)S(1)}, u32[]{:S(2)}, u32[]{:S(2)}) collective-permute-start(bf16[1552,256]{1,0:T(8,128)(2,1)S(1)} %get-tuple-element.63), channel_id=1, source_target_pairs={{0,1},{1,0},{2,3},{3,2},{4,5},{5,4},{6,7},{7,6},{8,9},{9,8},{10,11... | collective-permute-start | bytes 2383880 | tf_op jit(solution)/shard_map/ppermute | solution.py:491
  88.7 5.2 %collective-permute-start.22 = (bf16[144,256]{1,0:T(8,128)(2,1)S(1)}, bf16[144,256]{1,0:T(8,128)(2,1)S(1)}, u32[]{:S(2)}, u32[]{:S(2)}) collective-permute-start(bf16[144,256]{1,0:T(8,128)(2,1)S(1)} %get-tuple-element.71), channel_id=1, source_target_pairs={{0,2},{1,3},{2,0},{3,1},{4,6},{5,7},{6,4},{7,5},{8,10},{9,11},{10,... | collective-permute-start | bytes 221192 | tf_op jit(solution)/shard_map/ppermute | solution.py:499
  89.3 4.6 %collective-permute-start.23 = (bf16[144,256]{1,0:T(8,128)(2,1)S(1)}, bf16[144,256]{1,0:T(8,128)(2,1)S(1)}, u32[]{:S(2)}, u32[]{:S(2)}) collective-permute-start(bf16[144,256]{1,0:T(8,128)(2,1)S(1)} %get-tuple-element.72), channel_id=1, source_target_pairs={{0,3},{1,2},{2,1},{3,0},{4,7},{5,6},{6,5},{7,4},{8,11},{9,10},{10,... | collective-permute-start | bytes 221192 | tf_op jit(solution)/shard_map/ppermute | solution.py:499
  94.5 10.0 %collective-permute-start.24 = (f32[8,256]{1,0:T(8,128)S(1)}, f32[8,256]{1,0:T(8,128)S(1)}, u32[]{:S(2)}, u32[]{:S(2)}) collective-permute-start(f32[8,256]{1,0:T(8,128)S(1)} %shard_map.90.refs_0_), channel_id=1, source_target_pairs={{0,4},{4,8},{8,12},{12,0},{1,5},{5,9},{9,13},{13,1},{2,6},{6,10},{... | collective-permute-start | bytes 24584 | tf_op jit(solution)/shard_map/ppermute | solution.py:491
  100.5 4.5 %collective-permute-start.25 = (f32[8,256]{1,0:T(8,128)S(1)}, f32[8,256]{1,0:T(8,128)S(1)}, u32[]{:S(2)}, u32[]{:S(2)}) collective-permute-start(f32[8,256]{1,0:T(8,128)S(1)} %shard_map.90.refs_0_), channel_id=1, source_target_pairs={{0,8},{4,12},{8,0},{12,4},{1,9},{5,13},{9,1},{13,5},{2,10},{6,14},... | collective-permute-start | bytes 24584 | tf_op jit(solution)/shard_map/ppermute | solution.py:491
  100.8 4.3 %collective-permute-start.26 = (f32[8,256]{1,0:T(8,128)S(1)}, f32[8,256]{1,0:T(8,128)S(1)}, u32[]{:S(2)}, u32[]{:S(2)}) collective-permute-start(f32[8,256]{1,0:T(8,128)S(1)} %shard_map.90.refs_0_), channel_id=1, source_target_pairs={{0,12},{4,0},{8,4},{12,8},{1,13},{5,1},{9,5},{13,9},{2,14},{6,2},{... | collective-permute-start | bytes 24584 | tf_op jit(solution)/shard_map/ppermute | solution.py:491

commit v13 on v12

--- a/solution.py
+++ b/solution.py
@@ -28,6 +28,7 @@
         self.sector = lax.axis_size("sector")
         self.batch, self.slots, self.own_rows, self.order = vectors.shape
         assert self.batch == self.rep and self.sector % 4 == 0
+        assert self.sector & (self.sector - 1) == 0
         self.half = left_env.shape[2]
         self.chip_rows = self.own_rows * self.rep
         self.capacity = 2 * ((self.slots + 2 * self.sector - 1) // (2 * self.sector))
@@ -459,31 +460,25 @@
     )(plan, own, *arrived, *after)
 
 
-def mean_body(z, count, scale, *refs):
+def mean_body(z, scale, ours, theirs, *refs):
     out = refs[-1]
-    me = lax.axis_index("sector")
-    parts = [ref[0:1] for ref in refs[:count]]
-    total = parts[0]
-    if count > 1:
-        places = [lax.rem(me + z.sector - step, z.sector) for step in range(count)]
-        total = in_order(parts, places, count)
+    total = ours[0:1] + theirs[0:1]
     out[...] = total[:, : out.shape[1]] * scale
 
 
 def mean_over_sectors(z, array, entries, after):
-    held = [array]
-    if z.sector <= 4:
-        held += [shift(array, "sector", z.sector, step) for step in range(1, z.sector)]
-    else:
-        held = [total_over(array, "sector")]
+    step = 1
+    while 2 * step < z.sector:
+        array = array + exchange(z, array, step)
+        step *= 2
     made = pl.pallas_call(
-        functools.partial(mean_body, z, len(held), 1.0 / entries),
+        functools.partial(mean_body, z, 1.0 / entries),
         out_shape=jax.ShapeDtypeStruct((1, z.batch), jnp.float32),
-        in_specs=[VMEM] * len(held) + [ANY] * len(after),
+        in_specs=[VMEM] * 2 + [ANY] * len(after),
         out_specs=VMEM,
         compiler_params=pltpu.CompilerParams(vmem_limit_bytes=SMALL),
         cost_estimate=BRIEF,
-    )(*held, *after)
+    )(array, exchange(z, array, step), *after)
     return made.reshape(z.batch)
 
 
@@ -499,15 +494,8 @@
     return lax.ppermute(array, ("env", "rep"), perm)
 
 
-def total_over(array, axis):
-    size = lax.axis_size(axis)
-    if size & (size - 1):
-        return lax.psum(array, axis)
-    step = 1
-    while step < size:
-        array = array + lax.ppermute(array, axis, [(i, i ^ step) for i in range(size)])
-        step *= 2
-    return array
+def exchange(z, array, step):
+    return lax.ppermute(array, "sector", [(i, i ^ step) for i in range(z.sector)])
 
 
 def on_device(vectors, left_env, right_env, energy, partner):

time: 106 us -> 107 us (level)
  waiting for transfers between devices: 47.2 us -> 51 us
  starting transfers between devices: 32.9 us -> 30.7 us
    ppermute x15 -> x12, starting transfers between devices: 25.4 us -> 16.9 us  [shift(): lax.ppermute(array, axis, [(i, (i + step) % size) for i in range(size)])]
    ppermute x0 -> x2, starting transfers between devices: none -> 6.34 us  [exchange(): lax.ppermute(array, 'sector', [(i, i ^ step) for i in range(z.sector)])]
    ppermute x0 -> x2, waiting for transfers between devices: none -> 4.39 us  [exchange(): lax.ppermute(array, 'sector', [(i, i ^ step) for i in range(z.sector)])]
    ppermute x15 -> x12, waiting for transfers between devices: 13.7 us -> 13 us  [shift(): lax.ppermute(array, axis, [(i, (i + step) % size) for i in range(size)])]
  transfers between devices with their start and end apart: 27 -> 26, of which waited for: 11 -> 12; matrix products, arithmetic and copies ran while one was open for 1% -> 1% of each run, Pallas kernels for 20% -> 20%
where the time goes in v13:
time: 107 us
  waiting for transfers between devices  51 us (48%)
  starting transfers between devices  30.7 us (29%)
  Pallas kernels  23 us (21%)
    ppermute x12, waiting for transfers between devices, shift_both(): return lax.ppermute(array, ('env', 'rep'), perm)  33.6 us
    ppermute x12, starting transfers between devices, shift(): lax.ppermute(array, axis, [(i, (i + step) % size) for i in range(size)])  16.9 us
    ppermute x12, waiting for transfers between devices, shift(): lax.ppermute(array, axis, [(i, (i + step) % size) for i in range(size)])  13 us
    pallas_call x8, Pallas kernels, products(): pl.pallas_call(functools.partial(products_body, z, pieces, spans), out_sh...  7.53 us
    ppermute x12, starting transfers between devices, shift_both(): return lax.ppermute(array, ('env', 'rep'), perm)  7.46 us
    ppermute x2, starting transfers between devices, exchange(): lax.ppermute(array, 'sector', [(i, i ^ step) for i in range(z.sector)])  6.34 us
    pallas_call x5, Pallas kernels, terms(): pl.pallas_call(functools.partial(terms_body, z, spans, so_far is not None...  5.13 us
    ppermute x2, waiting for transfers between devices, exchange(): lax.ppermute(array, 'sector', [(i, i ^ step) for i in range(z.sector)])  4.39 us
  transfers between devices with their start and end apart: 26, of which 12 were waited for; matrix products, arithmetic and copies ran while one was open for 1% of the time, Pallas kernels for 20%

profile of v13, /device:TPU:0, one launch (start us, length us, event | category | flops | bytes accessed | tf_op | source)
XLA Modules:
  0.0 107.2 jit_solution(2306584497659759828)
XLA Ops:
  0.6 0.5 collective-permute-start.2
  1.1 0.1 collective-permute-start.3
  1.2 0.4 collective-permute-start.1
  1.7 2.6 %collective-permute-start = (s32[1,96]{1,0:T(1,128)}, s32[1,96]{1,0:T(1,128)S(1)}, u32[]{:S(2)}, u32[]{:S(2)}) collective-permute-start(s32[1,96]{1,0:T(1,128)} %partner.1), channel_id=1, source_target_pairs={{0,2},{2,0},{1,3},{3,1},{4,6},{6,4},{5,7},{7,5},{8,10},{10,8},{9,1... | collective-permute-start | bytes 1160 | tf_op jit(solution)/shard_map/ppermute | solution.py:486
  4.2 0.7 copy-done.3
  4.9 3.2 %shard_map.68 = (s32[74]{0:T(128)S(1)}, bf16[24,64,256]{2,1,0:T(8,128)(2,1)S(1)}, bf16[24,64,256]{2,1,0:T(8,128)(2,1)S(1)}, bf16[1,24,128,256]{3,2,1,0:T(8,128)(2,1)S(1)}) custom-call(s32[1,96]{1,0:T(1,128)S(1)} %copy-done.3, bf16[2,24,64,256]{3,2,1,0:T(8,128)(2,1)} %refs_3_.1, bf16[1,24,128,256]{3,2,1,0:T(8,128)(2,1)} %right.1), custom_call_target="tpu_custom_call" | custom-call | tf_op jit(solution)/shard_map/pallas_call | solution.py:100
  8.2 0.1 collective-permute-start.5
  8.3 1.5 %collective-permute-start.6 = (bf16[24,64,256]{2,1,0:T(8,128)(2,1)S(1)}, bf16[24,64,256]{2,1,0:T(8,128)(2,1)S(1)}, u32[]{:S(2)}, u32[]{:S(2)}) collective-permute-start(bf16[24,64,256]{2,1,0:T(8,128)(2,1)S(1)} %get-tuple-element.45), channel_id=1, source_target_pairs={{0,3},{1,2},{2,1},{3,0},{4,7},{5,6},{6,5},{7,4},{8,11},{9,10},{10,... | collective-permute-start | bytes 2359304 | tf_op jit(solution)/shard_map/ppermute | solution.py:494
  9.8 0.0 collective-permute-done.2.refs_2_
  9.8 0.0 collective-permute-done.3.refs_4_.refs_6_
  9.8 1.2 %shard_map.71 = (bf16[6,128,256]{2,1,0:T(8,128)(2,1)S(1)}, bf16[6,128,256]{2,1,0:T(8,128)(2,1)S(1)}) custom-call(s32[74]{0:T(128)S(1)} %get-tuple-element.39.refs_0_.plan, bf16[1,24,128,256]{3,2,1,0:T(8,128)(2,1)S(1)} %get-tuple-element.40.refs_1_, bf16[1,24,128,256]{3,2,1,0:T(8,128)(2,1)S(1)} %collective-permute-done.2.refs_2_, ...), custom_call_target="tpu_custom_call" | custom-call | tf_op jit(solution)/shard_map/pallas_call | solution.py:184
  11.0 1.6 %collective-permute-start.7 = (bf16[6,128,256]{2,1,0:T(8,128)(2,1)S(1)}, bf16[6,128,256]{2,1,0:T(8,128)(2,1)S(1)}, u32[]{:S(2)}, u32[]{:S(2)}) collective-permute-start(bf16[6,128,256]{2,1,0:T(8,128)(2,1)S(1)} %get-tuple-element.44.refs_5_), channel_id=1, source_target_pairs={{0,4},{4,8},{8,12},{12,0},{1,5},{5,9},{9,13},{13,1},{2,6},{6,10},{... | collective-permute-start | bytes 1179656 | tf_op jit(solution)/shard_map/ppermute | solution.py:486
  12.6 2.2 %collective-permute-start.8 = (bf16[6,128,256]{2,1,0:T(8,128)(2,1)S(1)}, bf16[6,128,256]{2,1,0:T(8,128)(2,1)S(1)}, u32[]{:S(2)}, u32[]{:S(2)}) collective-permute-start(bf16[6,128,256]{2,1,0:T(8,128)(2,1)S(1)} %get-tuple-element.46), channel_id=1, source_target_pairs={{0,12},{4,0},{8,4},{12,8},{1,13},{5,1},{9,5},{13,9},{2,14},{6,2},{... | collective-permute-start | bytes 1179656 | tf_op jit(solution)/shard_map/ppermute | solution.py:486
  14.9 0.9 shard_map.72.refs_5_
  15.8 0.9 collective-permute-start.4
  16.7 1.3 %shard_map.69.refs_6_.refs_1_ = s32[74]{0:T(128)S(1)} custom-call(s32[1,96]{1,0:T(1,128)S(1)} %collective-permute-done.partner.refs_2_), custom_call_target="tpu_custom_call" | custom-call | tf_op jit(solution)/shard_map/pallas_call | solution.py:122
  18.0 0.9 shard_map.73.refs_5_.refs_3_
  18.9 9.7 %collective-permute-done.5.refs_3_.refs_7_ = bf16[24,64,256]{2,1,0:T(8,128)(2,1)S(1)} collective-permute-done((bf16[24,64,256]{2,1,0:T(8,128)(2,1)S(1)}, bf16[24,64,256]{2,1,0:T(8,128)(2,1)S(1)}, u32[]{:S(2)}, u32[]{:S(2)}) %collective-permute-start.5) | collective-permute-done | bytes 786464 | tf_op jit(solution)/shard_map/ppermute | solution.py:494
  28.6 15.3 %collective-permute-done.6.refs_4_.refs_8_ = bf16[24,64,256]{2,1,0:T(8,128)(2,1)S(1)} collective-permute-done((bf16[24,64,256]{2,1,0:T(8,128)(2,1)S(1)}, bf16[24,64,256]{2,1,0:T(8,128)(2,1)S(1)}, u32[]{:S(2)}, u32[]{:S(2)}) %collective-permute-start.6) | collective-permute-done | bytes 786464 | tf_op jit(solution)/shard_map/ppermute | solution.py:494
  43.9 0.9 shard_map.74.refs_0_
  44.9 0.0 collective-permute-done.8.refs_2_.refs_3_
  44.9 0.0 copy-start
  44.9 1.6 %collective-permute-start.10 = (bf16[6,128,256]{2,1,0:T(8,128)(2,1)S(1)}, bf16[6,128,256]{2,1,0:T(8,128)(2,1)S(1)}, u32[]{:S(2)}, u32[]{:S(2)}) collective-permute-start(bf16[6,128,256]{2,1,0:T(8,128)(2,1)S(1)} %shard_map.75.refs_5_), channel_id=1, source_target_pairs={{0,4},{4,8},{8,12},{12,0},{1,5},{5,9},{9,13},{13,1},{2,6},{6,10},{... | collective-permute-start | bytes 1179656 | tf_op jit(solution)/shard_map/ppermute | solution.py:486
  46.6 0.9 shard_map.76.refs_4_
  47.5 1.1 shard_map.77
  48.6 0.6 collective-permute-start.9
  49.2 1.1 %collective-permute-start.14 = (bf16[6,64,256]{2,1,0:T(8,128)(2,1)S(1)}, bf16[6,64,256]{2,1,0:T(8,128)(2,1)S(1)}, u32[]{:S(2)}, u32[]{:S(2)}) collective-permute-start(bf16[6,64,256]{2,1,0:T(8,128)(2,1)S(1)} %get-tuple-element.49), channel_id=1, source_target_pairs={{0,3},{1,2},{2,1},{3,0},{4,7},{5,6},{6,5},{7,4},{8,11},{9,10},{10,... | collective-permute-start | bytes 589832 | tf_op jit(solution)/shard_map/ppermute | solution.py:494
  50.3 0.9 shard_map.78.refs_5_.refs_0_
  51.3 0.9 shard_map.79.refs_5_.refs_0_
  52.1 0.8 shard_map.80.refs_1_.refs_0_
  52.9 3.5 %collective-permute-done.9.refs_3_.refs_11_.refs_6_ = bf16[6,64,256]{2,1,0:T(8,128)(2,1)S(1)} collective-permute-done((bf16[6,64,256]{2,1,0:T(8,128)(2,1)S(1)}, bf16[6,64,256]{2,1,0:T(8,128)(2,1)S(1)}, u32[]{:S(2)}, u32[]{:S(2)}) %collective-permute-start.9) | collective-permute-done | bytes 196640 | tf_op jit(solution)/shard_map/ppermute | solution.py:494
  56.4 2.5 %collective-permute-start.13 = (bf16[6,128,256]{2,1,0:T(8,128)(2,1)S(1)}, bf16[6,128,256]{2,1,0:T(8,128)(2,1)S(1)}, u32[]{:S(2)}, u32[]{:S(2)}) collective-permute-start(bf16[6,128,256]{2,1,0:T(8,128)(2,1)S(1)} %shard_map.81.refs_1_), channel_id=1, source_target_pairs={{0,12},{4,0},{8,4},{12,8},{1,13},{5,1},{9,5},{13,9},{2,14},{6,2},{... | collective-permute-start | bytes 1179656 | tf_op jit(solution)/shard_map/ppermute | solution.py:486
  58.8 0.0 collective-permute-done.10.refs_2_.refs_4_
  58.8 0.5 collective-permute-done.14.refs_12_.refs_7_
  59.4 1.1 shard_map.84
  60.5 0.6 collective-permute-start.15
  61.1 3.2 %collective-permute-start.11 = (bf16[4,128,256]{2,1,0:T(8,128)(2,1)S(1)}, bf16[4,128,256]{2,1,0:T(8,128)(2,1)S(1)}, u32[]{:S(2)}, u32[]{:S(2)}) collective-permute-start(bf16[4,128,256]{2,1,0:T(8,128)(2,1)S(1)} %shard_map.82.refs_10_), channel_id=1, source_target_pairs={{0,8},{4,12},{8,0},{12,4},{1,9},{5,13},{9,1},{13,5},{2,10},{6,14},... | collective-permute-start | bytes 786440 | tf_op jit(solution)/shard_map/ppermute | solution.py:486
  64.3 0.9 collective-permute-start.16
  65.2 3.0 %collective-permute-done.15.refs_10_.refs_9_ = bf16[6,64,256]{2,1,0:T(8,128)(2,1)S(1)} collective-permute-done((bf16[6,64,256]{2,1,0:T(8,128)(2,1)S(1)}, bf16[6,64,256]{2,1,0:T(8,128)(2,1)S(1)}, u32[]{:S(2)}, u32[]{:S(2)}) %collective-permute-start.15) | collective-permute-done | bytes 196640 | tf_op jit(solution)/shard_map/ppermute | solution.py:494
  68.2 0.2 collective-permute-done.13.refs_4_
  68.4 1.1 shard_map.85
  69.5 0.6 collective-permute-start.17
  70.1 0.0 collective-permute-start.18
  70.1 9.0 %collective-permute-done.11.refs_1_.refs_4_ = bf16[4,128,256]{2,1,0:T(8,128)(2,1)S(1)} collective-permute-done((bf16[4,128,256]{2,1,0:T(8,128)(2,1)S(1)}, bf16[4,128,256]{2,1,0:T(8,128)(2,1)S(1)}, u32[]{:S(2)}, u32[]{:S(2)}) %collective-permute-start.11) | collective-permute-done | bytes 262176 | tf_op jit(solution)/shard_map/ppermute | solution.py:486
  79.0 0.0 copy-start.1
  79.1 0.0 copy-start.2
  79.1 0.9 shard_map.86
  80.0 0.6 collective-permute-start.19
  80.6 0.9 fusion.refs_10_
  81.5 3.4 %collective-permute-done.12.refs_4_ = bf16[2,128,256]{2,1,0:T(8,128)(2,1)S(1)} collective-permute-done((bf16[2,128,256]{2,1,0:T(8,128)(2,1)S(1)}, bf16[2,128,256]{2,1,0:T(8,128)(2,1)S(1)}, u32[]{:S(2)}, u32[]{:S(2)}) %collective-permute-start.12) | collective-permute-done | bytes 131104 | tf_op jit(solution)/shard_map/ppermute | solution.py:486
  84.9 1.5 %collective-permute-done.19.refs_16_.refs_15_ = bf16[4,64,256]{2,1,0:T(8,128)(2,1)S(1)} collective-permute-done((bf16[4,64,256]{2,1,0:T(8,128)(2,1)S(1)}, bf16[4,64,256]{2,1,0:T(8,128)(2,1)S(1)}, u32[]{:S(2)}, u32[]{:S(2)}) %collective-permute-start.19) | collective-permute-done | bytes 131104 | tf_op jit(solution)/shard_map/ppermute | solution.py:494
  86.4 1.0 shard_map.87
  87.4 1.3 %collective-permute-start.21 = (bf16[1552,256]{1,0:T(8,128)(2,1)S(1)}, bf16[1552,256]{1,0:T(8,128)(2,1)S(1)}, u32[]{:S(2)}, u32[]{:S(2)}) collective-permute-start(bf16[1552,256]{1,0:T(8,128)(2,1)S(1)} %get-tuple-element.63), channel_id=1, source_target_pairs={{0,1},{1,0},{2,3},{3,2},{4,5},{5,4},{6,7},{7,6},{8,9},{9,8},{10,11... | collective-permute-start | bytes 2383880 | tf_op jit(solution)/shard_map/ppermute | solution.py:486
  88.7 0.6 collective-permute-start.22
  89.3 0.8 collective-permute-start.23
  90.1 0.5 collective-permute-done.21.refs_4_.refs_0_
  90.6 3.2 %shard_map.88 = (f32[2,24,64,256]{3,2,1,0:T(8,128)S(1)}, f32[2,24,64,256]{3,2,1,0:T(8,128)}) custom-call(s32[74]{0:T(128)S(1)} %get-tuple-element.39.refs_0_.plan, s32[74]{0:T(128)S(1)} %shard_map.69.refs_6_.refs_1_, f32[24]{0:T(128)S(1)} %copy-done.2, bf16[2,24,64,256]{3,2,1,0:T(8,128)(2,1)S(1)} %copy-done.1, ...), custom_call_target="tpu_custom_call" | custom-call | tf_op jit(solution)/shard_map/pallas_call | solution.py:366
  93.9 0.6 shard_map.90
  94.5 6.0 %collective-permute-start.24 = (f32[8,256]{1,0:T(8,128)S(1)}, f32[8,256]{1,0:T(8,128)S(1)}, u32[]{:S(2)}, u32[]{:S(2)}) collective-permute-start(f32[8,256]{1,0:T(8,128)S(1)} %shard_map.90), channel_id=1, source_target_pairs={{0,4},{4,0},{8,12},{12,8},{1,5},{5,1},{9,13},{13,9},{2,6},{6,2},{1... | collective-permute-start | bytes 24584 | tf_op jit(solution)/shard_map/ppermute | solution.py:498
  100.5 1.6 %collective-permute-done.24 = f32[8,256]{1,0:T(8,128)S(1)} collective-permute-done((f32[8,256]{1,0:T(8,128)S(1)}, f32[8,256]{1,0:T(8,128)S(1)}, u32[]{:S(2)}, u32[]{:S(2)}) %collective-permute-start.24) | collective-permute-done | bytes 8224 | tf_op jit(solution)/shard_map/ppermute | solution.py:498
  102.2 0.3 collective-permute-start.25
  102.5 1.5 %shard_map.89 = (f32[2,24,64,256]{3,2,1,0:T(8,128)}, f32[8,128]{1,0:T(8,128)S(1)}) custom-call(s32[74]{0:T(128)S(1)} %get-tuple-element.39.refs_0_.plan, s32[74]{0:T(128)S(1)} %shard_map.69.refs_6_.refs_1_, f32[2,24,64,256]{3,2,1,0:T(8,128)S(1)} %get-tuple-element.69.refs_2_.refs_3_, ...), custom_call_target="tpu_custom_call", output_to_operand_aliasing={{0}: (7, {})} | custom-call | tf_op jit(solution)/shard_map/pallas_call | solution.py:411
  104.0 2.8 %collective-permute-done.25.theirs = f32[8,256]{1,0:T(8,128)S(1)} collective-permute-done((f32[8,256]{1,0:T(8,128)S(1)}, f32[8,256]{1,0:T(8,128)S(1)}, u32[]{:S(2)}, u32[]{:S(2)}) %collective-permute-start.25) | collective-permute-done | bytes 8224 | tf_op jit(solution)/shard_map/ppermute | solution.py:498
  106.7 0.5 shard_map.91
  (22 shorter events, 0.0 us)
Async XLA Ops:
  0.6 9.1 %collective-permute-start.2 = (bf16[1,24,128,256]{3,2,1,0:T(8,128)(2,1)}, bf16[1,24,128,256]{3,2,1,0:T(8,128)(2,1)S(1)}, u32[]{:S(2)}, u32[]{:S(2)}) collective-permute-start(bf16[1,24,128,256]{3,2,1,0:T(8,128)(2,1)} %right.1), channel_id=1, source_target_pairs={{0,1},{1,0},{2,3},{3,2},{4,5},{5,4},{6,7},{7,6},{8,9},{9,8},{10,11... | collective-permute-start | bytes 4718600 | tf_op jit(solution)/shard_map/ppermute | solution.py:486
  1.1 8.6 %collective-permute-start.3 = (bf16[2,24,64,256]{3,2,1,0:T(8,128)(2,1)}, bf16[2,24,64,256]{3,2,1,0:T(8,128)(2,1)S(1)}, u32[]{:S(2)}, u32[]{:S(2)}) collective-permute-start(bf16[2,24,64,256]{3,2,1,0:T(8,128)(2,1)} %refs_3_.1), channel_id=1, source_target_pairs={{0,1},{1,0},{2,3},{3,2},{4,5},{5,4},{6,7},{7,6},{8,9},{9,8},{10,11... | collective-permute-start | bytes 4718600 | tf_op jit(solution)/shard_map/ppermute | solution.py:486
  1.2 13.6 %collective-permute-start.1 = (bf16[1,24,128,256]{3,2,1,0:T(8,128)(2,1)}, bf16[1,24,128,256]{3,2,1,0:T(8,128)(2,1)S(1)}, u32[]{:S(2)}, u32[]{:S(2)}) collective-permute-start(bf16[1,24,128,256]{3,2,1,0:T(8,128)(2,1)} %refs_1_.9), channel_id=1, source_target_pairs={{0,1},{1,0},{2,3},{3,2},{4,5},{5,4},{6,7},{7,6},{8,9},{9,8},{10,11... | collective-permute-start | bytes 4718600 | tf_op jit(solution)/shard_map/ppermute | solution.py:486
  1.7 6.5 %collective-permute-start = (s32[1,96]{1,0:T(1,128)}, s32[1,96]{1,0:T(1,128)S(1)}, u32[]{:S(2)}, u32[]{:S(2)}) collective-permute-start(s32[1,96]{1,0:T(1,128)} %partner.1), channel_id=1, source_target_pairs={{0,2},{2,0},{1,3},{3,1},{4,6},{6,4},{5,7},{7,5},{8,10},{10,8},{9,1... | collective-permute-start | bytes 1160 | tf_op jit(solution)/shard_map/ppermute | solution.py:486
  4.2 0.7 copy-start.3
  8.2 20.5 %collective-permute-start.5 = (bf16[24,64,256]{2,1,0:T(8,128)(2,1)S(1)}, bf16[24,64,256]{2,1,0:T(8,128)(2,1)S(1)}, u32[]{:S(2)}, u32[]{:S(2)}) collective-permute-start(bf16[24,64,256]{2,1,0:T(8,128)(2,1)S(1)} %get-tuple-element.43.refs_3_.refs_5_), channel_id=1, source_target_pairs={{0,2},{1,3},{2,0},{3,1},{4,6},{5,7},{6,4},{7,5},{8,10},{9,11},{10,... | collective-permute-start | bytes 2359304 | tf_op jit(solution)/shard_map/ppermute | solution.py:494
  8.3 35.7 %collective-permute-start.6 = (bf16[24,64,256]{2,1,0:T(8,128)(2,1)S(1)}, bf16[24,64,256]{2,1,0:T(8,128)(2,1)S(1)}, u32[]{:S(2)}, u32[]{:S(2)}) collective-permute-start(bf16[24,64,256]{2,1,0:T(8,128)(2,1)S(1)} %get-tuple-element.45), channel_id=1, source_target_pairs={{0,3},{1,2},{2,1},{3,0},{4,7},{5,6},{6,5},{7,4},{8,11},{9,10},{10,... | collective-permute-start | bytes 2359304 | tf_op jit(solution)/shard_map/ppermute | solution.py:494
  11.0 33.9 %collective-permute-start.7 = (bf16[6,128,256]{2,1,0:T(8,128)(2,1)S(1)}, bf16[6,128,256]{2,1,0:T(8,128)(2,1)S(1)}, u32[]{:S(2)}, u32[]{:S(2)}) collective-permute-start(bf16[6,128,256]{2,1,0:T(8,128)(2,1)S(1)} %get-tuple-element.44.refs_5_), channel_id=1, source_target_pairs={{0,4},{4,8},{8,12},{12,0},{1,5},{5,9},{9,13},{13,1},{2,6},{6,10},{... | collective-permute-start | bytes 1179656 | tf_op jit(solution)/shard_map/ppermute | solution.py:486
  12.6 32.3 %collective-permute-start.8 = (bf16[6,128,256]{2,1,0:T(8,128)(2,1)S(1)}, bf16[6,128,256]{2,1,0:T(8,128)(2,1)S(1)}, u32[]{:S(2)}, u32[]{:S(2)}) collective-permute-start(bf16[6,128,256]{2,1,0:T(8,128)(2,1)S(1)} %get-tuple-element.46), channel_id=1, source_target_pairs={{0,12},{4,0},{8,4},{12,8},{1,13},{5,1},{9,5},{13,9},{2,14},{6,2},{... | collective-permute-start | bytes 1179656 | tf_op jit(solution)/shard_map/ppermute | solution.py:486
  15.8 37.1 %collective-permute-start.4 = (bf16[6,128,256]{2,1,0:T(8,128)(2,1)S(1)}, bf16[6,128,256]{2,1,0:T(8,128)(2,1)S(1)}, u32[]{:S(2)}, u32[]{:S(2)}) collective-permute-start(bf16[6,128,256]{2,1,0:T(8,128)(2,1)S(1)} %shard_map.72.refs_5_), channel_id=1, source_target_pairs={{0,8},{4,12},{8,0},{12,4},{1,9},{5,13},{9,1},{13,5},{2,10},{6,14},... | collective-permute-start | bytes 1179656 | tf_op jit(solution)/shard_map/ppermute | solution.py:486
  44.9 2.6 %copy-start = (bf16[1,24,128,256]{3,2,1,0:T(8,128)(2,1)S(1)}, bf16[1,24,128,256]{3,2,1,0:T(8,128)(2,1)}, u32[]{:S(2)}) copy-start(bf16[1,24,128,256]{3,2,1,0:T(8,128)(2,1)} %refs_1_.9) | copy-start | bytes 4718596
  44.9 13.9 %collective-permute-start.10 = (bf16[6,128,256]{2,1,0:T(8,128)(2,1)S(1)}, bf16[6,128,256]{2,1,0:T(8,128)(2,1)S(1)}, u32[]{:S(2)}, u32[]{:S(2)}) collective-permute-start(bf16[6,128,256]{2,1,0:T(8,128)(2,1)S(1)} %shard_map.75.refs_5_), channel_id=1, source_target_pairs={{0,4},{4,8},{8,12},{12,0},{1,5},{5,9},{9,13},{13,1},{2,6},{6,10},{... | collective-permute-start | bytes 1179656 | tf_op jit(solution)/shard_map/ppermute | solution.py:486
  48.6 7.8 %collective-permute-start.9 = (bf16[6,64,256]{2,1,0:T(8,128)(2,1)S(1)}, bf16[6,64,256]{2,1,0:T(8,128)(2,1)S(1)}, u32[]{:S(2)}, u32[]{:S(2)}) collective-permute-start(bf16[6,64,256]{2,1,0:T(8,128)(2,1)S(1)} %get-tuple-element.48), channel_id=1, source_target_pairs={{0,2},{1,3},{2,0},{3,1},{4,6},{5,7},{6,4},{7,5},{8,10},{9,11},{10,... | collective-permute-start | bytes 589832 | tf_op jit(solution)/shard_map/ppermute | solution.py:494
  49.2 10.2 %collective-permute-start.14 = (bf16[6,64,256]{2,1,0:T(8,128)(2,1)S(1)}, bf16[6,64,256]{2,1,0:T(8,128)(2,1)S(1)}, u32[]{:S(2)}, u32[]{:S(2)}) collective-permute-start(bf16[6,64,256]{2,1,0:T(8,128)(2,1)S(1)} %get-tuple-element.49), channel_id=1, source_target_pairs={{0,3},{1,2},{2,1},{3,0},{4,7},{5,6},{6,5},{7,4},{8,11},{9,10},{10,... | collective-permute-start | bytes 589832 | tf_op jit(solution)/shard_map/ppermute | solution.py:494
  56.4 12.0 %collective-permute-start.13 = (bf16[6,128,256]{2,1,0:T(8,128)(2,1)S(1)}, bf16[6,128,256]{2,1,0:T(8,128)(2,1)S(1)}, u32[]{:S(2)}, u32[]{:S(2)}) collective-permute-start(bf16[6,128,256]{2,1,0:T(8,128)(2,1)S(1)} %shard_map.81.refs_1_), channel_id=1, source_target_pairs={{0,12},{4,0},{8,4},{12,8},{1,13},{5,1},{9,5},{13,9},{2,14},{6,2},{... | collective-permute-start | bytes 1179656 | tf_op jit(solution)/shard_map/ppermute | solution.py:486
  60.5 7.8 %collective-permute-start.15 = (bf16[6,64,256]{2,1,0:T(8,128)(2,1)S(1)}, bf16[6,64,256]{2,1,0:T(8,128)(2,1)S(1)}, u32[]{:S(2)}, u32[]{:S(2)}) collective-permute-start(bf16[6,64,256]{2,1,0:T(8,128)(2,1)S(1)} %get-tuple-element.51), channel_id=1, source_target_pairs={{0,2},{1,3},{2,0},{3,1},{4,6},{5,7},{6,4},{7,5},{8,10},{9,11},{10,... | collective-permute-start | bytes 589832 | tf_op jit(solution)/shard_map/ppermute | solution.py:494
  61.1 18.0 %collective-permute-start.11 = (bf16[4,128,256]{2,1,0:T(8,128)(2,1)S(1)}, bf16[4,128,256]{2,1,0:T(8,128)(2,1)S(1)}, u32[]{:S(2)}, u32[]{:S(2)}) collective-permute-start(bf16[4,128,256]{2,1,0:T(8,128)(2,1)S(1)} %shard_map.82.refs_10_), channel_id=1, source_target_pairs={{0,8},{4,12},{8,0},{12,4},{1,9},{5,13},{9,1},{13,5},{2,10},{6,14},... | collective-permute-start | bytes 786440 | tf_op jit(solution)/shard_map/ppermute | solution.py:486
  64.3 14.7 %collective-permute-start.16 = (bf16[6,64,256]{2,1,0:T(8,128)(2,1)S(1)}, bf16[6,64,256]{2,1,0:T(8,128)(2,1)S(1)}, u32[]{:S(2)}, u32[]{:S(2)}) collective-permute-start(bf16[6,64,256]{2,1,0:T(8,128)(2,1)S(1)} %get-tuple-element.53), channel_id=1, source_target_pairs={{0,3},{1,2},{2,1},{3,0},{4,7},{5,6},{6,5},{7,4},{8,11},{9,10},{10,... | collective-permute-start | bytes 589832 | tf_op jit(solution)/shard_map/ppermute | solution.py:494
  69.5 9.6 %collective-permute-start.17 = (bf16[6,64,256]{2,1,0:T(8,128)(2,1)S(1)}, bf16[6,64,256]{2,1,0:T(8,128)(2,1)S(1)}, u32[]{:S(2)}, u32[]{:S(2)}) collective-permute-start(bf16[6,64,256]{2,1,0:T(8,128)(2,1)S(1)} %get-tuple-element.54), channel_id=1, source_target_pairs={{0,2},{1,3},{2,0},{3,1},{4,6},{5,7},{6,4},{7,5},{8,10},{9,11},{10,... | collective-permute-start | bytes 589832 | tf_op jit(solution)/shard_map/ppermute | solution.py:494
  70.1 14.8 %collective-permute-start.18 = (bf16[6,64,256]{2,1,0:T(8,128)(2,1)S(1)}, bf16[6,64,256]{2,1,0:T(8,128)(2,1)S(1)}, u32[]{:S(2)}, u32[]{:S(2)}) collective-permute-start(bf16[6,64,256]{2,1,0:T(8,128)(2,1)S(1)} %get-tuple-element.60), channel_id=1, source_target_pairs={{0,3},{1,2},{2,1},{3,0},{4,7},{5,6},{6,5},{7,4},{8,11},{9,10},{10,... | collective-permute-start | bytes 589832 | tf_op jit(solution)/shard_map/ppermute | solution.py:494
  79.0 5.9 %collective-permute-start.12 = (bf16[2,128,256]{2,1,0:T(8,128)(2,1)S(1)}, bf16[2,128,256]{2,1,0:T(8,128)(2,1)S(1)}, u32[]{:S(2)}, u32[]{:S(2)}) collective-permute-start(bf16[2,128,256]{2,1,0:T(8,128)(2,1)S(1)} %shard_map.83.refs_10_), channel_id=1, source_target_pairs={{0,8},{4,12},{8,0},{12,4},{1,9},{5,13},{9,1},{13,5},{2,10},{6,14},... | collective-permute-start | bytes 393224 | tf_op jit(solution)/shard_map/ppermute | solution.py:486
  79.0 1.6 %copy-start.1 = (bf16[2,24,64,256]{3,2,1,0:T(8,128)(2,1)S(1)}, bf16[2,24,64,256]{3,2,1,0:T(8,128)(2,1)}, u32[]{:S(2)}) copy-start(bf16[2,24,64,256]{3,2,1,0:T(8,128)(2,1)} %refs_3_.1) | copy-start | bytes 4718596
  79.1 1.6 %copy-start.2 = (f32[24]{0:T(128)S(1)}, f32[24]{0:T(128)}, u32[]{:S(2)}) copy-start(f32[24]{0:T(128)} %refs_2_.1) | copy-start | bytes 292
  80.0 6.4 %collective-permute-start.19 = (bf16[4,64,256]{2,1,0:T(8,128)(2,1)S(1)}, bf16[4,64,256]{2,1,0:T(8,128)(2,1)S(1)}, u32[]{:S(2)}, u32[]{:S(2)}) collective-permute-start(bf16[4,64,256]{2,1,0:T(8,128)(2,1)S(1)} %get-tuple-element.61), channel_id=1, source_target_pairs={{0,2},{1,3},{2,0},{3,1},{4,6},{5,7},{6,4},{7,5},{8,10},{9,11},{10,... | collective-permute-start | bytes 393224 | tf_op jit(solution)/shard_map/ppermute | solution.py:494
  80.6 5.8 %collective-permute-start.20 = (bf16[4,64,256]{2,1,0:T(8,128)(2,1)S(1)}, bf16[4,64,256]{2,1,0:T(8,128)(2,1)S(1)}, u32[]{:S(2)}, u32[]{:S(2)}) collective-permute-start(bf16[4,64,256]{2,1,0:T(8,128)(2,1)S(1)} %get-tuple-element.62), channel_id=1, source_target_pairs={{0,3},{1,2},{2,1},{3,0},{4,7},{5,6},{6,5},{7,4},{8,11},{9,10},{10,... | collective-permute-start | bytes 393224 | tf_op jit(solution)/shard_map/ppermute | solution.py:494
  87.4 3.2 %collective-permute-start.21 = (bf16[1552,256]{1,0:T(8,128)(2,1)S(1)}, bf16[1552,256]{1,0:T(8,128)(2,1)S(1)}, u32[]{:S(2)}, u32[]{:S(2)}) collective-permute-start(bf16[1552,256]{1,0:T(8,128)(2,1)S(1)} %get-tuple-element.63), channel_id=1, source_target_pairs={{0,1},{1,0},{2,3},{3,2},{4,5},{5,4},{6,7},{7,6},{8,9},{9,8},{10,11... | collective-permute-start | bytes 2383880 | tf_op jit(solution)/shard_map/ppermute | solution.py:486
  88.7 5.2 %collective-permute-start.22 = (bf16[144,256]{1,0:T(8,128)(2,1)S(1)}, bf16[144,256]{1,0:T(8,128)(2,1)S(1)}, u32[]{:S(2)}, u32[]{:S(2)}) collective-permute-start(bf16[144,256]{1,0:T(8,128)(2,1)S(1)} %get-tuple-element.71), channel_id=1, source_target_pairs={{0,2},{1,3},{2,0},{3,1},{4,6},{5,7},{6,4},{7,5},{8,10},{9,11},{10,... | collective-permute-start | bytes 221192 | tf_op jit(solution)/shard_map/ppermute | solution.py:494
  89.3 4.6 %collective-permute-start.23 = (bf16[144,256]{1,0:T(8,128)(2,1)S(1)}, bf16[144,256]{1,0:T(8,128)(2,1)S(1)}, u32[]{:S(2)}, u32[]{:S(2)}) collective-permute-start(bf16[144,256]{1,0:T(8,128)(2,1)S(1)} %get-tuple-element.72), channel_id=1, source_target_pairs={{0,3},{1,2},{2,1},{3,0},{4,7},{5,6},{6,5},{7,4},{8,11},{9,10},{10,... | collective-permute-start | bytes 221192 | tf_op jit(solution)/shard_map/ppermute | solution.py:494
  94.5 7.7 %collective-permute-start.24 = (f32[8,256]{1,0:T(8,128)S(1)}, f32[8,256]{1,0:T(8,128)S(1)}, u32[]{:S(2)}, u32[]{:S(2)}) collective-permute-start(f32[8,256]{1,0:T(8,128)S(1)} %shard_map.90), channel_id=1, source_target_pairs={{0,4},{4,0},{8,12},{12,8},{1,5},{5,1},{9,13},{13,9},{2,6},{6,2},{1... | collective-permute-start | bytes 24584 | tf_op jit(solution)/shard_map/ppermute | solution.py:498
  102.2 4.5 %collective-permute-start.25 = (f32[8,256]{1,0:T(8,128)S(1)}, f32[8,256]{1,0:T(8,128)S(1)}, u32[]{:S(2)}, u32[]{:S(2)}) collective-permute-start(f32[8,256]{1,0:T(8,128)S(1)} %add.3.ours), channel_id=1, source_target_pairs={{0,8},{4,12},{8,0},{12,4},{1,9},{5,13},{9,1},{13,5},{2,10},{6,14},... | collective-permute-start | bytes 24584 | tf_op jit(solution)/shard_map/ppermute | solution.py:498

commit v14 on v12

--- a/solution.py
+++ b/solution.py
@@ -318,11 +318,12 @@
             n += 1
 
 
-def add_terms(z, plans, image, parts, spans):
+def add_terms(z, plans, image, parts, spans, kinds):
     core = plans[0][z.core]
 
     def add(slot, blocks):
-        for s, block in enumerate(blocks):
+        for s in kinds:
+            block = blocks[s]
             v = lax.rem(core + z.rep - s, z.rep)
             image[v, slot] += block().astype(jnp.float32)
 
@@ -335,24 +336,30 @@
     energy, vectors = refs.pop(0), refs.pop(0)
     so_far, image, sem = refs[-3:]
 
-    def start(j, carry):
-        for v in range(z.batch):
-            so_far[v, j] = energy[j] * vectors[v, j].astype(jnp.float32)
-        return carry
-
-    lax.fori_loop(0, z.slots, start, 0, unroll=2)
+    core = plans[0][z.core]
     joined = [refs.pop(0) for _ in range(z.rep - 1)]
+    chunk_parts = []
     for spans in chunks:
         parts = [[(refs.pop(0), 0)] + [(ref, skip) for ref in joined]]
         for _ in range(1, z.env):
             parts.append([(refs.pop(0), 0) for _ in range(z.rep)])
-        add_terms(z, plans, so_far, parts, spans)
+        chunk_parts.append(parts)
         skip += sum(span[1] for span in spans)
     copies = []
-    for v in range(z.batch):
-        copies += split_copy(so_far.at[v], image.at[v], z.slots, sem.at[v])
-    for copy in copies:
-        copy.start()
+    for s in range(z.rep):
+        v = lax.rem(core + z.rep - s, z.rep)
+
+        def start(j, carry):
+            so_far[v, j] = energy[j] * vectors[v, j].astype(jnp.float32)
+            return carry
+
+        lax.fori_loop(0, z.slots, start, 0, unroll=4)
+        for parts, spans in zip(chunk_parts, chunks):
+            add_terms(z, plans, so_far, parts, spans, (s,))
+        made = split_copy(so_far.at[v], image.at[v], z.slots, sem.at[s])
+        for copy in made:
+            copy.start()
+        copies += made
     for copy in copies:
         copy.wait()
 
@@ -386,7 +393,7 @@
             sums[v, slot] = so_far[v, slot]
 
     for_terms(z, plans, parts, spans, take)
-    add_terms(z, plans, sums, parts, spans)
+    add_terms(z, plans, sums, parts, spans, range(z.rep))
     for wait in (False, True):
         used = []
 

time: 106 us -> 106 us (level)
  transfers between devices with their start and end apart: 27 -> 27, of which waited for: 11 -> 12; matrix products, arithmetic and copies ran while one was open for 1% -> 1% of each run, Pallas kernels for 20% -> 19%
where the time goes in v14:
time: 106 us
  waiting for transfers between devices  47.7 us (45%)
  starting transfers between devices  32.9 us (31%)
  Pallas kernels  22.6 us (21%)
    ppermute x12, waiting for transfers between devices, shift_both(): return lax.ppermute(array, ('env', 'rep'), perm)  34 us
    ppermute x15, starting transfers between devices, shift(): lax.ppermute(array, axis, [(i, (i + step) % size) for i in range(size)])  25.4 us
    ppermute x15, waiting for transfers between devices, shift(): lax.ppermute(array, axis, [(i, (i + step) % size) for i in range(size)])  13.7 us
    pallas_call x8, Pallas kernels, products(): pl.pallas_call(functools.partial(products_body, z, pieces, spans), out_sh...  7.53 us
    ppermute x12, starting transfers between devices, shift_both(): return lax.ppermute(array, ('env', 'rep'), perm)  7.46 us
    pallas_call x5, Pallas kernels, terms(): pl.pallas_call(functools.partial(terms_body, z, spans, so_far is not None...  5.13 us
    pallas_call x1, Pallas kernels, load(): pl.pallas_call(functools.partial(load_body, z), out_shape=[jax.ShapeDtype...  3.24 us
    pallas_call x1, Pallas kernels, gather_terms(): pl.pallas_call(functools.partial(gather_body, z, chunks, skip), out_shape...  2.76 us
  transfers between devices with their start and end apart: 27, of which 12 were waited for; matrix products, arithmetic and copies ran while one was open for 1% of the time, Pallas kernels for 19%

profile of v14, /device:TPU:0, one launch (start us, length us, event | category | flops | bytes accessed | tf_op | source)
XLA Modules:
  0.0 105.5 jit_solution(5630833142011271507)
XLA Ops:
  0.6 0.5 collective-permute-start.2
  1.1 0.1 collective-permute-start.3
  1.2 0.4 collective-permute-start.1
  1.7 2.6 %collective-permute-start = (s32[1,96]{1,0:T(1,128)}, s32[1,96]{1,0:T(1,128)S(1)}, u32[]{:S(2)}, u32[]{:S(2)}) collective-permute-start(s32[1,96]{1,0:T(1,128)} %partner.1), channel_id=1, source_target_pairs={{0,2},{2,0},{1,3},{3,1},{4,6},{6,4},{5,7},{7,5},{8,10},{10,8},{9,1... | collective-permute-start | bytes 1160 | tf_op jit(solution)/shard_map/ppermute | solution.py:498
  4.2 0.7 copy-done.3
  4.9 3.2 %shard_map.68 = (s32[74]{0:T(128)S(1)}, bf16[24,64,256]{2,1,0:T(8,128)(2,1)S(1)}, bf16[24,64,256]{2,1,0:T(8,128)(2,1)S(1)}, bf16[1,24,128,256]{3,2,1,0:T(8,128)(2,1)S(1)}) custom-call(s32[1,96]{1,0:T(1,128)S(1)} %copy-done.3, bf16[2,24,64,256]{3,2,1,0:T(8,128)(2,1)} %refs_3_.1, bf16[1,24,128,256]{3,2,1,0:T(8,128)(2,1)} %right.1), custom_call_target="tpu_custom_call" | custom-call | tf_op jit(solution)/shard_map/pallas_call | solution.py:99
  8.2 0.0 collective-permute-done.partner.refs_2_
  8.2 0.1 collective-permute-start.5
  8.3 1.5 %collective-permute-start.6 = (bf16[24,64,256]{2,1,0:T(8,128)(2,1)S(1)}, bf16[24,64,256]{2,1,0:T(8,128)(2,1)S(1)}, u32[]{:S(2)}, u32[]{:S(2)}) collective-permute-start(bf16[24,64,256]{2,1,0:T(8,128)(2,1)S(1)} %get-tuple-element.45), channel_id=1, source_target_pairs={{0,3},{1,2},{2,1},{3,0},{4,7},{5,6},{6,5},{7,4},{8,11},{9,10},{10,... | collective-permute-start | bytes 2359304 | tf_op jit(solution)/shard_map/ppermute | solution.py:506
  9.8 1.2 %shard_map.71 = (bf16[6,128,256]{2,1,0:T(8,128)(2,1)S(1)}, bf16[6,128,256]{2,1,0:T(8,128)(2,1)S(1)}) custom-call(s32[74]{0:T(128)S(1)} %get-tuple-element.39.refs_0_.plan, bf16[1,24,128,256]{3,2,1,0:T(8,128)(2,1)S(1)} %get-tuple-element.40.refs_1_, bf16[1,24,128,256]{3,2,1,0:T(8,128)(2,1)S(1)} %collective-permute-done.2.refs_2_, ...), custom_call_target="tpu_custom_call" | custom-call | tf_op jit(solution)/shard_map/pallas_call | solution.py:183
  11.0 1.6 %collective-permute-start.7 = (bf16[6,128,256]{2,1,0:T(8,128)(2,1)S(1)}, bf16[6,128,256]{2,1,0:T(8,128)(2,1)S(1)}, u32[]{:S(2)}, u32[]{:S(2)}) collective-permute-start(bf16[6,128,256]{2,1,0:T(8,128)(2,1)S(1)} %get-tuple-element.44.refs_5_), channel_id=1, source_target_pairs={{0,4},{4,8},{8,12},{12,0},{1,5},{5,9},{9,13},{13,1},{2,6},{6,10},{... | collective-permute-start | bytes 1179656 | tf_op jit(solution)/shard_map/ppermute | solution.py:498
  12.6 2.2 %collective-permute-start.8 = (bf16[6,128,256]{2,1,0:T(8,128)(2,1)S(1)}, bf16[6,128,256]{2,1,0:T(8,128)(2,1)S(1)}, u32[]{:S(2)}, u32[]{:S(2)}) collective-permute-start(bf16[6,128,256]{2,1,0:T(8,128)(2,1)S(1)} %get-tuple-element.46), channel_id=1, source_target_pairs={{0,12},{4,0},{8,4},{12,8},{1,13},{5,1},{9,5},{13,9},{2,14},{6,2},{... | collective-permute-start | bytes 1179656 | tf_op jit(solution)/shard_map/ppermute | solution.py:498
  14.9 0.0 collective-permute-done.1.refs_6_.refs_2_
  14.9 0.9 shard_map.72.refs_5_
  15.8 0.9 collective-permute-start.4
  16.7 1.3 %shard_map.69.refs_6_.refs_1_ = s32[74]{0:T(128)S(1)} custom-call(s32[1,96]{1,0:T(1,128)S(1)} %collective-permute-done.partner.refs_2_), custom_call_target="tpu_custom_call" | custom-call | tf_op jit(solution)/shard_map/pallas_call | solution.py:121
  18.0 0.9 shard_map.73.refs_5_.refs_3_
  18.9 9.7 %collective-permute-done.5.refs_3_.refs_7_ = bf16[24,64,256]{2,1,0:T(8,128)(2,1)S(1)} collective-permute-done((bf16[24,64,256]{2,1,0:T(8,128)(2,1)S(1)}, bf16[24,64,256]{2,1,0:T(8,128)(2,1)S(1)}, u32[]{:S(2)}, u32[]{:S(2)}) %collective-permute-start.5) | collective-permute-done | bytes 786464 | tf_op jit(solution)/shard_map/ppermute | solution.py:506
  28.6 15.3 %collective-permute-done.6.refs_4_.refs_8_ = bf16[24,64,256]{2,1,0:T(8,128)(2,1)S(1)} collective-permute-done((bf16[24,64,256]{2,1,0:T(8,128)(2,1)S(1)}, bf16[24,64,256]{2,1,0:T(8,128)(2,1)S(1)}, u32[]{:S(2)}, u32[]{:S(2)}) %collective-permute-start.6) | collective-permute-done | bytes 786464 | tf_op jit(solution)/shard_map/ppermute | solution.py:506
  43.9 0.9 shard_map.74.refs_0_
  44.9 0.0 copy-start
  44.9 1.6 %collective-permute-start.10 = (bf16[6,128,256]{2,1,0:T(8,128)(2,1)S(1)}, bf16[6,128,256]{2,1,0:T(8,128)(2,1)S(1)}, u32[]{:S(2)}, u32[]{:S(2)}) collective-permute-start(bf16[6,128,256]{2,1,0:T(8,128)(2,1)S(1)} %shard_map.75.refs_5_), channel_id=1, source_target_pairs={{0,4},{4,8},{8,12},{12,0},{1,5},{5,9},{9,13},{13,1},{2,6},{6,10},{... | collective-permute-start | bytes 1179656 | tf_op jit(solution)/shard_map/ppermute | solution.py:498
  46.6 0.9 shard_map.76.refs_4_
  47.5 1.1 %shard_map.77 = (bf16[6,64,256]{2,1,0:T(8,128)(2,1)S(1)}, bf16[6,64,256]{2,1,0:T(8,128)(2,1)S(1)}, bf16[6,64,256]{2,1,0:T(8,128)(2,1)S(1)}, bf16[6,64,256]{2,1,0:T(8,128)(2,1)S(1)}, f32[8,256]{1,0:T(8,128)S(1)}) custom-call(s32[74]{0:T(128)S(1)} %get-tuple-element.39.refs_0_.plan, bf16[1,24,128,256]{3,2,1,0:T(8,128)(2,1)S(1)} %copy-done, ...), custom_call_target="tpu_custom_call" | custom-call | tf_op jit(solution)/shard_map/pallas_call | solution.py:286
  48.6 0.6 collective-permute-start.9
  49.2 1.1 %collective-permute-start.14 = (bf16[6,64,256]{2,1,0:T(8,128)(2,1)S(1)}, bf16[6,64,256]{2,1,0:T(8,128)(2,1)S(1)}, u32[]{:S(2)}, u32[]{:S(2)}) collective-permute-start(bf16[6,64,256]{2,1,0:T(8,128)(2,1)S(1)} %get-tuple-element.49), channel_id=1, source_target_pairs={{0,3},{1,2},{2,1},{3,0},{4,7},{5,6},{6,5},{7,4},{8,11},{9,10},{10,... | collective-permute-start | bytes 589832 | tf_op jit(solution)/shard_map/ppermute | solution.py:506
  50.3 0.9 shard_map.78.refs_5_.refs_0_
  51.3 0.9 shard_map.79.refs_5_.refs_0_
  52.1 0.8 shard_map.80.refs_1_.refs_0_
  52.9 3.5 %collective-permute-done.9.refs_3_.refs_11_.refs_6_ = bf16[6,64,256]{2,1,0:T(8,128)(2,1)S(1)} collective-permute-done((bf16[6,64,256]{2,1,0:T(8,128)(2,1)S(1)}, bf16[6,64,256]{2,1,0:T(8,128)(2,1)S(1)}, u32[]{:S(2)}, u32[]{:S(2)}) %collective-permute-start.9) | collective-permute-done | bytes 196640 | tf_op jit(solution)/shard_map/ppermute | solution.py:506
  56.4 2.5 %collective-permute-start.13 = (bf16[6,128,256]{2,1,0:T(8,128)(2,1)S(1)}, bf16[6,128,256]{2,1,0:T(8,128)(2,1)S(1)}, u32[]{:S(2)}, u32[]{:S(2)}) collective-permute-start(bf16[6,128,256]{2,1,0:T(8,128)(2,1)S(1)} %shard_map.81.refs_1_), channel_id=1, source_target_pairs={{0,12},{4,0},{8,4},{12,8},{1,13},{5,1},{9,5},{13,9},{2,14},{6,2},{... | collective-permute-start | bytes 1179656 | tf_op jit(solution)/shard_map/ppermute | solution.py:498
  58.8 0.0 collective-permute-done.10.refs_2_.refs_4_
  58.8 0.5 collective-permute-done.14.refs_12_.refs_7_
  59.4 1.1 %shard_map.84 = (bf16[6,64,256]{2,1,0:T(8,128)(2,1)S(1)}, bf16[6,64,256]{2,1,0:T(8,128)(2,1)S(1)}, bf16[6,64,256]{2,1,0:T(8,128)(2,1)S(1)}, bf16[6,64,256]{2,1,0:T(8,128)(2,1)S(1)}, f32[8,256]{1,0:T(8,128)S(1)}) custom-call(s32[74]{0:T(128)S(1)} %get-tuple-element.39.refs_0_.plan, bf16[1,24,128,256]{3,2,1,0:T(8,128)(2,1)S(1)} %copy-done, ...), custom_call_target="tpu_custom_call" | custom-call | tf_op jit(solution)/shard_map/pallas_call | solution.py:286
  60.5 0.6 collective-permute-start.15
  61.1 3.2 %collective-permute-start.11 = (bf16[4,128,256]{2,1,0:T(8,128)(2,1)S(1)}, bf16[4,128,256]{2,1,0:T(8,128)(2,1)S(1)}, u32[]{:S(2)}, u32[]{:S(2)}) collective-permute-start(bf16[4,128,256]{2,1,0:T(8,128)(2,1)S(1)} %shard_map.82.refs_10_), channel_id=1, source_target_pairs={{0,8},{4,12},{8,0},{12,4},{1,9},{5,13},{9,1},{13,5},{2,10},{6,14},... | collective-permute-start | bytes 786440 | tf_op jit(solution)/shard_map/ppermute | solution.py:498
  64.3 0.9 collective-permute-start.16
  65.2 3.0 %collective-permute-done.15.refs_10_.refs_9_ = bf16[6,64,256]{2,1,0:T(8,128)(2,1)S(1)} collective-permute-done((bf16[6,64,256]{2,1,0:T(8,128)(2,1)S(1)}, bf16[6,64,256]{2,1,0:T(8,128)(2,1)S(1)}, u32[]{:S(2)}, u32[]{:S(2)}) %collective-permute-start.15) | collective-permute-done | bytes 196640 | tf_op jit(solution)/shard_map/ppermute | solution.py:506
  68.2 0.2 collective-permute-done.13.refs_4_
  68.4 1.1 %shard_map.85 = (bf16[6,64,256]{2,1,0:T(8,128)(2,1)S(1)}, bf16[6,64,256]{2,1,0:T(8,128)(2,1)S(1)}, bf16[6,64,256]{2,1,0:T(8,128)(2,1)S(1)}, bf16[6,64,256]{2,1,0:T(8,128)(2,1)S(1)}, f32[8,256]{1,0:T(8,128)S(1)}) custom-call(s32[74]{0:T(128)S(1)} %get-tuple-element.39.refs_0_.plan, bf16[1,24,128,256]{3,2,1,0:T(8,128)(2,1)S(1)} %copy-done, ...), custom_call_target="tpu_custom_call" | custom-call | tf_op jit(solution)/shard_map/pallas_call | solution.py:286
  69.5 0.6 collective-permute-start.17
  70.1 9.0 %collective-permute-done.11.refs_1_.refs_4_ = bf16[4,128,256]{2,1,0:T(8,128)(2,1)S(1)} collective-permute-done((bf16[4,128,256]{2,1,0:T(8,128)(2,1)S(1)}, bf16[4,128,256]{2,1,0:T(8,128)(2,1)S(1)}, u32[]{:S(2)}, u32[]{:S(2)}) %collective-permute-start.11) | collective-permute-done | bytes 262176 | tf_op jit(solution)/shard_map/ppermute | solution.py:498
  79.0 0.0 copy-start.1
  79.1 0.0 copy-start.2
  79.1 0.9 shard_map.86
  80.0 0.6 collective-permute-start.19
  80.6 0.9 fusion.refs_10_
  81.5 3.4 %collective-permute-done.12.refs_4_ = bf16[2,128,256]{2,1,0:T(8,128)(2,1)S(1)} collective-permute-done((bf16[2,128,256]{2,1,0:T(8,128)(2,1)S(1)}, bf16[2,128,256]{2,1,0:T(8,128)(2,1)S(1)}, u32[]{:S(2)}, u32[]{:S(2)}) %collective-permute-start.12) | collective-permute-done | bytes 131104 | tf_op jit(solution)/shard_map/ppermute | solution.py:498
  84.9 1.5 %collective-permute-done.19.refs_16_.refs_15_ = bf16[4,64,256]{2,1,0:T(8,128)(2,1)S(1)} collective-permute-done((bf16[4,64,256]{2,1,0:T(8,128)(2,1)S(1)}, bf16[4,64,256]{2,1,0:T(8,128)(2,1)S(1)}, u32[]{:S(2)}, u32[]{:S(2)}) %collective-permute-start.19) | collective-permute-done | bytes 131104 | tf_op jit(solution)/shard_map/ppermute | solution.py:506
  86.4 1.0 shard_map.87
  87.4 1.3 %collective-permute-start.21 = (bf16[1552,256]{1,0:T(8,128)(2,1)S(1)}, bf16[1552,256]{1,0:T(8,128)(2,1)S(1)}, u32[]{:S(2)}, u32[]{:S(2)}) collective-permute-start(bf16[1552,256]{1,0:T(8,128)(2,1)S(1)} %get-tuple-element.63), channel_id=1, source_target_pairs={{0,1},{1,0},{2,3},{3,2},{4,5},{5,4},{6,7},{7,6},{8,9},{9,8},{10,11... | collective-permute-start | bytes 2383880 | tf_op jit(solution)/shard_map/ppermute | solution.py:498
  88.7 0.6 collective-permute-start.22
  89.3 0.8 collective-permute-start.23
  90.1 0.5 collective-permute-done.21.refs_4_.refs_0_
  90.6 2.8 %shard_map.88 = (f32[2,24,64,256]{3,2,1,0:T(8,128)S(1)}, f32[2,24,64,256]{3,2,1,0:T(8,128)}) custom-call(s32[74]{0:T(128)S(1)} %get-tuple-element.39.refs_0_.plan, s32[74]{0:T(128)S(1)} %shard_map.69.refs_6_.refs_1_, f32[24]{0:T(128)S(1)} %copy-done.2, bf16[2,24,64,256]{3,2,1,0:T(8,128)(2,1)S(1)} %copy-done.1, ...), custom_call_target="tpu_custom_call" | custom-call | tf_op jit(solution)/shard_map/pallas_call | solution.py:372
  93.4 0.4 collective-permute-done.22.refs_5_.refs_1_
  93.8 0.0 collective-permute-done.23.refs_6_.refs_2_
  93.9 0.6 shard_map.90.refs_0_
  94.4 6.0 %collective-permute-start.24 = (f32[8,256]{1,0:T(8,128)S(1)}, f32[8,256]{1,0:T(8,128)S(1)}, u32[]{:S(2)}, u32[]{:S(2)}) collective-permute-start(f32[8,256]{1,0:T(8,128)S(1)} %shard_map.90.refs_0_), channel_id=1, source_target_pairs={{0,4},{4,8},{8,12},{12,0},{1,5},{5,9},{9,13},{13,1},{2,6},{6,10},{... | collective-permute-start | bytes 24584 | tf_op jit(solution)/shard_map/ppermute | solution.py:498
  100.5 0.3 collective-permute-start.25
  100.7 2.1 %collective-permute-start.26 = (f32[8,256]{1,0:T(8,128)S(1)}, f32[8,256]{1,0:T(8,128)S(1)}, u32[]{:S(2)}, u32[]{:S(2)}) collective-permute-start(f32[8,256]{1,0:T(8,128)S(1)} %shard_map.90.refs_0_), channel_id=1, source_target_pairs={{0,12},{4,0},{8,4},{12,8},{1,13},{5,1},{9,5},{13,9},{2,14},{6,2},{... | collective-permute-start | bytes 24584 | tf_op jit(solution)/shard_map/ppermute | solution.py:498
  102.9 1.5 %shard_map.89 = (f32[2,24,64,256]{3,2,1,0:T(8,128)}, f32[8,128]{1,0:T(8,128)S(1)}) custom-call(s32[74]{0:T(128)S(1)} %get-tuple-element.39.refs_0_.plan, s32[74]{0:T(128)S(1)} %shard_map.69.refs_6_.refs_1_, f32[2,24,64,256]{3,2,1,0:T(8,128)S(1)} %get-tuple-element.69.refs_2_.refs_3_, ...), custom_call_target="tpu_custom_call", output_to_operand_aliasing={{0}: (7, {})} | custom-call | tf_op jit(solution)/shard_map/pallas_call | solution.py:417
  104.4 0.6 collective-permute-done.25.refs_2_
  105.0 0.5 shard_map.91
  (23 shorter events, 0.1 us)
Async XLA Ops:
  0.6 9.1 %collective-permute-start.2 = (bf16[1,24,128,256]{3,2,1,0:T(8,128)(2,1)}, bf16[1,24,128,256]{3,2,1,0:T(8,128)(2,1)S(1)}, u32[]{:S(2)}, u32[]{:S(2)}) collective-permute-start(bf16[1,24,128,256]{3,2,1,0:T(8,128)(2,1)} %right.1), channel_id=1, source_target_pairs={{0,1},{1,0},{2,3},{3,2},{4,5},{5,4},{6,7},{7,6},{8,9},{9,8},{10,11... | collective-permute-start | bytes 4718600 | tf_op jit(solution)/shard_map/ppermute | solution.py:498
  1.1 8.6 %collective-permute-start.3 = (bf16[2,24,64,256]{3,2,1,0:T(8,128)(2,1)}, bf16[2,24,64,256]{3,2,1,0:T(8,128)(2,1)S(1)}, u32[]{:S(2)}, u32[]{:S(2)}) collective-permute-start(bf16[2,24,64,256]{3,2,1,0:T(8,128)(2,1)} %refs_3_.1), channel_id=1, source_target_pairs={{0,1},{1,0},{2,3},{3,2},{4,5},{5,4},{6,7},{7,6},{8,9},{9,8},{10,11... | collective-permute-start | bytes 4718600 | tf_op jit(solution)/shard_map/ppermute | solution.py:498
  1.2 13.6 %collective-permute-start.1 = (bf16[1,24,128,256]{3,2,1,0:T(8,128)(2,1)}, bf16[1,24,128,256]{3,2,1,0:T(8,128)(2,1)S(1)}, u32[]{:S(2)}, u32[]{:S(2)}) collective-permute-start(bf16[1,24,128,256]{3,2,1,0:T(8,128)(2,1)} %refs_1_.9), channel_id=1, source_target_pairs={{0,1},{1,0},{2,3},{3,2},{4,5},{5,4},{6,7},{7,6},{8,9},{9,8},{10,11... | collective-permute-start | bytes 4718600 | tf_op jit(solution)/shard_map/ppermute | solution.py:498
  1.7 6.5 %collective-permute-start = (s32[1,96]{1,0:T(1,128)}, s32[1,96]{1,0:T(1,128)S(1)}, u32[]{:S(2)}, u32[]{:S(2)}) collective-permute-start(s32[1,96]{1,0:T(1,128)} %partner.1), channel_id=1, source_target_pairs={{0,2},{2,0},{1,3},{3,1},{4,6},{6,4},{5,7},{7,5},{8,10},{10,8},{9,1... | collective-permute-start | bytes 1160 | tf_op jit(solution)/shard_map/ppermute | solution.py:498
  4.2 0.7 copy-start.3
  8.2 20.5 %collective-permute-start.5 = (bf16[24,64,256]{2,1,0:T(8,128)(2,1)S(1)}, bf16[24,64,256]{2,1,0:T(8,128)(2,1)S(1)}, u32[]{:S(2)}, u32[]{:S(2)}) collective-permute-start(bf16[24,64,256]{2,1,0:T(8,128)(2,1)S(1)} %get-tuple-element.43.refs_3_.refs_5_), channel_id=1, source_target_pairs={{0,2},{1,3},{2,0},{3,1},{4,6},{5,7},{6,4},{7,5},{8,10},{9,11},{10,... | collective-permute-start | bytes 2359304 | tf_op jit(solution)/shard_map/ppermute | solution.py:506
  8.3 35.7 %collective-permute-start.6 = (bf16[24,64,256]{2,1,0:T(8,128)(2,1)S(1)}, bf16[24,64,256]{2,1,0:T(8,128)(2,1)S(1)}, u32[]{:S(2)}, u32[]{:S(2)}) collective-permute-start(bf16[24,64,256]{2,1,0:T(8,128)(2,1)S(1)} %get-tuple-element.45), channel_id=1, source_target_pairs={{0,3},{1,2},{2,1},{3,0},{4,7},{5,6},{6,5},{7,4},{8,11},{9,10},{10,... | collective-permute-start | bytes 2359304 | tf_op jit(solution)/shard_map/ppermute | solution.py:506
  11.0 33.9 %collective-permute-start.7 = (bf16[6,128,256]{2,1,0:T(8,128)(2,1)S(1)}, bf16[6,128,256]{2,1,0:T(8,128)(2,1)S(1)}, u32[]{:S(2)}, u32[]{:S(2)}) collective-permute-start(bf16[6,128,256]{2,1,0:T(8,128)(2,1)S(1)} %get-tuple-element.44.refs_5_), channel_id=1, source_target_pairs={{0,4},{4,8},{8,12},{12,0},{1,5},{5,9},{9,13},{13,1},{2,6},{6,10},{... | collective-permute-start | bytes 1179656 | tf_op jit(solution)/shard_map/ppermute | solution.py:498
  12.6 32.3 %collective-permute-start.8 = (bf16[6,128,256]{2,1,0:T(8,128)(2,1)S(1)}, bf16[6,128,256]{2,1,0:T(8,128)(2,1)S(1)}, u32[]{:S(2)}, u32[]{:S(2)}) collective-permute-start(bf16[6,128,256]{2,1,0:T(8,128)(2,1)S(1)} %get-tuple-element.46), channel_id=1, source_target_pairs={{0,12},{4,0},{8,4},{12,8},{1,13},{5,1},{9,5},{13,9},{2,14},{6,2},{... | collective-permute-start | bytes 1179656 | tf_op jit(solution)/shard_map/ppermute | solution.py:498
  15.8 37.1 %collective-permute-start.4 = (bf16[6,128,256]{2,1,0:T(8,128)(2,1)S(1)}, bf16[6,128,256]{2,1,0:T(8,128)(2,1)S(1)}, u32[]{:S(2)}, u32[]{:S(2)}) collective-permute-start(bf16[6,128,256]{2,1,0:T(8,128)(2,1)S(1)} %shard_map.72.refs_5_), channel_id=1, source_target_pairs={{0,8},{4,12},{8,0},{12,4},{1,9},{5,13},{9,1},{13,5},{2,10},{6,14},... | collective-permute-start | bytes 1179656 | tf_op jit(solution)/shard_map/ppermute | solution.py:498
  44.9 2.6 %copy-start = (bf16[1,24,128,256]{3,2,1,0:T(8,128)(2,1)S(1)}, bf16[1,24,128,256]{3,2,1,0:T(8,128)(2,1)}, u32[]{:S(2)}) copy-start(bf16[1,24,128,256]{3,2,1,0:T(8,128)(2,1)} %refs_1_.9) | copy-start | bytes 4718596
  44.9 13.9 %collective-permute-start.10 = (bf16[6,128,256]{2,1,0:T(8,128)(2,1)S(1)}, bf16[6,128,256]{2,1,0:T(8,128)(2,1)S(1)}, u32[]{:S(2)}, u32[]{:S(2)}) collective-permute-start(bf16[6,128,256]{2,1,0:T(8,128)(2,1)S(1)} %shard_map.75.refs_5_), channel_id=1, source_target_pairs={{0,4},{4,8},{8,12},{12,0},{1,5},{5,9},{9,13},{13,1},{2,6},{6,10},{... | collective-permute-start | bytes 1179656 | tf_op jit(solution)/shard_map/ppermute | solution.py:498
  48.6 7.8 %collective-permute-start.9 = (bf16[6,64,256]{2,1,0:T(8,128)(2,1)S(1)}, bf16[6,64,256]{2,1,0:T(8,128)(2,1)S(1)}, u32[]{:S(2)}, u32[]{:S(2)}) collective-permute-start(bf16[6,64,256]{2,1,0:T(8,128)(2,1)S(1)} %get-tuple-element.48), channel_id=1, source_target_pairs={{0,2},{1,3},{2,0},{3,1},{4,6},{5,7},{6,4},{7,5},{8,10},{9,11},{10,... | collective-permute-start | bytes 589832 | tf_op jit(solution)/shard_map/ppermute | solution.py:506
  49.2 10.2 %collective-permute-start.14 = (bf16[6,64,256]{2,1,0:T(8,128)(2,1)S(1)}, bf16[6,64,256]{2,1,0:T(8,128)(2,1)S(1)}, u32[]{:S(2)}, u32[]{:S(2)}) collective-permute-start(bf16[6,64,256]{2,1,0:T(8,128)(2,1)S(1)} %get-tuple-element.49), channel_id=1, source_target_pairs={{0,3},{1,2},{2,1},{3,0},{4,7},{5,6},{6,5},{7,4},{8,11},{9,10},{10,... | collective-permute-start | bytes 589832 | tf_op jit(solution)/shard_map/ppermute | solution.py:506
  56.4 12.0 %collective-permute-start.13 = (bf16[6,128,256]{2,1,0:T(8,128)(2,1)S(1)}, bf16[6,128,256]{2,1,0:T(8,128)(2,1)S(1)}, u32[]{:S(2)}, u32[]{:S(2)}) collective-permute-start(bf16[6,128,256]{2,1,0:T(8,128)(2,1)S(1)} %shard_map.81.refs_1_), channel_id=1, source_target_pairs={{0,12},{4,0},{8,4},{12,8},{1,13},{5,1},{9,5},{13,9},{2,14},{6,2},{... | collective-permute-start | bytes 1179656 | tf_op jit(solution)/shard_map/ppermute | solution.py:498
  60.5 7.8 %collective-permute-start.15 = (bf16[6,64,256]{2,1,0:T(8,128)(2,1)S(1)}, bf16[6,64,256]{2,1,0:T(8,128)(2,1)S(1)}, u32[]{:S(2)}, u32[]{:S(2)}) collective-permute-start(bf16[6,64,256]{2,1,0:T(8,128)(2,1)S(1)} %get-tuple-element.51), channel_id=1, source_target_pairs={{0,2},{1,3},{2,0},{3,1},{4,6},{5,7},{6,4},{7,5},{8,10},{9,11},{10,... | collective-permute-start | bytes 589832 | tf_op jit(solution)/shard_map/ppermute | solution.py:506
  61.1 18.0 %collective-permute-start.11 = (bf16[4,128,256]{2,1,0:T(8,128)(2,1)S(1)}, bf16[4,128,256]{2,1,0:T(8,128)(2,1)S(1)}, u32[]{:S(2)}, u32[]{:S(2)}) collective-permute-start(bf16[4,128,256]{2,1,0:T(8,128)(2,1)S(1)} %shard_map.82.refs_10_), channel_id=1, source_target_pairs={{0,8},{4,12},{8,0},{12,4},{1,9},{5,13},{9,1},{13,5},{2,10},{6,14},... | collective-permute-start | bytes 786440 | tf_op jit(solution)/shard_map/ppermute | solution.py:498
  64.3 14.7 %collective-permute-start.16 = (bf16[6,64,256]{2,1,0:T(8,128)(2,1)S(1)}, bf16[6,64,256]{2,1,0:T(8,128)(2,1)S(1)}, u32[]{:S(2)}, u32[]{:S(2)}) collective-permute-start(bf16[6,64,256]{2,1,0:T(8,128)(2,1)S(1)} %get-tuple-element.53), channel_id=1, source_target_pairs={{0,3},{1,2},{2,1},{3,0},{4,7},{5,6},{6,5},{7,4},{8,11},{9,10},{10,... | collective-permute-start | bytes 589832 | tf_op jit(solution)/shard_map/ppermute | solution.py:506
  69.5 9.6 %collective-permute-start.17 = (bf16[6,64,256]{2,1,0:T(8,128)(2,1)S(1)}, bf16[6,64,256]{2,1,0:T(8,128)(2,1)S(1)}, u32[]{:S(2)}, u32[]{:S(2)}) collective-permute-start(bf16[6,64,256]{2,1,0:T(8,128)(2,1)S(1)} %get-tuple-element.54), channel_id=1, source_target_pairs={{0,2},{1,3},{2,0},{3,1},{4,6},{5,7},{6,4},{7,5},{8,10},{9,11},{10,... | collective-permute-start | bytes 589832 | tf_op jit(solution)/shard_map/ppermute | solution.py:506
  70.1 14.8 %collective-permute-start.18 = (bf16[6,64,256]{2,1,0:T(8,128)(2,1)S(1)}, bf16[6,64,256]{2,1,0:T(8,128)(2,1)S(1)}, u32[]{:S(2)}, u32[]{:S(2)}) collective-permute-start(bf16[6,64,256]{2,1,0:T(8,128)(2,1)S(1)} %get-tuple-element.60), channel_id=1, source_target_pairs={{0,3},{1,2},{2,1},{3,0},{4,7},{5,6},{6,5},{7,4},{8,11},{9,10},{10,... | collective-permute-start | bytes 589832 | tf_op jit(solution)/shard_map/ppermute | solution.py:506
  79.0 5.9 %collective-permute-start.12 = (bf16[2,128,256]{2,1,0:T(8,128)(2,1)S(1)}, bf16[2,128,256]{2,1,0:T(8,128)(2,1)S(1)}, u32[]{:S(2)}, u32[]{:S(2)}) collective-permute-start(bf16[2,128,256]{2,1,0:T(8,128)(2,1)S(1)} %shard_map.83.refs_10_), channel_id=1, source_target_pairs={{0,8},{4,12},{8,0},{12,4},{1,9},{5,13},{9,1},{13,5},{2,10},{6,14},... | collective-permute-start | bytes 393224 | tf_op jit(solution)/shard_map/ppermute | solution.py:498
  79.0 1.6 %copy-start.1 = (bf16[2,24,64,256]{3,2,1,0:T(8,128)(2,1)S(1)}, bf16[2,24,64,256]{3,2,1,0:T(8,128)(2,1)}, u32[]{:S(2)}) copy-start(bf16[2,24,64,256]{3,2,1,0:T(8,128)(2,1)} %refs_3_.1) | copy-start | bytes 4718596
  79.1 1.6 %copy-start.2 = (f32[24]{0:T(128)S(1)}, f32[24]{0:T(128)}, u32[]{:S(2)}) copy-start(f32[24]{0:T(128)} %refs_2_.1) | copy-start | bytes 292
  80.0 6.4 %collective-permute-start.19 = (bf16[4,64,256]{2,1,0:T(8,128)(2,1)S(1)}, bf16[4,64,256]{2,1,0:T(8,128)(2,1)S(1)}, u32[]{:S(2)}, u32[]{:S(2)}) collective-permute-start(bf16[4,64,256]{2,1,0:T(8,128)(2,1)S(1)} %get-tuple-element.61), channel_id=1, source_target_pairs={{0,2},{1,3},{2,0},{3,1},{4,6},{5,7},{6,4},{7,5},{8,10},{9,11},{10,... | collective-permute-start | bytes 393224 | tf_op jit(solution)/shard_map/ppermute | solution.py:506
  80.6 5.8 %collective-permute-start.20 = (bf16[4,64,256]{2,1,0:T(8,128)(2,1)S(1)}, bf16[4,64,256]{2,1,0:T(8,128)(2,1)S(1)}, u32[]{:S(2)}, u32[]{:S(2)}) collective-permute-start(bf16[4,64,256]{2,1,0:T(8,128)(2,1)S(1)} %get-tuple-element.62), channel_id=1, source_target_pairs={{0,3},{1,2},{2,1},{3,0},{4,7},{5,6},{6,5},{7,4},{8,11},{9,10},{10,... | collective-permute-start | bytes 393224 | tf_op jit(solution)/shard_map/ppermute | solution.py:506
  87.4 3.2 %collective-permute-start.21 = (bf16[1552,256]{1,0:T(8,128)(2,1)S(1)}, bf16[1552,256]{1,0:T(8,128)(2,1)S(1)}, u32[]{:S(2)}, u32[]{:S(2)}) collective-permute-start(bf16[1552,256]{1,0:T(8,128)(2,1)S(1)} %get-tuple-element.63), channel_id=1, source_target_pairs={{0,1},{1,0},{2,3},{3,2},{4,5},{5,4},{6,7},{7,6},{8,9},{9,8},{10,11... | collective-permute-start | bytes 2383880 | tf_op jit(solution)/shard_map/ppermute | solution.py:498
  88.7 5.1 %collective-permute-start.22 = (bf16[144,256]{1,0:T(8,128)(2,1)S(1)}, bf16[144,256]{1,0:T(8,128)(2,1)S(1)}, u32[]{:S(2)}, u32[]{:S(2)}) collective-permute-start(bf16[144,256]{1,0:T(8,128)(2,1)S(1)} %get-tuple-element.71), channel_id=1, source_target_pairs={{0,2},{1,3},{2,0},{3,1},{4,6},{5,7},{6,4},{7,5},{8,10},{9,11},{10,... | collective-permute-start | bytes 221192 | tf_op jit(solution)/shard_map/ppermute | solution.py:506
  89.3 4.6 %collective-permute-start.23 = (bf16[144,256]{1,0:T(8,128)(2,1)S(1)}, bf16[144,256]{1,0:T(8,128)(2,1)S(1)}, u32[]{:S(2)}, u32[]{:S(2)}) collective-permute-start(bf16[144,256]{1,0:T(8,128)(2,1)S(1)} %get-tuple-element.72), channel_id=1, source_target_pairs={{0,3},{1,2},{2,1},{3,0},{4,7},{5,6},{6,5},{7,4},{8,11},{9,10},{10,... | collective-permute-start | bytes 221192 | tf_op jit(solution)/shard_map/ppermute | solution.py:506
  94.4 10.0 %collective-permute-start.24 = (f32[8,256]{1,0:T(8,128)S(1)}, f32[8,256]{1,0:T(8,128)S(1)}, u32[]{:S(2)}, u32[]{:S(2)}) collective-permute-start(f32[8,256]{1,0:T(8,128)S(1)} %shard_map.90.refs_0_), channel_id=1, source_target_pairs={{0,4},{4,8},{8,12},{12,0},{1,5},{5,9},{9,13},{13,1},{2,6},{6,10},{... | collective-permute-start | bytes 24584 | tf_op jit(solution)/shard_map/ppermute | solution.py:498
  100.5 4.5 %collective-permute-start.25 = (f32[8,256]{1,0:T(8,128)S(1)}, f32[8,256]{1,0:T(8,128)S(1)}, u32[]{:S(2)}, u32[]{:S(2)}) collective-permute-start(f32[8,256]{1,0:T(8,128)S(1)} %shard_map.90.refs_0_), channel_id=1, source_target_pairs={{0,8},{4,12},{8,0},{12,4},{1,9},{5,13},{9,1},{13,5},{2,10},{6,14},... | collective-permute-start | bytes 24584 | tf_op jit(solution)/shard_map/ppermute | solution.py:498
  100.7 4.3 %collective-permute-start.26 = (f32[8,256]{1,0:T(8,128)S(1)}, f32[8,256]{1,0:T(8,128)S(1)}, u32[]{:S(2)}, u32[]{:S(2)}) collective-permute-start(f32[8,256]{1,0:T(8,128)S(1)} %shard_map.90.refs_0_), channel_id=1, source_target_pairs={{0,12},{4,0},{8,4},{12,8},{1,13},{5,1},{9,5},{13,9},{2,14},{6,2},{... | collective-permute-start | bytes 24584 | tf_op jit(solution)/shard_map/ppermute | solution.py:498
